TPU v7x, 32 devices: a whole 2x2x4 slice. The times are simulated.
32 devices in a mesh: dp: 8 (over z, core), tensor: 4 (over y, x).
Axes of the slice: x: 2, y: 2, z: 4, core: 2. Of those that a mesh axis runs over, the one named last changes fastest.
Arguments:
- tokens: bfloat16 [16384, 2048], P(('dp', 'tensor')), may hold values from -6 to 6
- cotangent: bfloat16 [16384, 2048], P(('dp', 'tensor')), may hold values from -6 to 6
- segment: int32 [16384], P('dp'), may hold values from -1 to 2, as said below
- first_gain: float32 [2048], replicated, may hold values from 0.1 to 1.9
- first_bias: float32 [2048], replicated, may hold values from -2 to 2
- query_weight: bfloat16 [2048, 2048], P('dp', 'tensor'), may hold values from -0.125 to 0.125
- key_weight: bfloat16 [2048, 2048], P('dp', 'tensor'), may hold values from -0.125 to 0.125
- value_weight: bfloat16 [2048, 4096], P('dp', 'tensor'), may hold values from -0.125 to 0.125
- gate_weight: bfloat16 [2048, 4096], P('dp', 'tensor'), may hold values from -0.125 to 0.125
- out_weight: bfloat16 [4096, 2048], P('tensor', 'dp'), may hold values from -0.09375 to 0.09375
- second_gain: float32 [2048], replicated, may hold values from 0.1 to 1.9
- second_bias: float32 [2048], replicated, may hold values from -2 to 2
- up_weight: bfloat16 [2048, 4096], P('dp', 'tensor'), may hold values from -0.125 to 0.125
- down_weight: bfloat16 [4096, 2048], P('tensor', 'dp'), may hold values from -0.09375 to 0.09375
Outputs:
- block_output: bfloat16 [16384, 2048], P(('dp', 'tensor'))
- tokens_grad: bfloat16 [16384, 2048], P(('dp', 'tensor'))
- first_gain_grad: float32 [2048], P(('dp', 'tensor'))
- first_bias_grad: float32 [2048], P(('dp', 'tensor'))
- query_weight_grad: float32 [2048, 2048], P('dp', 'tensor')
- key_weight_grad: float32 [2048, 2048], P('dp', 'tensor')
- value_weight_grad: float32 [2048, 4096], P('dp', 'tensor')
- gate_weight_grad: float32 [2048, 4096], P('dp', 'tensor')
- out_weight_grad: float32 [4096, 2048], P('tensor', 'dp')
- second_gain_grad: float32 [2048], P(('dp', 'tensor'))
- second_bias_grad: float32 [2048], P(('dp', 'tensor'))
- up_weight_grad: float32 [2048, 4096], P('dp', 'tensor')
- down_weight_grad: float32 [4096, 2048], P('tensor', 'dp')
Inputs may be any that keep to these rules, and one draw needn't show every extreme that they name: `segment`: in each aligned block of 2048 rows, sequence ids 0, 1 and 2 in this order, each on a run of 128 rows or more, then -1 (padding, one row or more) to the block's end; sequence 1 starts within the block's first 512 rows and ends within its last 512 rows.
All inputs are finite; a program needn't handle non-finite values.
Results may differ from a plain program's by a relative error of at most 0.02.
Values may be sent and summed in bfloat16 or wider, within the bound.
A program may use at most 320 MiB of HBM per device.

v0:
```python
import jax
import jax.numpy as jnp
from jax import lax
from jax.sharding import PartitionSpec as P

KEY = 256
VAL = 512
BLOCK = 512


norm_epsilon = 1e-05
group_floor = 0.5


def layer_norm(values, norm_gain, norm_bias):
    average = jnp.mean(values, axis=-1, keepdims=True)
    centred = values - average
    variance = jnp.mean(centred * centred, axis=-1, keepdims=True)
    return centred * lax.rsqrt(variance + norm_epsilon) * norm_gain + norm_bias


def gelu_tanh(values):
    return jax.nn.gelu(values, approximate=True)


def positions_of(segments):
    length_all = segments.shape[0]
    row_index = jnp.arange(length_all, dtype=jnp.int32)
    boundary = jnp.concatenate(
        [jnp.ones((1,), jnp.int32), (segments[1:] != segments[:-1]).astype(jnp.int32)]
    )
    run_start = lax.cummax(jnp.where(boundary > 0, row_index, 0), axis=0)
    return row_index - run_start


def angle_tables(positions, half_width):
    frequency = jnp.exp(-jnp.log(10000.0) * jnp.arange(half_width, dtype=jnp.float32) / half_width)
    angles = positions.astype(jnp.float32)[:, None] * frequency[None, :]
    return (jnp.cos(angles)[:, None, :], jnp.sin(angles)[:, None, :])


def rotate(stacked, positions):
    half_width = stacked.shape[-1] // 2
    cosine, sine_part = angle_tables(positions, half_width)
    first_half = stacked[..., :half_width]
    second_half = stacked[..., half_width:]
    return jnp.concatenate(
        [
            first_half * cosine - second_half * sine_part,
            second_half * cosine + first_half * sine_part,
        ],
        axis=-1,
    )


def unrotate(stacked, positions):
    half_width = stacked.shape[-1] // 2
    cosine, sine_part = angle_tables(positions, half_width)
    first_half = stacked[..., :half_width]
    second_half = stacked[..., half_width:]
    return jnp.concatenate(
        [
            first_half * cosine + second_half * sine_part,
            second_half * cosine - first_half * sine_part,
        ],
        axis=-1,
    )


def decay_mask(row_ids, segment_rows, segment_all, log_decay):
    col_ids = jnp.arange(segment_all.shape[0], dtype=jnp.int32)
    distance = row_ids[:, None] - col_ids[None, :]
    linked = (
        (distance >= 0)
        & (segment_rows[:, None] == segment_all[None, :])
        & (segment_rows[:, None] >= 0)
    )
    exponent = jnp.where(linked, distance, 0).astype(jnp.float32)
    weight = jnp.exp(log_decay[:, None, None] * exponent[None])
    return jnp.where(linked[None], weight, 0.0)


def gate_group(gate_raw, retained):
    centred = retained - jnp.mean(retained, axis=-1, keepdims=True)
    grouped = centred * lax.rsqrt(jnp.mean(centred * centred, axis=-1, keepdims=True) + group_floor)
    return jax.nn.silu(gate_raw) * grouped.reshape(gate_raw.shape)


def matmul_transposed(left, right):
    return lax.dot_general(
        left, right, (((1,), (1,)), ((), ())), preferred_element_type=jnp.float32
    )


def transposed_matmul(left, right):
    return lax.dot_general(
        left, right, (((0,), (0,)), ((), ())), preferred_element_type=jnp.float32
    )


def body(
    tokens,
    cotangent,
    segment,
    first_gain,
    first_bias,
    query_weight,
    key_weight,
    value_weight,
    gate_weight,
    out_weight,
    second_gain,
    second_bias,
    up_weight,
    down_weight,
):
    fetched = (
        lax.all_gather(query_weight, "dp", axis=0, tiled=True),
        lax.all_gather(key_weight, "dp", axis=0, tiled=True),
        lax.all_gather(value_weight, "dp", axis=0, tiled=True),
        lax.all_gather(gate_weight, "dp", axis=0, tiled=True),
        lax.all_gather(up_weight, "dp", axis=0, tiled=True),
        lax.all_gather(out_weight, "dp", axis=1, tiled=True),
        lax.all_gather(down_weight, "dp", axis=1, tiled=True),
    )
    heads_here = query_weight.shape[1] // KEY
    key_cols = heads_here * KEY
    value_cols = heads_here * VAL
    joined_in = jnp.concatenate([fetched[0], fetched[1], fetched[2], fetched[3]], axis=1)
    tok_rows = tokens.astype(jnp.float32)
    normed1_exact, norm1_pull = jax.vjp(layer_norm, tok_rows, first_gain, first_bias)
    normed1_all = lax.all_gather(normed1_exact.astype(jnp.bfloat16), "tensor", axis=0, tiled=True)
    projected = jnp.dot(normed1_all, joined_in, preferred_element_type=jnp.float32)
    buffer_rows = projected.shape[0]
    positions = positions_of(segment)
    query_raw = projected[:, :key_cols].reshape(buffer_rows, heads_here, KEY)
    key_raw = projected[:, key_cols : 2 * key_cols].reshape(buffer_rows, heads_here, KEY)
    value_low = (
        projected[:, 2 * key_cols : 2 * key_cols + value_cols]
        .astype(jnp.bfloat16)
        .reshape(buffer_rows, heads_here, VAL)
    )
    gate_raw = projected[:, 2 * key_cols + value_cols :]
    key_scale = KEY ** (-0.5)
    query_low = rotate(query_raw, positions).astype(jnp.bfloat16)
    key_low = (rotate(key_raw, positions) * key_scale).astype(jnp.bfloat16)
    head_ids = (
        lax.axis_index("tensor") * heads_here + jnp.arange(heads_here, dtype=jnp.int32)
    ).astype(jnp.float32)
    log_decay = jnp.log1p(-jnp.exp2(-5.0 - head_ids))
    starts = jnp.arange(buffer_rows // BLOCK, dtype=jnp.int32) * BLOCK

    def weights_at(offset):
        row_ids = offset + jnp.arange(BLOCK, dtype=jnp.int32)
        query_block = lax.dynamic_slice_in_dim(query_low, offset, BLOCK, 0)
        segment_block = lax.dynamic_slice_in_dim(segment, offset, BLOCK, 0)
        scores = jnp.einsum(
            "qhk,nhk->hqn", query_block, key_low, preferred_element_type=jnp.float32
        )
        masking = decay_mask(row_ids, segment_block, segment, log_decay)
        return (query_block, masking, scores)

    def forward_block(offset):
        block_parts = weights_at(offset)
        weights = (block_parts[1] * block_parts[2]).astype(jnp.bfloat16)
        return jnp.einsum("hqn,nhv->qhv", weights, value_low, preferred_element_type=jnp.float32)

    retained = lax.map(forward_block, starts).reshape(buffer_rows, heads_here, VAL)
    gated_exact, gate_pull = jax.vjp(gate_group, gate_raw, retained)
    gated = gated_exact.astype(jnp.bfloat16)
    branch_out = lax.psum_scatter(
        jnp.dot(gated, fetched[5], preferred_element_type=jnp.float32).astype(jnp.bfloat16),
        "tensor",
        scatter_dimension=0,
        tiled=True,
    ).astype(jnp.float32)
    mixed = tok_rows + branch_out
    normed2_exact, norm2_pull = jax.vjp(layer_norm, mixed, second_gain, second_bias)
    normed2_all = lax.all_gather(normed2_exact.astype(jnp.bfloat16), "tensor", axis=0, tiled=True)
    up_field = jnp.dot(normed2_all, fetched[4], preferred_element_type=jnp.float32)
    hidden_exact, gelu_pull = jax.vjp(gelu_tanh, up_field)
    hidden = hidden_exact.astype(jnp.bfloat16)
    ffn_out = lax.psum_scatter(
        jnp.dot(hidden, fetched[6], preferred_element_type=jnp.float32).astype(jnp.bfloat16),
        "tensor",
        scatter_dimension=0,
        tiled=True,
    ).astype(jnp.float32)
    result = (mixed + ffn_out).astype(jnp.bfloat16)
    regathered = (
        lax.all_gather(query_weight, "dp", axis=0, tiled=True),
        lax.all_gather(key_weight, "dp", axis=0, tiled=True),
        lax.all_gather(value_weight, "dp", axis=0, tiled=True),
        lax.all_gather(gate_weight, "dp", axis=0, tiled=True),
        lax.all_gather(up_weight, "dp", axis=0, tiled=True),
        lax.all_gather(out_weight, "dp", axis=1, tiled=True),
        lax.all_gather(down_weight, "dp", axis=1, tiled=True),
    )
    joined_back = jnp.concatenate(
        [regathered[0], regathered[1], regathered[2], regathered[3]], axis=1
    )
    cot_all = lax.all_gather(cotangent, "tensor", axis=0, tiled=True)
    hidden_grad = matmul_transposed(cot_all, regathered[6])
    down_grad_part = transposed_matmul(hidden, cot_all)
    up_grad = gelu_pull(hidden_grad)[0].astype(jnp.bfloat16)
    up_grad_part = transposed_matmul(normed2_all, up_grad)
    normed2_grad = lax.psum_scatter(
        matmul_transposed(up_grad, regathered[4]).astype(jnp.bfloat16),
        "tensor",
        scatter_dimension=0,
        tiled=True,
    ).astype(jnp.float32)
    mixed_part, gain2_grad, bias2_grad = norm2_pull(normed2_grad)
    mixed_grad = mixed_part + cotangent.astype(jnp.float32)
    mixed_all = lax.all_gather(mixed_grad.astype(jnp.bfloat16), "tensor", axis=0, tiled=True)
    gated_grad = matmul_transposed(mixed_all, regathered[5])
    out_grad_part = transposed_matmul(gated, mixed_all)
    gate_grad, retained_grad = gate_pull(gated_grad)
    gate_low = gate_grad.astype(jnp.bfloat16)
    retained_low = retained_grad.astype(jnp.bfloat16)

    def backward_block(totals, offset):
        value_total, key_total = totals
        query_block, masking, scores = weights_at(offset)
        weights = (masking * scores).astype(jnp.bfloat16)
        output_block = lax.dynamic_slice_in_dim(retained_low, offset, BLOCK, 0)
        value_total = value_total + jnp.einsum(
            "hqn,qhv->nhv", weights, output_block, preferred_element_type=jnp.float32
        )
        weight_grad = jnp.einsum(
            "qhv,nhv->hqn", output_block, value_low, preferred_element_type=jnp.float32
        )
        score_grad = (masking * weight_grad).astype(jnp.bfloat16)
        key_total = key_total + jnp.einsum(
            "hqn,qhk->nhk", score_grad, query_block, preferred_element_type=jnp.float32
        )
        query_part = jnp.einsum(
            "hqn,nhk->qhk", score_grad, key_low, preferred_element_type=jnp.float32
        )
        return ((value_total, key_total), query_part)

    value_zeros = jnp.zeros((buffer_rows, heads_here, VAL), jnp.float32)
    key_zeros = jnp.zeros((buffer_rows, heads_here, KEY), jnp.float32)
    (value_grad, key_grad), query_grad = lax.scan(backward_block, (value_zeros, key_zeros), starts)
    query_grad = query_grad.reshape(buffer_rows, heads_here, KEY)
    query_grad_low = (
        unrotate(query_grad, positions).astype(jnp.bfloat16).reshape(buffer_rows, key_cols)
    )
    key_grad_low = (
        (unrotate(key_grad, positions) * key_scale)
        .astype(jnp.bfloat16)
        .reshape(buffer_rows, key_cols)
    )
    value_grad_low = value_grad.astype(jnp.bfloat16).reshape(buffer_rows, value_cols)
    joined_grad = jnp.concatenate([query_grad_low, key_grad_low, value_grad_low, gate_low], axis=1)
    joined_weight_grad = transposed_matmul(normed1_all, joined_grad)
    normed1_grad = lax.psum_scatter(
        matmul_transposed(joined_grad, joined_back).astype(jnp.bfloat16),
        "tensor",
        scatter_dimension=0,
        tiled=True,
    ).astype(jnp.float32)
    input_part, gain1_grad, bias1_grad = norm1_pull(normed1_grad)
    input_grad = (input_part + mixed_grad).astype(jnp.bfloat16)
    query_grad_part = joined_weight_grad[:, :key_cols]
    key_grad_part = joined_weight_grad[:, key_cols : 2 * key_cols]
    value_grad_part = joined_weight_grad[:, 2 * key_cols : 2 * key_cols + value_cols]
    gate_grad_part = joined_weight_grad[:, 2 * key_cols + value_cols :]
    summed = (
        lax.psum_scatter(
            query_grad_part.astype(jnp.bfloat16), "dp", scatter_dimension=0, tiled=True
        ).astype(jnp.float32),
        lax.psum_scatter(
            key_grad_part.astype(jnp.bfloat16), "dp", scatter_dimension=0, tiled=True
        ).astype(jnp.float32),
        lax.psum_scatter(
            value_grad_part.astype(jnp.bfloat16), "dp", scatter_dimension=0, tiled=True
        ).astype(jnp.float32),
        lax.psum_scatter(
            gate_grad_part.astype(jnp.bfloat16), "dp", scatter_dimension=0, tiled=True
        ).astype(jnp.float32),
        lax.psum_scatter(
            up_grad_part.astype(jnp.bfloat16), "dp", scatter_dimension=0, tiled=True
        ).astype(jnp.float32),
        lax.psum_scatter(
            out_grad_part.astype(jnp.bfloat16), "dp", scatter_dimension=1, tiled=True
        ).astype(jnp.float32),
        lax.psum_scatter(
            down_grad_part.astype(jnp.bfloat16), "dp", scatter_dimension=1, tiled=True
        ).astype(jnp.float32),
    )
    norm_sums = (
        lax.psum_scatter(gain1_grad, ("dp", "tensor"), scatter_dimension=0, tiled=True),
        lax.psum_scatter(bias1_grad, ("dp", "tensor"), scatter_dimension=0, tiled=True),
        lax.psum_scatter(gain2_grad, ("dp", "tensor"), scatter_dimension=0, tiled=True),
        lax.psum_scatter(bias2_grad, ("dp", "tensor"), scatter_dimension=0, tiled=True),
    )
    return (
        result,
        input_grad,
        norm_sums[0],
        norm_sums[1],
        summed[0],
        summed[1],
        summed[2],
        summed[3],
        summed[5],
        norm_sums[2],
        norm_sums[3],
        summed[4],
        summed[6],
    )


def solution(mesh):
    placed = (
        P(("dp", "tensor"), None),
        P(("dp", "tensor"), None),
        P("dp"),
        P(),
        P(),
        P("dp", "tensor"),
        P("dp", "tensor"),
        P("dp", "tensor"),
        P("dp", "tensor"),
        P("tensor", "dp"),
        P(),
        P(),
        P("dp", "tensor"),
        P("tensor", "dp"),
    )
    return jax.shard_map(
        body,
        mesh=mesh,
        in_specs=placed,
        out_specs=(
            P(("dp", "tensor"), None),
            P(("dp", "tensor"), None),
            P(("dp", "tensor")),
            P(("dp", "tensor")),
            P("dp", "tensor"),
            P("dp", "tensor"),
            P("dp", "tensor"),
            P("dp", "tensor"),
            P("tensor", "dp"),
            P(("dp", "tensor")),
            P(("dp", "tensor")),
            P("dp", "tensor"),
            P("tensor", "dp"),
        ),
        check_vma=False,
    )
```

profile of v0, /device:TPU:0, one launch (start us, length us, event | category | flops | bytes accessed | tf_op | source)
XLA Modules:
  0.0 1777.5 jit_solution(17197856075165018354)
XLA Ops:
  20.1 21.4 %all-gather.14.cloned.1.call-done = bf16[2048,512]{1,0:T(8,128)(2,1)} async-done(((bf16[256,512]{1,0:T(8,128)(2,1)}), bf16[2048,512]{1,0:T(8,128)(2,1)}) %all-gather.14.cloned.1.call-update) | async-done | bytes 2097168 | tf_op jit(solution)/shard_map/all_gather | solution.py:118
  44.6 27.1 %all-gather.16.cloned.1.call-done = bf16[2048,512]{1,0:T(8,128)(2,1)} async-done(((bf16[256,512]{1,0:T(8,128)(2,1)}), bf16[2048,512]{1,0:T(8,128)(2,1)}) %all-gather.16.cloned.1.call-update) | async-done | bytes 2097168 | tf_op jit(solution)/shard_map/all_gather | solution.py:119
  74.9 45.1 %all-gather.18.cloned.1.call-done = bf16[2048,1024]{1,0:T(8,128)(2,1)} async-done(((bf16[256,1024]{1,0:T(8,128)(2,1)}), bf16[2048,1024]{1,0:T(8,128)(2,1)}) %all-gather.18.cloned.1.call-update) | async-done | bytes 4194320 | tf_op jit(solution)/shard_map/all_gather | solution.py:120
  124.7 42.7 %all-gather.20.cloned.1.call-done = bf16[2048,1024]{1,0:T(8,128)(2,1)} async-done(((bf16[256,1024]{1,0:T(8,128)(2,1)}), bf16[2048,1024]{1,0:T(8,128)(2,1)}) %all-gather.20.cloned.1.call-update) | async-done | bytes 4194320 | tf_op jit(solution)/shard_map/all_gather | solution.py:121
  172.2 83.8 %all-gather.12.cloned.1.call-done = bf16[2048,2048]{1,0:T(8,128)(2,1)} async-done(((bf16[512,2048]{1,0:T(8,128)(2,1)}), bf16[2048,2048]{1,0:T(8,128)(2,1)}) %all-gather.12.cloned.1.call-update) | async-done | bytes 8388624 | tf_op jit(solution)/shard_map/all_gather | solution.py:132
  256.0 34.2 %fusion.74 = f32[2048,3072]{1,0:T(8,128)} fusion(bf16[2048,2048]{1,0:T(8,128)(2,1)} %all-gather.12.cloned.1.call-done, bf16[2048,3072]{1,0:T(8,128)(2,1)} %constant_dynamic-update-slice_fusion), kind=kOutput, calls=%fused_computation.161 | convolution fusion | flops 25769803776 | bytes 46137344 | tf_op jit(solution)/shard_map/dot_general | solution.py:133
  290.2 7.8 fusion.69
  298.1 6.2 slice.122
  310.1 5.9 reshape.483
  328.6 69.0 %while.26 = (s32[]{:T(128)}, f32[4,512,2,512]{3,1,2,0:T(8,128)}, s32[4]{0:T(128)S(1)}, s32[2048]{0:T(1024)S(1)}, bf16[2048,2,256]{2,0,1:T(8,128)(2,1)}, /*index=...) while((s32[]{:T(128)}, f32[4,512,2,512]{3,1,2,0:T(8,128)}, ...), condition=%wide.region_5.6_spmd.clone, body=%wide.region_4.5_spmd.clone.sunk | while | flops 3242198016 | bytes 19431612 | solution.py:168
  336.8 9.1 bitcast_dynamic-update-slice_fusion.2
  354.0 9.1 bitcast_dynamic-update-slice_fusion.2
  371.3 9.1 bitcast_dynamic-update-slice_fusion.2
  388.5 9.1 bitcast_dynamic-update-slice_fusion.2
  397.7 16.2 copy.79
  427.0 9.4 copy.98
  440.6 9.7 copy.97
  450.3 8.9 copy.126
  459.2 12.5 multiply_convert_fusion.4
  471.7 13.9 convolution_convert_fusion.3
  487.8 84.5 %reduce-scatter.12.cloned.1.call-done = bf16[512,2048]{1,0:T(8,128)(2,1)} async-done(((bf16[2048,2048]{1,0:T(8,128)(2,1)}), bf16[512,2048]{1,0:T(8,128)(2,1)}) %reduce-scatter.12.cloned.1.call-update) | async-done | bytes 2097168 | tf_op jit(solution)/shard_map/reduce_scatter | solution.py:171
  578.1 43.7 %all-gather.28.cloned.1.call-done = bf16[1024,2048]{1,0:T(8,128)(2,1)} async-done(((bf16[1024,256]{1,0:T(8,128)(2,1)}), bf16[1024,2048]{1,0:T(8,128)(2,1)}) %all-gather.28.cloned.1.call-update) | async-done | bytes 4194320 | tf_op jit(solution)/shard_map/all_gather | solution.py:124
  621.8 87.9 %all-gather.30.cloned.1.call-done = bf16[2048,2048]{1,0:T(8,128)(2,1)} async-done(((bf16[512,2048]{1,0:T(8,128)(2,1)}), bf16[2048,2048]{1,0:T(8,128)(2,1)}) %all-gather.30.cloned.1.call-update) | async-done | bytes 8388624 | tf_op jit(solution)/shard_map/all_gather | solution.py:202
  709.7 14.7 fusion.75
  724.3 34.1 %all-gather.26.cloned.1.call-done = bf16[2048,1024]{1,0:T(8,128)(2,1)} async-done(((bf16[256,1024]{1,0:T(8,128)(2,1)}), bf16[2048,1024]{1,0:T(8,128)(2,1)}) %all-gather.26.cloned.1.call-update) | async-done | bytes 4194320 | tf_op jit(solution)/shard_map/all_gather | solution.py:122
  758.4 88.9 %all-gather.24.cloned.1.call-done = bf16[2048,2048]{1,0:T(8,128)(2,1)} async-done(((bf16[512,2048]{1,0:T(8,128)(2,1)}), bf16[2048,2048]{1,0:T(8,128)(2,1)}) %all-gather.24.cloned.1.call-update) | async-done | bytes 8388624 | tf_op jit(solution)/shard_map/all_gather | solution.py:179
  847.3 22.0 %fusion.33 = (bf16[2048,1024]{1,0:T(8,128)(2,1)S(1)}, f32[2048,1024]{1,0:T(8,128)}) fusion(f32[2048,1024]{1,0:T(8,128)} %fusion.75, bf16[2048,2048]{1,0:T(8,128)(2,1)} %all-gather.24.cloned.1.call-done, bf16[2048,1024]{1,0:T(8,128)(2,1)} %all-gather.26.cloned.1.call-done), kind=kOutput, calls=%fused_computation.51 | convolution fusion | flops 8631877632 | bytes 33554432 | tf_op jit(solution)/shard_map/dot_general | solution.py:180
  871.3 10.9 convolution_convert_fusion.1
  882.3 15.4 convolution_convert_fusion.2
  897.8 71.1 %reduce-scatter.16.cloned.1.call-done = bf16[512,2048]{1,0:T(8,128)(2,1)} async-done(((bf16[2048,2048]{1,0:T(8,128)(2,1)}), bf16[512,2048]{1,0:T(8,128)(2,1)}) %reduce-scatter.16.cloned.1.call-update) | async-done | bytes 2097168 | tf_op jit(solution)/shard_map/reduce_scatter | solution.py:207
  973.1 85.2 %reduce-scatter.14.cloned.1.call-done = bf16[512,2048]{1,0:T(8,128)(2,1)} async-done(((bf16[2048,2048]{1,0:T(8,128)(2,1)}), bf16[512,2048]{1,0:T(8,128)(2,1)}) %reduce-scatter.14.cloned.1.call-update) | async-done | bytes 2097168 | tf_op jit(solution)/shard_map/reduce_scatter | solution.py:183
  1067.5 14.1 convolution_convert_fusion.7
  1081.6 10.8 copy.84
  1092.5 10.9 reshape.487
  1103.3 16.0 convolution_convert_fusion.5
  1119.4 35.7 %all-gather.32.cloned.1.call-done = bf16[2048,2048]{1,0:T(8,128)(2,1)} async-done(((bf16[512,2048]{1,0:T(8,128)(2,1)}), bf16[2048,2048]{1,0:T(8,128)(2,1)}) %all-gather.32.cloned.1.call-update) | async-done | bytes 8388624 | tf_op jit(solution)/shard_map/all_gather | solution.py:215
  1155.2 24.9 %fusion.61 = (f32[2048,1024]{1,0:T(8,128)}, bf16[2048,1024]{1,0:T(8,128)(2,1)}) fusion(f32[2048,3072]{1,0:T(8,128)} %fusion.74, f32[2048,1024]{1,0:T(8,128)} %copy.98, f32[2048,1024]{1,0:T(8,128)} %bitcast.112, f32[2048,1024]{1,0:T(8,128)} %copy.97, bf16[2048,2048]{1,0:T(8,128)(2,1)} %all-gather.32.cloned.1.call-done, ...), kind=kOutput, calls=%fused_computation.125 | convolution fusion | flops 8621391872 | bytes 58720256 | tf_op jit(solution)/shard_map/dot_general | solution.py:90
  1180.0 9.3 copy.100
  1189.3 8.2 multiply_reduce_fusion
  1206.8 134.6 %while.27 = (s32[]{:T(128)}, f32[2048,2,512]{0,2,1:T(8,128)}, f32[2048,2,256]{0,2,1:T(8,128)}, f32[4,512,2,256]{3,1,0,2:T(8,128)}, s32[4]{0:T(128)S(1)}, /*index...) while((s32[]{:T(128)}, f32[2048,2,512]{0,2,1:T(8,128)}, ...), condition=%wide.region_18.19_spmd.clone, body=%wide.region_17.18_spmd.clone.sunk | while | flops 7551845376 | bytes 124815200 | solution.py:244
  1213.9 7.4 multiply_convert_fusion.8
  1221.3 5.9 bitcast_add_fusion.5
  1229.6 9.3 bitcast_add_fusion.4
  1245.8 7.4 multiply_convert_fusion.8
  1253.2 7.2 bitcast_add_fusion.5
  1262.7 10.5 bitcast_add_fusion.4
  1280.1 7.4 multiply_convert_fusion.8
  1287.5 7.2 bitcast_add_fusion.5
  1297.0 10.5 bitcast_add_fusion.4
  1314.4 7.3 multiply_convert_fusion.8
  1321.6 7.1 bitcast_add_fusion.5
  1331.0 10.4 bitcast_add_fusion.4
  1341.4 5.9 copy.89
  1358.9 6.4 copy.99
  1365.3 34.9 %convolution_convert_fusion = bf16[2048,3072]{1,0:T(8,128)(2,1)} fusion(bf16[2048,2048]{1,0:T(8,128)(2,1)} %all-gather.12.cloned.1.call-done, bf16[2048,1024]{1,0:T(8,128)(2,1)} %get-tuple-element.289, bf16[2048,1024]{1,0:T(8,128)(2,1)} %copy.99, bf16[2048,512]{1,0:T(8,128)(2,1)} %bitcast.119, bf16[2048,512]{1,0:T(8,128)(2,1)S(1)} %bitcast.117), kind=kOutput, calls=%fused_computation.44 | convolution fusion | flops 25826426880 | bytes 33554432 | tf_op jit(solution)/shard_map/dot_general | solution.py:96
  1405.4 14.3 convolution_convert_fusion.6
  1419.8 6.1 fusion.70
  1426.7 33.7 %convolution_convert_fusion.4 = bf16[2048,2048]{1,0:T(8,128)(2,1)} fusion(bf16[2048,3072]{1,0:T(8,128)(2,1)} %constant_dynamic-update-slice_fusion, bf16[2048,1024]{1,0:T(8,128)(2,1)} %get-tuple-element.289, bf16[2048,1024]{1,0:T(8,128)(2,1)} %copy.99, bf16[2048,512]{1,0:T(8,128)(2,1)} %bitcast.120, bf16[2048,512]{1,0:T(8,128)(2,1)S(1)} %bitcast.118), kind=kOutput, calls=%fused_computation.67 | convolution fusion | flops 25824329728 | bytes 33554432 | tf_op jit(solution)/shard_map/dot_general | solution.py:90
  1466.7 11.0 reduce-scatter.22.cloned.1.call-done
  1479.5 49.3 %reduce-scatter.28.cloned.1.call-done = bf16[1024,256]{1,0:T(8,128)(2,1)} async-done(((bf16[1024,2048]{1,0:T(8,128)(2,1)}), bf16[1024,256]{1,0:T(8,128)(2,1)}) %reduce-scatter.28.cloned.1.call-update) | async-done | bytes 524304 | tf_op jit(solution)/shard_map/reduce_scatter | solution.py:285
  1530.8 48.4 %reduce-scatter.24.cloned.1.call-done = bf16[256,1024]{1,0:T(8,128)(2,1)} async-done(((bf16[2048,1024]{1,0:T(8,128)(2,1)}), bf16[256,1024]{1,0:T(8,128)(2,1)}) %reduce-scatter.24.cloned.1.call-update) | async-done | bytes 524304 | tf_op jit(solution)/shard_map/reduce_scatter | solution.py:276
  1581.3 48.5 %reduce-scatter.26.cloned.1.call-done = bf16[256,1024]{1,0:T(8,128)(2,1)} async-done(((bf16[2048,1024]{1,0:T(8,128)(2,1)}), bf16[256,1024]{1,0:T(8,128)(2,1)}) %reduce-scatter.26.cloned.1.call-update) | async-done | bytes 524304 | tf_op jit(solution)/shard_map/reduce_scatter | solution.py:279
  1631.9 85.8 %reduce-scatter.18.cloned.1.call-done = bf16[512,2048]{1,0:T(8,128)(2,1)} async-done(((bf16[2048,2048]{1,0:T(8,128)(2,1)}), bf16[512,2048]{1,0:T(8,128)(2,1)}) %reduce-scatter.18.cloned.1.call-update) | async-done | bytes 2097168 | tf_op jit(solution)/shard_map/reduce_scatter | solution.py:257
  1722.9 39.8 %all-reduce.4 = (f32[2048]{0:T(1024)S(1)}, f32[2048]{0:T(1024)S(1)}, f32[2048]{0:T(1024)S(1)}, f32[2048]{0:T(1024)S(1)}) all-reduce(f32[2048]{0:T(1024)S(1)} %get-tuple-element.235, f32[2048]{0:T(1024)S(1)} %get-tuple-element.238, f32[2048]{0:T(1024)S(1)} %copy-done.33, ...), channel_id=6, replica_groups=mesh['dp'=8,'tensor'=4] {'dp','tensor'}, use_global_device_ids=true, to_apply=%region_23.24.clone | all-reduce | flops 8192 | bytes 65536
  (301 shorter events, 195.1 us)
Async XLA Ops:
  7.2 4.8 copy-start.1
  7.2 5.6 copy-start.28
  7.2 5.6 copy-start.41
  7.2 34.3 %all-gather.14.cloned.1.call-start = ((), (), s32[]{:S(2)}) async-start(), calls=%async_computation.12 | async-start | bytes 2359296 | tf_op jit(solution)/shard_map/all_gather | solution.py:118
  7.9 63.8 %all-gather.16.cloned.1.call-start = ((), (), s32[]{:S(2)}) async-start(), calls=%async_computation.13 | async-start | bytes 2359296 | tf_op jit(solution)/shard_map/all_gather | solution.py:119
  8.7 111.3 %all-gather.18.cloned.1.call-start = ((), (), s32[]{:S(2)}) async-start(), calls=%async_computation.14 | async-start | bytes 4718592 | tf_op jit(solution)/shard_map/all_gather | solution.py:120
  9.4 157.9 %all-gather.20.cloned.1.call-start = ((), (), s32[]{:S(2)}) async-start(), calls=%async_computation.15 | async-start | bytes 4718592 | tf_op jit(solution)/shard_map/all_gather | solution.py:121
  10.0 246.0 %all-gather.12.cloned.1.call-start = ((), (), s32[]{:S(2)}) async-start(), calls=%async_computation.11 | async-start | bytes 10485760 | tf_op jit(solution)/shard_map/all_gather | solution.py:132
  12.7 7.4 copy-start.37
  12.8 7.3 copy-start.35
  15.0 456.8 %all-gather.22.cloned.1.call-start = ((), (), s32[]{:S(2)}) async-start(), calls=%async_computation.16 | async-start | bytes 4718592 | tf_op jit(solution)/shard_map/all_gather | solution.py:123
  15.5 556.8 %reduce-scatter.12.cloned.1.call-start = ((), (), s32[]{:S(2)}) async-start(), calls=%async_computation.17 | async-start | bytes 10485760 | tf_op jit(solution)/shard_map/reduce_scatter | solution.py:171
  20.1 305.3 %copy-start.15 = (f32[2048,128]{1,0:T(8,128)}, f32[2048,128]{1,0:T(8,128)S(1)}, u32[]{:S(2)}) copy-start(f32[2048,128]{1,0:T(8,128)S(1)} %get-tuple-element.313) | copy-start | bytes 3145732
  20.1 305.3 %copy-start.17 = (f32[2048,128]{1,0:T(8,128)}, f32[2048,128]{1,0:T(8,128)S(1)}, u32[]{:S(2)}) copy-start(f32[2048,128]{1,0:T(8,128)S(1)} %get-tuple-element.314) | copy-start | bytes 3145732
  316.0 4.8 copy-start.13
  316.0 6.2 copy-start.14
  397.6 16.2 copy-start.6
  397.6 16.2 copy-start.44
  417.9 18.5 %copy-start.22 = (f32[4,512,2]{1,2,0:T(2,128)}, f32[4,512,2]{1,2,0:T(2,128)S(1)}, u32[]{:S(2)}) copy-start(f32[4,512,2]{1,2,0:T(2,128)S(1)} %broadcast_multiply_fusion) | copy-start | bytes 49156
  450.3 8.9 copy-start.10
  485.6 86.7 %copy-start.2 = (bf16[512,2048]{1,0:T(8,128)(2,1)S(1)}, bf16[512,2048]{1,0:T(8,128)(2,1)}, u32[]{:S(2)}) copy-start(bf16[512,2048]{1,0:T(8,128)(2,1)} %param.18) | copy-start | bytes 6291460
  485.6 136.2 %all-gather.28.cloned.1.call-start = ((), (), s32[]{:S(2)}) async-start(), calls=%async_computation.20 | async-start | bytes 4718592 | tf_op jit(solution)/shard_map/all_gather | solution.py:124
  486.4 223.3 %all-gather.30.cloned.1.call-start = ((), (), s32[]{:S(2)}) async-start(), calls=%async_computation.22 | async-start | bytes 10485760 | tf_op jit(solution)/shard_map/all_gather | solution.py:202
  487.1 271.3 %all-gather.26.cloned.1.call-start = ((), (), s32[]{:S(2)}) async-start(), calls=%async_computation.19 | async-start | bytes 4718592 | tf_op jit(solution)/shard_map/all_gather | solution.py:122
  487.7 87.9 %copy-start.30 = (f32[2048]{0:T(1024)S(1)}, f32[2048]{0:T(1024)}, u32[]{:S(2)}) copy-start(f32[2048]{0:T(1024)} %param.28) | copy-start | bytes 24580
  487.7 87.9 %copy-start.42 = (f32[2048]{0:T(1024)S(1)}, f32[2048]{0:T(1024)}, u32[]{:S(2)}) copy-start(f32[2048]{0:T(1024)} %param.29) | copy-start | bytes 24580
  487.7 359.6 %all-gather.24.cloned.1.call-start = ((), (), s32[]{:S(2)}) async-start(), calls=%async_computation.18 | async-start | bytes 10485760 | tf_op jit(solution)/shard_map/all_gather | solution.py:179
  578.0 390.9 %reduce-scatter.16.cloned.1.call-start = ((), (), s32[]{:S(2)}) async-start(), calls=%async_computation.23 | async-start | bytes 10485760 | tf_op jit(solution)/shard_map/reduce_scatter | solution.py:207
  847.3 24.0 %copy-start.43 = (bf16[2048,1024]{1,0:T(8,128)(2,1)S(1)}, bf16[2048,1024]{1,0:T(8,128)(2,1)}, u32[]{:S(2)}) copy-start(bf16[2048,1024]{1,0:T(8,128)(2,1)} %all-gather.26.cloned.1.call-done) | copy-start | bytes 12582916
  882.3 176.1 %reduce-scatter.14.cloned.1.call-start = ((), (), s32[]{:S(2)}) async-start(), calls=%async_computation.21 | async-start | bytes 10485760 | tf_op jit(solution)/shard_map/reduce_scatter | solution.py:183
  897.7 257.5 %all-gather.32.cloned.1.call-start = ((), (), s32[]{:S(2)}) async-start(), calls=%async_computation.24 | async-start | bytes 10485760 | tf_op jit(solution)/shard_map/all_gather | solution.py:215
  1058.3 7.2 copy-start.11
  1067.4 393.0 %reduce-scatter.30.cloned.1.call-start = ((), (), s32[]{:S(2)}) async-start(), calls=%async_computation.31 | async-start | bytes 4718592 | tf_op jit(solution)/shard_map/reduce_scatter | solution.py:282
  1081.6 381.0 %reduce-scatter.32.cloned.1.call-start = ((), (), s32[]{:S(2)}) async-start(), calls=%async_computation.32 | async-start | bytes 4718592 | tf_op jit(solution)/shard_map/reduce_scatter | solution.py:288
  1119.4 345.5 %reduce-scatter.20.cloned.1.call-start = ((), (), s32[]{:S(2)}) async-start(), calls=%async_computation.26 | async-start | bytes 2359296 | tf_op jit(solution)/shard_map/reduce_scatter | solution.py:270
  1180.0 9.3 copy-start.23
  1189.3 8.3 copy-start.27
  1189.3 8.4 copy-start.4
  1189.3 8.4 copy-start.25
  1189.3 13.4 slice-start.2
  1197.8 5.3 slice-start.3
  1221.3 6.0 copy-start.5
  1221.3 6.0 copy-start.7
  1253.2 7.2 copy-start.5
  1253.2 7.2 copy-start.7
  1287.5 7.2 copy-start.5
  1287.5 7.2 copy-start.7
  1321.6 7.2 copy-start.5
  1321.6 7.2 copy-start.7
  1341.4 5.9 copy-start.16
  1341.4 6.0 copy-start.18
  1404.7 72.9 %reduce-scatter.22.cloned.1.call-start = ((), (), s32[]{:S(2)}) async-start(), calls=%async_computation.27 | async-start | bytes 2359296 | tf_op jit(solution)/shard_map/reduce_scatter | solution.py:273
  1405.3 123.4 %reduce-scatter.28.cloned.1.call-start = ((), (), s32[]{:S(2)}) async-start(), calls=%async_computation.30 | async-start | bytes 4718592 | tf_op jit(solution)/shard_map/reduce_scatter | solution.py:285
  1419.7 159.4 %reduce-scatter.24.cloned.1.call-start = ((), (), s32[]{:S(2)}) async-start(), calls=%async_computation.28 | async-start | bytes 4718592 | tf_op jit(solution)/shard_map/reduce_scatter | solution.py:276
  1425.9 203.9 %reduce-scatter.26.cloned.1.call-start = ((), (), s32[]{:S(2)}) async-start(), calls=%async_computation.29 | async-start | bytes 4718592 | tf_op jit(solution)/shard_map/reduce_scatter | solution.py:279
  1426.6 291.1 %reduce-scatter.18.cloned.1.call-start = ((), (), s32[]{:S(2)}) async-start(), calls=%async_computation.25 | async-start | bytes 10485760 | tf_op jit(solution)/shard_map/reduce_scatter | solution.py:257
  1462.6 255.1 %copy-start.3 = (bf16[512,2048]{1,0:T(8,128)(2,1)S(1)}, bf16[512,2048]{1,0:T(8,128)(2,1)}, u32[]{:S(2)}) copy-start(bf16[512,2048]{1,0:T(8,128)(2,1)} %param.18) | copy-start | bytes 6291460
  1462.6 255.1 %copy-start.29 = (f32[2048]{0:T(1024)S(1)}, f32[2048]{0:T(1024)}, u32[]{:S(2)}) copy-start(f32[2048]{0:T(1024)} %param.21) | copy-start | bytes 24580
  1462.6 255.1 %copy-start.32 = (f32[512]{0:T(512)S(1)}, f32[512]{0:T(512)}, u32[]{:S(2)}) copy-start(f32[512]{0:T(512)} %copy-done.31) | copy-start | bytes 6148
  1479.5 241.2 %copy-start.38 = (f32[512]{0:T(512)S(1)}, f32[512]{0:T(512)}, u32[]{:S(2)}) copy-start(f32[512]{0:T(512)} %copy-done.37) | copy-start | bytes 6148
  1479.5 241.2 %copy-start.36 = (f32[512]{0:T(512)S(1)}, f32[512]{0:T(512)}, u32[]{:S(2)}) copy-start(f32[512]{0:T(512)} %copy-done.35) | copy-start | bytes 6148
  1631.9 91.0 %copy-start.33 = (f32[2048]{0:T(1024)S(1)}, f32[2048]{0:T(1024)}, u32[]{:S(2)}) copy-start(f32[2048]{0:T(1024)} %get-tuple-element.233) | copy-start | bytes 24580
  1631.9 91.0 %copy-start.34 = (f32[2048]{0:T(1024)S(1)}, f32[2048]{0:T(1024)}, u32[]{:S(2)}) copy-start(f32[2048]{0:T(1024)} %get-tuple-element.237) | copy-start | bytes 24580
  1631.9 133.1 %copy-start.40 = (f32[512]{0:T(512)S(1)}, f32[512]{0:T(512)}, u32[]{:S(2)}) copy-start(f32[512]{0:T(512)} %copy-done.39) | copy-start | bytes 6148
  (21 other events, 62.5 us)
Sparse Core Ops, SparseCore 0:
  9.6 31.8 all-gather.13
  43.1 28.5 all-gather.15
  73.3 46.6 all-gather.17
  121.5 45.8 all-gather.19
  169.6 86.3 all-gather.11
  257.4 47.7 all-gather.21
  485.8 86.4 reduce-scatter.11
  574.0 47.7 all-gather.27
  623.8 85.8 all-gather.29
  711.2 47.1 all-gather.25
  760.9 86.3 all-gather.23
  882.4 86.4 reduce-scatter.15
  971.9 86.3 reduce-scatter.13
  1067.5 87.5 all-gather.31
  1157.4 49.9 reduce-scatter.29
  1209.7 48.1 reduce-scatter.31
  1404.9 35.9 reduce-scatter.19
  1443.1 34.5 reduce-scatter.21
  1480.1 48.6 reduce-scatter.27
  1531.0 48.1 reduce-scatter.23
  1581.6 48.1 reduce-scatter.25
  1633.1 84.5 reduce-scatter.17
where the time goes:
time: 1790 us; the launch traced here: 1780 us
  waiting for transfers between devices  1000 us (56%)
  matrix products  392 us (22%)
  local copies, waits for them, and re-layouts  173 us (10%)
  other arithmetic  139 us (8%)
  blocking collectives  39.8 us (2%)
    all_gather x1, waiting for transfers between devices, body(): lax.all_gather(normed2_exact.astype(jnp.bfloat16), 'tensor', axis=0, tile...  88.9 us
    all_gather x1, waiting for transfers between devices, body(): cot_all = lax.all_gather(cotangent, 'tensor', axis=0, tiled=True)  87.9 us
    reduce_scatter x1, waiting for transfers between devices, body(): lax.psum_scatter(matmul_transposed(joined_grad, joined_back).astype(jnp.b...  85.8 us
    reduce_scatter x1, waiting for transfers between devices, body(): lax.psum_scatter(jnp.dot(hidden, fetched[6], preferred_element_type=jnp.f...  85.2 us
    reduce_scatter x1, waiting for transfers between devices, body(): lax.psum_scatter(jnp.dot(gated, fetched[5], preferred_element_type=jnp.fl...  84.5 us
    dot_general x4, matrix products, matmul_transposed(): lax.dot_general(left, right, (((1,), (1,)), ((), ())), preferred_element_...  84.1 us
    all_gather x1, waiting for transfers between devices, body(): lax.all_gather(normed1_exact.astype(jnp.bfloat16), 'tensor', axis=0, tile...  83.8 us
    dot_general x4, matrix products, transposed_matmul(): lax.dot_general(left, right, (((0,), (0,)), ((), ())), preferred_element_...  79.3 us
  transfers between devices with their start and end apart: 22, of which 18 were waited for; matrix products, arithmetic and copies ran while one was open for 35% of the time, Pallas kernels for 0%

commit v1 on v0

v1 whole, which is shorter than its diff:
```python
import functools

import jax
import jax.numpy as jnp
from jax import lax
from jax.experimental import pallas as pl
from jax.experimental.pallas import tpu as pltpu
from jax.sharding import PartitionSpec as P

KEY = 256
VAL = 512
CHUNK = 256
HEAD = 2 * KEY + 2 * VAL

norm_epsilon = 1e-05
group_floor = 0.5
key_scale = KEY ** (-0.5)

f32 = jnp.float32
bf16 = jnp.bfloat16


def dot_nn(left, right):
    return lax.dot_general(left, right, (((1,), (0,)), ((), ())), preferred_element_type=f32)


def dot_nt(left, right):
    return lax.dot_general(left, right, (((1,), (1,)), ((), ())), preferred_element_type=f32)


def dot_tn(left, right):
    return lax.dot_general(left, right, (((0,), (0,)), ((), ())), preferred_element_type=f32)


def tensor_permute(values, bit):
    pairs = [(i, i ^ bit) for i in range(4)]
    return lax.ppermute(values, "tensor", pairs)


def gather_pieces(own, devices):
    if devices != 4:
        whole = lax.all_gather(own, "tensor", axis=0, tiled=True)
        return list(jnp.split(whole, devices, axis=0))
    half = own.shape[0] // 2
    from_x = tensor_permute(own, 1)
    from_y = tensor_permute(own, 2)
    lower = tensor_permute(from_y[:half], 1)
    upper = tensor_permute(from_x[half:], 2)
    return [own, from_x, from_y, jnp.concatenate([lower, upper], axis=0)]


def scatter_sum(terms):
    if len(terms) != 4:
        stacked = jnp.concatenate([term.astype(bf16) for term in terms], axis=0)
        return lax.psum_scatter(stacked, "tensor", scatter_dimension=0, tiled=True).astype(f32)
    own, over_x, over_y, across = terms
    half = own.shape[0] // 2
    across = across.astype(bf16)
    first = tensor_permute(across[:half], 1)
    second = tensor_permute(across[half:], 2)
    over_y = jnp.concatenate([over_y[:half] + first.astype(f32), over_y[half:]], axis=0)
    over_x = jnp.concatenate([over_x[:half], over_x[half:] + second.astype(f32)], axis=0)
    by_x = tensor_permute(over_x.astype(bf16), 1)
    by_y = tensor_permute(over_y.astype(bf16), 2)
    return own + by_x.astype(f32) + by_y.astype(f32)


def normalize(values):
    average = jnp.mean(values, axis=-1, keepdims=True)
    centred = values - average
    variance = jnp.mean(centred * centred, axis=-1, keepdims=True)
    scale = lax.rsqrt(variance + norm_epsilon)
    return centred * scale, scale


def normalize_back(normed_grad, unit, scale, gain):
    g = normed_grad * gain
    mean_g = jnp.mean(g, axis=-1, keepdims=True)
    mean_gx = jnp.mean(g * unit, axis=-1, keepdims=True)
    return scale * (g - mean_g - unit * mean_gx)


def gelu_both(values):
    inner = 0.7978845608 * (values + 0.044715 * values * values * values)
    t = jnp.tanh(inner)
    slope = 0.7978845608 * (1.0 + 3.0 * 0.044715 * values * values)
    return 0.5 * values * (1.0 + t), 0.5 * (1.0 + t) + 0.5 * values * (1.0 - t * t) * slope


def turn(block, cosine, sine):
    a = block[:, : KEY // 2]
    b = block[:, KEY // 2 :]
    return jnp.concatenate([a * cosine - b * sine, b * cosine + a * sine], axis=1)


def turn_back(block, cosine, sine):
    a = block[:, : KEY // 2]
    b = block[:, KEY // 2 :]
    return jnp.concatenate([a * cosine + b * sine, b * cosine - a * sine], axis=1)


def head_parts(field, angles, head):
    base = head * HEAD
    cosine = angles[:, : KEY // 2]
    sine = angles[:, KEY // 2 :]
    query = turn(field[:, base : base + KEY].astype(f32), cosine, sine).astype(bf16)
    key = turn(field[:, base + KEY : base + 2 * KEY].astype(f32), cosine, sine)
    key = (key * key_scale).astype(bf16)
    value = field[:, base + 2 * KEY : base + 2 * KEY + VAL]
    gate = field[:, base + 2 * KEY + VAL : base + HEAD].astype(f32)
    return query, key, value, gate


def retention_forward(heads, which, field_ref, angle_ref, info_ref, row_ref, decay_ref, gated_ref, grouped_ref, scale_ref, past_ref, state_ref):
    @pl.when(pl.program_id(0) == 0)
    def _():
        state_ref[...] = jnp.zeros_like(state_ref)

    angles = angle_ref[...]
    info = info_ref[...]
    same = info[:, 0:1] == row_ref[0]
    for head in range(heads):
        query, key, value, gate = head_parts(field_ref[...], angles, head)
        into = info[:, 1 + 2 * head : 2 + 2 * head]
        onward = info[:, 2 + 2 * head : 3 + 2 * head]
        state = state_ref[head]
        past_ref[0, head] = state.astype(bf16)
        scores = dot_nt(query, key)
        weights = (jnp.where(same, decay_ref[head], 0.0) * scores).astype(bf16)
        retained = dot_nn(weights, value) + into * dot_nn(query, state.astype(bf16))
        moved = (key.astype(f32) * onward).astype(bf16)
        state_ref[head] = into[CHUNK - 1 :, :] * state + dot_tn(moved, value)
        centred = retained - jnp.mean(retained, axis=-1, keepdims=True)
        scale = lax.rsqrt(jnp.mean(centred * centred, axis=-1, keepdims=True) + group_floor)
        grouped = centred * scale
        gated = gate / (1.0 + jnp.exp(-gate)) * grouped
        columns = slice(head * VAL, (head + 1) * VAL)
        gated_ref[:, columns] = gated.astype(bf16)
        grouped_ref[:, columns] = grouped.astype(bf16)
        scale_ref[:, head * 128 : (head + 1) * 128] = jnp.broadcast_to(scale, (CHUNK, 128))


def retention_backward(heads, which, field_ref, angle_ref, info_ref, row_ref, decay_ref, grad_ref, grouped_ref, scale_ref, past_ref, back_ref, state_ref):
    @pl.when(pl.program_id(0) == 0)
    def _():
        state_ref[...] = jnp.zeros_like(state_ref)

    angles = angle_ref[...]
    cosine = angles[:, : KEY // 2]
    sine = angles[:, KEY // 2 :]
    info = info_ref[...]
    same = info[:, 0:1] == row_ref[0]
    for head in range(heads):
        query, key, value, gate = head_parts(field_ref[...], angles, head)
        into = info[:, 1 + 2 * head : 2 + 2 * head]
        onward = info[:, 2 + 2 * head : 3 + 2 * head]
        columns = slice(head * VAL, (head + 1) * VAL)
        gated_grad = grad_ref[:, columns].astype(f32)
        grouped = grouped_ref[:, columns].astype(f32)
        scale = scale_ref[:, head * 128 : head * 128 + 1]
        sigmoid = 1.0 / (1.0 + jnp.exp(-gate))
        gate_grad = gated_grad * grouped * (sigmoid * (1.0 + gate * (1.0 - sigmoid)))
        c = gated_grad * (gate * sigmoid)
        mean_c = jnp.mean(c, axis=-1, keepdims=True)
        mean_cx = jnp.mean(c * grouped, axis=-1, keepdims=True)
        out_grad = (scale * (c - mean_c - grouped * mean_cx)).astype(bf16)
        state = state_ref[head]
        state_low = state.astype(bf16)
        past = past_ref[0, head]
        masked = jnp.where(same, decay_ref[head], 0.0)
        weights = (masked * dot_nt(query, key)).astype(bf16)
        score_grad = (masked * dot_nt(out_grad, value)).astype(bf16)
        value_grad = dot_tn(weights, out_grad) + onward * dot_nn(key, state_low)
        query_grad = dot_nn(score_grad, key) + into * dot_nt(out_grad, past)
        key_grad = dot_tn(score_grad, query) + onward * dot_nt(value, state_low)
        moved = (query.astype(f32) * into).astype(bf16)
        state_ref[head] = into[CHUNK - 1 :, :] * state + dot_tn(moved, out_grad)
        base = head * HEAD
        back_ref[:, base : base + KEY] = turn_back(query_grad, cosine, sine).astype(bf16)
        back_ref[:, base + KEY : base + 2 * KEY] = (turn_back(key_grad, cosine, sine) * key_scale).astype(bf16)
        back_ref[:, base + 2 * KEY : base + 2 * KEY + VAL] = value_grad.astype(bf16)
        back_ref[:, base + 2 * KEY + VAL : base + HEAD] = gate_grad.astype(bf16)


def retention_tables(segment, heads, first_head):
    rows = segment.shape[0]
    chunks = rows // CHUNK
    index = jnp.arange(rows, dtype=jnp.int32)
    boundary = jnp.concatenate([jnp.ones((1,), jnp.int32), (segment[1:] != segment[:-1]).astype(jnp.int32)])
    position = index - lax.cummax(jnp.where(boundary > 0, index, 0), axis=0)
    half = KEY // 2
    frequency = jnp.exp(-jnp.log(10000.0) * jnp.arange(half, dtype=f32) / half)
    angles = position.astype(f32)[:, None] * frequency[None, :]
    angles = jnp.concatenate([jnp.cos(angles), jnp.sin(angles)], axis=1)
    head_ids = (first_head + jnp.arange(heads, dtype=jnp.int32)).astype(f32)
    log_decay = jnp.log1p(-jnp.exp2(-5.0 - head_ids))
    last = segment.reshape(chunks, CHUNK)[:, -1]
    before = jnp.concatenate([jnp.full((1,), -2, jnp.int32), last[:-1]])
    offset = (index % CHUNK).astype(f32)
    linked_in = (segment == jnp.repeat(before, CHUNK)) & (segment >= 0)
    linked_on = (segment == jnp.repeat(last, CHUNK)) & (segment >= 0)
    columns = [segment.astype(f32)]
    for head in range(heads):
        columns.append(jnp.where(linked_in, jnp.exp(log_decay[head] * (offset + 1.0)), 0.0))
        columns.append(jnp.where(linked_on, jnp.exp(log_decay[head] * (CHUNK - 1.0 - offset)), 0.0))
    info = jnp.stack(columns, axis=1)
    info = jnp.pad(info, ((0, 0), (0, 128 - info.shape[1])))
    keys = jnp.where(segment >= 0, segment, -7).astype(f32).reshape(chunks, 1, CHUNK)
    distance = (jnp.arange(CHUNK)[:, None] - jnp.arange(CHUNK)[None, :]).astype(f32)
    decay = jnp.where(distance >= 0, jnp.exp(log_decay[:, None, None] * jnp.maximum(distance, 0.0)), 0.0)
    return angles, info, keys, decay


def retention_call(backward, which, piece_rows, heads, field, tables, extra):
    rows = field.shape[0]
    chunks = rows // CHUNK
    angles, info, keys, decay = tables
    per_piece = piece_rows // CHUNK

    def step(i):
        return chunks - 1 - i if backward else i

    def place(i, which_ref):
        c = step(i)
        return ((c // per_piece) ^ which_ref[0]) * per_piece + c % per_piece

    def placed(width):
        return pl.BlockSpec((CHUNK, width), lambda i, w: (place(i, w), 0))

    in_specs = [
        placed(heads * HEAD),
        pl.BlockSpec((CHUNK, KEY), lambda i, w: (step(i), 0)),
        pl.BlockSpec((CHUNK, 128), lambda i, w: (step(i), 0)),
        pl.BlockSpec((1, 1, CHUNK), lambda i, w: (step(i), 0, 0)),
        pl.BlockSpec((heads, CHUNK, CHUNK), lambda i, w: (0, 0, 0)),
    ]
    past_spec = pl.BlockSpec((1, heads, KEY, VAL), lambda i, w: (step(i), 0, 0, 0))
    if backward:
        in_specs += [placed(heads * VAL), placed(heads * VAL), placed(heads * 128), past_spec]
        out_specs = placed(heads * HEAD)
        out_shape = jax.ShapeDtypeStruct((rows, heads * HEAD), bf16)
    else:
        out_specs = [placed(heads * VAL), placed(heads * VAL), placed(heads * 128), past_spec]
        out_shape = [
            jax.ShapeDtypeStruct((rows, heads * VAL), bf16),
            jax.ShapeDtypeStruct((rows, heads * VAL), bf16),
            jax.ShapeDtypeStruct((rows, heads * 128), f32),
            jax.ShapeDtypeStruct((chunks, heads, KEY, VAL), bf16),
        ]
    products = 15 if backward else 7
    return pl.pallas_call(
        functools.partial(retention_backward if backward else retention_forward, heads),
        grid_spec=pltpu.PrefetchScalarGridSpec(
            num_scalar_prefetch=1,
            grid=(chunks,),
            in_specs=in_specs,
            out_specs=out_specs,
            scratch_shapes=[pltpu.VMEM((heads, KEY, VAL), f32)],
        ),
        out_shape=out_shape,
        compiler_params=pltpu.CompilerParams(
            dimension_semantics=("arbitrary",), vmem_limit_bytes=48 * 1024 * 1024
        ),
        cost_estimate=pl.CostEstimate(
            flops=products * chunks * heads * 2 * CHUNK * CHUNK * CHUNK,
            bytes_accessed=(5 if backward else 4) * rows * heads * HEAD,
            transcendentals=rows * heads * VAL,
        ),
        name="retention_backward" if backward else "retention_forward",
    )(which, field, angles, info, keys, decay, *extra)


def body(tokens, cotangent, segment, first_gain, first_bias, query_weight, key_weight, value_weight, gate_weight, out_weight, second_gain, second_bias, up_weight, down_weight):
    devices = lax.axis_size("tensor")
    rows = tokens.shape[0]
    heads = query_weight.shape[1] // KEY
    here = lax.axis_index("tensor")
    which = (here if devices == 4 else jnp.zeros_like(here)).astype(jnp.int32).reshape(1)

    def per_piece(values):
        return [values[i * rows : (i + 1) * rows] for i in range(devices)]

    shards = []
    for h in range(heads):
        shards += [
            query_weight[:, h * KEY : (h + 1) * KEY],
            key_weight[:, h * KEY : (h + 1) * KEY],
            value_weight[:, h * VAL : (h + 1) * VAL],
            gate_weight[:, h * VAL : (h + 1) * VAL],
        ]
    w_in = lax.all_gather(jnp.concatenate(shards, axis=1), "dp", axis=0, tiled=True)
    w_out = lax.all_gather(out_weight, "dp", axis=1, tiled=True)
    w_down = lax.all_gather(down_weight, "dp", axis=1, tiled=True)
    w_up = lax.all_gather(up_weight, "dp", axis=0, tiled=True)

    token_rows = tokens.astype(f32)
    unit1, scale1 = normalize(token_rows)
    normed1 = (unit1 * first_gain + first_bias).astype(bf16)
    normed1_all = jnp.concatenate(gather_pieces(normed1, devices), axis=0)
    cot_pieces = gather_pieces(cotangent, devices)
    tables = retention_tables(segment, heads, here * heads)
    field = dot_nn(normed1_all, w_in).astype(bf16)
    gated, grouped, group_scale, past = retention_call(False, which, rows, heads, field, tables, ())
    branch = scatter_sum([dot_nn(piece, w_out) for piece in per_piece(gated)])

    mixed = token_rows + branch
    unit2, scale2 = normalize(mixed)
    normed2 = (unit2 * second_gain + second_bias).astype(bf16)
    normed2_pieces = gather_pieces(normed2, devices)
    hidden_grads = [dot_nt(piece, w_down) for piece in cot_pieces]
    hidden, up_grad = [], []
    for piece, hidden_grad in zip(normed2_pieces, hidden_grads):
        value, slope = gelu_both(dot_nn(piece, w_up))
        hidden.append(value.astype(bf16))
        up_grad.append((hidden_grad * slope).astype(bf16))
    normed2_grad = scatter_sum([dot_nt(piece, w_up) for piece in up_grad])
    mixed_grad = cotangent.astype(f32) + normalize_back(normed2_grad, unit2, scale2, second_gain)
    gain2_grad = jnp.sum(normed2_grad * unit2, axis=0)
    bias2_grad = jnp.sum(normed2_grad, axis=0)
    mixed_pieces = gather_pieces(mixed_grad.astype(bf16), devices)
    ffn = scatter_sum([dot_nn(piece, w_down) for piece in hidden])
    result = (mixed + ffn).astype(bf16)
    normed2_all = jnp.concatenate(normed2_pieces, axis=0)
    up_grad_all = jnp.concatenate(up_grad, axis=0)
    cot_all = jnp.concatenate(cot_pieces, axis=0)
    hidden_all = jnp.concatenate(hidden, axis=0)
    up_weight_grad = dot_tn(normed2_all, up_grad_all).astype(bf16)
    down_weight_grad = dot_tn(hidden_all, cot_all).astype(bf16)

    gated_grad = jnp.concatenate([dot_nt(piece, w_out).astype(bf16) for piece in mixed_pieces], axis=0)
    mixed_all = jnp.concatenate(mixed_pieces, axis=0)
    back = retention_call(True, which, rows, heads, field, tables, (gated_grad, grouped, group_scale, past))
    out_weight_grad = dot_tn(gated, mixed_all).astype(bf16)
    normed1_grad = scatter_sum([dot_nt(piece, w_in) for piece in per_piece(back)])
    in_weight_grad = dot_tn(normed1_all, back).astype(bf16)
    input_grad = mixed_grad + normalize_back(normed1_grad, unit1, scale1, first_gain)
    gain1_grad = jnp.sum(normed1_grad * unit1, axis=0)
    bias1_grad = jnp.sum(normed1_grad, axis=0)

    up_sum = lax.psum_scatter(up_weight_grad, "dp", scatter_dimension=0, tiled=True).astype(f32)
    down_sum = lax.psum_scatter(down_weight_grad, "dp", scatter_dimension=1, tiled=True).astype(f32)
    out_sum = lax.psum_scatter(out_weight_grad, "dp", scatter_dimension=1, tiled=True).astype(f32)
    in_sum = lax.psum_scatter(in_weight_grad, "dp", scatter_dimension=0, tiled=True).astype(f32)

    def columns_of(start, width):
        return jnp.concatenate(
            [in_sum[:, h * HEAD + start : h * HEAD + start + width] for h in range(heads)], axis=1
        )

    norm_sums = [
        lax.psum_scatter(v, ("dp", "tensor"), scatter_dimension=0, tiled=True)
        for v in (gain1_grad, bias1_grad, gain2_grad, bias2_grad)
    ]
    return (
        result,
        input_grad.astype(bf16),
        norm_sums[0],
        norm_sums[1],
        columns_of(0, KEY),
        columns_of(KEY, KEY),
        columns_of(2 * KEY, VAL),
        columns_of(2 * KEY + VAL, VAL),
        out_sum,
        norm_sums[2],
        norm_sums[3],
        up_sum,
        down_sum,
    )


def solution(mesh):
    rows = P(("dp", "tensor"), None)
    vector = P(("dp", "tensor"))
    into = P("dp", "tensor")
    back = P("tensor", "dp")
    return jax.shard_map(
        body,
        mesh=mesh,
        in_specs=(rows, rows, P("dp"), P(), P(), into, into, into, into, back, P(), P(), into, back),
        out_specs=(rows, rows, vector, vector, into, into, into, into, back, vector, vector, into, back),
        check_vma=False,
    )
```

time: 1790 us -> 905 us (0.51)
  waiting for transfers between devices: 1000 us -> 410 us
  matrix products: 392 us -> 242 us
  local copies, waits for them, and re-layouts: 173 us -> 61.7 us
  other arithmetic: 139 us -> 50.2 us
  starting transfers between devices: 0.88 us -> 43.9 us
  Pallas kernels: 0 us -> 39.1 us
    reduce_scatter x11 -> x4, waiting for transfers between devices: 484 us -> 0.01 us  [the longest x1 0.01 us: body(): lax.psum_scatter(up_weight_grad, 'dp', scatter_dimension=0, tiled=True)]
    all_gather x11 -> x4, waiting for transfers between devices: 511 us -> 36.8 us  [the longest x1 36.8 us: body(): lax.all_gather(jnp.concatenate(shards, axis=1), 'dp', axis=0, tiled=True)]
    ppermute x0 -> x32, waiting for transfers between devices: none -> 371 us  [tensor_permute(): return lax.ppermute(values, 'tensor', pairs)]
    dot_general x32 -> x33, matrix products: 392 us -> 242 us  [the longest x16 95.5 us: dot_nt(): lax.dot_general(left, right, (((1,), (1,)), ((), ())), preferred_element_...]
    convert_element_type x24 -> x6, other arithmetic: 63.2 us -> 11.7 us  [the longest x1 5.28 us: body(): input_grad.astype(bf16)]
    reshape x6 -> x1, local copies, waits for them, and re-layouts: 43.1 us -> 0.01 us  [retention_tables(): last = segment.reshape(chunks, CHUNK)[:, -1]]
    ppermute x0 -> x32, starting transfers between devices: none -> 42.7 us  [tensor_permute(): return lax.ppermute(values, 'tensor', pairs)]
    pallas_call x0 -> x2, Pallas kernels: none -> 39.1 us  [retention_call(): pl.pallas_call(functools.partial(retention_backward if backward else rete...]
  transfers between devices with their start and end apart: 22 -> 40, of which waited for: 18 -> 19; matrix products, arithmetic and copies ran while one was open for 35% -> 34% of each run, Pallas kernels for 0% -> 4%
where the time goes in v1:
time: 905 us; the launch traced here: 901 us
  waiting for transfers between devices  410 us (45%)
  matrix products  242 us (27%)
  local copies, waits for them, and re-layouts  61.7 us (7%)
  other arithmetic  50.2 us (6%)
  starting transfers between devices  43.9 us (5%)
  Pallas kernels  39.1 us (4%)
  blocking collectives  39 us (4%)
  between operations  15.6 us (2%)
    ppermute x32, waiting for transfers between devices, tensor_permute(): return lax.ppermute(values, 'tensor', pairs)  371 us
    dot_general x16, matrix products, dot_nt(): lax.dot_general(left, right, (((1,), (1,)), ((), ())), preferred_element_...  95.5 us
    dot_general x13, matrix products, dot_nn(): lax.dot_general(left, right, (((1,), (0,)), ((), ())), preferred_element_...  82.2 us
    dot_general x4, matrix products, dot_tn(): lax.dot_general(left, right, (((0,), (0,)), ((), ())), preferred_element_...  64.4 us
    ppermute x32, starting transfers between devices, tensor_permute(): return lax.ppermute(values, 'tensor', pairs)  42.7 us
    pallas_call x2, Pallas kernels, retention_call(): pl.pallas_call(functools.partial(retention_backward if backward else rete...  39.1 us
    unnamed x1, blocking collectives  39 us
    unnamed x175, local copies, waits for them, and re-layouts  38.6 us
  transfers between devices with their start and end apart: 40, of which 19 were waited for; matrix products, arithmetic and copies ran while one was open for 34% of the time, Pallas kernels for 4%

profile of v1, /device:TPU:0, one launch (start us, length us, event | category | flops | bytes accessed | tf_op | source)
XLA Modules:
  0.0 901.3 jit_solution(9697490730271084309)
XLA Ops:
  23.2 2.9 constant_dynamic-update-slice_fusion.4
  26.1 3.0 collective-permute-start.1
  36.9 3.7 multiply_cosine_fusion
  40.6 34.2 %collective-permute-done.1 = bf16[512,2048]{1,0:T(8,128)(2,1)S(1)} collective-permute-done((bf16[512,2048]{1,0:T(8,128)(2,1)}, bf16[512,2048]{1,0:T(8,128)(2,1)S(1)}, u32[]{:S(2)}, u32[]{:S(2)}) %collective-permute-start.1) | collective-permute-done | bytes 2097184 | tf_op jit(solution)/shard_map/ppermute | solution.py:37
  80.9 3.2 constant_dynamic-update-slice_fusion.3
  85.5 14.0 %collective-permute-done.2 = bf16[256,2048]{1,0:T(8,128)(2,1)S(1)} collective-permute-done((bf16[256,2048]{1,0:T(8,128)(2,1)S(1)}, bf16[256,2048]{1,0:T(8,128)(2,1)S(1)}, u32[]{:S(2)}, u32[]{:S(2)}) %collective-permute-start.2) | collective-permute-done | bytes 1048608 | tf_op jit(solution)/shard_map/ppermute | solution.py:37
  103.4 36.8 %all-gather.5.cloned.1.call-done = bf16[2048,3072]{1,0:T(8,128)(2,1)} async-done(((bf16[256,3072]{1,0:T(8,128)(2,1)}), bf16[2048,3072]{1,0:T(8,128)(2,1)}) %all-gather.5.cloned.1.call-update) | async-done | bytes 12582928 | tf_op jit(solution)/shard_map/all_gather | solution.py:291
  140.1 32.7 %convolution_convert_fusion.1.field_ref = bf16[2048,3072]{1,0:T(8,128)(2,1)} fusion(bf16[2048,2048]{1,0:T(8,128)(2,1)} %constant_dynamic-update-slice_fusion, bf16[2048,3072]{1,0:T(8,128)(2,1)} %all-gather.5.cloned.1.call-done), kind=kOutput, calls=%fused_computation.1 | convolution fusion | flops 25776095232 | bytes 33554432 | tf_op jit(solution)/shard_map/dot_general | solution.py:24
  172.9 15.8 %retention_forward.1 = (bf16[2048,1024]{1,0:T(8,128)(2,1)}, bf16[2048,1024]{1,0:T(8,128)(2,1)}, f32[2048,256]{1,0:T(8,128)S(1)}, bf16[8,2,256,512]{3,2,1,0:T(8,128)(2,1)}) custom-call(s32[1]{0:T(128)} %bitcast.which, bf16[2048,3072]{1,0:T(8,128)(2,1)} %convolution_convert_fusion.1.field_ref, f32[2048,256]{1,0:T(8,128)S(1)} %pad_maximum_fusion.1.angle_ref, ...), custom_call_target="tpu_custom_call" | custom-call | flops 3758096384 | bytes 25165824 | tf_op jit(solution)/shard_map/retention_forward/pallas_call | solution.py:251
  190.0 5.0 convolution_convert_fusion.5
  198.2 2.4 fusion.107
  200.6 2.4 fusion.110
  203.2 18.5 %collective-permute-done.6 = bf16[256,2048]{1,0:T(8,128)(2,1)S(1)} collective-permute-done((bf16[256,2048]{1,0:T(8,128)(2,1)S(1)}, bf16[256,2048]{1,0:T(8,128)(2,1)S(1)}, u32[]{:S(2)}, u32[]{:S(2)}) %collective-permute-start.6) | collective-permute-done | bytes 1048608 | tf_op jit(solution)/shard_map/ppermute | solution.py:37
  227.2 3.6 fusion.112
  230.8 40.2 %collective-permute-done.7 = bf16[512,2048]{1,0:T(8,128)(2,1)S(1)} collective-permute-done((bf16[512,2048]{1,0:T(8,128)(2,1)S(1)}, bf16[512,2048]{1,0:T(8,128)(2,1)S(1)}, u32[]{:S(2)}, u32[]{:S(2)}) %collective-permute-start.7) | collective-permute-done | bytes 2097184 | tf_op jit(solution)/shard_map/ppermute | solution.py:37
  274.4 2.8 constant_dynamic-update-slice_fusion.14
  280.1 37.1 %collective-permute-done.16 = bf16[512,2048]{1,0:T(8,128)(2,1)S(1)} collective-permute-done((bf16[512,2048]{1,0:T(8,128)(2,1)S(1)}, bf16[512,2048]{1,0:T(8,128)(2,1)S(1)}, u32[]{:S(2)}, u32[]{:S(2)}) %collective-permute-start.16) | collective-permute-done | bytes 2097184 | tf_op jit(solution)/shard_map/ppermute | solution.py:37
  325.1 7.5 multiply_convert_fusion.3
  332.6 6.9 fusion.63
  339.5 21.5 %collective-permute-done.9 = bf16[512,2048]{1,0:T(8,128)(2,1)} collective-permute-done((bf16[512,2048]{1,0:T(8,128)(2,1)}, bf16[512,2048]{1,0:T(8,128)(2,1)}, u32[]{:S(2)}, u32[]{:S(2)}) %collective-permute-start.9) | collective-permute-done | bytes 2097184 | tf_op jit(solution)/shard_map/ppermute | solution.py:37
  365.8 5.3 multiply_convert_fusion.2
  371.1 4.5 multiply_convert_fusion
  375.6 3.5 fusion.69
  379.2 3.3 fusion.81
  382.5 2.4 fusion.140
  384.9 2.4 fusion.141
  387.3 2.3 fusion.138
  389.7 2.3 fusion.137
  392.8 2.8 slice-done.5
  405.0 4.1 multiply_convert_fusion.1
  409.1 4.8 fusion.75
  413.9 2.4 convolution_convert_fusion.3
  419.0 10.6 %fusion.31 = bf16[2048,1024]{1,0:T(8,128)(2,1)} fusion(bf16[2048,2048]{1,0:T(8,128)(2,1)S(1)} %constant_dynamic-update-slice_fusion.10, bf16[512,1024]{1,0:T(8,128)(2,1)S(1)} %copy-done.67, bf16[512,1024]{1,0:T(8,128)(2,1)S(1)} %fusion.81, bf16[512,1024]{1,0:T(8,128)(2,1)S(1)} %fusion.69, bf16[512,1024]{1,0:T(8,128)(2,1)S(1)} %fusion.63), kind=kOutput, calls=%fused_computation.46 | convolution fusion | flops 8608808960 | bytes 16777216 | tf_op jit(solution)/shard_map/dot_general | solution.py:32
  432.9 5.3 convolution_convert_fusion.4
  439.2 17.0 %collective-permute-done.20 = bf16[256,2048]{1,0:T(8,128)(2,1)S(1)} collective-permute-done((bf16[256,2048]{1,0:T(8,128)(2,1)}, bf16[256,2048]{1,0:T(8,128)(2,1)S(1)}, u32[]{:S(2)}, u32[]{:S(2)}) %collective-permute-start.20) | collective-permute-done | bytes 1048608 | tf_op jit(solution)/shard_map/ppermute | solution.py:37
  460.3 19.9 %collective-permute-done.14 = bf16[256,2048]{1,0:T(8,128)(2,1)S(1)} collective-permute-done((bf16[256,2048]{1,0:T(8,128)(2,1)S(1)}, bf16[256,2048]{1,0:T(8,128)(2,1)S(1)}, u32[]{:S(2)}, u32[]{:S(2)}) %collective-permute-start.14) | collective-permute-done | bytes 1048608 | tf_op jit(solution)/shard_map/ppermute | solution.py:37
  483.5 2.4 fusion.139
  485.9 4.7 fusion.136
  490.7 34.4 %collective-permute-done.21 = bf16[512,2048]{1,0:T(8,128)(2,1)S(1)} collective-permute-done((bf16[512,2048]{1,0:T(8,128)(2,1)S(1)}, bf16[512,2048]{1,0:T(8,128)(2,1)S(1)}, u32[]{:S(2)}, u32[]{:S(2)}) %collective-permute-start.21) | collective-permute-done | bytes 2097184 | tf_op jit(solution)/shard_map/ppermute | solution.py:37
  525.1 40.4 %collective-permute-done.15 = bf16[512,2048]{1,0:T(8,128)(2,1)S(1)} collective-permute-done((bf16[512,2048]{1,0:T(8,128)(2,1)S(1)}, bf16[512,2048]{1,0:T(8,128)(2,1)S(1)}, u32[]{:S(2)}, u32[]{:S(2)}) %collective-permute-start.15) | collective-permute-done | bytes 2097184 | tf_op jit(solution)/shard_map/ppermute | solution.py:37
  566.8 5.9 multiply_reduce_fusion
  572.8 4.3 constant_dynamic-update-slice_fusion.9
  581.6 11.1 %fusion.34 = bf16[1024,2048]{1,0:T(8,128)(2,1)} fusion(bf16[2048,2048]{1,0:T(8,128)(2,1)S(1)} %constant_dynamic-update-slice_fusion.15, bf16[512,1024]{1,0:T(8,128)(2,1)S(1)} %copy-done.65, bf16[512,1024]{1,0:T(8,128)(2,1)S(1)} %copy-done.64, bf16[512,1024]{1,0:T(8,128)(2,1)S(1)} %copy-done.62, bf16[512,1024]{1,0:T(8,128)(2,1)S(1)} %copy-done.60), kind=kOutput, calls=%fused_computation.47 | convolution fusion | flops 8608808960 | bytes 16777216 | tf_op jit(solution)/shard_map/dot_general | solution.py:32
  595.3 6.6 convolution_convert_fusion.8
  601.9 35.9 %collective-permute-done.25 = bf16[512,2048]{1,0:T(8,128)(2,1)S(1)} collective-permute-done((bf16[512,2048]{1,0:T(8,128)(2,1)}, bf16[512,2048]{1,0:T(8,128)(2,1)S(1)}, u32[]{:S(2)}, u32[]{:S(2)}) %collective-permute-start.25) | collective-permute-done | bytes 2097184 | tf_op jit(solution)/shard_map/ppermute | solution.py:37
  637.8 2.3 collective-permute-start.26
  642.0 3.4 convolution_convert_fusion.6
  645.9 3.4 convolution_convert_fusion.7
  649.2 11.3 %collective-permute-done.26 = bf16[256,2048]{1,0:T(8,128)(2,1)S(1)} collective-permute-done((bf16[256,2048]{1,0:T(8,128)(2,1)S(1)}, bf16[256,2048]{1,0:T(8,128)(2,1)S(1)}, u32[]{:S(2)}, u32[]{:S(2)}) %collective-permute-start.26) | collective-permute-done | bytes 1048608 | tf_op jit(solution)/shard_map/ppermute | solution.py:37
  662.7 11.0 %convolution_convert_fusion.2 = bf16[1024,2048]{1,0:T(8,128)(2,1)} fusion(bf16[2048,1024]{1,0:T(8,128)(2,1)S(1)} %copy-done.56, bf16[2048,2048]{1,0:T(8,128)(2,1)S(1)} %constant_dynamic-update-slice_fusion.5), kind=kOutput, calls=%fused_computation.48 | convolution fusion | flops 8592031744 | bytes 16777216 | tf_op jit(solution)/shard_map/dot_general | solution.py:32
  673.9 5.3 fusion.102
  679.3 2.4 pad_maximum_fusion.grad_ref
  682.3 23.3 %retention_backward.1 = bf16[2048,3072]{1,0:T(8,128)(2,1)} custom-call(s32[1]{0:T(128)} %bitcast.which, bf16[2048,3072]{1,0:T(8,128)(2,1)} %convolution_convert_fusion.1.field_ref, f32[2048,256]{1,0:T(8,128)S(1)} %pad_maximum_fusion.1.angle_ref, f32[2048,128]{1,0:T(8,128)S(1)} %pad.4.info_ref, f32[8,1,256]{2,1,0:T(1,128)S(1)} %bitcast.77, ...), custom_call_target="tpu_custom_call" | custom-call | flops 8053063680 | bytes 31457280 | tf_op jit(solution)/shard_map/retention_backward/pallas_call | solution.py:251
  705.5 31.8 %convolution_convert_fusion = bf16[2048,3072]{1,0:T(8,128)(2,1)} fusion(bf16[2048,2048]{1,0:T(8,128)(2,1)S(1)} %bitcast.81, bf16[2048,3072]{1,0:T(8,128)(2,1)} %retention_backward.1), kind=kOutput, calls=%fused_computation | convolution fusion | flops 25776095232 | bytes 33554432 | tf_op jit(solution)/shard_map/dot_general | solution.py:32
  737.4 10.6 %fusion.45 = bf16[512,2048]{1,0:T(8,128)(2,1)S(1)} fusion(bf16[2048,3072]{1,0:T(8,128)(2,1)} %all-gather.5.cloned.1.call-done, bf16[2048,3072]{1,0:T(8,128)(2,1)} %retention_backward.1), kind=kOutput, calls=%fused_computation.67 | convolution fusion | flops 6443499520 | bytes 17825792 | tf_op jit(solution)/shard_map/dot_general | solution.py:28
  751.3 10.8 %fusion.37 = f32[512,2048]{1,0:T(8,128)S(1)} fusion(bf16[2048,3072]{1,0:T(8,128)(2,1)} %all-gather.5.cloned.1.call-done, bf16[2048,3072]{1,0:T(8,128)(2,1)} %retention_backward.1), kind=kOutput, calls=%fused_computation.51 | convolution fusion | flops 6442450944 | bytes 19922944 | tf_op jit(solution)/shard_map/dot_general | solution.py:28
  762.2 10.8 %fusion.41 = f32[512,2048]{1,0:T(8,128)S(1)} fusion(bf16[2048,3072]{1,0:T(8,128)(2,1)} %all-gather.5.cloned.1.call-done, bf16[2048,3072]{1,0:T(8,128)(2,1)} %retention_backward.1), kind=kOutput, calls=%fused_computation.55 | convolution fusion | flops 6442450944 | bytes 19922944 | tf_op jit(solution)/shard_map/dot_general | solution.py:28
  778.1 2.1 convert_element_type.244
  780.2 39.5 %collective-permute-done.31 = bf16[512,2048]{1,0:T(8,128)(2,1)} collective-permute-done((bf16[512,2048]{1,0:T(8,128)(2,1)}, bf16[512,2048]{1,0:T(8,128)(2,1)}, u32[]{:S(2)}, u32[]{:S(2)}) %collective-permute-start.31) | collective-permute-done | bytes 2097184 | tf_op jit(solution)/shard_map/ppermute | solution.py:37
  821.6 16.5 %fusion.13 = (f32[2048]{0:T(1024)S(1)}, f32[512]{0:T(512)S(1)}, f32[512]{0:T(512)S(1)}, f32[2048]{0:T(1024)S(1)}, f32[512,2048]{1,0:T(8,128)}) fusion(bf16[512,2048]{1,0:T(8,128)(2,1)S(1)} %copy-done.8, f32[512]{0:T(512)S(1)} %copy-done.46, f32[512]{0:T(512)S(1)} %copy-done.44, f32[2048]{0:T(1024)S(1)} %copy-done.40, ...), kind=kOutput, calls=%fused_computation.18 | convolution fusion | flops 6457125888 | bytes 26247168 | tf_op jit(solution)/shard_map/dot_general | solution.py:28
  838.1 39.0 %all-reduce.5 = (f32[2048]{0:T(1024)S(1)}, f32[2048]{0:T(1024)S(1)}, f32[2048]{0:T(1024)S(1)}, f32[2048]{0:T(1024)S(1)}) all-reduce(f32[2048]{0:T(1024)S(1)} %get-tuple-element.23, f32[2048]{0:T(1024)S(1)} %get-tuple-element.28, f32[2048]{0:T(1024)S(1)} %copy-done.41, ...), channel_id=2, replica_groups=mesh['dp'=8,'tensor'=4] {'dp','tensor'}, use_global_device_ids=true, to_apply=%region_11.12.clone | all-reduce | flops 8192 | bytes 65536
  879.4 5.3 fusion.12
  884.7 2.1 convert_element_type.246
  886.8 2.1 convert_element_type.242
  (331 shorter events, 120.3 us)
Async XLA Ops:
  7.2 14.9 %copy-start.6 = (bf16[512,2048]{1,0:T(8,128)(2,1)S(1)}, bf16[512,2048]{1,0:T(8,128)(2,1)}, u32[]{:S(2)}) copy-start(bf16[512,2048]{1,0:T(8,128)(2,1)} %param.14) | copy-start | bytes 6291460
  7.2 132.9 %all-gather.5.cloned.1.call-start = ((), (), s32[]{:S(2)}) async-start(), calls=%async_computation.4 | async-start | bytes 14155776 | tf_op jit(solution)/shard_map/all_gather | solution.py:291
  20.5 169.5 %all-gather.7.cloned.1.call-start = ((), (), s32[]{:S(2)}) async-start(), calls=%async_computation.5 | async-start | bytes 4718592 | tf_op jit(solution)/shard_map/all_gather | solution.py:292
  21.3 303.8 %all-gather.9.cloned.1.call-start = ((), (), s32[]{:S(2)}) async-start(), calls=%async_computation.6 | async-start | bytes 4718592 | tf_op jit(solution)/shard_map/all_gather | solution.py:294
  22.0 310.6 %all-gather.11.cloned.1.call-start = ((), (), s32[]{:S(2)}) async-start(), calls=%async_computation.7 | async-start | bytes 4718592 | tf_op jit(solution)/shard_map/all_gather | solution.py:293
  26.1 48.8 %collective-permute-start.1 = (bf16[512,2048]{1,0:T(8,128)(2,1)}, bf16[512,2048]{1,0:T(8,128)(2,1)S(1)}, u32[]{:S(2)}, u32[]{:S(2)}) collective-permute-start(bf16[512,2048]{1,0:T(8,128)(2,1)} %get-tuple-element.46), channel_id=1, source_target_pairs={{0,2},{1,3},{2,0},{3,1},{4,6},{5,7},{6,4},{7,5},{8,10},{9,11},{10,... | collective-permute-start | bytes 6291464 | tf_op jit(solution)/shard_map/ppermute | solution.py:37
  29.0 47.8 %collective-permute-start = (bf16[512,2048]{1,0:T(8,128)(2,1)}, bf16[512,2048]{1,0:T(8,128)(2,1)}, u32[]{:S(2)}, u32[]{:S(2)}) collective-permute-start(bf16[512,2048]{1,0:T(8,128)(2,1)} %get-tuple-element.46), channel_id=1, source_target_pairs={{0,1},{1,0},{2,3},{3,2},{4,5},{5,4},{6,7},{7,6},{8,9},{9,8},{10,11... | collective-permute-start | bytes 6291464 | tf_op jit(solution)/shard_map/ppermute | solution.py:37
  30.5 747.5 %reduce-scatter.9.cloned.1.call-start = ((), (), s32[]{:S(2)}) async-start(), calls=%async_computation.10 | async-start | bytes 4718592 | tf_op jit(solution)/shard_map/reduce_scatter | solution.py:340
  74.9 24.5 %collective-permute-start.2 = (bf16[256,2048]{1,0:T(8,128)(2,1)S(1)}, bf16[256,2048]{1,0:T(8,128)(2,1)S(1)}, u32[]{:S(2)}, u32[]{:S(2)}) collective-permute-start(bf16[256,2048]{1,0:T(8,128)(2,1)S(1)} %slice.272), channel_id=1, source_target_pairs={{0,1},{1,0},{2,3},{3,2},{4,5},{5,4},{6,7},{7,6},{8,9},{9,8},{10,11... | collective-permute-start | bytes 3145736 | tf_op jit(solution)/shard_map/ppermute | solution.py:37
  78.3 24.0 %collective-permute-start.3 = (bf16[256,2048]{1,0:T(8,128)(2,1)S(1)}, bf16[256,2048]{1,0:T(8,128)(2,1)S(1)}, u32[]{:S(2)}, u32[]{:S(2)}) collective-permute-start(bf16[256,2048]{1,0:T(8,128)(2,1)S(1)} %slice.273), channel_id=1, source_target_pairs={{0,2},{1,3},{2,0},{3,1},{4,6},{5,7},{6,4},{7,5},{8,10},{9,11},{10,... | collective-permute-start | bytes 3145736 | tf_op jit(solution)/shard_map/ppermute | solution.py:37
  140.1 32.7 %copy-start = (f32[2,256,256]{2,1,0:T(8,128)S(1)}, f32[2,256,256]{2,1,0:T(8,128)}, u32[]{:S(2)}) copy-start(f32[2,256,256]{2,1,0:T(8,128)} %exponential_select_fusion.decay_ref) | copy-start | bytes 1572868
  195.2 27.8 %collective-permute-start.4 = (bf16[256,2048]{1,0:T(8,128)(2,1)S(1)}, bf16[256,2048]{1,0:T(8,128)(2,1)S(1)}, u32[]{:S(2)}, u32[]{:S(2)}) collective-permute-start(bf16[256,2048]{1,0:T(8,128)(2,1)S(1)} %get-tuple-element.55), channel_id=1, source_target_pairs={{0,2},{1,3},{2,0},{3,1},{4,6},{5,7},{6,4},{7,5},{8,10},{9,11},{10,... | collective-permute-start | bytes 3145736 | tf_op jit(solution)/shard_map/ppermute | solution.py:37
  196.7 25.0 %collective-permute-start.6 = (bf16[256,2048]{1,0:T(8,128)(2,1)S(1)}, bf16[256,2048]{1,0:T(8,128)(2,1)S(1)}, u32[]{:S(2)}, u32[]{:S(2)}) collective-permute-start(bf16[256,2048]{1,0:T(8,128)(2,1)S(1)} %get-tuple-element.56), channel_id=1, source_target_pairs={{0,1},{1,0},{2,3},{3,2},{4,5},{5,4},{6,7},{7,6},{8,9},{9,8},{10,11... | collective-permute-start | bytes 3145736 | tf_op jit(solution)/shard_map/ppermute | solution.py:37
  222.4 48.6 %collective-permute-start.7 = (bf16[512,2048]{1,0:T(8,128)(2,1)S(1)}, bf16[512,2048]{1,0:T(8,128)(2,1)S(1)}, u32[]{:S(2)}, u32[]{:S(2)}) collective-permute-start(bf16[512,2048]{1,0:T(8,128)(2,1)S(1)} %pad_maximum_fusion.3), channel_id=1, source_target_pairs={{0,2},{1,3},{2,0},{3,1},{4,6},{5,7},{6,4},{7,5},{8,10},{9,11},{10,... | collective-permute-start | bytes 6291464 | tf_op jit(solution)/shard_map/ppermute | solution.py:37
  223.6 48.6 %copy-start.7 = (bf16[512,2048]{1,0:T(8,128)(2,1)S(1)}, bf16[512,2048]{1,0:T(8,128)(2,1)}, u32[]{:S(2)}) copy-start(bf16[512,2048]{1,0:T(8,128)(2,1)} %param.14) | copy-start | bytes 6291460
  223.6 48.6 %collective-permute-start.5 = (bf16[512,2048]{1,0:T(8,128)(2,1)S(1)}, bf16[512,2048]{1,0:T(8,128)(2,1)S(1)}, u32[]{:S(2)}, u32[]{:S(2)}) collective-permute-start(bf16[512,2048]{1,0:T(8,128)(2,1)S(1)} %pad_maximum_fusion.2), channel_id=1, source_target_pairs={{0,1},{1,0},{2,3},{3,2},{4,5},{5,4},{6,7},{7,6},{8,9},{9,8},{10,11... | collective-permute-start | bytes 6291464 | tf_op jit(solution)/shard_map/ppermute | solution.py:37
  225.2 92.0 %collective-permute-start.16 = (bf16[512,2048]{1,0:T(8,128)(2,1)S(1)}, bf16[512,2048]{1,0:T(8,128)(2,1)S(1)}, u32[]{:S(2)}, u32[]{:S(2)}) collective-permute-start(bf16[512,2048]{1,0:T(8,128)(2,1)S(1)} %copy-done.30), channel_id=1, source_target_pairs={{0,1},{1,0},{2,3},{3,2},{4,5},{5,4},{6,7},{7,6},{8,9},{9,8},{10,11... | collective-permute-start | bytes 6291464 | tf_op jit(solution)/shard_map/ppermute | solution.py:37
  225.7 95.5 %collective-permute-start.17 = (bf16[512,2048]{1,0:T(8,128)(2,1)S(1)}, bf16[512,2048]{1,0:T(8,128)(2,1)S(1)}, u32[]{:S(2)}, u32[]{:S(2)}) collective-permute-start(bf16[512,2048]{1,0:T(8,128)(2,1)S(1)} %copy-done.30), channel_id=1, source_target_pairs={{0,2},{1,3},{2,0},{3,1},{4,6},{5,7},{6,4},{7,5},{8,10},{9,11},{10,... | collective-permute-start | bytes 6291464 | tf_op jit(solution)/shard_map/ppermute | solution.py:37
  277.2 83.8 %collective-permute-start.9 = (bf16[512,2048]{1,0:T(8,128)(2,1)}, bf16[512,2048]{1,0:T(8,128)(2,1)}, u32[]{:S(2)}, u32[]{:S(2)}) collective-permute-start(bf16[512,2048]{1,0:T(8,128)(2,1)} %get-tuple-element.34), channel_id=1, source_target_pairs={{0,2},{1,3},{2,0},{3,1},{4,6},{5,7},{6,4},{7,5},{8,10},{9,11},{10,... | collective-permute-start | bytes 6291464 | tf_op jit(solution)/shard_map/ppermute | solution.py:37
  278.6 85.2 %collective-permute-start.8 = (bf16[512,2048]{1,0:T(8,128)(2,1)}, bf16[512,2048]{1,0:T(8,128)(2,1)}, u32[]{:S(2)}, u32[]{:S(2)}) collective-permute-start(bf16[512,2048]{1,0:T(8,128)(2,1)} %get-tuple-element.34), channel_id=1, source_target_pairs={{0,1},{1,0},{2,3},{3,2},{4,5},{5,4},{6,7},{7,6},{8,9},{9,8},{10,11... | collective-permute-start | bytes 6291464 | tf_op jit(solution)/shard_map/ppermute | solution.py:37
  319.7 89.3 %collective-permute-start.19 = (bf16[256,2048]{1,0:T(8,128)(2,1)}, bf16[256,2048]{1,0:T(8,128)(2,1)}, u32[]{:S(2)}, u32[]{:S(2)}) collective-permute-start(bf16[256,2048]{1,0:T(8,128)(2,1)} %slice.295), channel_id=1, source_target_pairs={{0,2},{1,3},{2,0},{3,1},{4,6},{5,7},{6,4},{7,5},{8,10},{9,11},{10,... | collective-permute-start | bytes 3145736 | tf_op jit(solution)/shard_map/ppermute | solution.py:37
  323.6 85.5 %collective-permute-start.18 = (bf16[256,2048]{1,0:T(8,128)(2,1)}, bf16[256,2048]{1,0:T(8,128)(2,1)}, u32[]{:S(2)}, u32[]{:S(2)}) collective-permute-start(bf16[256,2048]{1,0:T(8,128)(2,1)} %slice.294), channel_id=1, source_target_pairs={{0,1},{1,0},{2,3},{3,2},{4,5},{5,4},{6,7},{7,6},{8,9},{9,8},{10,11... | collective-permute-start | bytes 3145736 | tf_op jit(solution)/shard_map/ppermute | solution.py:37
  332.6 33.2 %copy-start.52 = (bf16[2048,1024]{1,0:T(8,128)(2,1)S(1)}, bf16[2048,1024]{1,0:T(8,128)(2,1)}, u32[]{:S(2)}) copy-start(bf16[2048,1024]{1,0:T(8,128)(2,1)} %all-gather.9.cloned.1.call-done) | copy-start | bytes 12582916
  339.5 78.5 %copy-start.57 = (bf16[512,1024]{1,0:T(8,128)(2,1)}, bf16[512,1024]{1,0:T(8,128)(2,1)S(1)}, u32[]{:S(2)}) copy-start(bf16[512,1024]{1,0:T(8,128)(2,1)S(1)} %fusion.63) | copy-start | bytes 3145732
  362.3 42.7 %collective-permute-start.10 = (bf16[256,2048]{1,0:T(8,128)(2,1)S(1)}, bf16[256,2048]{1,0:T(8,128)(2,1)S(1)}, u32[]{:S(2)}, u32[]{:S(2)}) collective-permute-start(bf16[256,2048]{1,0:T(8,128)(2,1)S(1)} %slice.286), channel_id=1, source_target_pairs={{0,1},{1,0},{2,3},{3,2},{4,5},{5,4},{6,7},{7,6},{8,9},{9,8},{10,11... | collective-permute-start | bytes 3145736 | tf_op jit(solution)/shard_map/ppermute | solution.py:37
  365.1 39.8 %collective-permute-start.11 = (bf16[256,2048]{1,0:T(8,128)(2,1)S(1)}, bf16[256,2048]{1,0:T(8,128)(2,1)S(1)}, u32[]{:S(2)}, u32[]{:S(2)}) collective-permute-start(bf16[256,2048]{1,0:T(8,128)(2,1)S(1)} %slice.287), channel_id=1, source_target_pairs={{0,2},{1,3},{2,0},{3,1},{4,6},{5,7},{6,4},{7,5},{8,10},{9,11},{10,... | collective-permute-start | bytes 3145736 | tf_op jit(solution)/shard_map/ppermute | solution.py:37
  384.9 12.4 %copy-start.28 = (f32[512,2048]{1,0:T(8,128)}, f32[512,2048]{1,0:T(8,128)S(1)}, u32[]{:S(2)}) copy-start(f32[512,2048]{1,0:T(8,128)S(1)} %fusion.140) | copy-start | bytes 12582916
  429.6 455.1 %reduce-scatter.11.cloned.1.call-start = ((), (), s32[]{:S(2)}) async-start(), calls=%async_computation.11 | async-start | bytes 4718592 | tf_op jit(solution)/shard_map/reduce_scatter | solution.py:341
  429.8 26.4 %collective-permute-start.20 = (bf16[256,2048]{1,0:T(8,128)(2,1)}, bf16[256,2048]{1,0:T(8,128)(2,1)S(1)}, u32[]{:S(2)}, u32[]{:S(2)}) collective-permute-start(bf16[256,2048]{1,0:T(8,128)(2,1)} %get-tuple-element.51), channel_id=1, source_target_pairs={{0,2},{1,3},{2,0},{3,1},{4,6},{5,7},{6,4},{7,5},{8,10},{9,11},{10,... | collective-permute-start | bytes 3145736 | tf_op jit(solution)/shard_map/ppermute | solution.py:37
  431.4 26.9 %collective-permute-start.22 = (bf16[256,2048]{1,0:T(8,128)(2,1)}, bf16[256,2048]{1,0:T(8,128)(2,1)S(1)}, u32[]{:S(2)}, u32[]{:S(2)}) collective-permute-start(bf16[256,2048]{1,0:T(8,128)(2,1)} %get-tuple-element.52), channel_id=1, source_target_pairs={{0,1},{1,0},{2,3},{3,2},{4,5},{5,4},{6,7},{7,6},{8,9},{9,8},{10,11... | collective-permute-start | bytes 3145736 | tf_op jit(solution)/shard_map/ppermute | solution.py:37
  432.9 23.3 %copy-start.29 = (f32[512,2048]{1,0:T(8,128)S(1)}, f32[512,2048]{1,0:T(8,128)}, u32[]{:S(2)}) copy-start(f32[512,2048]{1,0:T(8,128)} %copy-done.28) | copy-start | bytes 12582916
  438.2 18.3 %copy-start.21 = (bf16[256,2048]{1,0:T(8,128)(2,1)S(1)}, bf16[256,2048]{1,0:T(8,128)(2,1)}, u32[]{:S(2)}) copy-start(bf16[256,2048]{1,0:T(8,128)(2,1)} %slice.388) | copy-start | bytes 3145732
  438.4 42.9 %collective-permute-start.12 = (bf16[256,2048]{1,0:T(8,128)(2,1)S(1)}, bf16[256,2048]{1,0:T(8,128)(2,1)S(1)}, u32[]{:S(2)}, u32[]{:S(2)}) collective-permute-start(bf16[256,2048]{1,0:T(8,128)(2,1)S(1)} %get-tuple-element.53), channel_id=1, source_target_pairs={{0,2},{1,3},{2,0},{3,1},{4,6},{5,7},{6,4},{7,5},{8,10},{9,11},{10,... | collective-permute-start | bytes 3145736 | tf_op jit(solution)/shard_map/ppermute | solution.py:37
  439.0 19.3 %copy-start.27 = (f32[512,2048]{1,0:T(8,128)S(1)}, f32[512,2048]{1,0:T(8,128)}, u32[]{:S(2)}) copy-start(f32[512,2048]{1,0:T(8,128)} %copy-done.26) | copy-start | bytes 12582916
  439.1 41.1 %collective-permute-start.14 = (bf16[256,2048]{1,0:T(8,128)(2,1)S(1)}, bf16[256,2048]{1,0:T(8,128)(2,1)S(1)}, u32[]{:S(2)}, u32[]{:S(2)}) collective-permute-start(bf16[256,2048]{1,0:T(8,128)(2,1)S(1)} %get-tuple-element.54), channel_id=1, source_target_pairs={{0,1},{1,0},{2,3},{3,2},{4,5},{5,4},{6,7},{7,6},{8,9},{9,8},{10,11... | collective-permute-start | bytes 3145736 | tf_op jit(solution)/shard_map/ppermute | solution.py:37
  456.7 23.5 %copy-start.25 = (f32[512,2048]{1,0:T(8,128)S(1)}, f32[512,2048]{1,0:T(8,128)}, u32[]{:S(2)}) copy-start(f32[512,2048]{1,0:T(8,128)} %copy-done.24) | copy-start | bytes 12582916
  456.7 68.4 %collective-permute-start.21 = (bf16[512,2048]{1,0:T(8,128)(2,1)S(1)}, bf16[512,2048]{1,0:T(8,128)(2,1)S(1)}, u32[]{:S(2)}, u32[]{:S(2)}) collective-permute-start(bf16[512,2048]{1,0:T(8,128)(2,1)S(1)} %pad_maximum_fusion.6), channel_id=1, source_target_pairs={{0,1},{1,0},{2,3},{3,2},{4,5},{5,4},{6,7},{7,6},{8,9},{9,8},{10,11... | collective-permute-start | bytes 6291464 | tf_op jit(solution)/shard_map/ppermute | solution.py:37
  458.6 21.8 %copy-start.19 = (bf16[256,2048]{1,0:T(8,128)(2,1)S(1)}, bf16[256,2048]{1,0:T(8,128)(2,1)}, u32[]{:S(2)}) copy-start(bf16[256,2048]{1,0:T(8,128)(2,1)} %slice.389) | copy-start | bytes 3145732
  458.8 22.6 %copy-start.23 = (f32[512,2048]{1,0:T(8,128)S(1)}, f32[512,2048]{1,0:T(8,128)}, u32[]{:S(2)}) copy-start(f32[512,2048]{1,0:T(8,128)} %copy-done.22) | copy-start | bytes 12582916
  458.8 66.3 %collective-permute-start.23 = (bf16[512,2048]{1,0:T(8,128)(2,1)S(1)}, bf16[512,2048]{1,0:T(8,128)(2,1)S(1)}, u32[]{:S(2)}, u32[]{:S(2)}) collective-permute-start(bf16[512,2048]{1,0:T(8,128)(2,1)S(1)} %pad_maximum_fusion.7), channel_id=1, source_target_pairs={{0,2},{1,3},{2,0},{3,1},{4,6},{5,7},{6,4},{7,5},{8,10},{9,11},{10,... | collective-permute-start | bytes 6291464 | tf_op jit(solution)/shard_map/ppermute | solution.py:37
  480.7 84.8 %collective-permute-start.15 = (bf16[512,2048]{1,0:T(8,128)(2,1)S(1)}, bf16[512,2048]{1,0:T(8,128)(2,1)S(1)}, u32[]{:S(2)}, u32[]{:S(2)}) collective-permute-start(bf16[512,2048]{1,0:T(8,128)(2,1)S(1)} %pad_maximum_fusion.5), channel_id=1, source_target_pairs={{0,2},{1,3},{2,0},{3,1},{4,6},{5,7},{6,4},{7,5},{8,10},{9,11},{10,... | collective-permute-start | bytes 6291464 | tf_op jit(solution)/shard_map/ppermute | solution.py:37
  481.9 84.9 %collective-permute-start.13 = (bf16[512,2048]{1,0:T(8,128)(2,1)S(1)}, bf16[512,2048]{1,0:T(8,128)(2,1)}, u32[]{:S(2)}, u32[]{:S(2)}) collective-permute-start(bf16[512,2048]{1,0:T(8,128)(2,1)S(1)} %pad_maximum_fusion.4), channel_id=1, source_target_pairs={{0,1},{1,0},{2,3},{3,2},{4,5},{5,4},{6,7},{7,6},{8,9},{9,8},{10,11... | collective-permute-start | bytes 6291464 | tf_op jit(solution)/shard_map/ppermute | solution.py:37
  485.9 80.9 %copy-start.5 = (f32[512,2048]{1,0:T(8,128)S(1)}, f32[512,2048]{1,0:T(8,128)}, u32[]{:S(2)}) copy-start(f32[512,2048]{1,0:T(8,128)} %copy-done.4) | copy-start | bytes 12582916
  490.6 82.1 %copy-start.31 = (bf16[512,2048]{1,0:T(8,128)(2,1)S(1)}, bf16[512,2048]{1,0:T(8,128)(2,1)}, u32[]{:S(2)}) copy-start(bf16[512,2048]{1,0:T(8,128)(2,1)} %param.15) | copy-start | bytes 6291460
  592.7 294.1 %reduce-scatter.7.cloned.1.call-start = ((), (), s32[]{:S(2)}) async-start(), calls=%async_computation.9 | async-start | bytes 4718592 | tf_op jit(solution)/shard_map/reduce_scatter | solution.py:342
  593.1 44.6 %collective-permute-start.25 = (bf16[512,2048]{1,0:T(8,128)(2,1)}, bf16[512,2048]{1,0:T(8,128)(2,1)S(1)}, u32[]{:S(2)}, u32[]{:S(2)}) collective-permute-start(bf16[512,2048]{1,0:T(8,128)(2,1)} %get-tuple-element.36), channel_id=1, source_target_pairs={{0,2},{1,3},{2,0},{3,1},{4,6},{5,7},{6,4},{7,5},{8,10},{9,11},{10,... | collective-permute-start | bytes 6291464 | tf_op jit(solution)/shard_map/ppermute | solution.py:37
  593.7 46.5 %collective-permute-start.24 = (bf16[512,2048]{1,0:T(8,128)(2,1)}, bf16[512,2048]{1,0:T(8,128)(2,1)S(1)}, u32[]{:S(2)}, u32[]{:S(2)}) collective-permute-start(bf16[512,2048]{1,0:T(8,128)(2,1)} %get-tuple-element.36), channel_id=1, source_target_pairs={{0,1},{1,0},{2,3},{3,2},{4,5},{5,4},{6,7},{7,6},{8,9},{9,8},{10,11... | collective-permute-start | bytes 6291464 | tf_op jit(solution)/shard_map/ppermute | solution.py:37
  595.3 46.7 %copy-start.51 = (bf16[1024,2048]{1,0:T(8,128)(2,1)S(1)}, bf16[1024,2048]{1,0:T(8,128)(2,1)}, u32[]{:S(2)}) copy-start(bf16[1024,2048]{1,0:T(8,128)(2,1)} %all-gather.7.cloned.1.call-done) | copy-start | bytes 12582916
  637.8 22.7 %collective-permute-start.26 = (bf16[256,2048]{1,0:T(8,128)(2,1)S(1)}, bf16[256,2048]{1,0:T(8,128)(2,1)S(1)}, u32[]{:S(2)}, u32[]{:S(2)}) collective-permute-start(bf16[256,2048]{1,0:T(8,128)(2,1)S(1)} %slice.300), channel_id=1, source_target_pairs={{0,1},{1,0},{2,3},{3,2},{4,5},{5,4},{6,7},{7,6},{8,9},{9,8},{10,11... | collective-permute-start | bytes 3145736 | tf_op jit(solution)/shard_map/ppermute | solution.py:37
  640.3 21.3 %collective-permute-start.27 = (bf16[256,2048]{1,0:T(8,128)(2,1)S(1)}, bf16[256,2048]{1,0:T(8,128)(2,1)S(1)}, u32[]{:S(2)}, u32[]{:S(2)}) collective-permute-start(bf16[256,2048]{1,0:T(8,128)(2,1)S(1)} %slice.301), channel_id=1, source_target_pairs={{0,2},{1,3},{2,0},{3,1},{4,6},{5,7},{6,4},{7,5},{8,10},{9,11},{10,... | collective-permute-start | bytes 3145736 | tf_op jit(solution)/shard_map/ppermute | solution.py:37
  645.9 16.8 %copy-start.56 = (bf16[2048,1024]{1,0:T(8,128)(2,1)S(1)}, bf16[2048,1024]{1,0:T(8,128)(2,1)}, u32[]{:S(2)}) copy-start(bf16[2048,1024]{1,0:T(8,128)(2,1)} %get-tuple-element.17) | copy-start | bytes 12582916
  673.7 215.2 %reduce-scatter.5.cloned.1.call-start = ((), (), s32[]{:S(2)}) async-start(), calls=%async_computation.8 | async-start | bytes 14155776 | tf_op jit(solution)/shard_map/reduce_scatter | solution.py:343
  679.3 26.2 %slice-start.2 = ((s8[8388608]{0:T(1024)(128)(4,1)}), s8[4194304]{0:T(1024)(128)(4,1)S(1)}, s32[]{:S(2)}) async-start(s8[8388608]{0:T(1024)(128)(4,1)} %bitcast.80), calls=%async_computation.14 | async-start | bytes 8388608
  682.3 23.3 %slice-start.3 = ((s8[8388608]{0:T(1024)(128)(4,1)}), s8[4194304]{0:T(1024)(128)(4,1)S(1)}, s32[]{:S(2)}) async-start(s8[8388608]{0:T(1024)(128)(4,1)} %bitcast.80), calls=%async_computation.15 | async-start | bytes 8388608
  748.3 27.6 %collective-permute-start.28 = (bf16[256,2048]{1,0:T(8,128)(2,1)S(1)}, bf16[256,2048]{1,0:T(8,128)(2,1)S(1)}, u32[]{:S(2)}, u32[]{:S(2)}) collective-permute-start(bf16[256,2048]{1,0:T(8,128)(2,1)S(1)} %get-tuple-element.49), channel_id=1, source_target_pairs={{0,2},{1,3},{2,0},{3,1},{4,6},{5,7},{6,4},{7,5},{8,10},{9,11},{10,... | collective-permute-start | bytes 3145736 | tf_op jit(solution)/shard_map/ppermute | solution.py:37
  749.8 23.5 %collective-permute-start.30 = (bf16[256,2048]{1,0:T(8,128)(2,1)S(1)}, bf16[256,2048]{1,0:T(8,128)(2,1)S(1)}, u32[]{:S(2)}, u32[]{:S(2)}) collective-permute-start(bf16[256,2048]{1,0:T(8,128)(2,1)S(1)} %get-tuple-element.50), channel_id=1, source_target_pairs={{0,1},{1,0},{2,3},{3,2},{4,5},{5,4},{6,7},{7,6},{8,9},{9,8},{10,11... | collective-permute-start | bytes 3145736 | tf_op jit(solution)/shard_map/ppermute | solution.py:37
  775.1 46.4 %copy-start.8 = (bf16[512,2048]{1,0:T(8,128)(2,1)S(1)}, bf16[512,2048]{1,0:T(8,128)(2,1)}, u32[]{:S(2)}) copy-start(bf16[512,2048]{1,0:T(8,128)(2,1)} %param.14) | copy-start | bytes 6291460
  775.1 46.4 %copy-start.40 = (f32[2048]{0:T(1024)S(1)}, f32[2048]{0:T(1024)}, u32[]{:S(2)}) copy-start(f32[2048]{0:T(1024)} %param.17) | copy-start | bytes 24580
  775.1 46.4 %copy-start.44 = (f32[512]{0:T(512)S(1)}, f32[512]{0:T(512)}, u32[]{:S(2)}) copy-start(f32[512]{0:T(512)} %copy-done.43) | copy-start | bytes 6148
  775.1 46.4 %copy-start.46 = (f32[512]{0:T(512)S(1)}, f32[512]{0:T(512)}, u32[]{:S(2)}) copy-start(f32[512]{0:T(512)} %copy-done.45) | copy-start | bytes 6148
  775.1 44.5 %collective-permute-start.31 = (bf16[512,2048]{1,0:T(8,128)(2,1)}, bf16[512,2048]{1,0:T(8,128)(2,1)}, u32[]{:S(2)}, u32[]{:S(2)}) collective-permute-start(bf16[512,2048]{1,0:T(8,128)(2,1)} %pad_maximum_fusion.9), channel_id=1, source_target_pairs={{0,2},{1,3},{2,0},{3,1},{4,6},{5,7},{6,4},{7,5},{8,10},{9,11},{10,... | collective-permute-start | bytes 6291464 | tf_op jit(solution)/shard_map/ppermute | solution.py:37
  777.7 43.9 %collective-permute-start.29 = (bf16[512,2048]{1,0:T(8,128)(2,1)}, bf16[512,2048]{1,0:T(8,128)(2,1)}, u32[]{:S(2)}, u32[]{:S(2)}) collective-permute-start(bf16[512,2048]{1,0:T(8,128)(2,1)} %pad_maximum_fusion.8), channel_id=1, source_target_pairs={{0,1},{1,0},{2,3},{3,2},{4,5},{5,4},{6,7},{7,6},{8,9},{9,8},{10,11... | collective-permute-start | bytes 6291464 | tf_op jit(solution)/shard_map/ppermute | solution.py:37
  780.2 57.9 %copy-start.41 = (f32[2048]{0:T(1024)S(1)}, f32[2048]{0:T(1024)}, u32[]{:S(2)}) copy-start(f32[2048]{0:T(1024)} %get-tuple-element.21) | copy-start | bytes 24580
  780.2 57.9 %copy-start.42 = (f32[2048]{0:T(1024)S(1)}, f32[2048]{0:T(1024)}, u32[]{:S(2)}) copy-start(f32[2048]{0:T(1024)} %get-tuple-element.27) | copy-start | bytes 24580
  (50 other events, 214.3 us)
Sparse Core Ops, SparseCore 0:
  20.7 119.4 all-gather.4
  141.7 46.0 all-gather.6
  189.4 45.2 all-gather.8
  236.2 46.5 all-gather.10
  429.7 48.1 reduce-scatter.8
  592.8 47.3 reduce-scatter.10
  673.8 48.1 reduce-scatter.6
  737.5 128.1 reduce-scatter.4

commit v2 on v1

--- a/solution.py
+++ b/solution.py
@@ -10,7 +10,7 @@
 KEY = 256
 VAL = 512
 CHUNK = 256
-HEAD = 2 * KEY + 2 * VAL
+QKV = 2 * KEY + VAL
 
 norm_epsilon = 1e-05
 group_floor = 0.5
@@ -37,22 +37,27 @@
     return lax.ppermute(values, "tensor", pairs)
 
 
-def gather_pieces(own, devices):
+def after(values, *tokens):
+    return lax.optimization_barrier((values, tokens))[0]
+
+
+def gather_pieces(own, devices, between=()):
     if devices != 4:
         whole = lax.all_gather(own, "tensor", axis=0, tiled=True)
         return list(jnp.split(whole, devices, axis=0))
     half = own.shape[0] // 2
     from_x = tensor_permute(own, 1)
     from_y = tensor_permute(own, 2)
-    lower = tensor_permute(from_y[:half], 1)
-    upper = tensor_permute(from_x[half:], 2)
+    lower, upper = after((from_y[:half], from_x[half:]), *between)
+    lower = tensor_permute(lower, 1)
+    upper = tensor_permute(upper, 2)
     return [own, from_x, from_y, jnp.concatenate([lower, upper], axis=0)]
 
 
 def scatter_sum(terms):
     if len(terms) != 4:
         stacked = jnp.concatenate([term.astype(bf16) for term in terms], axis=0)
-        return lax.psum_scatter(stacked, "tensor", scatter_dimension=0, tiled=True).astype(f32)
+        return lax.psum_scatter(stacked, "tensor", scatter_dimension=0, tiled=True).astype(f32), (stacked,), (stacked,)
     own, over_x, over_y, across = terms
     half = own.shape[0] // 2
     across = across.astype(bf16)
@@ -62,7 +67,67 @@
     over_x = jnp.concatenate([over_x[:half], over_x[half:] + second.astype(f32)], axis=0)
     by_x = tensor_permute(over_x.astype(bf16), 1)
     by_y = tensor_permute(over_y.astype(bf16), 2)
-    return own + by_x.astype(f32) + by_y.astype(f32)
+    return own + by_x.astype(f32) + by_y.astype(f32), (first, second), (by_x, by_y)
+
+
+def spread_sum_kernel(tensor_devices, devices, given_ref, sum_ref, landed_ref, send_sem, recv_sem):
+    here = lax.axis_index("dp") * tensor_devices + lax.axis_index("tensor")
+
+    def partner(k):
+        other = lax.rem(here + k, devices)
+        return other, (lax.div(other, tensor_devices), lax.rem(other, tensor_devices))
+
+    def copy(k):
+        other, device = partner(k)
+        return pltpu.make_async_remote_copy(
+            src_ref=given_ref.at[other],
+            dst_ref=landed_ref.at[k],
+            send_sem=send_sem.at[k],
+            recv_sem=recv_sem.at[k],
+            device_id=device,
+            device_id_type=pl.DeviceIdType.MESH,
+        )
+
+    barrier = pltpu.get_barrier_semaphore()
+
+    @pl.loop(1, devices)
+    def _(k):
+        pl.semaphore_signal(barrier, inc=1, device_id=partner(k)[1], device_id_type=pl.DeviceIdType.MESH)
+
+    pl.semaphore_wait(barrier, devices - 1)
+
+    @pl.loop(1, devices)
+    def _(k):
+        copy(k).start()
+
+    sum_ref[...] = given_ref[here]
+
+    @pl.loop(1, devices)
+    def _(k):
+        copy(k).wait()
+        sum_ref[...] += landed_ref[k]
+
+
+def spread_sum(vectors):
+    dp, tensor = lax.axis_size("dp"), lax.axis_size("tensor")
+    devices = dp * tensor
+    part = vectors[0].shape[0] // devices
+    given = jnp.stack([v.reshape(devices, part) for v in vectors], axis=1)
+    given = jnp.pad(given, ((0, 0), (0, 8 - len(vectors)), (0, 128 - part)))
+    total = pl.pallas_call(
+        functools.partial(spread_sum_kernel, tensor, devices),
+        out_shape=jax.ShapeDtypeStruct((8, 128), f32),
+        in_specs=[pl.BlockSpec(memory_space=pltpu.VMEM)],
+        out_specs=pl.BlockSpec(memory_space=pltpu.VMEM),
+        scratch_shapes=[
+            pltpu.VMEM((devices, 8, 128), f32),
+            pltpu.SemaphoreType.DMA((devices,)),
+            pltpu.SemaphoreType.DMA((devices,)),
+        ],
+        compiler_params=pltpu.CompilerParams(collective_id=1, has_side_effects=True),
+        name="spread_sum",
+    )(given)
+    return [total[i, :part] for i in range(len(vectors))]
 
 
 def normalize(values):
@@ -99,19 +164,19 @@
     return jnp.concatenate([a * cosine + b * sine, b * cosine - a * sine], axis=1)
 
 
-def head_parts(field, angles, head):
-    base = head * HEAD
+def head_parts(field_ref, angles, heads, head):
     cosine = angles[:, : KEY // 2]
     sine = angles[:, KEY // 2 :]
-    query = turn(field[:, base : base + KEY].astype(f32), cosine, sine).astype(bf16)
-    key = turn(field[:, base + KEY : base + 2 * KEY].astype(f32), cosine, sine)
+    query_at = head * KEY
+    key_at = (heads + head) * KEY
+    value_at = 2 * heads * KEY + head * VAL
+    query = turn(field_ref[:, query_at : query_at + KEY].astype(f32), cosine, sine).astype(bf16)
+    key = turn(field_ref[:, key_at : key_at + KEY].astype(f32), cosine, sine)
     key = (key * key_scale).astype(bf16)
-    value = field[:, base + 2 * KEY : base + 2 * KEY + VAL]
-    gate = field[:, base + 2 * KEY + VAL : base + HEAD].astype(f32)
-    return query, key, value, gate
-
-
-def retention_forward(heads, which, field_ref, angle_ref, info_ref, row_ref, decay_ref, gated_ref, grouped_ref, scale_ref, past_ref, state_ref):
+    return query, key, field_ref[:, value_at : value_at + VAL]
+
+
+def retention_forward(heads, which, field_ref, gate_ref, angle_ref, info_ref, row_ref, decay_ref, gated_ref, grouped_ref, scale_ref, past_ref, state_ref):
     @pl.when(pl.program_id(0) == 0)
     def _():
         state_ref[...] = jnp.zeros_like(state_ref)
@@ -120,7 +185,9 @@
     info = info_ref[...]
     same = info[:, 0:1] == row_ref[0]
     for head in range(heads):
-        query, key, value, gate = head_parts(field_ref[...], angles, head)
+        query, key, value = head_parts(field_ref, angles, heads, head)
+        columns = slice(head * VAL, (head + 1) * VAL)
+        gate = gate_ref[:, columns].astype(f32)
         into = info[:, 1 + 2 * head : 2 + 2 * head]
         onward = info[:, 2 + 2 * head : 3 + 2 * head]
         state = state_ref[head]
@@ -134,13 +201,12 @@
         scale = lax.rsqrt(jnp.mean(centred * centred, axis=-1, keepdims=True) + group_floor)
         grouped = centred * scale
         gated = gate / (1.0 + jnp.exp(-gate)) * grouped
-        columns = slice(head * VAL, (head + 1) * VAL)
         gated_ref[:, columns] = gated.astype(bf16)
         grouped_ref[:, columns] = grouped.astype(bf16)
         scale_ref[:, head * 128 : (head + 1) * 128] = jnp.broadcast_to(scale, (CHUNK, 128))
 
 
-def retention_backward(heads, which, field_ref, angle_ref, info_ref, row_ref, decay_ref, grad_ref, grouped_ref, scale_ref, past_ref, back_ref, state_ref):
+def retention_backward(heads, which, field_ref, gate_ref, angle_ref, info_ref, row_ref, decay_ref, grad_ref, grouped_ref, scale_ref, past_ref, back_ref, state_ref):
     @pl.when(pl.program_id(0) == 0)
     def _():
         state_ref[...] = jnp.zeros_like(state_ref)
@@ -151,16 +217,14 @@
     info = info_ref[...]
     same = info[:, 0:1] == row_ref[0]
     for head in range(heads):
-        query, key, value, gate = head_parts(field_ref[...], angles, head)
+        query, key, value = head_parts(field_ref, angles, heads, head)
+        columns = slice(head * VAL, (head + 1) * VAL)
+        gate = gate_ref[:, columns].astype(f32)
         into = info[:, 1 + 2 * head : 2 + 2 * head]
         onward = info[:, 2 + 2 * head : 3 + 2 * head]
-        columns = slice(head * VAL, (head + 1) * VAL)
-        gated_grad = grad_ref[:, columns].astype(f32)
         grouped = grouped_ref[:, columns].astype(f32)
         scale = scale_ref[:, head * 128 : head * 128 + 1]
-        sigmoid = 1.0 / (1.0 + jnp.exp(-gate))
-        gate_grad = gated_grad * grouped * (sigmoid * (1.0 + gate * (1.0 - sigmoid)))
-        c = gated_grad * (gate * sigmoid)
+        c = grad_ref[:, columns].astype(f32) * (gate / (1.0 + jnp.exp(-gate)))
         mean_c = jnp.mean(c, axis=-1, keepdims=True)
         mean_cx = jnp.mean(c * grouped, axis=-1, keepdims=True)
         out_grad = (scale * (c - mean_c - grouped * mean_cx)).astype(bf16)
@@ -175,11 +239,12 @@
         key_grad = dot_tn(score_grad, query) + onward * dot_nt(value, state_low)
         moved = (query.astype(f32) * into).astype(bf16)
         state_ref[head] = into[CHUNK - 1 :, :] * state + dot_tn(moved, out_grad)
-        base = head * HEAD
-        back_ref[:, base : base + KEY] = turn_back(query_grad, cosine, sine).astype(bf16)
-        back_ref[:, base + KEY : base + 2 * KEY] = (turn_back(key_grad, cosine, sine) * key_scale).astype(bf16)
-        back_ref[:, base + 2 * KEY : base + 2 * KEY + VAL] = value_grad.astype(bf16)
-        back_ref[:, base + 2 * KEY + VAL : base + HEAD] = gate_grad.astype(bf16)
+        query_at = head * KEY
+        key_at = (heads + head) * KEY
+        value_at = 2 * heads * KEY + head * VAL
+        back_ref[:, query_at : query_at + KEY] = turn_back(query_grad, cosine, sine).astype(bf16)
+        back_ref[:, key_at : key_at + KEY] = (turn_back(key_grad, cosine, sine) * key_scale).astype(bf16)
+        back_ref[:, value_at : value_at + VAL] = value_grad.astype(bf16)
 
 
 def retention_tables(segment, heads, first_head):
@@ -211,7 +276,7 @@
     return angles, info, keys, decay
 
 
-def retention_call(backward, which, piece_rows, heads, field, tables, extra):
+def retention_call(backward, which, piece_rows, heads, field, gate, tables, extra):
     rows = field.shape[0]
     chunks = rows // CHUNK
     angles, info, keys, decay = tables
@@ -228,7 +293,8 @@
         return pl.BlockSpec((CHUNK, width), lambda i, w: (place(i, w), 0))
 
     in_specs = [
-        placed(heads * HEAD),
+        placed(heads * QKV),
+        placed(heads * VAL),
         pl.BlockSpec((CHUNK, KEY), lambda i, w: (step(i), 0)),
         pl.BlockSpec((CHUNK, 128), lambda i, w: (step(i), 0)),
         pl.BlockSpec((1, 1, CHUNK), lambda i, w: (step(i), 0, 0)),
@@ -237,8 +303,8 @@
     past_spec = pl.BlockSpec((1, heads, KEY, VAL), lambda i, w: (step(i), 0, 0, 0))
     if backward:
         in_specs += [placed(heads * VAL), placed(heads * VAL), placed(heads * 128), past_spec]
-        out_specs = placed(heads * HEAD)
-        out_shape = jax.ShapeDtypeStruct((rows, heads * HEAD), bf16)
+        out_specs = placed(heads * QKV)
+        out_shape = jax.ShapeDtypeStruct((rows, heads * QKV), bf16)
     else:
         out_specs = [placed(heads * VAL), placed(heads * VAL), placed(heads * 128), past_spec]
         out_shape = [
@@ -263,11 +329,248 @@
         ),
         cost_estimate=pl.CostEstimate(
             flops=products * chunks * heads * 2 * CHUNK * CHUNK * CHUNK,
-            bytes_accessed=(5 if backward else 4) * rows * heads * HEAD,
+            bytes_accessed=(5 if backward else 4) * rows * heads * (QKV + VAL),
             transcendentals=rows * heads * VAL,
         ),
         name="retention_backward" if backward else "retention_forward",
-    )(which, field, angles, info, keys, decay, *extra)
+    )(which, field, gate, angles, info, keys, decay, *extra)
+
+
+MESH = pl.DeviceIdType.MESH
+
+
+def opening_kernel(
+    query_ref, key_ref, value_ref, gate_ref, token_ref, gain_ref, bias_ref, cot_ref,
+    w_qkv_ref, w_gate_ref, normed_ref, cot_all_ref,
+    w_qkv, w_gate, normed, token_own, cot_own, cot_got,
+    local_sem, out_sem, up_send, up_recv, down_send, down_recv, core_send, core_recv, row_send, row_recv,
+):
+    dp = lax.axis_index("dp")
+    tensor = lax.axis_index("tensor")
+    z = lax.div(dp, 2)
+    layers = lax.div(lax.axis_size("dp"), 2)
+    shard_rows = query_ref.shape[0]
+    rows = token_ref.shape[0]
+    half = rows // 2
+    above = (dp + 2, tensor)
+    below = (dp - 2, tensor)
+    twin = (dp + 1 - 2 * lax.rem(dp, 2), tensor)
+    over_x = (dp, tensor + 1 - 2 * lax.rem(tensor, 2))
+    over_y = (dp, lax.rem(tensor + 2, 4))
+
+    keys = query_ref.shape[1]
+    values = value_ref.shape[1]
+    mine = pl.ds(pl.multiple_of(dp * shard_rows, shard_rows), shard_rows)
+    places = [
+        (query_ref, w_qkv.at[mine, pl.ds(0, keys)]),
+        (key_ref, w_qkv.at[mine, pl.ds(keys, keys)]),
+        (value_ref, w_qkv.at[mine, pl.ds(2 * keys, values)]),
+        (gate_ref, w_gate.at[mine]),
+        (token_ref, token_own),
+        (cot_ref.at[pl.ds(0, half)], cot_own),
+    ]
+    local = [pltpu.make_async_copy(a, b, local_sem.at[i]) for i, (a, b) in enumerate(places)]
+    for copy in local:
+        copy.start()
+
+    barrier = pltpu.get_barrier_semaphore()
+
+    def greet(device):
+        pl.semaphore_signal(barrier, inc=1, device_id=device, device_id_type=MESH)
+
+    for device in (twin, over_x, over_y):
+        greet(device)
+    pl.when(z < layers - 1)(lambda: greet(above))
+    pl.when(z > 0)(lambda: greet(below))
+    pl.semaphore_wait(barrier, 3 + (z < layers - 1).astype(jnp.int32) + (z > 0).astype(jnp.int32))
+    for copy in local[:4]:
+        copy.wait()
+
+    def weight_copies(shard, send_sem, recv_sem, step, device):
+        place = pl.ds(pl.multiple_of(shard * shard_rows, shard_rows), shard_rows)
+        return [
+            pltpu.make_async_remote_copy(
+                src_ref=ref.at[place], dst_ref=ref.at[place],
+                send_sem=send_sem.at[step, i], recv_sem=recv_sem.at[step, i],
+                device_id=device, device_id_type=MESH,
+            )
+            for i, ref in enumerate((w_qkv, w_gate))
+        ]
+
+    def shard_out(shard, slot):
+        place = pl.ds(pl.multiple_of(shard * shard_rows, shard_rows), shard_rows)
+        return [
+            pltpu.make_async_copy(w_qkv.at[place], w_qkv_ref.at[place], out_sem.at[slot, 0]),
+            pltpu.make_async_copy(w_gate.at[place], w_gate_ref.at[place], out_sem.at[slot, 1]),
+        ]
+
+    def start(copies):
+        for copy in copies:
+            copy.start()
+
+    def wait_send(copies):
+        for copy in copies:
+            copy.wait_send()
+
+    def wait_recv(copies):
+        for copy in copies:
+            copy.wait_recv()
+
+    def up(j):
+        return weight_copies(dp - 2 * j, up_send, up_recv, j, above)
+
+    def down(j):
+        return weight_copies(dp + 2 * j, down_send, down_recv, j, below)
+
+    def to_twin(j):
+        return weight_copies(dp + 2 * j, core_send, core_recv, j + 3, twin)
+
+    def from_twin(j):
+        return weight_copies(twin[0] + 2 * j, core_send, core_recv, j + 3, twin)
+
+    def step(j):
+        @pl.when(z - j >= 0)
+        def _():
+            wait_recv(weight_copies(dp - 2 * j, up_send, up_recv, j - 1, twin))
+            if j < 3:
+                pl.when(z < layers - 1)(lambda: start(up(j)))
+            start(to_twin(-j))
+            start(shard_out(dp - 2 * j, 3 - j))
+
+        @pl.when(z + j < layers)
+        def _():
+            wait_recv(weight_copies(dp + 2 * j, down_send, down_recv, j - 1, twin))
+            if j < 3:
+                pl.when(z > 0)(lambda: start(down(j)))
+            start(to_twin(j))
+            start(shard_out(dp + 2 * j, 3 + j))
+
+    pl.when(z < layers - 1)(lambda: start(up(0)))
+    pl.when(z > 0)(lambda: start(down(0)))
+    start(to_twin(0))
+    start(shard_out(dp, 3))
+
+    local[4].wait()
+
+    @pl.loop(0, rows // 64)
+    def _(i):
+        block = pl.ds(pl.multiple_of(i * 64, 64), 64)
+        unit, _ = normalize(token_own[block, :].astype(f32))
+        normed[block, :] = (unit * gain_ref[...] + bias_ref[...]).astype(bf16)
+
+    def row_copy(index, src, dst, device):
+        return pltpu.make_async_remote_copy(
+            src_ref=src, dst_ref=dst, send_sem=row_send.at[index], recv_sem=row_recv.at[index],
+            device_id=device, device_id_type=MESH,
+        )
+
+    local[5].wait()
+    over = [
+        row_copy(0, normed.at[pl.ds(0, rows)], normed.at[pl.ds(rows, rows)], over_x),
+        row_copy(1, normed.at[pl.ds(0, rows)], normed.at[pl.ds(2 * rows, rows)], over_y),
+    ]
+    start(over)
+    step(1)
+    wait_recv(over)
+    onward = [
+        row_copy(2, normed.at[pl.ds(2 * rows, half)], normed.at[pl.ds(3 * rows, half)], over_x),
+        row_copy(3, normed.at[pl.ds(rows + half, half)], normed.at[pl.ds(3 * rows + half, half)], over_y),
+    ]
+    start(onward)
+    cots = [
+        row_copy(4, cot_own, cot_got.at[0], over_x),
+        row_copy(5, cot_own, cot_got.at[1], over_y),
+    ]
+    start(cots)
+    step(2)
+    wait_recv(onward)
+    normed_out = pltpu.make_async_copy(normed, normed_ref, local_sem.at[6])
+    normed_out.start()
+    wait_recv(cots)
+    cot_out = pltpu.make_async_copy(cot_got, cot_all_ref, local_sem.at[7])
+    cot_out.start()
+    step(3)
+
+    for j in range(-3, 4):
+        @pl.when((z + j >= 0) & (z + j < layers))
+        def _():
+            wait_recv(from_twin(j))
+            start(shard_out(twin[0] + 2 * j, 10 + j))
+    wait_send(over + onward + cots)
+    for j in range(3):
+        pl.when((z < layers - 1) & (z - j >= 0))(lambda: wait_send(up(j)))
+        pl.when((z > 0) & (z + j < layers))(lambda: wait_send(down(j)))
+    normed_out.wait()
+    cot_out.wait()
+    for j in range(-3, 4):
+        @pl.when((z + j >= 0) & (z + j < layers))
+        def _():
+            wait_send(to_twin(j))
+            for copy in shard_out(dp + 2 * j, 3 + j) + shard_out(twin[0] + 2 * j, 10 + j):
+                copy.wait()
+
+
+def opening_exchange(query_weight, key_weight, value_weight, gate_weight, tokens, gain, bias, cotangent):
+    dp = lax.axis_size("dp")
+    depth, keys = query_weight.shape
+    values = value_weight.shape[1]
+    rows, width = tokens.shape
+    anywhere = pl.BlockSpec(memory_space=pl.ANY)
+    in_vmem = pl.BlockSpec(memory_space=pltpu.VMEM)
+    return pl.pallas_call(
+        opening_kernel,
+        out_shape=[
+            jax.ShapeDtypeStruct((dp * depth, 2 * keys + values), bf16),
+            jax.ShapeDtypeStruct((dp * depth, values), bf16),
+            jax.ShapeDtypeStruct((4 * rows, width), bf16),
+            jax.ShapeDtypeStruct((2, rows // 2, width), bf16),
+        ],
+        in_specs=[anywhere] * 5 + [in_vmem] * 2 + [anywhere],
+        out_specs=[anywhere] * 4,
+        scratch_shapes=[
+            pltpu.VMEM((dp * depth, 2 * keys + values), bf16),
+            pltpu.VMEM((dp * depth, values), bf16),
+            pltpu.VMEM((4 * rows, width), bf16),
+            pltpu.VMEM((rows, width), bf16),
+            pltpu.VMEM((rows // 2, width), bf16),
+            pltpu.VMEM((2, rows // 2, width), bf16),
+            pltpu.SemaphoreType.DMA((8,)),
+            pltpu.SemaphoreType.DMA((14, 2)),
+            pltpu.SemaphoreType.DMA((3, 2)),
+            pltpu.SemaphoreType.DMA((3, 2)),
+            pltpu.SemaphoreType.DMA((3, 2)),
+            pltpu.SemaphoreType.DMA((3, 2)),
+            pltpu.SemaphoreType.DMA((7, 2)),
+            pltpu.SemaphoreType.DMA((7, 2)),
+            pltpu.SemaphoreType.DMA((6,)),
+            pltpu.SemaphoreType.DMA((6,)),
+        ],
+        compiler_params=pltpu.CompilerParams(
+            collective_id=2, has_side_effects=True, vmem_limit_bytes=60 * 1024 * 1024
+        ),
+        name="opening_exchange",
+    )(query_weight, key_weight, value_weight, gate_weight, tokens, gain.reshape(1, width), bias.reshape(1, width), cotangent)
+
+
+def opening(query_weight, key_weight, value_weight, gate_weight, tokens, gain, bias, cotangent, devices):
+    if devices == 4 and lax.axis_size("dp") == 8:
+        w_qkv, w_gate, normed1_all, cot_half = opening_exchange(
+            query_weight, key_weight, value_weight, gate_weight, tokens, gain, bias, cotangent
+        )
+        half = tokens.shape[0] // 2
+        rest = after(cotangent, cot_half)[half:]
+        rest_x = tensor_permute(rest, 1)
+        rest_y = tensor_permute(rest, 2)
+        lower = tensor_permute(cot_half[1], 1)
+        upper = tensor_permute(rest_x, 2)
+        cots = [cotangent, cot_half[0], rest_x, cot_half[1], rest_y, lower, upper]
+        return w_qkv, w_gate, normed1_all, cots, (rest_x, rest_y)
+    w_qkv = lax.all_gather(jnp.concatenate([query_weight, key_weight, value_weight], axis=1), "dp", axis=0, tiled=True)
+    w_gate = lax.all_gather(gate_weight, "dp", axis=0, tiled=True)
+    unit, _ = normalize(tokens.astype(f32))
+    normed1_all = jnp.concatenate(gather_pieces((unit * gain + bias).astype(bf16), devices), axis=0)
+    cots = gather_pieces(cotangent, devices)
+    return w_qkv, w_gate, normed1_all, cots, (cots[0],)
 
 
 def body(tokens, cotangent, segment, first_gain, first_bias, query_weight, key_weight, value_weight, gate_weight, out_weight, second_gain, second_bias, up_weight, down_weight):
@@ -280,86 +583,94 @@
     def per_piece(values):
         return [values[i * rows : (i + 1) * rows] for i in range(devices)]
 
-    shards = []
-    for h in range(heads):
-        shards += [
-            query_weight[:, h * KEY : (h + 1) * KEY],
-            key_weight[:, h * KEY : (h + 1) * KEY],
-            value_weight[:, h * VAL : (h + 1) * VAL],
-            gate_weight[:, h * VAL : (h + 1) * VAL],
-        ]
-    w_in = lax.all_gather(jnp.concatenate(shards, axis=1), "dp", axis=0, tiled=True)
-    w_out = lax.all_gather(out_weight, "dp", axis=1, tiled=True)
-    w_down = lax.all_gather(down_weight, "dp", axis=1, tiled=True)
-    w_up = lax.all_gather(up_weight, "dp", axis=0, tiled=True)
+    w_qkv, w_gate, normed1_all, cots, cot_begun = opening(
+        query_weight, key_weight, value_weight, gate_weight, tokens, first_gain, first_bias, cotangent, devices
+    )
+    w_out = lax.all_gather(after(out_weight, w_gate), "dp", axis=1, tiled=True)
+    w_down = lax.all_gather(after(down_weight, w_out), "dp", axis=1, tiled=True)
+    w_up = lax.all_gather(after(up_weight, w_down), "dp", axis=0, tiled=True)
 
     token_rows = tokens.astype(f32)
     unit1, scale1 = normalize(token_rows)
-    normed1 = (unit1 * first_gain + first_bias).astype(bf16)
-    normed1_all = jnp.concatenate(gather_pieces(normed1, devices), axis=0)
-    cot_pieces = gather_pieces(cotangent, devices)
     tables = retention_tables(segment, heads, here * heads)
-    field = dot_nn(normed1_all, w_in).astype(bf16)
-    gated, grouped, group_scale, past = retention_call(False, which, rows, heads, field, tables, ())
-    branch = scatter_sum([dot_nn(piece, w_out) for piece in per_piece(gated)])
+    field = dot_nn(normed1_all, w_qkv).astype(bf16)
+    gate = dot_nn(normed1_all, w_gate).astype(bf16)
+    gated, grouped, group_scale, past = retention_call(
+        False, which, rows, heads, field, after(gate, *cot_begun), tables, ()
+    )
+    branch, begun, _ = scatter_sum([dot_nn(piece, w_out) for piece in per_piece(after(gated, *cots))])
 
     mixed = token_rows + branch
     unit2, scale2 = normalize(mixed)
     normed2 = (unit2 * second_gain + second_bias).astype(bf16)
-    normed2_pieces = gather_pieces(normed2, devices)
-    hidden_grads = [dot_nt(piece, w_down) for piece in cot_pieces]
-    hidden, up_grad = [], []
-    for piece, hidden_grad in zip(normed2_pieces, hidden_grads):
+    cot_all = jnp.concatenate(after(cots, *begun), axis=0)
+    hidden_grads = per_piece(dot_nt(cot_all, after(w_down, normed2)).astype(bf16))
+
+    def feed(piece, hidden_grad):
         value, slope = gelu_both(dot_nn(piece, w_up))
-        hidden.append(value.astype(bf16))
-        up_grad.append((hidden_grad * slope).astype(bf16))
-    normed2_grad = scatter_sum([dot_nt(piece, w_up) for piece in up_grad])
+        return after((value.astype(bf16), (hidden_grad.astype(f32) * slope).astype(bf16)))
+
+    fed_own = feed(normed2, hidden_grads[0])
+    normed2_pieces = gather_pieces(normed2, devices, fed_own)
+    fed = [fed_own] + [feed(piece, grad) for piece, grad in zip(normed2_pieces[1:-1], hidden_grads[1:-1])]
+    fed.append(feed(after(normed2_pieces[-1], *fed), hidden_grads[-1]))
+    hidden = [f[0] for f in fed]
+    up_grad = [f[1] for f in fed]
+    terms = [dot_nt(piece, w_up) for piece in up_grad]
+    normed2_grad, _, _ = scatter_sum(terms)
     mixed_grad = cotangent.astype(f32) + normalize_back(normed2_grad, unit2, scale2, second_gain)
     gain2_grad = jnp.sum(normed2_grad * unit2, axis=0)
     bias2_grad = jnp.sum(normed2_grad, axis=0)
-    mixed_pieces = gather_pieces(mixed_grad.astype(bf16), devices)
-    ffn = scatter_sum([dot_nn(piece, w_down) for piece in hidden])
+    mixed_low = mixed_grad.astype(bf16)
+    mixed_pieces = gather_pieces(mixed_low, devices)
+
+    hidden_all = jnp.concatenate(after(hidden, *terms), axis=0)
+    down_weight_grad = dot_tn(hidden_all, cot_all).astype(bf16)
+    down_sum = lax.psum_scatter(down_weight_grad, "dp", scatter_dimension=1, tiled=True).astype(f32)
+    normed2_all = jnp.concatenate(after(normed2_pieces, mixed_low), axis=0)
+    up_weight_grad = dot_tn(normed2_all, jnp.concatenate(up_grad, axis=0)).astype(bf16)
+    up_sum = lax.psum_scatter(up_weight_grad, "dp", scatter_dimension=0, tiled=True).astype(f32)
+    ffn_terms = per_piece(dot_nn(after(hidden_all, mixed_low), w_down).astype(bf16))
+
+    gated_grad, gate_grad = [], []
+    for piece, unit, raw in zip(mixed_pieces, per_piece(grouped), per_piece(gate)):
+        grad = dot_nt(after(piece, *ffn_terms), w_out)
+        raw = raw.astype(f32)
+        sigmoid = 1.0 / (1.0 + jnp.exp(-raw))
+        both = after((
+            grad.astype(bf16),
+            (grad * unit.astype(f32) * (sigmoid * (1.0 + raw * (1.0 - sigmoid)))).astype(bf16),
+        ))
+        gated_grad.append(both[0])
+        gate_grad.append(both[1])
+    gate_weight_grad = dot_tn(normed1_all, jnp.concatenate(gate_grad, axis=0)).astype(bf16)
+    gate_sum = lax.psum_scatter(gate_weight_grad, "dp", scatter_dimension=0, tiled=True).astype(f32)
+    ffn, ffn_begun, ffn_done = scatter_sum([term.astype(f32) for term in after(ffn_terms, mixed_pieces[3])])
     result = (mixed + ffn).astype(bf16)
-    normed2_all = jnp.concatenate(normed2_pieces, axis=0)
-    up_grad_all = jnp.concatenate(up_grad, axis=0)
-    cot_all = jnp.concatenate(cot_pieces, axis=0)
-    hidden_all = jnp.concatenate(hidden, axis=0)
-    up_weight_grad = dot_tn(normed2_all, up_grad_all).astype(bf16)
-    down_weight_grad = dot_tn(hidden_all, cot_all).astype(bf16)
-
-    gated_grad = jnp.concatenate([dot_nt(piece, w_out).astype(bf16) for piece in mixed_pieces], axis=0)
-    mixed_all = jnp.concatenate(mixed_pieces, axis=0)
-    back = retention_call(True, which, rows, heads, field, tables, (gated_grad, grouped, group_scale, past))
-    out_weight_grad = dot_tn(gated, mixed_all).astype(bf16)
-    normed1_grad = scatter_sum([dot_nt(piece, w_in) for piece in per_piece(back)])
-    in_weight_grad = dot_tn(normed1_all, back).astype(bf16)
+    out_weight_grad = dot_tn(gated, jnp.concatenate(after(mixed_pieces, gate_weight_grad), axis=0)).astype(bf16)
+    out_sum = lax.psum_scatter(out_weight_grad, "dp", scatter_dimension=1, tiled=True).astype(f32)
+    back = retention_call(
+        True, which, rows, heads, field, gate, tables,
+        (jnp.concatenate(after(gated_grad, out_weight_grad, *ffn_begun), axis=0), grouped, group_scale, past),
+    )
+    terms = [dot_nt(first, w_qkv) + dot_nt(second, w_gate) for first, second in zip(per_piece(back), gate_grad)]
+    normed1_grad, begun, _ = scatter_sum(terms)
+    qkv_weight_grad = dot_tn(normed1_all, after(back, terms[-1], *ffn_done, up_sum, down_sum)).astype(bf16)
+    qkv_sum = lax.psum_scatter(qkv_weight_grad, "dp", scatter_dimension=0, tiled=True)
     input_grad = mixed_grad + normalize_back(normed1_grad, unit1, scale1, first_gain)
     gain1_grad = jnp.sum(normed1_grad * unit1, axis=0)
     bias1_grad = jnp.sum(normed1_grad, axis=0)
-
-    up_sum = lax.psum_scatter(up_weight_grad, "dp", scatter_dimension=0, tiled=True).astype(f32)
-    down_sum = lax.psum_scatter(down_weight_grad, "dp", scatter_dimension=1, tiled=True).astype(f32)
-    out_sum = lax.psum_scatter(out_weight_grad, "dp", scatter_dimension=1, tiled=True).astype(f32)
-    in_sum = lax.psum_scatter(in_weight_grad, "dp", scatter_dimension=0, tiled=True).astype(f32)
-
-    def columns_of(start, width):
-        return jnp.concatenate(
-            [in_sum[:, h * HEAD + start : h * HEAD + start + width] for h in range(heads)], axis=1
-        )
-
-    norm_sums = [
-        lax.psum_scatter(v, ("dp", "tensor"), scatter_dimension=0, tiled=True)
-        for v in (gain1_grad, bias1_grad, gain2_grad, bias2_grad)
-    ]
+    norm_sums = spread_sum([gain1_grad, bias1_grad, gain2_grad, bias2_grad])
+    keys_end = heads * KEY
     return (
         result,
         input_grad.astype(bf16),
         norm_sums[0],
         norm_sums[1],
-        columns_of(0, KEY),
-        columns_of(KEY, KEY),
-        columns_of(2 * KEY, VAL),
-        columns_of(2 * KEY + VAL, VAL),
+        qkv_sum[:, :keys_end].astype(f32),
+        qkv_sum[:, keys_end : 2 * keys_end].astype(f32),
+        qkv_sum[:, 2 * keys_end :].astype(f32),
+        gate_sum,
         out_sum,
         norm_sums[2],
         norm_sums[3],

time: 905 us -> 792 us (0.88)
  waiting for transfers between devices: 410 us -> 216 us
  Pallas kernels: 39.1 us -> 161 us
  blocking collectives: 39 us -> 0 us
  local copies, waits for them, and re-layouts: 61.7 us -> 34.7 us
  matrix products: 242 us -> 266 us
  starting transfers between devices: 43.9 us -> 26.1 us
  other arithmetic: 50.2 us -> 64.8 us
    ppermute x32 -> x28, waiting for transfers between devices: 371 us -> 212 us  [tensor_permute(): return lax.ppermute(values, 'tensor', pairs)]
    pallas_call x0 -> x2, Pallas kernels: none -> 123 us  [the longest x1 113 us: opening_exchange(): pl.pallas_call(opening_kernel, out_shape=[jax.ShapeDtypeStruct((dp * dept...]
    unnamed x1 -> x0, blocking collectives: 39 us -> none
    all_gather x4 -> x3, waiting for transfers between devices: 36.8 us -> 3.89 us  [the longest x1 3.89 us: body(): w_out = lax.all_gather(after(out_weight, w_gate), 'dp', axis=1, tiled=True)]
    unnamed x175 -> x155, local copies, waits for them, and re-layouts: 38.6 us -> 12.9 us
    ppermute x32 -> x28, starting transfers between devices: 42.7 us -> 24.9 us  [tensor_permute(): return lax.ppermute(values, 'tensor', pairs)]
    convert_element_type x0 -> x6, other arithmetic: none -> 16.5 us  [the longest x1 5.21 us: body(): result = (mixed + ffn).astype(bf16)]
    dot_general x16 -> x17, matrix products: 95.5 us -> 110 us  [dot_nt(): lax.dot_general(left, right, (((1,), (1,)), ((), ())), preferred_element_...]
  transfers between devices with their start and end apart: 40 -> 36, of which waited for: 19 -> 18; matrix products, arithmetic and copies ran while one was open for 34% -> 42% of each run, Pallas kernels for 4% -> 6%
where the time goes in v2:
time: 792 us; the launch traced here: 784 us
  matrix products  266 us (34%)
  waiting for transfers between devices  216 us (27%)
  Pallas kernels  161 us (20%)
  other arithmetic  64.8 us (8%)
  local copies, waits for them, and re-layouts  34.7 us (4%)
  starting transfers between devices  26.1 us (3%)
  between operations  15.6 us (2%)
    ppermute x28, waiting for transfers between devices, tensor_permute(): return lax.ppermute(values, 'tensor', pairs)  212 us
    pallas_call x1, Pallas kernels, opening_exchange(): pl.pallas_call(opening_kernel, out_shape=[jax.ShapeDtypeStruct((dp * dept...  113 us
    dot_general x17, matrix products, dot_nt(): lax.dot_general(left, right, (((1,), (1,)), ((), ())), preferred_element_...  110 us
    dot_general x11, matrix products, dot_nn(): lax.dot_general(left, right, (((1,), (0,)), ((), ())), preferred_element_...  82 us
    dot_general x5, matrix products, dot_tn(): lax.dot_general(left, right, (((0,), (0,)), ((), ())), preferred_element_...  74.1 us
    pallas_call x2, Pallas kernels, retention_call(): pl.pallas_call(functools.partial(retention_backward if backward else rete...  37.9 us
    ppermute x28, starting transfers between devices, tensor_permute(): return lax.ppermute(values, 'tensor', pairs)  24.9 us
  transfers between devices with their start and end apart: 36, of which 18 were waited for; matrix products, arithmetic and copies ran while one was open for 42% of the time, Pallas kernels for 6%

profile of v2, /device:TPU:0, one launch (start us, length us, event | category | flops | bytes accessed | tf_op | source)
XLA Modules:
  0.0 784.2 jit_solution(11284667327522134870)
XLA Ops:
  7.2 113.5 %opening_exchange.1 = (bf16[2048,2048]{1,0:T(8,128)(2,1)}, bf16[2048,1024]{1,0:T(8,128)(2,1)}, bf16[2048,2048]{1,0:T(8,128)(2,1)}, bf16[2,256,2048]{2,1,0:T(8,128)(2,1)}) custom-call(bf16[256,512]{1,0:T(8,128)(2,1)} %query_ref.1, bf16[256,512]{1,0:T(8,128)(2,1)} %key_ref.1, bf16[256,1024]{1,0:T(8,128)(2,1)} %value_ref.1, bf16[256,1024]{1,0:T(8,128)(2,1)} %gate_ref.1, ...), custom_call_target="tpu_custom_call" | custom-call | tf_op jit(solution)/shard_map/opening_exchange/pallas_call | solution.py:520
  125.3 2.7 slice_bitcast_fusion
  130.8 14.2 %convolution_convert_fusion.5.gate_ref = bf16[2048,1024]{1,0:T(8,128)(2,1)} fusion(bf16[2048,2048]{1,0:T(8,128)(2,1)} %get-tuple-element.82, bf16[2048,1024]{1,0:T(8,128)(2,1)} %get-tuple-element.84), kind=kOutput, calls=%fused_computation.64 | convolution fusion | flops 8592031744 | bytes 16777216 | tf_op jit(solution)/shard_map/dot_general | solution.py:24
  144.9 23.7 %convolution_convert_fusion.2.field_ref = bf16[2048,2048]{1,0:T(8,128)(2,1)} fusion(bf16[2048,2048]{1,0:T(8,128)(2,1)} %get-tuple-element.82, bf16[2048,2048]{1,0:T(8,128)(2,1)} %get-tuple-element.83), kind=kOutput, calls=%fused_computation.18 | convolution fusion | flops 17184063488 | bytes 25165824 | tf_op jit(solution)/shard_map/dot_general | solution.py:24
  168.8 3.9 all-gather.4.cloned.1.call-done
  174.8 3.7 multiply_cosine_fusion
  178.6 16.3 %retention_forward.1 = (bf16[2048,1024]{1,0:T(8,128)(2,1)}, bf16[2048,1024]{1,0:T(8,128)(2,1)}, f32[2048,256]{1,0:T(8,128)S(1)}, bf16[8,2,256,512]{3,2,1,0:T(8,128)(2,1)}) custom-call(s32[1]{0:T(128)} %bitcast.which, bf16[2048,2048]{1,0:T(8,128)(2,1)} %convolution_convert_fusion.2.field_ref, bf16[2048,1024]{1,0:T(8,128)(2,1)} %convolution_convert_fusion.5.gate_ref, ...), custom_call_target="tpu_custom_call" | custom-call | flops 3758096384 | bytes 25165824 | tf_op jit(solution)/shard_map/retention_forward/pallas_call | solution.py:317
  195.0 5.3 collective-permute-done.3
  200.3 4.0 convolution_convert_fusion.6
  206.5 2.4 fusion.124
  208.8 2.4 fusion.127
  211.5 17.9 %collective-permute-done.6 = bf16[256,2048]{1,0:T(8,128)(2,1)S(1)} collective-permute-done((bf16[256,2048]{1,0:T(8,128)(2,1)S(1)}, bf16[256,2048]{1,0:T(8,128)(2,1)S(1)}, u32[]{:S(2)}, u32[]{:S(2)}) %collective-permute-start.6) | collective-permute-done | bytes 1048608 | tf_op jit(solution)/shard_map/ppermute | solution.py:37
  235.2 42.7 %collective-permute-done.7 = bf16[512,2048]{1,0:T(8,128)(2,1)} collective-permute-done((bf16[512,2048]{1,0:T(8,128)(2,1)}, bf16[512,2048]{1,0:T(8,128)(2,1)}, u32[]{:S(2)}, u32[]{:S(2)}) %collective-permute-start.7) | collective-permute-done | bytes 2097184 | tf_op jit(solution)/shard_map/ppermute | solution.py:37
  277.9 2.7 collective-permute-done.5
  280.6 7.4 fusion.148
  296.5 38.1 %collective-permute-done.9 = bf16[512,2048]{1,0:T(8,128)(2,1)S(1)} collective-permute-done((bf16[512,2048]{1,0:T(8,128)(2,1)S(1)}, bf16[512,2048]{1,0:T(8,128)(2,1)S(1)}, u32[]{:S(2)}, u32[]{:S(2)}) %collective-permute-start.9) | collective-permute-done | bytes 2097184 | tf_op jit(solution)/shard_map/ppermute | solution.py:37
  337.7 10.9 %convolution_convert_fusion.4 = bf16[2048,1024]{1,0:T(8,128)(2,1)} fusion(bf16[2048,2048]{1,0:T(8,128)(2,1)S(1)} %constant_dynamic-update-slice_fusion, bf16[1024,2048]{1,0:T(8,128)(2,1)S(1)} %copy-done.47), kind=kOutput, calls=%fused_computation.63 | convolution fusion | flops 8592031744 | bytes 16777216 | tf_op jit(solution)/shard_map/dot_general | solution.py:28
  348.6 5.3 fusion.149
  354.0 2.4 fusion.150
  356.8 7.4 fusion.105
  365.6 2.4 fusion.152
  368.2 2.4 fusion.153
  370.7 14.9 %collective-permute-done.10 = bf16[256,2048]{1,0:T(8,128)(2,1)S(1)} collective-permute-done((bf16[256,2048]{1,0:T(8,128)(2,1)S(1)}, bf16[256,2048]{1,0:T(8,128)(2,1)S(1)}, u32[]{:S(2)}, u32[]{:S(2)}) %collective-permute-start.10) | collective-permute-done | bytes 1048608 | tf_op jit(solution)/shard_map/ppermute | solution.py:37
  386.5 3.6 fusion.113
  391.2 2.4 fusion.154
  394.6 4.3 fusion.151
  400.9 13.3 %collective-permute-done.12 = bf16[256,2048]{1,0:T(8,128)(2,1)S(1)} collective-permute-done((bf16[256,2048]{1,0:T(8,128)(2,1)S(1)}, bf16[256,2048]{1,0:T(8,128)(2,1)S(1)}, u32[]{:S(2)}, u32[]{:S(2)}) %collective-permute-start.12) | collective-permute-done | bytes 1048608 | tf_op jit(solution)/shard_map/ppermute | solution.py:37
  417.0 8.0 %collective-permute-done.14 = bf16[256,2048]{1,0:T(8,128)(2,1)S(1)} collective-permute-done((bf16[256,2048]{1,0:T(8,128)(2,1)S(1)}, bf16[256,2048]{1,0:T(8,128)(2,1)S(1)}, u32[]{:S(2)}, u32[]{:S(2)}) %collective-permute-start.14) | collective-permute-done | bytes 1048608 | tf_op jit(solution)/shard_map/ppermute | solution.py:37
  427.3 11.0 %convolution_convert_fusion.3 = bf16[1024,2048]{1,0:T(8,128)(2,1)} fusion(bf16[2048,1024]{1,0:T(8,128)(2,1)S(1)} %constant_dynamic-update-slice_fusion.9, bf16[2048,2048]{1,0:T(8,128)(2,1)S(1)} %bitcast.96), kind=kOutput, calls=%fused_computation.62 | convolution fusion | flops 8592031744 | bytes 16777216 | tf_op jit(solution)/shard_map/dot_general | solution.py:32
  438.5 26.0 %collective-permute-done.13 = bf16[512,2048]{1,0:T(8,128)(2,1)} collective-permute-done((bf16[512,2048]{1,0:T(8,128)(2,1)}, bf16[512,2048]{1,0:T(8,128)(2,1)}, u32[]{:S(2)}, u32[]{:S(2)}) %collective-permute-start.13) | collective-permute-done | bytes 2097184 | tf_op jit(solution)/shard_map/ppermute | solution.py:37
  464.4 6.6 multiply_reduce_fusion
  471.1 4.1 fusion.141
  476.9 9.3 %convolution_convert_fusion.1 = bf16[2048,2048]{1,0:T(8,128)(2,1)S(1)} fusion(bf16[2048,1024]{1,0:T(8,128)(2,1)S(1)} %copy-done.36, bf16[1024,2048]{1,0:T(8,128)(2,1)S(1)} %copy-done.48), kind=kOutput, calls=%fused_computation.17 | convolution fusion | flops 8594128896 | bytes 16777216 | tf_op jit(solution)/shard_map/dot_general | solution.py:24
  486.3 4.5 fusion.142
  491.7 14.2 %fusion.46 = bf16[2048,1024]{1,0:T(8,128)(2,1)} fusion(bf16[512,1024]{1,0:T(8,128)(2,1)} %copy-done.61, bf16[512,1024]{1,0:T(8,128)(2,1)S(1)} %copy-done.53, bf16[512,1024]{1,0:T(8,128)(2,1)} %copy-done.54, bf16[512,1024]{1,0:T(8,128)(2,1)} %copy-done.55, bf16[512,2048]{1,0:T(8,128)(2,1)} %copy-done.32, bf16[512,2048]{1,0:T(8,128)(2,1)S(1)} %copy-done.29, ...), kind=kOutput, calls=%fused_computation.60 | convolution fusion | flops 8642363392 | bytes 16777216 | tf_op jit(solution)/shard_map/dot_general | solution.py:32
  506.2 6.6 fusion.155
  512.9 5.7 collective-permute-done.17
  522.9 5.3 fusion.156
  528.2 5.4 fusion.157
  533.6 6.3 collective-permute-done.18
  540.8 12.9 %fusion.81 = (bf16[512,1024]{1,0:T(8,128)(2,1)S(1)}, bf16[512,1024]{1,0:T(8,128)(2,1)S(1)}, bf16[512,1024]{1,0:T(8,128)(2,1)S(1)}, bf16[512,1024]{1,0:T(8,128)(2...) fusion(bf16[2048,1024]{1,0:T(8,128)(2,1)} %convolution_convert_, ...), kind=kOutput, calls=%fused_computation.114 | convolution fusion | flops 2174746624 | bytes 29360128 | tf_op jit(solution)/shard_map/dot_general | solution.py:28
  555.5 10.5 %fusion.43 = bf16[2048,1024]{1,0:T(8,128)(2,1)} fusion(bf16[2048,2048]{1,0:T(8,128)(2,1)S(1)} %bitcast.109, bf16[512,1024]{1,0:T(8,128)(2,1)S(1)} %get-tuple-element.135, bf16[512,1024]{1,0:T(8,128)(2,1)S(1)} %get-tuple-element.134, bf16[512,1024]{1,0:T(8,128)(2,1)S(1)} %get-tuple-element.133, bf16[512,1024]{1,0:T(8,128)(2,1)S(1)} %get-tuple-element.132), kind=kOutput, calls=%fused_computation.59 | convolution fusion | flops 8608808960 | bytes 16777216 | tf_op jit(solution)/shard_map/dot_general | solution.py:32
  566.1 3.3 fusion.144
  571.6 14.0 %fusion.51 = bf16[1024,2048]{1,0:T(8,128)(2,1)} fusion(bf16[2048,1024]{1,0:T(8,128)(2,1)} %get-tuple-element.89, bf16[512,2048]{1,0:T(8,128)(2,1)S(1)} %copy-done.34, bf16[512,2048]{1,0:T(8,128)(2,1)} %collective-permute-done.16, bf16[512,2048]{1,0:T(8,128)(2,1)} %collective-permute-done.17, bf16[512,2048]{1,0:T(8,128)(2,1)} %get-tuple-element.136), kind=kOutput, calls=%fused_computation.61 | convolution fusion | flops 8625586176 | bytes 16777216 | tf_op jit(solution)/shard_map/dot_general | solution.py:32
  585.7 7.1 fusion.160
  600.2 2.6 pad_maximum_fusion.grad_ref
  602.9 21.6 %retention_backward.1 = bf16[2048,2048]{1,0:T(8,128)(2,1)} custom-call(s32[1]{0:T(128)} %bitcast.which, bf16[2048,2048]{1,0:T(8,128)(2,1)} %convolution_convert_fusion.2.field_ref, bf16[2048,1024]{1,0:T(8,128)(2,1)} %convolution_convert_fusion.5.gate_ref, f32[2048,256]{1,0:T(8,128)S(1)} %copy-done.1, f32[2048,128]{1,0:T(8,128)S(1)} %copy-done.3, ...), custom_call_target="tpu_custom_call" | custom-call | flops 8053063680 | bytes 31457280 | tf_op jit(solution)/shard_map/retention_backward/pallas_call | solution.py:317
  624.5 7.1 convolution_add_fusion.1
  633.7 2.1 convert_element_type.332
  638.6 24.3 %convolution_convert_fusion = bf16[2048,2048]{1,0:T(8,128)(2,1)} fusion(bf16[2048,2048]{1,0:T(8,128)(2,1)} %get-tuple-element.82, bf16[2048,2048]{1,0:T(8,128)(2,1)} %retention_backward.1), kind=kOutput, calls=%fused_computation.16 | convolution fusion | flops 17184063488 | bytes 25165824 | tf_op jit(solution)/shard_map/dot_general | solution.py:32
  663.0 5.1 fusion.159
  668.1 4.5 fusion.161
  677.1 7.0 convolution_add_fusion.2
  684.1 9.1 %convolution_add_fusion = f32[512,2048]{1,0:T(8,128)S(1)} fusion(f32[512,2048]{1,0:T(8,128)} %fusion.161, bf16[2048,2048]{1,0:T(8,128)(2,1)} %get-tuple-element.83, bf16[2048,2048]{1,0:T(8,128)(2,1)S(1)} %bitcast.94), kind=kOutput, calls=%fused_computation.75 | convolution fusion | flops 4296015872 | bytes 18874368 | tf_op jit(solution)/shard_map/dot_general | solution.py:28
  701.9 4.8 fusion.158
  706.7 5.2 add_convert_fusion
  712.0 23.5 %collective-permute-done.27 = bf16[512,2048]{1,0:T(8,128)(2,1)} collective-permute-done((bf16[512,2048]{1,0:T(8,128)(2,1)}, bf16[512,2048]{1,0:T(8,128)(2,1)}, u32[]{:S(2)}, u32[]{:S(2)}) %collective-permute-start.27) | collective-permute-done | bytes 2097184 | tf_op jit(solution)/shard_map/ppermute | solution.py:37
  735.5 3.0 collective-permute-done.25
  738.5 12.8 %fusion.26 = (f32[2048]{0:T(1024)S(1)}, f32[512]{0:T(512)S(1)}, f32[512]{0:T(512)S(1)}, f32[2048]{0:T(1024)S(1)}, f32[512,2048]{1,0:T(8,128)}) fusion(bf16[512,2048]{1,0:T(8,128)(2,1)S(1)} %copy-done.9, f32[512]{0:T(512)S(1)} %add_rsqrt_fusion, f32[512]{0:T(512)S(1)} %broadcast_multiply_fusion.2, f32[2048]{0:T(1024)S(1)} %copy-done.39, ...), kind=kOutput, calls=%fused_computation.32 | convolution fusion | flops 4310690816 | bytes 25198592 | tf_op jit(solution)/shard_map/dot_general | solution.py:28
  752.2 9.8 %spread_sum.1 = f32[8,128]{1,0:T(8,128)} custom-call(f32[32,8,128]{2,1,0:T(8,128)} %select_maximum_fusion.given_ref), custom_call_target="tpu_custom_call" | custom-call | tf_op jit(solution)/shard_map/spread_sum/pallas_call | solution.py:117
  763.5 5.3 fusion.25
  768.7 2.1 convert_element_type.339
  772.9 2.1 slice_convert_fusion.6
  775.1 2.1 slice_convert_fusion.7
  (305 shorter events, 83.7 us)
Async XLA Ops:
  7.2 113.6 %copy-start.10 = (bf16[512,2048]{1,0:T(8,128)(2,1)S(1)}, bf16[512,2048]{1,0:T(8,128)(2,1)}, u32[]{:S(2)}) copy-start(bf16[512,2048]{1,0:T(8,128)(2,1)} %cot_ref.1) | copy-start | bytes 6291460
  7.2 165.5 %all-gather.4.cloned.1.call-start = ((), (), s32[]{:S(2)}) async-start(), calls=%async_computation.5 | async-start | bytes 4718592 | tf_op jit(solution)/shard_map/all_gather | solution.py:589
  120.7 7.5 copy-start.37
  121.8 56.8 %collective-permute-start.1 = (bf16[256,2048]{1,0:T(8,128)(2,1)}, bf16[256,2048]{1,0:T(8,128)(2,1)}, u32[]{:S(2)}, u32[]{:S(2)}) collective-permute-start(bf16[256,2048]{1,0:T(8,128)(2,1)} %slice.232), channel_id=1, source_target_pairs={{0,2},{1,3},{2,0},{3,1},{4,6},{5,7},{6,4},{7,5},{8,10},{9,11},{10,... | collective-permute-start | bytes 3145736 | tf_op jit(solution)/shard_map/ppermute | solution.py:37
  123.4 51.3 %collective-permute-start = (bf16[256,2048]{1,0:T(8,128)(2,1)}, bf16[256,2048]{1,0:T(8,128)(2,1)}, u32[]{:S(2)}, u32[]{:S(2)}) collective-permute-start(bf16[256,2048]{1,0:T(8,128)(2,1)} %slice.232), channel_id=1, source_target_pairs={{0,1},{1,0},{2,3},{3,2},{4,5},{5,4},{6,7},{7,6},{8,9},{9,8},{10,11... | collective-permute-start | bytes 3145736 | tf_op jit(solution)/shard_map/ppermute | solution.py:37
  125.2 109.7 %all-gather.6.cloned.1.call-start = ((), (), s32[]{:S(2)}) async-start(), calls=%async_computation.6 | async-start | bytes 4718592 | tf_op jit(solution)/shard_map/all_gather | solution.py:590
  128.0 67.0 %collective-permute-start.2 = (bf16[256,2048]{1,0:T(8,128)(2,1)S(1)}, bf16[256,2048]{1,0:T(8,128)(2,1)}, u32[]{:S(2)}, u32[]{:S(2)}) collective-permute-start(bf16[256,2048]{1,0:T(8,128)(2,1)S(1)} %get-tuple-element.96), channel_id=1, source_target_pairs={{0,1},{1,0},{2,3},{3,2},{4,5},{5,4},{6,7},{7,6},{8,9},{9,8},{10,11... | collective-permute-start | bytes 3145736 | tf_op jit(solution)/shard_map/ppermute | solution.py:37
  172.7 175.9 %all-gather.8.cloned.1.call-start = ((), (), s32[]{:S(2)}) async-start(), calls=%async_computation.7 | async-start | bytes 4718592 | tf_op jit(solution)/shard_map/all_gather | solution.py:591
  174.5 20.5 %copy-start.2 = (f32[2048,128]{1,0:T(8,128)}, f32[2048,128]{1,0:T(8,128)S(1)}, u32[]{:S(2)}) copy-start(f32[2048,128]{1,0:T(8,128)S(1)} %pad.8.info_ref) | copy-start | bytes 3145732
  174.7 20.3 %copy-start.4 = (f32[2,256,256]{2,1,0:T(8,128)}, f32[2,256,256]{2,1,0:T(8,128)S(1)}, u32[]{:S(2)}) copy-start(f32[2,256,256]{2,1,0:T(8,128)S(1)} %exponential_select_fusion.decay_ref) | copy-start | bytes 1572868
  174.7 25.6 %collective-permute-start.3 = (bf16[256,2048]{1,0:T(8,128)(2,1)}, bf16[256,2048]{1,0:T(8,128)(2,1)S(1)}, u32[]{:S(2)}, u32[]{:S(2)}) collective-permute-start(bf16[256,2048]{1,0:T(8,128)(2,1)} %collective-permute-done), channel_id=1, source_target_pairs={{0,2},{1,3},{2,0},{3,1},{4,6},{5,7},{6,4},{7,5},{8,10},{9,11},{10,... | collective-permute-start | bytes 3145736 | tf_op jit(solution)/shard_map/ppermute | solution.py:37
  178.6 16.4 %copy-start = (f32[2048,256]{1,0:T(8,128)}, f32[2048,256]{1,0:T(8,128)S(1)}, u32[]{:S(2)}) copy-start(f32[2048,256]{1,0:T(8,128)S(1)} %pad_maximum_fusion.1.angle_ref) | copy-start | bytes 6291460
  178.6 21.7 %copy-start.44 = (bf16[1024,2048]{1,0:T(8,128)(2,1)S(1)}, bf16[1024,2048]{1,0:T(8,128)(2,1)}, u32[]{:S(2)}) copy-start(bf16[1024,2048]{1,0:T(8,128)(2,1)} %all-gather.4.cloned.1.call-done) | copy-start | bytes 12582916
  204.4 28.3 %collective-permute-start.4 = (bf16[256,2048]{1,0:T(8,128)(2,1)S(1)}, bf16[256,2048]{1,0:T(8,128)(2,1)S(1)}, u32[]{:S(2)}, u32[]{:S(2)}) collective-permute-start(bf16[256,2048]{1,0:T(8,128)(2,1)S(1)} %get-tuple-element.192), channel_id=1, source_target_pairs={{0,2},{1,3},{2,0},{3,1},{4,6},{5,7},{6,4},{7,5},{8,10},{9,11},{10,... | collective-permute-start | bytes 3145736 | tf_op jit(solution)/shard_map/ppermute | solution.py:37
  204.8 24.7 %collective-permute-start.6 = (bf16[256,2048]{1,0:T(8,128)(2,1)S(1)}, bf16[256,2048]{1,0:T(8,128)(2,1)S(1)}, u32[]{:S(2)}, u32[]{:S(2)}) collective-permute-start(bf16[256,2048]{1,0:T(8,128)(2,1)S(1)} %get-tuple-element.193), channel_id=1, source_target_pairs={{0,1},{1,0},{2,3},{3,2},{4,5},{5,4},{6,7},{7,6},{8,9},{9,8},{10,11... | collective-permute-start | bytes 3145736 | tf_op jit(solution)/shard_map/ppermute | solution.py:37
  231.4 46.5 %collective-permute-start.7 = (bf16[512,2048]{1,0:T(8,128)(2,1)}, bf16[512,2048]{1,0:T(8,128)(2,1)}, u32[]{:S(2)}, u32[]{:S(2)}) collective-permute-start(bf16[512,2048]{1,0:T(8,128)(2,1)} %pad_maximum_fusion.3), channel_id=1, source_target_pairs={{0,2},{1,3},{2,0},{3,1},{4,6},{5,7},{6,4},{7,5},{8,10},{9,11},{10,... | collective-permute-start | bytes 6291464 | tf_op jit(solution)/shard_map/ppermute | solution.py:37
  234.7 45.9 %collective-permute-start.5 = (bf16[512,2048]{1,0:T(8,128)(2,1)}, bf16[512,2048]{1,0:T(8,128)(2,1)}, u32[]{:S(2)}, u32[]{:S(2)}) collective-permute-start(bf16[512,2048]{1,0:T(8,128)(2,1)} %pad_maximum_fusion.2), channel_id=1, source_target_pairs={{0,1},{1,0},{2,3},{3,2},{4,5},{5,4},{6,7},{7,6},{8,9},{9,8},{10,11... | collective-permute-start | bytes 6291464 | tf_op jit(solution)/shard_map/ppermute | solution.py:37
  235.0 396.6 %reduce-scatter.8.cloned.1.call-start = ((), (), s32[]{:S(2)}) async-start(), calls=%async_computation.9 | async-start | bytes 4718592 | tf_op jit(solution)/shard_map/reduce_scatter | solution.py:629
  289.9 44.7 %collective-permute-start.9 = (bf16[512,2048]{1,0:T(8,128)(2,1)S(1)}, bf16[512,2048]{1,0:T(8,128)(2,1)S(1)}, u32[]{:S(2)}, u32[]{:S(2)}) collective-permute-start(bf16[512,2048]{1,0:T(8,128)(2,1)S(1)} %add_convert_fusion.1), channel_id=1, source_target_pairs={{0,2},{1,3},{2,0},{3,1},{4,6},{5,7},{6,4},{7,5},{8,10},{9,11},{10,... | collective-permute-start | bytes 6291464 | tf_op jit(solution)/shard_map/ppermute | solution.py:37
  290.8 44.9 %collective-permute-start.8 = (bf16[512,2048]{1,0:T(8,128)(2,1)S(1)}, bf16[512,2048]{1,0:T(8,128)(2,1)S(1)}, u32[]{:S(2)}, u32[]{:S(2)}) collective-permute-start(bf16[512,2048]{1,0:T(8,128)(2,1)S(1)} %add_convert_fusion.1), channel_id=1, source_target_pairs={{0,1},{1,0},{2,3},{3,2},{4,5},{5,4},{6,7},{7,6},{8,9},{9,8},{10,11... | collective-permute-start | bytes 6291464 | tf_op jit(solution)/shard_map/ppermute | solution.py:37
  294.9 42.7 %copy-start.47 = (bf16[1024,2048]{1,0:T(8,128)(2,1)S(1)}, bf16[1024,2048]{1,0:T(8,128)(2,1)}, u32[]{:S(2)}) copy-start(bf16[1024,2048]{1,0:T(8,128)(2,1)} %all-gather.6.cloned.1.call-done) | copy-start | bytes 12582916
  296.5 41.2 %copy-start.26 = (bf16[2048,2048]{1,0:T(8,128)(2,1)}, bf16[2048,2048]{1,0:T(8,128)(2,1)S(1)}, u32[]{:S(2)}) copy-start(bf16[2048,2048]{1,0:T(8,128)(2,1)S(1)} %constant_dynamic-update-slice_fusion) | copy-start | bytes 25165828
  356.8 7.4 copy-start.21
  364.2 30.5 %copy-start.55 = (bf16[512,1024]{1,0:T(8,128)(2,1)}, bf16[512,1024]{1,0:T(8,128)(2,1)S(1)}, u32[]{:S(2)}) copy-start(bf16[512,1024]{1,0:T(8,128)(2,1)S(1)} %get-tuple-element.104) | copy-start | bytes 3145732
  364.2 21.4 %collective-permute-start.10 = (bf16[256,2048]{1,0:T(8,128)(2,1)S(1)}, bf16[256,2048]{1,0:T(8,128)(2,1)S(1)}, u32[]{:S(2)}, u32[]{:S(2)}) collective-permute-start(bf16[256,2048]{1,0:T(8,128)(2,1)S(1)} %copy-done.21), channel_id=1, source_target_pairs={{0,1},{1,0},{2,3},{3,2},{4,5},{5,4},{6,7},{7,6},{8,9},{9,8},{10,11... | collective-permute-start | bytes 3145736 | tf_op jit(solution)/shard_map/ppermute | solution.py:37
  365.1 21.3 %collective-permute-start.11 = (bf16[256,2048]{1,0:T(8,128)(2,1)S(1)}, bf16[256,2048]{1,0:T(8,128)(2,1)S(1)}, u32[]{:S(2)}, u32[]{:S(2)}) collective-permute-start(bf16[256,2048]{1,0:T(8,128)(2,1)S(1)} %slice.319), channel_id=1, source_target_pairs={{0,2},{1,3},{2,0},{3,1},{4,6},{5,7},{6,4},{7,5},{8,10},{9,11},{10,... | collective-permute-start | bytes 3145736 | tf_op jit(solution)/shard_map/ppermute | solution.py:37
  393.7 20.5 %collective-permute-start.12 = (bf16[256,2048]{1,0:T(8,128)(2,1)S(1)}, bf16[256,2048]{1,0:T(8,128)(2,1)S(1)}, u32[]{:S(2)}, u32[]{:S(2)}) collective-permute-start(bf16[256,2048]{1,0:T(8,128)(2,1)S(1)} %get-tuple-element.187), channel_id=1, source_target_pairs={{0,2},{1,3},{2,0},{3,1},{4,6},{5,7},{6,4},{7,5},{8,10},{9,11},{10,... | collective-permute-start | bytes 3145736 | tf_op jit(solution)/shard_map/ppermute | solution.py:37
  399.0 26.1 %collective-permute-start.14 = (bf16[256,2048]{1,0:T(8,128)(2,1)S(1)}, bf16[256,2048]{1,0:T(8,128)(2,1)S(1)}, u32[]{:S(2)}, u32[]{:S(2)}) collective-permute-start(bf16[256,2048]{1,0:T(8,128)(2,1)S(1)} %get-tuple-element.188), channel_id=1, source_target_pairs={{0,1},{1,0},{2,3},{3,2},{4,5},{5,4},{6,7},{7,6},{8,9},{9,8},{10,11... | collective-permute-start | bytes 3145736 | tf_op jit(solution)/shard_map/ppermute | solution.py:37
  400.9 26.4 %copy-start.35 = (bf16[2048,1024]{1,0:T(8,128)(2,1)}, bf16[2048,1024]{1,0:T(8,128)(2,1)S(1)}, u32[]{:S(2)}) copy-start(bf16[2048,1024]{1,0:T(8,128)(2,1)S(1)} %constant_dynamic-update-slice_fusion.9) | copy-start | bytes 12582916
  414.2 13.1 %slice-start.2 = ((s8[8388608]{0:T(1024)(128)(4,1)}), s8[4194304]{0:T(1024)(128)(4,1)S(1)}, s32[]{:S(2)}) async-start(s8[8388608]{0:T(1024)(128)(4,1)} %bitcast.95), calls=%async_computation.15 | async-start | bytes 8388608
  416.3 11.1 %slice-start.3 = ((s8[8388608]{0:T(1024)(128)(4,1)}), s8[4194304]{0:T(1024)(128)(4,1)S(1)}, s32[]{:S(2)}) async-start(s8[8388608]{0:T(1024)(128)(4,1)} %bitcast.95), calls=%async_computation.16 | async-start | bytes 8388608
  416.3 48.2 %collective-permute-start.13 = (bf16[512,2048]{1,0:T(8,128)(2,1)}, bf16[512,2048]{1,0:T(8,128)(2,1)}, u32[]{:S(2)}, u32[]{:S(2)}) collective-permute-start(bf16[512,2048]{1,0:T(8,128)(2,1)} %pad_maximum_fusion.4), channel_id=1, source_target_pairs={{0,1},{1,0},{2,3},{3,2},{4,5},{5,4},{6,7},{7,6},{8,9},{9,8},{10,11... | collective-permute-start | bytes 6291464 | tf_op jit(solution)/shard_map/ppermute | solution.py:37
  426.8 37.6 %collective-permute-start.15 = (bf16[512,2048]{1,0:T(8,128)(2,1)}, bf16[512,2048]{1,0:T(8,128)(2,1)}, u32[]{:S(2)}, u32[]{:S(2)}) collective-permute-start(bf16[512,2048]{1,0:T(8,128)(2,1)} %pad_maximum_fusion.5), channel_id=1, source_target_pairs={{0,2},{1,3},{2,0},{3,1},{4,6},{5,7},{6,4},{7,5},{8,10},{9,11},{10,... | collective-permute-start | bytes 6291464 | tf_op jit(solution)/shard_map/ppermute | solution.py:37
  438.4 195.3 %reduce-scatter.6.cloned.1.call-start = ((), (), s32[]{:S(2)}) async-start(), calls=%async_computation.8 | async-start | bytes 4718592 | tf_op jit(solution)/shard_map/reduce_scatter | solution.py:632
  438.4 32.6 %copy-start.7 = (f32[512,2048]{1,0:T(8,128)S(1)}, f32[512,2048]{1,0:T(8,128)}, u32[]{:S(2)}) copy-start(f32[512,2048]{1,0:T(8,128)} %copy-done.6) | copy-start | bytes 12582916
  438.5 32.6 %copy-start.12 = (bf16[512,2048]{1,0:T(8,128)(2,1)S(1)}, bf16[512,2048]{1,0:T(8,128)(2,1)}, u32[]{:S(2)}) copy-start(bf16[512,2048]{1,0:T(8,128)(2,1)} %cot_ref.1) | copy-start | bytes 6291460
  471.1 5.8 copy-start.36
  475.2 43.3 %collective-permute-start.17 = (bf16[512,2048]{1,0:T(8,128)(2,1)}, bf16[512,2048]{1,0:T(8,128)(2,1)}, u32[]{:S(2)}, u32[]{:S(2)}) collective-permute-start(bf16[512,2048]{1,0:T(8,128)(2,1)} %get-tuple-element.136), channel_id=1, source_target_pairs={{0,1},{1,0},{2,3},{3,2},{4,5},{5,4},{6,7},{7,6},{8,9},{9,8},{10,11... | collective-permute-start | bytes 6291464 | tf_op jit(solution)/shard_map/ppermute | solution.py:37
  476.6 43.3 %collective-permute-start.16 = (bf16[512,2048]{1,0:T(8,128)(2,1)}, bf16[512,2048]{1,0:T(8,128)(2,1)}, u32[]{:S(2)}, u32[]{:S(2)}) collective-permute-start(bf16[512,2048]{1,0:T(8,128)(2,1)} %get-tuple-element.136), channel_id=1, source_target_pairs={{0,2},{1,3},{2,0},{3,1},{4,6},{5,7},{6,4},{7,5},{8,10},{9,11},{10,... | collective-permute-start | bytes 6291464 | tf_op jit(solution)/shard_map/ppermute | solution.py:37
  505.9 262.8 %reduce-scatter.12.cloned.1.call-start = ((), (), s32[]{:S(2)}) async-start(), calls=%async_computation.11 | async-start | bytes 4718592 | tf_op jit(solution)/shard_map/reduce_scatter | solution.py:647
  506.2 16.7 %copy-start.45 = (bf16[1024,2048]{1,0:T(8,128)(2,1)S(1)}, bf16[1024,2048]{1,0:T(8,128)(2,1)}, u32[]{:S(2)}) copy-start(bf16[1024,2048]{1,0:T(8,128)(2,1)} %all-gather.4.cloned.1.call-done) | copy-start | bytes 12582916
  521.2 18.7 %collective-permute-start.18 = (bf16[256,2048]{1,0:T(8,128)(2,1)S(1)}, bf16[256,2048]{1,0:T(8,128)(2,1)S(1)}, u32[]{:S(2)}, u32[]{:S(2)}) collective-permute-start(bf16[256,2048]{1,0:T(8,128)(2,1)S(1)} %slice.331), channel_id=1, source_target_pairs={{0,1},{1,0},{2,3},{3,2},{4,5},{5,4},{6,7},{7,6},{8,9},{9,8},{10,11... | collective-permute-start | bytes 3145736 | tf_op jit(solution)/shard_map/ppermute | solution.py:37
  522.6 18.1 %collective-permute-start.19 = (bf16[256,2048]{1,0:T(8,128)(2,1)S(1)}, bf16[256,2048]{1,0:T(8,128)(2,1)S(1)}, u32[]{:S(2)}, u32[]{:S(2)}) collective-permute-start(bf16[256,2048]{1,0:T(8,128)(2,1)S(1)} %slice.332), channel_id=1, source_target_pairs={{0,2},{1,3},{2,0},{3,1},{4,6},{5,7},{6,4},{7,5},{8,10},{9,11},{10,... | collective-permute-start | bytes 3145736 | tf_op jit(solution)/shard_map/ppermute | solution.py:37
  528.2 27.3 %slice-start.6 = ((s8[8388608]{0:T(1024)(128)(4,1)}), s8[4194304]{0:T(1024)(128)(4,1)S(1)}, s32[]{:S(2)}) async-start(s8[8388608]{0:T(1024)(128)(4,1)} %bitcast.108), calls=%async_computation.19 | async-start | bytes 8388608
  540.8 13.0 %copy-start.33 = (bf16[512,2048]{1,0:T(8,128)(2,1)}, bf16[512,2048]{1,0:T(8,128)(2,1)S(1)}, u32[]{:S(2)}) copy-start(bf16[512,2048]{1,0:T(8,128)(2,1)S(1)} %constant_dynamic-update-slice_fusion.13) | copy-start | bytes 6291460
  540.8 14.7 %slice-start.7 = ((s8[8388608]{0:T(1024)(128)(4,1)}), s8[4194304]{0:T(1024)(128)(4,1)S(1)}, s32[]{:S(2)}) async-start(s8[8388608]{0:T(1024)(128)(4,1)} %bitcast.108), calls=%async_computation.20 | async-start | bytes 8388608
  553.8 12.2 %copy-start.59 = (bf16[512,1024]{1,0:T(8,128)(2,1)}, bf16[512,1024]{1,0:T(8,128)(2,1)S(1)}, u32[]{:S(2)}) copy-start(bf16[512,1024]{1,0:T(8,128)(2,1)S(1)} %get-tuple-element.135) | copy-start | bytes 3145732
  566.1 204.8 %reduce-scatter.14.cloned.1.call-start = ((), (), s32[]{:S(2)}) async-start(), calls=%async_computation.12 | async-start | bytes 4718592 | tf_op jit(solution)/shard_map/reduce_scatter | solution.py:651
  569.4 27.7 %collective-permute-start.20 = (bf16[256,2048]{1,0:T(8,128)(2,1)}, bf16[256,2048]{1,0:T(8,128)(2,1)S(1)}, u32[]{:S(2)}, u32[]{:S(2)}) collective-permute-start(bf16[256,2048]{1,0:T(8,128)(2,1)} %get-tuple-element.185), channel_id=1, source_target_pairs={{0,2},{1,3},{2,0},{3,1},{4,6},{5,7},{6,4},{7,5},{8,10},{9,11},{10,... | collective-permute-start | bytes 3145736 | tf_op jit(solution)/shard_map/ppermute | solution.py:37
  570.6 22.4 %collective-permute-start.22 = (bf16[256,2048]{1,0:T(8,128)(2,1)}, bf16[256,2048]{1,0:T(8,128)(2,1)}, u32[]{:S(2)}, u32[]{:S(2)}) collective-permute-start(bf16[256,2048]{1,0:T(8,128)(2,1)} %get-tuple-element.186), channel_id=1, source_target_pairs={{0,1},{1,0},{2,3},{3,2},{4,5},{5,4},{6,7},{7,6},{8,9},{9,8},{10,11... | collective-permute-start | bytes 3145736 | tf_op jit(solution)/shard_map/ppermute | solution.py:37
  585.6 187.3 %reduce-scatter.10.cloned.1.call-start = ((), (), s32[]{:S(2)}) async-start(), calls=%async_computation.10 | async-start | bytes 9437184 | tf_op jit(solution)/shard_map/reduce_scatter | solution.py:659
  585.7 7.1 copy-start.13
  585.7 7.2 copy-start.14
  596.3 40.3 %collective-permute-start.23 = (bf16[512,2048]{1,0:T(8,128)(2,1)}, bf16[512,2048]{1,0:T(8,128)(2,1)}, u32[]{:S(2)}, u32[]{:S(2)}) collective-permute-start(bf16[512,2048]{1,0:T(8,128)(2,1)} %pad_maximum_fusion.7), channel_id=1, source_target_pairs={{0,2},{1,3},{2,0},{3,1},{4,6},{5,7},{6,4},{7,5},{8,10},{9,11},{10,... | collective-permute-start | bytes 6291464 | tf_op jit(solution)/shard_map/ppermute | solution.py:37
  599.1 39.5 %collective-permute-start.21 = (bf16[512,2048]{1,0:T(8,128)(2,1)}, bf16[512,2048]{1,0:T(8,128)(2,1)}, u32[]{:S(2)}, u32[]{:S(2)}) collective-permute-start(bf16[512,2048]{1,0:T(8,128)(2,1)} %pad_maximum_fusion.6), channel_id=1, source_target_pairs={{0,1},{1,0},{2,3},{3,2},{4,5},{5,4},{6,7},{7,6},{8,9},{9,8},{10,11... | collective-permute-start | bytes 6291464 | tf_op jit(solution)/shard_map/ppermute | solution.py:37
  600.2 24.2 %slice-start.4 = ((s8[8388608]{0:T(1024)(128)(4,1)}), s8[4194304]{0:T(1024)(128)(4,1)S(1)}, s32[]{:S(2)}) async-start(s8[8388608]{0:T(1024)(128)(4,1)} %bitcast.106), calls=%async_computation.17 | async-start | bytes 8388608
  602.9 21.6 %slice-start.5 = ((s8[8388608]{0:T(1024)(128)(4,1)}), s8[4194304]{0:T(1024)(128)(4,1)S(1)}, s32[]{:S(2)}) async-start(s8[8388608]{0:T(1024)(128)(4,1)} %bitcast.106), calls=%async_computation.18 | async-start | bytes 8388608
  663.0 14.1 %slice-start = ((s8[8388608]{0:T(1024)(128)(4,1)}), s8[4194304]{0:T(1024)(128)(4,1)S(1)}, s32[]{:S(2)}) async-start(s8[8388608]{0:T(1024)(128)(4,1)} %bitcast.93), calls=%async_computation.13 | async-start | bytes 8388608
  668.1 9.0 %slice-start.1 = ((s8[8388608]{0:T(1024)(128)(4,1)}), s8[4194304]{0:T(1024)(128)(4,1)S(1)}, s32[]{:S(2)}) async-start(s8[8388608]{0:T(1024)(128)(4,1)} %bitcast.93), calls=%async_computation.14 | async-start | bytes 8388608
  674.0 22.7 %collective-permute-start.24 = (bf16[256,2048]{1,0:T(8,128)(2,1)}, bf16[256,2048]{1,0:T(8,128)(2,1)}, u32[]{:S(2)}, u32[]{:S(2)}) collective-permute-start(bf16[256,2048]{1,0:T(8,128)(2,1)} %get-tuple-element.182), channel_id=1, source_target_pairs={{0,2},{1,3},{2,0},{3,1},{4,6},{5,7},{6,4},{7,5},{8,10},{9,11},{10,... | collective-permute-start | bytes 3145736 | tf_op jit(solution)/shard_map/ppermute | solution.py:37
  675.7 17.8 %collective-permute-start.26 = (bf16[256,2048]{1,0:T(8,128)(2,1)}, bf16[256,2048]{1,0:T(8,128)(2,1)}, u32[]{:S(2)}, u32[]{:S(2)}) collective-permute-start(bf16[256,2048]{1,0:T(8,128)(2,1)} %get-tuple-element.183), channel_id=1, source_target_pairs={{0,1},{1,0},{2,3},{3,2},{4,5},{5,4},{6,7},{7,6},{8,9},{9,8},{10,11... | collective-permute-start | bytes 3145736 | tf_op jit(solution)/shard_map/ppermute | solution.py:37
  696.5 39.0 %collective-permute-start.27 = (bf16[512,2048]{1,0:T(8,128)(2,1)}, bf16[512,2048]{1,0:T(8,128)(2,1)}, u32[]{:S(2)}, u32[]{:S(2)}) collective-permute-start(bf16[512,2048]{1,0:T(8,128)(2,1)} %pad_maximum_fusion.9), channel_id=1, source_target_pairs={{0,2},{1,3},{2,0},{3,1},{4,6},{5,7},{6,4},{7,5},{8,10},{9,11},{10,... | collective-permute-start | bytes 6291464 | tf_op jit(solution)/shard_map/ppermute | solution.py:37
  700.0 38.5 %collective-permute-start.25 = (bf16[512,2048]{1,0:T(8,128)(2,1)}, bf16[512,2048]{1,0:T(8,128)(2,1)}, u32[]{:S(2)}, u32[]{:S(2)}) collective-permute-start(bf16[512,2048]{1,0:T(8,128)(2,1)} %pad_maximum_fusion.8), channel_id=1, source_target_pairs={{0,1},{1,0},{2,3},{3,2},{4,5},{5,4},{6,7},{7,6},{8,9},{9,8},{10,11... | collective-permute-start | bytes 6291464 | tf_op jit(solution)/shard_map/ppermute | solution.py:37
  706.7 31.7 %copy-start.39 = (f32[2048]{0:T(1024)S(1)}, f32[2048]{0:T(1024)}, u32[]{:S(2)}) copy-start(f32[2048]{0:T(1024)} %param.17) | copy-start | bytes 24580
  (42 other events, 146.5 us)
Sparse Core Ops, SparseCore 0:
  125.4 47.2 all-gather.3
  174.3 44.3 all-gather.5
  235.1 44.8 all-gather.7
  438.5 48.4 reduce-scatter.7
  506.0 47.6 reduce-scatter.5
  566.2 47.5 reduce-scatter.11
  616.0 48.1 reduce-scatter.13
  666.5 87.7 reduce-scatter.9

commit v3 on v2

--- a/solution.py
+++ b/solution.py
@@ -573,6 +573,312 @@
     return w_qkv, w_gate, normed1_all, cots, (cots[0],)
 
 
+def closing_kernel(
+    heads, normed_ref, back_ref, weight_ref, gate_terms_ref, token_ref, mixed_ref, gain_ref, late_ref,
+    grad_ref, query_out, key_out, value_out, sums_ref,
+    back, weight, terms, columns, half_in, full_in, products, twin_in, line_in, token_own, mixed_own,
+    given, landed, total,
+    load_sem, column_sem, out_sem, half_send, half_recv, full_send, full_recv, twin_send, twin_recv,
+    line_send, line_recv, sum_send, sum_recv,
+):
+    dp = lax.axis_index("dp")
+    tensor = lax.axis_index("tensor")
+    z = lax.div(dp, 2)
+    core = lax.rem(dp, 2)
+    rows = token_ref.shape[0]
+    half = rows // 2
+    depth = columns.shape[2] // 2
+    width = terms.shape[1]
+    at_end = (z == 0) | (z == 3)
+    upper = z >= 2
+    twin = (dp + 1 - 2 * core, tensor)
+    over_x = (dp, tensor + 1 - 2 * lax.rem(tensor, 2))
+    over_y = (dp, lax.rem(tensor + 2, 4))
+    here = dp * 4 + tensor
+    peers = 32
+
+    def layer(index):
+        return (2 * index + core, tensor)
+
+    def seen(index):
+        return jnp.where(upper, 3 - index, index)
+
+    end = layer(seen(0))
+    near = layer(seen(1))
+    opposite = layer(seen(2))
+    targets = [seen(3), seen(2), jnp.where(at_end, seen(1), seen(0)), z]
+
+    def column_copy(k):
+        place = pl.ds(pl.multiple_of(targets[k] * 2 * depth, 2 * depth), 2 * depth)
+        return pltpu.make_async_copy(normed_ref.at[:, place], columns.at[k % 2], column_sem.at[k])
+
+    loads = [
+        pltpu.make_async_copy(src, dst, load_sem.at[i])
+        for i, (src, dst) in enumerate(
+            ((back_ref, back), (weight_ref, weight), (gate_terms_ref, terms), (token_ref, token_own), (mixed_ref, mixed_own))
+        )
+    ]
+    column_copy(0).start()
+    loads[0].start()
+    column_copy(1).start()
+    for copy in loads[1:]:
+        copy.start()
+
+    barrier = pltpu.get_barrier_semaphore()
+
+    def partner(k):
+        other = lax.rem(here + k, peers)
+        return other, (lax.div(other, 4), lax.rem(other, 4))
+
+    @pl.loop(1, peers)
+    def _(k):
+        pl.semaphore_signal(barrier, inc=1, device_id=partner(k)[1], device_id_type=MESH)
+
+    pl.semaphore_wait(barrier, peers - 1)
+
+    def remote(src, dst, send, recv, device):
+        return pltpu.make_async_remote_copy(
+            src_ref=src, dst_ref=dst, send_sem=send, recv_sem=recv, device_id=device, device_id_type=MESH
+        )
+
+    mine = pl.ds(pl.multiple_of(core * depth, depth), depth)
+    theirs = pl.ds(pl.multiple_of((1 - core) * depth, depth), depth)
+
+    def to_twin(k):
+        return remote(products.at[k, theirs], twin_in.at[k], twin_send.at[k], twin_recv.at[k], twin)
+
+    def multiply(k):
+        column_copy(k).wait()
+
+        @pl.loop(0, width // 512)
+        def _(j):
+            tile = pl.ds(pl.multiple_of(j * 512, 512), 512)
+            products[k, :, tile] = dot_tn(columns[k % 2], back[:, tile]).astype(bf16)
+
+        if k + 2 < 4:
+            column_copy(k + 2).start()
+        to_twin(k).start()
+
+    def merge(k, *arrived):
+        @pl.loop(0, depth // 64)
+        def _(i):
+            block = pl.ds(pl.multiple_of(i * 64, 64), 64)
+            inner = pl.ds(pl.multiple_of(core * depth + i * 64, 64), 64)
+            value = products[k, inner].astype(f32) + twin_in[k, block].astype(f32)
+            for slot in arrived:
+                value = value + line_in[slot, block].astype(f32)
+            products[k, inner] = value.astype(bf16)
+
+    def along(k, slot, device):
+        return remote(products.at[k, mine], line_in.at[slot], line_send.at[k], line_recv.at[slot], device)
+
+    def line_wait(slot):
+        along(0, slot, end).wait_recv()
+
+    def rows_of(r, start=0, count=rows):
+        return pl.ds(r * rows + start, count)
+
+    def project(r):
+        @pl.loop(0, width // 256)
+        def _(j):
+            tile = pl.ds(pl.multiple_of(j * 256, 256), 256)
+            grown = terms[rows_of(r), tile].astype(f32) + dot_nt(back[rows_of(r), :], weight[tile, :])
+            terms[rows_of(r), tile] = grown.astype(bf16)
+
+    halves = [
+        remote(terms.at[rows_of(3, 0, half)], half_in.at[0], half_send.at[0], half_recv.at[0], over_x),
+        remote(terms.at[rows_of(3, half, half)], half_in.at[1], half_send.at[1], half_recv.at[1], over_y),
+    ]
+    fulls = [
+        remote(terms.at[rows_of(1)], full_in.at[0], full_send.at[0], full_recv.at[0], over_x),
+        remote(terms.at[rows_of(2)], full_in.at[1], full_send.at[1], full_recv.at[1], over_y),
+    ]
+
+    def add_half(r, start, slot):
+        @pl.loop(0, half // 64)
+        def _(i):
+            block = pl.ds(pl.multiple_of(i * 64, 64), 64)
+            place = pl.ds(pl.multiple_of(r * rows + start + i * 64, 64), 64)
+            terms[place, :] = (terms[place, :].astype(f32) + half_in[slot, block].astype(f32)).astype(bf16)
+
+    loads[0].wait()
+    multiply(0)
+    loads[1].wait()
+    loads[2].wait()
+    project(3)
+    for copy in halves:
+        copy.start()
+    multiply(1)
+    to_twin(0).wait_recv()
+
+    @pl.when(at_end)
+    def _():
+        merge(0)
+        along(0, 0, near).start()
+
+    project(1)
+    project(2)
+    to_twin(1).wait_recv()
+
+    @pl.when(at_end)
+    def _():
+        merge(1)
+        along(1, 1, near).start()
+
+    for copy in halves:
+        copy.wait_recv()
+    add_half(2, 0, 0)
+    add_half(1, half, 1)
+    for copy in fulls:
+        copy.start()
+    multiply(2)
+    to_twin(2).wait_recv()
+
+    @pl.when(at_end)
+    def _():
+        merge(2)
+        along(2, 2, near).start()
+
+    @pl.when(jnp.logical_not(at_end))
+    def _():
+        line_wait(0)
+        merge(0, 0)
+        along(0, 3, opposite).start()
+
+    multiply(3)
+    project(0)
+    to_twin(3).wait_recv()
+
+    @pl.when(jnp.logical_not(at_end))
+    def _():
+        line_wait(1)
+        merge(1, 1)
+        along(1, 4, opposite).start()
+        line_wait(3)
+        merge(2, 3)
+        along(2, 0, end).start()
+
+    loads[3].wait()
+    loads[4].wait()
+    for copy in fulls:
+        copy.wait_recv()
+    total[...] = jnp.zeros_like(total)
+
+    @pl.loop(0, rows // 64)
+    def _(i):
+        block = pl.ds(pl.multiple_of(i * 64, 64), 64)
+        normed_grad = terms[block, :].astype(f32) + full_in[0, block].astype(f32) + full_in[1, block].astype(f32)
+        unit, scale = normalize(token_own[block, :].astype(f32))
+        grad = mixed_own[block, :] + normalize_back(normed_grad, unit, scale, gain_ref[...])
+        full_in[0, block] = grad.astype(bf16)
+        total[0:1, :] += jnp.sum(normed_grad * unit, axis=0, keepdims=True)
+        total[1:2, :] += jnp.sum(normed_grad, axis=0, keepdims=True)
+
+    grad_out = pltpu.make_async_copy(full_in.at[0], grad_ref, out_sem.at[0])
+    grad_out.start()
+
+    total[2:4, :] = late_ref[...]
+    for k in range(peers // 2):
+        given[k] = total[:, k * 128 : (k + 1) * 128]
+
+    def sum_copy(k):
+        other, device = partner(k)
+        return remote(given.at[lax.div(other, 2)], landed.at[k], sum_send.at[k], sum_recv.at[k], device)
+
+    @pl.loop(1, peers)
+    def _(k):
+        sum_copy(k).start()
+
+    @pl.when(at_end)
+    def _():
+        line_wait(0)
+        merge(3, 0)
+
+    @pl.when(jnp.logical_not(at_end))
+    def _():
+        line_wait(2)
+        line_wait(4)
+        merge(3, 2, 4)
+
+    @pl.loop(0, depth // 64)
+    def _(i):
+        block = pl.ds(pl.multiple_of(i * 64, 64), 64)
+        inner = pl.ds(pl.multiple_of(core * depth + i * 64, 64), 64)
+        mixed_own[block, :] = products[3, inner].astype(f32)
+
+    keys = heads * KEY
+    values = heads * VAL
+    outs = [
+        pltpu.make_async_copy(mixed_own.at[pl.ds(0, depth), pl.ds(0, keys)], query_out, out_sem.at[1]),
+        pltpu.make_async_copy(mixed_own.at[pl.ds(0, depth), pl.ds(keys, keys)], key_out, out_sem.at[2]),
+        pltpu.make_async_copy(mixed_own.at[pl.ds(0, depth), pl.ds(2 * keys, values)], value_out, out_sem.at[3]),
+    ]
+    for copy in outs:
+        copy.start()
+    sums_ref[...] = given[lax.div(here, 2)]
+
+    @pl.loop(1, peers)
+    def _(k):
+        sum_copy(k).wait()
+        sums_ref[...] += landed[k]
+
+    for copy in halves + fulls:
+        copy.wait_send()
+    for k in range(4):
+        to_twin(k).wait_send()
+    for k in range(3):
+        along(k, k, near).wait_send()
+    grad_out.wait()
+    for copy in outs:
+        copy.wait()
+
+
+def closing_exchange(heads, normed, back, weight, gate_terms, tokens, mixed_grad, gain, late):
+    rows, width = tokens.shape
+    depth = width // 8
+    keys, values = heads * KEY, heads * VAL
+    anywhere = pl.BlockSpec(memory_space=pl.ANY)
+    in_vmem = pl.BlockSpec(memory_space=pltpu.VMEM)
+    sem = pltpu.SemaphoreType.DMA
+    grad, query, key, value, sums = pl.pallas_call(
+        functools.partial(closing_kernel, heads),
+        out_shape=[
+            jax.ShapeDtypeStruct((rows, width), bf16),
+            jax.ShapeDtypeStruct((depth, keys), f32),
+            jax.ShapeDtypeStruct((depth, keys), f32),
+            jax.ShapeDtypeStruct((depth, values), f32),
+            jax.ShapeDtypeStruct((8, 128), f32),
+        ],
+        in_specs=[anywhere] * 6 + [in_vmem] * 2,
+        out_specs=[anywhere] * 4 + [in_vmem],
+        scratch_shapes=[
+            pltpu.VMEM((4 * rows, width), bf16),
+            pltpu.VMEM((width, width), bf16),
+            pltpu.VMEM((4 * rows, width), bf16),
+            pltpu.VMEM((2, 4 * rows, 2 * depth), bf16),
+            pltpu.VMEM((2, rows // 2, width), bf16),
+            pltpu.VMEM((2, rows, width), bf16),
+            pltpu.VMEM((4, 2 * depth, width), bf16),
+            pltpu.VMEM((4, depth, width), bf16),
+            pltpu.VMEM((5, depth, width), bf16),
+            pltpu.VMEM((rows, width), bf16),
+            pltpu.VMEM((rows, width), f32),
+            pltpu.VMEM((16, 8, 128), f32),
+            pltpu.VMEM((32, 8, 128), f32),
+            pltpu.VMEM((8, width), f32),
+            sem((5,)), sem((4,)), sem((4,)),
+            sem((2,)), sem((2,)), sem((2,)), sem((2,)),
+            sem((4,)), sem((4,)), sem((3,)), sem((5,)),
+            sem((32,)), sem((32,)),
+        ],
+        compiler_params=pltpu.CompilerParams(
+            collective_id=3, has_side_effects=True, vmem_limit_bytes=60 * 1024 * 1024
+        ),
+        name="closing_exchange",
+    )(normed, back, weight, gate_terms, tokens, mixed_grad, gain.reshape(1, width), late)
+    return grad, query, key, value, sums
+
+
 def body(tokens, cotangent, segment, first_gain, first_bias, query_weight, key_weight, value_weight, gate_weight, out_weight, second_gain, second_bias, up_weight, down_weight):
     devices = lax.axis_size("tensor")
     rows = tokens.shape[0]
@@ -591,7 +897,6 @@
     w_up = lax.all_gather(after(up_weight, w_down), "dp", axis=0, tiled=True)
 
     token_rows = tokens.astype(f32)
-    unit1, scale1 = normalize(token_rows)
     tables = retention_tables(segment, heads, here * heads)
     field = dot_nn(normed1_all, w_qkv).astype(bf16)
     gate = dot_nn(normed1_all, w_gate).astype(bf16)
@@ -643,7 +948,8 @@
         ))
         gated_grad.append(both[0])
         gate_grad.append(both[1])
-    gate_weight_grad = dot_tn(normed1_all, jnp.concatenate(gate_grad, axis=0)).astype(bf16)
+    gate_grad_all = jnp.concatenate(gate_grad, axis=0)
+    gate_weight_grad = dot_tn(normed1_all, gate_grad_all).astype(bf16)
     gate_sum = lax.psum_scatter(gate_weight_grad, "dp", scatter_dimension=0, tiled=True).astype(f32)
     ffn, ffn_begun, ffn_done = scatter_sum([term.astype(f32) for term in after(ffn_terms, mixed_pieces[3])])
     result = (mixed + ffn).astype(bf16)
@@ -653,23 +959,37 @@
         True, which, rows, heads, field, gate, tables,
         (jnp.concatenate(after(gated_grad, out_weight_grad, *ffn_begun), axis=0), grouped, group_scale, past),
     )
-    terms = [dot_nt(first, w_qkv) + dot_nt(second, w_gate) for first, second in zip(per_piece(back), gate_grad)]
-    normed1_grad, begun, _ = scatter_sum(terms)
-    qkv_weight_grad = dot_tn(normed1_all, after(back, terms[-1], *ffn_done, up_sum, down_sum)).astype(bf16)
-    qkv_sum = lax.psum_scatter(qkv_weight_grad, "dp", scatter_dimension=0, tiled=True)
-    input_grad = mixed_grad + normalize_back(normed1_grad, unit1, scale1, first_gain)
-    gain1_grad = jnp.sum(normed1_grad * unit1, axis=0)
-    bias1_grad = jnp.sum(normed1_grad, axis=0)
-    norm_sums = spread_sum([gain1_grad, bias1_grad, gain2_grad, bias2_grad])
     keys_end = heads * KEY
+    if devices == 4 and lax.axis_size("dp") == 8:
+        gate_terms = dot_nt(gate_grad_all, w_gate).astype(bf16)
+        input_grad, query_sum, key_sum, value_sum, sums = closing_exchange(
+            heads, normed1_all, back, w_qkv, after(gate_terms, *ffn_done, up_sum, down_sum), tokens, mixed_grad, first_gain,
+            jnp.stack([gain2_grad, bias2_grad]),
+        )
+        part = first_gain.shape[0] // 32
+        sums = lax.dynamic_slice_in_dim(sums, (here % 2) * part, part, 1)
+        norm_sums = [sums[0], sums[1], sums[2], sums[3]]
+    else:
+        terms = [dot_nt(first, w_qkv) + dot_nt(second, w_gate) for first, second in zip(per_piece(back), gate_grad)]
+        normed1_grad, _, _ = scatter_sum(terms)
+        qkv_weight_grad = dot_tn(normed1_all, back).astype(bf16)
+        qkv_sum = lax.psum_scatter(qkv_weight_grad, "dp", scatter_dimension=0, tiled=True).astype(f32)
+        query_sum = qkv_sum[:, :keys_end]
+        key_sum = qkv_sum[:, keys_end : 2 * keys_end]
+        value_sum = qkv_sum[:, 2 * keys_end :]
+        unit1, scale1 = normalize(token_rows)
+        input_grad = (mixed_grad + normalize_back(normed1_grad, unit1, scale1, first_gain)).astype(bf16)
+        gain1_grad = jnp.sum(normed1_grad * unit1, axis=0)
+        bias1_grad = jnp.sum(normed1_grad, axis=0)
+        norm_sums = spread_sum([gain1_grad, bias1_grad, gain2_grad, bias2_grad])
     return (
         result,
-        input_grad.astype(bf16),
+        input_grad,
         norm_sums[0],
         norm_sums[1],
-        qkv_sum[:, :keys_end].astype(f32),
-        qkv_sum[:, keys_end : 2 * keys_end].astype(f32),
-        qkv_sum[:, 2 * keys_end :].astype(f32),
+        query_sum,
+        key_sum,
+        value_sum,
         gate_sum,
         out_sum,
         norm_sums[2],

time: 792 us -> 789 us (level)
  Pallas kernels: 161 us -> 255 us
  matrix products: 266 us -> 201 us
  other arithmetic: 64.8 us -> 44.1 us
  waiting for transfers between devices: 216 us -> 196 us
  local copies, waits for them, and re-layouts: 34.7 us -> 44.8 us
    pallas_call x1, Pallas kernels: 9.82 us -> 104 us  [closing_exchange(): pl.pallas_call(functools.partial(closing_kernel, heads), out_shape=[jax.S...]
    dot_general x17 -> x10, matrix products: 110 us -> 66.5 us  [dot_nt(): lax.dot_general(left, right, (((1,), (1,)), ((), ())), preferred_element_...]
    dot_general x5 -> x4, matrix products: 74.1 us -> 50.2 us  [dot_tn(): lax.dot_general(left, right, (((0,), (0,)), ((), ())), preferred_element_...]
    ppermute x28 -> x24, waiting for transfers between devices: 212 us -> 193 us  [tensor_permute(): return lax.ppermute(values, 'tensor', pairs)]
    convert_element_type x3 -> x0, other arithmetic: 9.53 us -> none  [the longest x1 5.27 us: body(): input_grad.astype(bf16)]
    unnamed x155 -> x142, local copies, waits for them, and re-layouts: 12.9 us -> 18 us
    ppermute x28 -> x24, starting transfers between devices: 24.9 us -> 24.1 us  [tensor_permute(): return lax.ppermute(values, 'tensor', pairs)]
  transfers between devices with their start and end apart: 36 -> 31, of which waited for: 18 -> 17; matrix products, arithmetic and copies ran while one was open for 42% -> 32% of each run, Pallas kernels for 6% -> 18%
where the time goes in v3:
time: 789 us; the launch traced here: 782 us
  Pallas kernels  255 us (32%)
  matrix products  201 us (25%)
  waiting for transfers between devices  196 us (25%)
  local copies, waits for them, and re-layouts  44.8 us (6%)
  other arithmetic  44.1 us (6%)
  starting transfers between devices  25.1 us (3%)
  between operations  15.4 us (2%)
    ppermute x24, waiting for transfers between devices, tensor_permute(): return lax.ppermute(values, 'tensor', pairs)  193 us
    pallas_call x1, Pallas kernels, opening_exchange(): pl.pallas_call(opening_kernel, out_shape=[jax.ShapeDtypeStruct((dp * dept...  113 us
    pallas_call x1, Pallas kernels, closing_exchange(): pl.pallas_call(functools.partial(closing_kernel, heads), out_shape=[jax.S...  104 us
    dot_general x11, matrix products, dot_nn(): lax.dot_general(left, right, (((1,), (0,)), ((), ())), preferred_element_...  84.7 us
    dot_general x10, matrix products, dot_nt(): lax.dot_general(left, right, (((1,), (1,)), ((), ())), preferred_element_...  66.5 us
    dot_general x4, matrix products, dot_tn(): lax.dot_general(left, right, (((0,), (0,)), ((), ())), preferred_element_...  50.2 us
    pallas_call x2, Pallas kernels, retention_call(): pl.pallas_call(functools.partial(retention_backward if backward else rete...  37.5 us
    ppermute x24, starting transfers between devices, tensor_permute(): return lax.ppermute(values, 'tensor', pairs)  24.1 us
  transfers between devices with their start and end apart: 31, of which 17 were waited for; matrix products, arithmetic and copies ran while one was open for 32% of the time, Pallas kernels for 18%

profile of v3, /device:TPU:0, one launch (start us, length us, event | category | flops | bytes accessed | tf_op | source)
XLA Modules:
  0.0 781.5 jit_solution(17507652788831675866)
XLA Ops:
  7.2 113.4 %opening_exchange.1 = (bf16[2048,2048]{1,0:T(8,128)(2,1)}, bf16[2048,1024]{1,0:T(8,128)(2,1)}, bf16[2048,2048]{1,0:T(8,128)(2,1)}, bf16[2,256,2048]{2,1,0:T(8,128)(2,1)}) custom-call(bf16[256,512]{1,0:T(8,128)(2,1)} %query_ref.1, bf16[256,512]{1,0:T(8,128)(2,1)} %key_ref.1, bf16[256,1024]{1,0:T(8,128)(2,1)} %value_ref.1, bf16[256,1024]{1,0:T(8,128)(2,1)} %gate_ref.1, ...), custom_call_target="tpu_custom_call" | custom-call | tf_op jit(solution)/shard_map/opening_exchange/pallas_call | solution.py:520
  121.7 1.6 collective-permute-start.1
  123.3 1.8 collective-permute-start
  125.2 2.7 slice_bitcast_fusion
  130.7 14.1 %convolution_convert_fusion.5.gate_ref = bf16[2048,1024]{1,0:T(8,128)(2,1)} fusion(bf16[2048,2048]{1,0:T(8,128)(2,1)} %get-tuple-element.87.normed_ref, bf16[2048,1024]{1,0:T(8,128)(2,1)} %get-tuple-element.89), kind=kOutput, calls=%fused_computation.40 | convolution fusion | flops 8592031744 | bytes 16777216 | tf_op jit(solution)/shard_map/dot_general | solution.py:24
  144.8 23.7 %convolution_convert_fusion.2.field_ref = bf16[2048,2048]{1,0:T(8,128)(2,1)} fusion(bf16[2048,2048]{1,0:T(8,128)(2,1)} %get-tuple-element.87.normed_ref, bf16[2048,2048]{1,0:T(8,128)(2,1)} %get-tuple-element.88.weight_ref), kind=kOutput, calls=%fused_computation.18 | convolution fusion | flops 17184063488 | bytes 25165824 | tf_op jit(solution)/shard_map/dot_general | solution.py:24
  168.6 2.5 all-gather.4.cloned.1.call-done
  174.7 3.7 multiply_cosine_fusion
  178.5 16.3 %retention_forward.1 = (bf16[2048,1024]{1,0:T(8,128)(2,1)}, bf16[2048,1024]{1,0:T(8,128)(2,1)}, f32[2048,256]{1,0:T(8,128)S(1)}, bf16[8,2,256,512]{3,2,1,0:T(8,128)(2,1)}) custom-call(s32[1]{0:T(128)} %bitcast.which, bf16[2048,2048]{1,0:T(8,128)(2,1)} %convolution_convert_fusion.2.field_ref, bf16[2048,1024]{1,0:T(8,128)(2,1)} %convolution_convert_fusion.5.gate_ref, ...), custom_call_target="tpu_custom_call" | custom-call | flops 3758096384 | bytes 25165824 | tf_op jit(solution)/shard_map/retention_forward/pallas_call | solution.py:317
  194.8 3.9 collective-permute-done.3
  198.7 4.0 convolution_convert_fusion.7
  205.9 2.4 fusion.95
  208.2 2.4 fusion.98
  210.9 17.8 %collective-permute-done.6 = bf16[256,2048]{1,0:T(8,128)(2,1)S(1)} collective-permute-done((bf16[256,2048]{1,0:T(8,128)(2,1)S(1)}, bf16[256,2048]{1,0:T(8,128)(2,1)S(1)}, u32[]{:S(2)}, u32[]{:S(2)}) %collective-permute-start.6) | collective-permute-done | bytes 1048608 | tf_op jit(solution)/shard_map/ppermute | solution.py:37
  229.1 1.6 pad_maximum_fusion.3
  231.5 1.6 pad_maximum_fusion.2
  234.8 42.0 %collective-permute-done.7 = bf16[512,2048]{1,0:T(8,128)(2,1)} collective-permute-done((bf16[512,2048]{1,0:T(8,128)(2,1)}, bf16[512,2048]{1,0:T(8,128)(2,1)}, u32[]{:S(2)}, u32[]{:S(2)}) %collective-permute-start.7) | collective-permute-done | bytes 2097184 | tf_op jit(solution)/shard_map/ppermute | solution.py:37
  276.9 2.2 collective-permute-done.5
  279.0 7.4 fusion.117
  296.0 37.1 %collective-permute-done.9 = bf16[512,2048]{1,0:T(8,128)(2,1)S(1)} collective-permute-done((bf16[512,2048]{1,0:T(8,128)(2,1)S(1)}, bf16[512,2048]{1,0:T(8,128)(2,1)S(1)}, u32[]{:S(2)}, u32[]{:S(2)}) %collective-permute-start.9) | collective-permute-done | bytes 2097184 | tf_op jit(solution)/shard_map/ppermute | solution.py:37
  336.2 10.9 %convolution_convert_fusion.4 = bf16[2048,1024]{1,0:T(8,128)(2,1)} fusion(bf16[2048,2048]{1,0:T(8,128)(2,1)S(1)} %constant_dynamic-update-slice_fusion, bf16[1024,2048]{1,0:T(8,128)(2,1)S(1)} %copy-done.48), kind=kOutput, calls=%fused_computation.39 | convolution fusion | flops 8592031744 | bytes 16777216 | tf_op jit(solution)/shard_map/dot_general | solution.py:28
  347.2 5.3 fusion.118
  352.5 2.4 fusion.119
  355.3 7.4 fusion.82
  365.7 4.3 fusion.120
  370.1 4.3 fusion.121
  374.4 4.5 fusion.122
  378.9 5.2 collective-permute-done.10
  385.4 3.6 fusion.90
  389.1 2.4 fusion.123
  394.4 2.1 copy-done.38
  396.5 11.1 %convolution_convert_fusion.3 = bf16[1024,2048]{1,0:T(8,128)(2,1)} fusion(bf16[2048,1024]{1,0:T(8,128)(2,1)S(1)} %constant_dynamic-update-slice_fusion.9, bf16[2048,2048]{1,0:T(8,128)(2,1)S(1)} %bitcast.87), kind=kOutput, calls=%fused_computation.38 | convolution fusion | flops 8592031744 | bytes 16777216 | tf_op jit(solution)/shard_map/dot_general | solution.py:32
  408.3 2.1 slice.335
  410.4 1.7 slice.334
  413.1 2.0 fusion.92
  415.8 18.1 %collective-permute-done.14 = bf16[256,2048]{1,0:T(8,128)(2,1)S(1)} collective-permute-done((bf16[256,2048]{1,0:T(8,128)(2,1)S(1)}, bf16[256,2048]{1,0:T(8,128)(2,1)S(1)}, u32[]{:S(2)}, u32[]{:S(2)}) %collective-permute-start.14) | collective-permute-done | bytes 1048608 | tf_op jit(solution)/shard_map/ppermute | solution.py:37
  435.1 37.4 %collective-permute-done.13 = bf16[512,2048]{1,0:T(8,128)(2,1)S(1)} collective-permute-done((bf16[512,2048]{1,0:T(8,128)(2,1)S(1)}, bf16[512,2048]{1,0:T(8,128)(2,1)S(1)}, u32[]{:S(2)}, u32[]{:S(2)}) %collective-permute-start.13) | collective-permute-done | bytes 2097184 | tf_op jit(solution)/shard_map/ppermute | solution.py:37
  472.5 2.6 multiply_reduce_fusion
  475.2 3.8 fusion.111
  480.2 14.0 %fusion.23 = bf16[2048,1024]{1,0:T(8,128)(2,1)} fusion(bf16[512,1024]{1,0:T(8,128)(2,1)} %copy-done.55, bf16[512,1024]{1,0:T(8,128)(2,1)S(1)} %copy-done.51, bf16[512,1024]{1,0:T(8,128)(2,1)} %copy-done.52, bf16[512,1024]{1,0:T(8,128)(2,1)} %copy-done.53, bf16[512,2048]{1,0:T(8,128)(2,1)} %copy-done.34, bf16[512,2048]{1,0:T(8,128)(2,1)S(1)} %copy-done.31, ...), kind=kOutput, calls=%fused_computation.36 | convolution fusion | flops 8642363392 | bytes 16777216 | tf_op jit(solution)/shard_map/dot_general | solution.py:32
  494.3 12.2 %convolution_convert_fusion.1 = bf16[2048,2048]{1,0:T(8,128)(2,1)S(1)} fusion(bf16[2048,1024]{1,0:T(8,128)(2,1)} %copy-done.38, bf16[1024,2048]{1,0:T(8,128)(2,1)} %all-gather.6.cloned.1.call-done), kind=kOutput, calls=%fused_computation.17 | convolution fusion | flops 8594128896 | bytes 16777216 | tf_op jit(solution)/shard_map/dot_general | solution.py:24
  506.5 4.2 fusion.112
  511.4 4.0 fusion.124
  515.4 7.0 collective-permute-done.17
  526.2 5.3 fusion.125
  531.6 5.5 fusion.126
  537.0 6.0 collective-permute-done.18
  543.6 14.2 %fusion.58 = (bf16[512,1024]{1,0:T(8,128)(2,1)S(1)}, bf16[512,1024]{1,0:T(8,128)(2,1)S(1)}, bf16[512,1024]{1,0:T(8,128)(2,1)S(1)}, bf16[512,1024]{1,0:T(8,128)(2...) fusion(bf16[2048,1024]{1,0:T(8,128)(2,1)} %convolution_convert_, ...), kind=kOutput, calls=%fused_computation.87 | convolution fusion | flops 2174746624 | bytes 29360128 | tf_op jit(solution)/shard_map/dot_general | solution.py:28
  558.1 2.0 copy-done.39
  560.1 10.5 %convolution_convert_fusion.6 = bf16[2048,1024]{1,0:T(8,128)(2,1)} fusion(bf16[2048,2048]{1,0:T(8,128)(2,1)S(1)} %bitcast.85, bf16[2048,1024]{1,0:T(8,128)(2,1)S(1)} %constant_dynamic-update-slice_fusion.15), kind=kOutput, calls=%fused_computation.41 | convolution fusion | flops 8592031744 | bytes 16777216 | tf_op jit(solution)/shard_map/dot_general | solution.py:32
  570.7 14.5 %fusion.28 = bf16[1024,2048]{1,0:T(8,128)(2,1)} fusion(bf16[2048,1024]{1,0:T(8,128)(2,1)} %get-tuple-element.94, bf16[512,2048]{1,0:T(8,128)(2,1)} %copy-done.35, bf16[512,2048]{1,0:T(8,128)(2,1)} %collective-permute-done.16, bf16[512,2048]{1,0:T(8,128)(2,1)} %collective-permute-done.17, bf16[512,2048]{1,0:T(8,128)(2,1)} %get-tuple-element.141), kind=kOutput, calls=%fused_computation.37 | convolution fusion | flops 8625586176 | bytes 16777216 | tf_op jit(solution)/shard_map/dot_general | solution.py:32
  585.2 3.1 fusion.113
  593.5 12.4 %collective-permute-done.22 = bf16[256,2048]{1,0:T(8,128)(2,1)} collective-permute-done((bf16[256,2048]{1,0:T(8,128)(2,1)}, bf16[256,2048]{1,0:T(8,128)(2,1)}, u32[]{:S(2)}, u32[]{:S(2)}) %collective-permute-start.22) | collective-permute-done | bytes 1048608 | tf_op jit(solution)/shard_map/ppermute | solution.py:37
  605.9 1.6 add_convert_fusion.2
  610.6 1.6 pad_maximum_fusion.6
  612.7 10.9 %convolution_convert_fusion.gate_terms_ref = bf16[2048,2048]{1,0:T(8,128)(2,1)} fusion(bf16[2048,1024]{1,0:T(8,128)(2,1)S(1)} %copy-done.40, bf16[2048,1024]{1,0:T(8,128)(2,1)S(1)} %copy-done.44), kind=kOutput, calls=%fused_computation.16 | convolution fusion | flops 8594128896 | bytes 16777216 | tf_op jit(solution)/shard_map/dot_general | solution.py:28
  623.7 2.4 pad_maximum_fusion.grad_ref
  627.3 21.3 %retention_backward.1.back_ref = bf16[2048,2048]{1,0:T(8,128)(2,1)} custom-call(s32[1]{0:T(128)} %bitcast.which, bf16[2048,2048]{1,0:T(8,128)(2,1)} %convolution_convert_fusion.2.field_ref, bf16[2048,1024]{1,0:T(8,128)(2,1)} %convolution_convert_fusion.5.gate_ref, f32[2048,256]{1,0:T(8,128)S(1)} %copy-done.1, f32[2048,128]{1,0:T(8,128)S(1)} %copy-done.3, ...), custom_call_target="tpu_custom_call" | custom-call | flops 8053063680 | bytes 31457280 | tf_op jit(solution)/shard_map/retention_backward/pallas_call | solution.py:317
  648.6 2.1 convert_element_type.298
  651.4 7.1 add_convert_fusion
  658.5 2.1 convert_element_type.296
  660.6 104.1 %closing_exchange.1 = (bf16[512,2048]{1,0:T(8,128)(2,1)}, f32[256,512]{1,0:T(8,128)}, f32[256,512]{1,0:T(8,128)}, f32[256,1024]{1,0:T(8,128)}, f32[8,128]{1,0:T(8,128)}) custom-call(bf16[2048,2048]{1,0:T(8,128)(2,1)} %get-tuple-element.87.normed_ref, bf16[2048,2048]{1,0:T(8,128)(2,1)} %retention_backward.1.back_ref, ...), custom_call_target="tpu_custom_call" | custom-call | tf_op jit(solution)/shard_map/closing_exchange/pallas_call | solution.py:843
  766.2 2.1 convert_element_type.299
  768.3 2.2 convert_element_type.300
  (253 shorter events, 60.3 us)
Async XLA Ops:
  7.2 113.5 %copy-start.8 = (bf16[512,2048]{1,0:T(8,128)(2,1)S(1)}, bf16[512,2048]{1,0:T(8,128)(2,1)}, u32[]{:S(2)}) copy-start(bf16[512,2048]{1,0:T(8,128)(2,1)} %cot_ref.1) | copy-start | bytes 6291460
  7.2 163.9 %all-gather.4.cloned.1.call-start = ((), (), s32[]{:S(2)}) async-start(), calls=%async_computation.4 | async-start | bytes 4718592 | tf_op jit(solution)/shard_map/all_gather | solution.py:895
  120.7 7.5 copy-start.41
  121.7 56.8 %collective-permute-start.1 = (bf16[256,2048]{1,0:T(8,128)(2,1)}, bf16[256,2048]{1,0:T(8,128)(2,1)}, u32[]{:S(2)}, u32[]{:S(2)}) collective-permute-start(bf16[256,2048]{1,0:T(8,128)(2,1)} %slice.191), channel_id=1, source_target_pairs={{0,2},{1,3},{2,0},{3,1},{4,6},{5,7},{6,4},{7,5},{8,10},{9,11},{10,... | collective-permute-start | bytes 3145736 | tf_op jit(solution)/shard_map/ppermute | solution.py:37
  123.3 49.8 %collective-permute-start = (bf16[256,2048]{1,0:T(8,128)(2,1)}, bf16[256,2048]{1,0:T(8,128)(2,1)}, u32[]{:S(2)}, u32[]{:S(2)}) collective-permute-start(bf16[256,2048]{1,0:T(8,128)(2,1)} %slice.191), channel_id=1, source_target_pairs={{0,1},{1,0},{2,3},{3,2},{4,5},{5,4},{6,7},{7,6},{8,9},{9,8},{10,11... | collective-permute-start | bytes 3145736 | tf_op jit(solution)/shard_map/ppermute | solution.py:37
  125.2 109.4 %all-gather.6.cloned.1.call-start = ((), (), s32[]{:S(2)}) async-start(), calls=%async_computation.5 | async-start | bytes 4718592 | tf_op jit(solution)/shard_map/all_gather | solution.py:896
  127.9 66.9 %collective-permute-start.2 = (bf16[256,2048]{1,0:T(8,128)(2,1)S(1)}, bf16[256,2048]{1,0:T(8,128)(2,1)}, u32[]{:S(2)}, u32[]{:S(2)}) collective-permute-start(bf16[256,2048]{1,0:T(8,128)(2,1)S(1)} %get-tuple-element.101), channel_id=1, source_target_pairs={{0,1},{1,0},{2,3},{3,2},{4,5},{5,4},{6,7},{7,6},{8,9},{9,8},{10,11... | collective-permute-start | bytes 3145736 | tf_op jit(solution)/shard_map/ppermute | solution.py:37
  171.1 176.0 %all-gather.8.cloned.1.call-start = ((), (), s32[]{:S(2)}) async-start(), calls=%async_computation.6 | async-start | bytes 4718592 | tf_op jit(solution)/shard_map/all_gather | solution.py:897
  172.9 21.9 %copy-start.2 = (f32[2048,128]{1,0:T(8,128)}, f32[2048,128]{1,0:T(8,128)S(1)}, u32[]{:S(2)}) copy-start(f32[2048,128]{1,0:T(8,128)S(1)} %pad.4.info_ref) | copy-start | bytes 3145732
  173.1 21.7 %copy-start.4 = (f32[2,256,256]{2,1,0:T(8,128)}, f32[2,256,256]{2,1,0:T(8,128)S(1)}, u32[]{:S(2)}) copy-start(f32[2,256,256]{2,1,0:T(8,128)S(1)} %exponential_select_fusion.decay_ref) | copy-start | bytes 1572868
  173.1 25.6 %collective-permute-start.3 = (bf16[256,2048]{1,0:T(8,128)(2,1)}, bf16[256,2048]{1,0:T(8,128)(2,1)S(1)}, u32[]{:S(2)}, u32[]{:S(2)}) collective-permute-start(bf16[256,2048]{1,0:T(8,128)(2,1)} %collective-permute-done), channel_id=1, source_target_pairs={{0,2},{1,3},{2,0},{3,1},{4,6},{5,7},{6,4},{7,5},{8,10},{9,11},{10,... | collective-permute-start | bytes 3145736 | tf_op jit(solution)/shard_map/ppermute | solution.py:37
  178.5 16.3 %copy-start = (f32[2048,256]{1,0:T(8,128)}, f32[2048,256]{1,0:T(8,128)S(1)}, u32[]{:S(2)}) copy-start(f32[2048,256]{1,0:T(8,128)S(1)} %pad_maximum_fusion.1.angle_ref) | copy-start | bytes 6291460
  178.5 20.2 %copy-start.45 = (bf16[1024,2048]{1,0:T(8,128)(2,1)S(1)}, bf16[1024,2048]{1,0:T(8,128)(2,1)}, u32[]{:S(2)}) copy-start(bf16[1024,2048]{1,0:T(8,128)(2,1)} %all-gather.4.cloned.1.call-done) | copy-start | bytes 12582916
  202.9 28.3 %collective-permute-start.4 = (bf16[256,2048]{1,0:T(8,128)(2,1)S(1)}, bf16[256,2048]{1,0:T(8,128)(2,1)S(1)}, u32[]{:S(2)}, u32[]{:S(2)}) collective-permute-start(bf16[256,2048]{1,0:T(8,128)(2,1)S(1)} %get-tuple-element.196), channel_id=1, source_target_pairs={{0,2},{1,3},{2,0},{3,1},{4,6},{5,7},{6,4},{7,5},{8,10},{9,11},{10,... | collective-permute-start | bytes 3145736 | tf_op jit(solution)/shard_map/ppermute | solution.py:37
  204.4 24.3 %collective-permute-start.6 = (bf16[256,2048]{1,0:T(8,128)(2,1)S(1)}, bf16[256,2048]{1,0:T(8,128)(2,1)S(1)}, u32[]{:S(2)}, u32[]{:S(2)}) collective-permute-start(bf16[256,2048]{1,0:T(8,128)(2,1)S(1)} %get-tuple-element.197), channel_id=1, source_target_pairs={{0,1},{1,0},{2,3},{3,2},{4,5},{5,4},{6,7},{7,6},{8,9},{9,8},{10,11... | collective-permute-start | bytes 3145736 | tf_op jit(solution)/shard_map/ppermute | solution.py:37
  230.7 46.2 %collective-permute-start.7 = (bf16[512,2048]{1,0:T(8,128)(2,1)}, bf16[512,2048]{1,0:T(8,128)(2,1)}, u32[]{:S(2)}, u32[]{:S(2)}) collective-permute-start(bf16[512,2048]{1,0:T(8,128)(2,1)} %pad_maximum_fusion.3), channel_id=1, source_target_pairs={{0,2},{1,3},{2,0},{3,1},{4,6},{5,7},{6,4},{7,5},{8,10},{9,11},{10,... | collective-permute-start | bytes 6291464 | tf_op jit(solution)/shard_map/ppermute | solution.py:37
  233.1 45.9 %collective-permute-start.5 = (bf16[512,2048]{1,0:T(8,128)(2,1)}, bf16[512,2048]{1,0:T(8,128)(2,1)}, u32[]{:S(2)}, u32[]{:S(2)}) collective-permute-start(bf16[512,2048]{1,0:T(8,128)(2,1)} %pad_maximum_fusion.2), channel_id=1, source_target_pairs={{0,1},{1,0},{2,3},{3,2},{4,5},{5,4},{6,7},{7,6},{8,9},{9,8},{10,11... | collective-permute-start | bytes 6291464 | tf_op jit(solution)/shard_map/ppermute | solution.py:37
  234.6 414.0 %reduce-scatter.7.cloned.1.call-start = ((), (), s32[]{:S(2)}) async-start(), calls=%async_computation.8 | async-start | bytes 4718592 | tf_op jit(solution)/shard_map/reduce_scatter | solution.py:934
  288.4 44.7 %collective-permute-start.9 = (bf16[512,2048]{1,0:T(8,128)(2,1)S(1)}, bf16[512,2048]{1,0:T(8,128)(2,1)S(1)}, u32[]{:S(2)}, u32[]{:S(2)}) collective-permute-start(bf16[512,2048]{1,0:T(8,128)(2,1)S(1)} %add_convert_fusion.1), channel_id=1, source_target_pairs={{0,2},{1,3},{2,0},{3,1},{4,6},{5,7},{6,4},{7,5},{8,10},{9,11},{10,... | collective-permute-start | bytes 6291464 | tf_op jit(solution)/shard_map/ppermute | solution.py:37
  289.9 44.4 %collective-permute-start.8 = (bf16[512,2048]{1,0:T(8,128)(2,1)S(1)}, bf16[512,2048]{1,0:T(8,128)(2,1)S(1)}, u32[]{:S(2)}, u32[]{:S(2)}) collective-permute-start(bf16[512,2048]{1,0:T(8,128)(2,1)S(1)} %add_convert_fusion.1), channel_id=1, source_target_pairs={{0,1},{1,0},{2,3},{3,2},{4,5},{5,4},{6,7},{7,6},{8,9},{9,8},{10,11... | collective-permute-start | bytes 6291464 | tf_op jit(solution)/shard_map/ppermute | solution.py:37
  294.4 41.8 %copy-start.48 = (bf16[1024,2048]{1,0:T(8,128)(2,1)S(1)}, bf16[1024,2048]{1,0:T(8,128)(2,1)}, u32[]{:S(2)}) copy-start(bf16[1024,2048]{1,0:T(8,128)(2,1)} %all-gather.6.cloned.1.call-done) | copy-start | bytes 12582916
  296.0 40.2 %copy-start.28 = (bf16[2048,2048]{1,0:T(8,128)(2,1)}, bf16[2048,2048]{1,0:T(8,128)(2,1)S(1)}, u32[]{:S(2)}) copy-start(bf16[2048,2048]{1,0:T(8,128)(2,1)S(1)} %constant_dynamic-update-slice_fusion) | copy-start | bytes 25165828
  347.2 5.3 copy-start.33
  347.2 5.3 copy-start.49
  355.3 7.4 copy-start.23
  362.7 7.4 copy-start.52
  362.7 7.4 copy-start.53
  362.7 11.7 %copy-start.50 = (bf16[512,1024]{1,0:T(8,128)(2,1)}, bf16[512,1024]{1,0:T(8,128)(2,1)S(1)}, u32[]{:S(2)}) copy-start(bf16[512,1024]{1,0:T(8,128)(2,1)S(1)} %get-tuple-element.113) | copy-start | bytes 3145732
  362.7 21.4 %collective-permute-start.10 = (bf16[256,2048]{1,0:T(8,128)(2,1)S(1)}, bf16[256,2048]{1,0:T(8,128)(2,1)S(1)}, u32[]{:S(2)}, u32[]{:S(2)}) collective-permute-start(bf16[256,2048]{1,0:T(8,128)(2,1)S(1)} %copy-done.23), channel_id=1, source_target_pairs={{0,1},{1,0},{2,3},{3,2},{4,5},{5,4},{6,7},{7,6},{8,9},{9,8},{10,11... | collective-permute-start | bytes 3145736 | tf_op jit(solution)/shard_map/ppermute | solution.py:37
  364.3 21.0 %collective-permute-start.11 = (bf16[256,2048]{1,0:T(8,128)(2,1)S(1)}, bf16[256,2048]{1,0:T(8,128)(2,1)S(1)}, u32[]{:S(2)}, u32[]{:S(2)}) collective-permute-start(bf16[256,2048]{1,0:T(8,128)(2,1)S(1)} %slice.265), channel_id=1, source_target_pairs={{0,2},{1,3},{2,0},{3,1},{4,6},{5,7},{6,4},{7,5},{8,10},{9,11},{10,... | collective-permute-start | bytes 3145736 | tf_op jit(solution)/shard_map/ppermute | solution.py:37
  385.4 11.1 %slice-start.2 = ((s8[8388608]{0:T(1024)(128)(4,1)}), s8[4194304]{0:T(1024)(128)(4,1)S(1)}, s32[]{:S(2)}) async-start(s8[8388608]{0:T(1024)(128)(4,1)} %bitcast.86), calls=%async_computation.13 | async-start | bytes 8388608
  389.1 7.4 slice-start.3
  392.6 20.4 %collective-permute-start.12 = (bf16[256,2048]{1,0:T(8,128)(2,1)}, bf16[256,2048]{1,0:T(8,128)(2,1)}, u32[]{:S(2)}, u32[]{:S(2)}) collective-permute-start(bf16[256,2048]{1,0:T(8,128)(2,1)} %get-tuple-element.191), channel_id=1, source_target_pairs={{0,2},{1,3},{2,0},{3,1},{4,6},{5,7},{6,4},{7,5},{8,10},{9,11},{10,... | collective-permute-start | bytes 3145736 | tf_op jit(solution)/shard_map/ppermute | solution.py:37
  407.6 250.9 %reduce-scatter.5.cloned.1.call-start = ((), (), s32[]{:S(2)}) async-start(), calls=%async_computation.7 | async-start | bytes 4718592 | tf_op jit(solution)/shard_map/reduce_scatter | solution.py:937
  407.7 5.4 copy-start.16
  407.7 26.2 %collective-permute-start.14 = (bf16[256,2048]{1,0:T(8,128)(2,1)S(1)}, bf16[256,2048]{1,0:T(8,128)(2,1)S(1)}, u32[]{:S(2)}, u32[]{:S(2)}) collective-permute-start(bf16[256,2048]{1,0:T(8,128)(2,1)S(1)} %get-tuple-element.192), channel_id=1, source_target_pairs={{0,1},{1,0},{2,3},{3,2},{4,5},{5,4},{6,7},{7,6},{8,9},{9,8},{10,11... | collective-permute-start | bytes 3145736 | tf_op jit(solution)/shard_map/ppermute | solution.py:37
  412.2 21.7 %copy-start.15 = (f32[512,2048]{1,0:T(8,128)S(1)}, f32[512,2048]{1,0:T(8,128)}, u32[]{:S(2)}) copy-start(f32[512,2048]{1,0:T(8,128)} %fusion.122) | copy-start | bytes 12582916
  415.3 57.3 %copy-start.7 = (f32[512,2048]{1,0:T(8,128)S(1)}, f32[512,2048]{1,0:T(8,128)}, u32[]{:S(2)}) copy-start(f32[512,2048]{1,0:T(8,128)} %copy-done.6) | copy-start | bytes 12582916
  415.3 57.2 %copy-start.14 = (f32[512,2048]{1,0:T(8,128)S(1)}, f32[512,2048]{1,0:T(8,128)}, u32[]{:S(2)}) copy-start(f32[512,2048]{1,0:T(8,128)} %fusion.120) | copy-start | bytes 12582916
  415.3 57.2 %collective-permute-start.13 = (bf16[512,2048]{1,0:T(8,128)(2,1)S(1)}, bf16[512,2048]{1,0:T(8,128)(2,1)S(1)}, u32[]{:S(2)}, u32[]{:S(2)}) collective-permute-start(bf16[512,2048]{1,0:T(8,128)(2,1)S(1)} %pad_maximum_fusion.4), channel_id=1, source_target_pairs={{0,1},{1,0},{2,3},{3,2},{4,5},{5,4},{6,7},{7,6},{8,9},{9,8},{10,11... | collective-permute-start | bytes 6291464 | tf_op jit(solution)/shard_map/ppermute | solution.py:37
  434.4 40.7 %copy-start.10 = (bf16[512,2048]{1,0:T(8,128)(2,1)S(1)}, bf16[512,2048]{1,0:T(8,128)(2,1)}, u32[]{:S(2)}) copy-start(bf16[512,2048]{1,0:T(8,128)(2,1)} %cot_ref.1) | copy-start | bytes 6291460
  434.5 38.1 %collective-permute-start.15 = (bf16[512,2048]{1,0:T(8,128)(2,1)S(1)}, bf16[512,2048]{1,0:T(8,128)(2,1)S(1)}, u32[]{:S(2)}, u32[]{:S(2)}) collective-permute-start(bf16[512,2048]{1,0:T(8,128)(2,1)S(1)} %pad_maximum_fusion.5), channel_id=1, source_target_pairs={{0,2},{1,3},{2,0},{3,1},{4,6},{5,7},{6,4},{7,5},{8,10},{9,11},{10,... | collective-permute-start | bytes 6291464 | tf_op jit(solution)/shard_map/ppermute | solution.py:37
  479.0 43.3 %collective-permute-start.17 = (bf16[512,2048]{1,0:T(8,128)(2,1)}, bf16[512,2048]{1,0:T(8,128)(2,1)}, u32[]{:S(2)}, u32[]{:S(2)}) collective-permute-start(bf16[512,2048]{1,0:T(8,128)(2,1)} %get-tuple-element.141), channel_id=1, source_target_pairs={{0,1},{1,0},{2,3},{3,2},{4,5},{5,4},{6,7},{7,6},{8,9},{9,8},{10,11... | collective-permute-start | bytes 6291464 | tf_op jit(solution)/shard_map/ppermute | solution.py:37
  479.6 44.0 %collective-permute-start.16 = (bf16[512,2048]{1,0:T(8,128)(2,1)}, bf16[512,2048]{1,0:T(8,128)(2,1)}, u32[]{:S(2)}, u32[]{:S(2)}) collective-permute-start(bf16[512,2048]{1,0:T(8,128)(2,1)} %get-tuple-element.141), channel_id=1, source_target_pairs={{0,2},{1,3},{2,0},{3,1},{4,6},{5,7},{6,4},{7,5},{8,10},{9,11},{10,... | collective-permute-start | bytes 6291464 | tf_op jit(solution)/shard_map/ppermute | solution.py:37
  494.3 271.9 %reduce-scatter.9.cloned.1.call-start = ((), (), s32[]{:S(2)}) async-start(), calls=%async_computation.9 | async-start | bytes 4718592 | tf_op jit(solution)/shard_map/reduce_scatter | solution.py:953
  525.0 18.1 %collective-permute-start.18 = (bf16[256,2048]{1,0:T(8,128)(2,1)S(1)}, bf16[256,2048]{1,0:T(8,128)(2,1)S(1)}, u32[]{:S(2)}, u32[]{:S(2)}) collective-permute-start(bf16[256,2048]{1,0:T(8,128)(2,1)S(1)} %slice.277), channel_id=1, source_target_pairs={{0,1},{1,0},{2,3},{3,2},{4,5},{5,4},{6,7},{7,6},{8,9},{9,8},{10,11... | collective-permute-start | bytes 3145736 | tf_op jit(solution)/shard_map/ppermute | solution.py:37
  525.6 17.9 %collective-permute-start.19 = (bf16[256,2048]{1,0:T(8,128)(2,1)S(1)}, bf16[256,2048]{1,0:T(8,128)(2,1)S(1)}, u32[]{:S(2)}, u32[]{:S(2)}) collective-permute-start(bf16[256,2048]{1,0:T(8,128)(2,1)S(1)} %slice.278), channel_id=1, source_target_pairs={{0,2},{1,3},{2,0},{3,1},{4,6},{5,7},{6,4},{7,5},{8,10},{9,11},{10,... | collective-permute-start | bytes 3145736 | tf_op jit(solution)/shard_map/ppermute | solution.py:37
  531.5 28.6 %slice-start = ((s8[8388608]{0:T(1024)(128)(4,1)}), s8[4194304]{0:T(1024)(128)(4,1)S(1)}, s32[]{:S(2)}) async-start(s8[8388608]{0:T(1024)(128)(4,1)} %bitcast.84), calls=%async_computation.11 | async-start | bytes 8388608
  543.6 14.2 %copy-start.35 = (bf16[512,2048]{1,0:T(8,128)(2,1)}, bf16[512,2048]{1,0:T(8,128)(2,1)S(1)}, u32[]{:S(2)}) copy-start(bf16[512,2048]{1,0:T(8,128)(2,1)S(1)} %constant_dynamic-update-slice_fusion.13) | copy-start | bytes 6291460
  543.6 16.5 %slice-start.1 = ((s8[8388608]{0:T(1024)(128)(4,1)}), s8[4194304]{0:T(1024)(128)(4,1)S(1)}, s32[]{:S(2)}) async-start(s8[8388608]{0:T(1024)(128)(4,1)} %bitcast.84), calls=%async_computation.12 | async-start | bytes 8388608
  570.6 197.7 %reduce-scatter.11.cloned.1.call-start = ((), (), s32[]{:S(2)}) async-start(), calls=%async_computation.10 | async-start | bytes 4718592 | tf_op jit(solution)/shard_map/reduce_scatter | solution.py:957
  588.4 17.5 %collective-permute-start.22 = (bf16[256,2048]{1,0:T(8,128)(2,1)}, bf16[256,2048]{1,0:T(8,128)(2,1)}, u32[]{:S(2)}, u32[]{:S(2)}) collective-permute-start(bf16[256,2048]{1,0:T(8,128)(2,1)} %get-tuple-element.190), channel_id=1, source_target_pairs={{0,1},{1,0},{2,3},{3,2},{4,5},{5,4},{6,7},{7,6},{8,9},{9,8},{10,11... | collective-permute-start | bytes 3145736 | tf_op jit(solution)/shard_map/ppermute | solution.py:37
  589.4 20.8 %collective-permute-start.20 = (bf16[256,2048]{1,0:T(8,128)(2,1)}, bf16[256,2048]{1,0:T(8,128)(2,1)S(1)}, u32[]{:S(2)}, u32[]{:S(2)}) collective-permute-start(bf16[256,2048]{1,0:T(8,128)(2,1)} %get-tuple-element.189), channel_id=1, source_target_pairs={{0,2},{1,3},{2,0},{3,1},{4,6},{5,7},{6,4},{7,5},{8,10},{9,11},{10,... | collective-permute-start | bytes 3145736 | tf_op jit(solution)/shard_map/ppermute | solution.py:37
  590.0 15.9 %copy-start.12 = (bf16[512,2048]{1,0:T(8,128)(2,1)S(1)}, bf16[512,2048]{1,0:T(8,128)(2,1)}, u32[]{:S(2)}) copy-start(bf16[512,2048]{1,0:T(8,128)(2,1)} %get-tuple-element.127) | copy-start | bytes 6291460
  592.0 18.2 %copy-start.11 = (bf16[512,2048]{1,0:T(8,128)(2,1)S(1)}, bf16[512,2048]{1,0:T(8,128)(2,1)}, u32[]{:S(2)}) copy-start(bf16[512,2048]{1,0:T(8,128)(2,1)} %get-tuple-element.125) | copy-start | bytes 6291460
  607.5 5.2 copy-start.44
  609.1 42.3 %collective-permute-start.23 = (bf16[512,2048]{1,0:T(8,128)(2,1)}, bf16[512,2048]{1,0:T(8,128)(2,1)}, u32[]{:S(2)}, u32[]{:S(2)}) collective-permute-start(bf16[512,2048]{1,0:T(8,128)(2,1)} %pad_maximum_fusion.7), channel_id=1, source_target_pairs={{0,2},{1,3},{2,0},{3,1},{4,6},{5,7},{6,4},{7,5},{8,10},{9,11},{10,... | collective-permute-start | bytes 6291464 | tf_op jit(solution)/shard_map/ppermute | solution.py:37
  612.1 11.5 %copy-start.24 = (bf16[512,1024]{1,0:T(8,128)(2,1)S(1)}, bf16[512,1024]{1,0:T(8,128)(2,1)}, u32[]{:S(2)}) copy-start(bf16[512,1024]{1,0:T(8,128)(2,1)} %get-tuple-element.145) | copy-start | bytes 3145732
  612.1 11.5 %copy-start.25 = (bf16[512,1024]{1,0:T(8,128)(2,1)S(1)}, bf16[512,1024]{1,0:T(8,128)(2,1)}, u32[]{:S(2)}) copy-start(bf16[512,1024]{1,0:T(8,128)(2,1)} %get-tuple-element.146) | copy-start | bytes 3145732
  612.1 11.5 %copy-start.26 = (bf16[512,1024]{1,0:T(8,128)(2,1)S(1)}, bf16[512,1024]{1,0:T(8,128)(2,1)}, u32[]{:S(2)}) copy-start(bf16[512,1024]{1,0:T(8,128)(2,1)} %get-tuple-element.147) | copy-start | bytes 3145732
  612.1 11.5 %copy-start.27 = (bf16[512,1024]{1,0:T(8,128)(2,1)S(1)}, bf16[512,1024]{1,0:T(8,128)(2,1)}, u32[]{:S(2)}) copy-start(bf16[512,1024]{1,0:T(8,128)(2,1)} %get-tuple-element.148) | copy-start | bytes 3145732
  612.1 39.3 %collective-permute-start.21 = (bf16[512,2048]{1,0:T(8,128)(2,1)}, bf16[512,2048]{1,0:T(8,128)(2,1)}, u32[]{:S(2)}, u32[]{:S(2)}) collective-permute-start(bf16[512,2048]{1,0:T(8,128)(2,1)} %pad_maximum_fusion.6), channel_id=1, source_target_pairs={{0,1},{1,0},{2,3},{3,2},{4,5},{5,4},{6,7},{7,6},{8,9},{9,8},{10,11... | collective-permute-start | bytes 6291464 | tf_op jit(solution)/shard_map/ppermute | solution.py:37
  764.7 5.8 copy-start.17
  768.3 5.2 copy-start.22
  (27 other events, 87.9 us)
Sparse Core Ops, SparseCore 0:
  125.3 45.8 all-gather.3
  172.7 45.9 all-gather.5
  234.7 44.4 all-gather.7
  407.8 46.3 reduce-scatter.6
  494.4 48.0 reduce-scatter.4
  570.8 47.1 reduce-scatter.8
  620.3 48.1 reduce-scatter.10

commit v4 on v2

--- a/solution.py
+++ b/solution.py
@@ -184,6 +184,7 @@
     angles = angle_ref[...]
     info = info_ref[...]
     same = info[:, 0:1] == row_ref[0]
+    scales = []
     for head in range(heads):
         query, key, value = head_parts(field_ref, angles, heads, head)
         columns = slice(head * VAL, (head + 1) * VAL)
@@ -203,7 +204,12 @@
         gated = gate / (1.0 + jnp.exp(-gate)) * grouped
         gated_ref[:, columns] = gated.astype(bf16)
         grouped_ref[:, columns] = grouped.astype(bf16)
-        scale_ref[:, head * 128 : (head + 1) * 128] = jnp.broadcast_to(scale, (CHUNK, 128))
+        scales.append(scale)
+    lane = lax.broadcasted_iota(jnp.int32, (CHUNK, 128), 1)
+    spread = jnp.zeros((CHUNK, 128), f32)
+    for head in range(heads):
+        spread = jnp.where(lane == head, scales[head], spread)
+    scale_ref[...] = spread
 
 
 def retention_backward(heads, which, field_ref, gate_ref, angle_ref, info_ref, row_ref, decay_ref, grad_ref, grouped_ref, scale_ref, past_ref, back_ref, state_ref):
@@ -223,7 +229,7 @@
         into = info[:, 1 + 2 * head : 2 + 2 * head]
         onward = info[:, 2 + 2 * head : 3 + 2 * head]
         grouped = grouped_ref[:, columns].astype(f32)
-        scale = scale_ref[:, head * 128 : head * 128 + 1]
+        scale = scale_ref[:, head : head + 1]
         c = grad_ref[:, columns].astype(f32) * (gate / (1.0 + jnp.exp(-gate)))
         mean_c = jnp.mean(c, axis=-1, keepdims=True)
         mean_cx = jnp.mean(c * grouped, axis=-1, keepdims=True)
@@ -302,15 +308,15 @@
     ]
     past_spec = pl.BlockSpec((1, heads, KEY, VAL), lambda i, w: (step(i), 0, 0, 0))
     if backward:
-        in_specs += [placed(heads * VAL), placed(heads * VAL), placed(heads * 128), past_spec]
+        in_specs += [placed(heads * VAL), placed(heads * VAL), placed(128), past_spec]
         out_specs = placed(heads * QKV)
         out_shape = jax.ShapeDtypeStruct((rows, heads * QKV), bf16)
     else:
-        out_specs = [placed(heads * VAL), placed(heads * VAL), placed(heads * 128), past_spec]
+        out_specs = [placed(heads * VAL), placed(heads * VAL), placed(128), past_spec]
         out_shape = [
             jax.ShapeDtypeStruct((rows, heads * VAL), bf16),
             jax.ShapeDtypeStruct((rows, heads * VAL), bf16),
-            jax.ShapeDtypeStruct((rows, heads * 128), f32),
+            jax.ShapeDtypeStruct((rows, 128), f32),
             jax.ShapeDtypeStruct((chunks, heads, KEY, VAL), bf16),
         ]
     products = 15 if backward else 7
@@ -573,6 +579,676 @@
     return w_qkv, w_gate, normed1_all, cots, (cots[0],)
 
 
+def closing_kernel(
+    heads,
+    normed1_ref, up_ref, down_ref, feed_ref, w_out_ref, w_qkv_ref, w_gate_ref,
+    gate_ref, grouped_ref, gated_ref, scale_ref, field_ref, past_ref, angle_ref, info_ref,
+    low_ref, plus_ref, token_ref, row_ref, decay_ref, gain_ref, late_ref,
+    result_ref, grad_ref, query_out, key_out, value_out, gate_out, out_out, up_out, down_out, sums_ref,
+    big, units, columns, terms, half_in, full_in, products, twin_in, line_in,
+    state_ref, past_in, scale_in, angle_in, info_in, blocks, given, landed, total,
+    unit_sem, column_sem, chunk_sem, block_sem, out_sem, mixed_sem, over_send, over_recv, onward_send, onward_recv,
+    half_send, half_recv, full_send, full_recv, twin_send, twin_recv, line_send, line_recv, sum_send, sum_recv,
+    twin_free, line_free, half_free, full_free,
+):
+    dp = lax.axis_index("dp")
+    tensor = lax.axis_index("tensor")
+    z = lax.div(dp, 2)
+    core = lax.rem(dp, 2)
+    rows = token_ref.shape[0]
+    half = rows // 2
+    width = token_ref.shape[1]
+    unit = units.shape[2]
+    depth = columns.shape[2] // 2
+    at_end = (z == 0) | (z == 3)
+    upper = z >= 2
+    twin = (dp + 1 - 2 * core, tensor)
+    over_x = (dp, tensor + 1 - 2 * lax.rem(tensor, 2))
+    over_y = (dp, lax.rem(tensor + 2, 4))
+    here = dp * 4 + tensor
+    peers = 32
+    last = 5
+
+    def layer(index):
+        return (2 * index + core, tensor)
+
+    def seen(index):
+        return jnp.where(upper, 3 - index, index)
+
+    end = layer(seen(0))
+    near = layer(seen(1))
+    opposite = layer(seen(2))
+    targets = [seen(3), seen(2), jnp.where(at_end, seen(1), seen(0)), z]
+
+    def remote(src, dst, send, recv, device):
+        return pltpu.make_async_remote_copy(
+            src_ref=src, dst_ref=dst, send_sem=send, recv_sem=recv, device_id=device, device_id_type=MESH
+        )
+
+    def block_of(start, count):
+        return pl.ds(pl.multiple_of(start, count), count)
+
+
+    def whole(index, ref, sem):
+        return [pltpu.make_async_copy(ref, units.at[index], unit_sem.at[sem])]
+
+    def folded(index, ref, sem):
+        return [
+            pltpu.make_async_copy(ref.at[:, pl.ds(0, unit)], units.at[index, pl.ds(0, unit)], unit_sem.at[sem]),
+            pltpu.make_async_copy(ref.at[:, pl.ds(unit, unit)], units.at[index, pl.ds(unit, unit)], unit_sem.at[sem + 1]),
+        ]
+
+    def part(index, ref, start, sem):
+        return [pltpu.make_async_copy(ref.at[:, pl.ds(start, unit)], units.at[index], unit_sem.at[sem])]
+
+    def start(copies):
+        for copy in copies:
+            copy.start()
+
+    def wait(copies):
+        for copy in copies:
+            copy.wait()
+
+    out_load = folded(3, w_out_ref, 4)
+    feed_load = [
+        pltpu.make_async_copy(feed_ref.at[pl.ds((i + 1) * rows, rows)], terms.at[i], unit_sem.at[i]) for i in range(3)
+    ]
+    gated_load = whole(2, gated_ref, 6)
+    w_gate_load = whole(3, w_gate_ref, 7)
+    w_value_load = part(2, w_qkv_ref, unit, 8)
+    w_key_load = part(1, w_qkv_ref, 0, 9)
+
+
+    sources = [up_ref, down_ref, normed1_ref, None, normed1_ref, normed1_ref]
+
+    def given_copy(r, k):
+        place = block_of(targets[k] * 2 * depth, 2 * depth)
+        return pltpu.make_async_copy(sources[r].at[place], products.at[r, k], column_sem.at[4 * r + k])
+
+    def column_copy(r, k):
+        place = block_of(targets[k] * 2 * depth, 2 * depth)
+        return pltpu.make_async_copy(sources[r].at[:, place], columns.at[k % 2], column_sem.at[k])
+
+    def prefetch(r):
+        column_copy(r, 0).start()
+        column_copy(r, 1).start()
+
+    mine = block_of(core * depth, depth)
+    theirs = block_of((1 - core) * depth, depth)
+
+    def to_twin(r, k):
+        return remote(
+            products.at[r % 2, k, theirs], twin_in.at[k % 2], twin_send.at[r % 2, k], twin_recv.at[k % 2], twin
+        )
+
+    def along(r, k, slot, device):
+        return remote(
+            products.at[r % 2, k, mine], line_in.at[slot], line_send.at[r % 2, k], line_recv.at[slot], device
+        )
+
+    def send_to_twin(r, k):
+        if r >= 1 or k >= 2:
+            pl.semaphore_wait(twin_free.at[k % 2], 1)
+        to_twin(r, k).start()
+
+    def multiply(r, k):
+        to_twin(r - 2, k).wait_send()
+        if k < 3:
+            along(r - 2, k, 0, end).wait_send()
+        else:
+            wait(outputs(r - 2))
+        if sources[r] is not None:
+            column_copy(r, k).wait()
+
+        @pl.loop(0, unit // 256)
+        def _(j):
+            tile = block_of(j * 256, 256)
+            product = None
+            for place in (pl.ds(0, 2 * rows), pl.ds(2 * rows, 2 * rows)):
+                if r < 4:
+                    right = units[(None, None, 0, 2)[r], place, tile]
+                else:
+                    right = big[place, block_of((r - 4) * unit + j * 256, 256)]
+                if sources[r] is None:
+                    left = big[place, block_of(targets[k] * 2 * depth, 2 * depth)]
+                else:
+                    left = columns[k % 2, place]
+                more = dot_tn(left, right)
+                product = more if product is None else product + more
+            products[r % 2, k, :, tile] = product.astype(bf16)
+
+        if sources[r] is not None and k + 2 < 4:
+            column_copy(r, k + 2).start()
+        send_to_twin(r, k)
+
+    def add_to_mine(r, k, others):
+        @pl.loop(0, depth // 64)
+        def _(i):
+            inner = block_of(core * depth + i * 64, 64)
+            value = products[r % 2, k, inner].astype(f32)
+            for ref, index in others:
+                value = value + ref[index, block_of(i * 64, 64)].astype(f32)
+            products[r % 2, k, inner] = value.astype(bf16)
+
+    def settle(r, k):
+        to_twin(r, k).wait_recv()
+        add_to_mine(r, k, [(twin_in, k % 2)])
+        if r < last or k < 2:
+            pl.semaphore_signal(twin_free.at[k % 2], inc=1, device_id=twin, device_id_type=MESH)
+
+    def push(r, k):
+        @pl.when(at_end)
+        def _():
+            if r >= 1:
+                pl.semaphore_wait(line_free.at[k], 1)
+            along(r, k, k, near).start()
+
+    def line_wait(slot):
+        along(0, 0, slot, end).wait_recv()
+
+    def used(device, index):
+        pl.semaphore_signal(line_free.at[index], inc=1, device_id=device, device_id_type=MESH)
+
+    def pass_on(r, which):
+        arrived, sender, slot, device = ((0, end, 3, opposite), (1, end, 4, opposite), (3, opposite, 0, end))[which]
+
+        @pl.when(jnp.logical_not(at_end))
+        def _():
+            line_wait(arrived)
+            add_to_mine(r, which, [(line_in, arrived)])
+            if r < last:
+                used(sender, (0, 1, 0)[which])
+            if r >= 1:
+                pl.semaphore_wait(line_free.at[which], 1)
+            along(r, which, slot, device).start()
+
+    def outputs(r):
+        keys = heads * KEY
+        slot = products.at[r % 2, 3]
+        if r == 4:
+            return [
+                pltpu.make_async_copy(slot.at[mine, pl.ds(0, keys)], query_out, out_sem.at[0, 0]),
+                pltpu.make_async_copy(slot.at[mine, pl.ds(keys, keys)], key_out, out_sem.at[0, 1]),
+            ]
+        out = (up_out, down_out, gate_out, out_out, None, value_out)[r]
+        return [pltpu.make_async_copy(slot.at[mine], out, out_sem.at[r % 2, 0])]
+
+    def finish(r):
+        @pl.when(at_end)
+        def _():
+            line_wait(0)
+            add_to_mine(r, 3, [(line_in, 0)])
+            if r < last:
+                used(near, 2)
+
+        @pl.when(jnp.logical_not(at_end))
+        def _():
+            line_wait(2)
+            line_wait(4)
+            add_to_mine(r, 3, [(line_in, 2), (line_in, 4)])
+            if r < last:
+                used(end, 2)
+                used(opposite, 1)
+
+        start(outputs(r))
+
+
+    def rows_of(r, first=0, count=rows):
+        return pl.ds(r * rows + first, count)
+
+    over = [
+        remote(big.at[rows_of(0)], big.at[rows_of(1)], over_send.at[0], over_recv.at[0], over_x),
+        remote(big.at[rows_of(0)], big.at[rows_of(2)], over_send.at[1], over_recv.at[1], over_y),
+    ]
+    onward = [
+        remote(big.at[rows_of(2, 0, half)], big.at[rows_of(3, 0, half)], onward_send.at[0], onward_recv.at[0], over_x),
+        remote(big.at[rows_of(1, half, half)], big.at[rows_of(3, half, half)], onward_send.at[1], onward_recv.at[1], over_y),
+    ]
+    halves = [
+        remote(terms.at[2, pl.ds(0, half)], half_in.at[0], half_send.at[0], half_recv.at[0], over_x),
+        remote(terms.at[2, pl.ds(half, half)], half_in.at[1], half_send.at[1], half_recv.at[1], over_y),
+    ]
+    fulls = [
+        remote(terms.at[0], full_in.at[0], full_send.at[0], full_recv.at[0], over_x),
+        remote(terms.at[1], full_in.at[1], full_send.at[1], full_recv.at[1], over_y),
+    ]
+    sides = (over_x, over_y)
+
+    def send_halves(stage):
+        for i, copy in enumerate(halves):
+            if stage == 1:
+                pl.semaphore_wait(half_free.at[i], 1)
+            copy.start()
+
+    def take_halves(stage):
+        for copy in halves:
+            copy.wait_recv()
+        for term, first, slot in ((1, 0, 0), (0, half, 1)):
+            @pl.loop(0, half // 64)
+            def _(i):
+                place = block_of(first + i * 64, 64)
+                grown = terms[term, place].astype(f32) + half_in[slot, block_of(i * 64, 64)].astype(f32)
+                terms[term, place] = grown.astype(bf16)
+
+        for i, copy in enumerate(fulls):
+            if stage == 0:
+                pl.semaphore_signal(half_free.at[i], inc=1, device_id=sides[i], device_id_type=MESH)
+            else:
+                pl.semaphore_wait(full_free.at[i], 1)
+            copy.start()
+
+    def project(r):
+        slot = (2, 0, 1, 2)[r]
+
+        @pl.loop(0, width // 256)
+        def _(j):
+            tile = block_of(j * 256, 256)
+            term = dot_nt(big[rows_of(r), pl.ds(0, unit)], units[1, tile])
+            term = term + dot_nt(big[rows_of(r), pl.ds(unit, unit)], units[2, tile])
+            term = term + dot_nt(units[0, rows_of(r)], units[3, tile])
+            terms[slot, :, tile] = term.astype(bf16)
+
+
+    def gate_copies(r):
+        return [
+            pltpu.make_async_copy(
+                ref.at[rows_of(r), pl.ds(h * VAL, VAL)],
+                columns.at[r % 2, pl.ds((2 * i + h) * rows, rows)],
+                chunk_sem.at[r % 2, 2 * i + h],
+            )
+            for i, ref in enumerate((gate_ref, grouped_ref))
+            for h in range(heads)
+        ]
+
+    def gate_back(r):
+        wait(gate_copies(r))
+
+        @pl.loop(0, unit // 256)
+        def _(j):
+            grad = dot_nt(big[rows_of(r), pl.ds(0, unit)], units[3, block_of(j * 256, 256)])
+            grad = grad + dot_nt(big[rows_of(r), pl.ds(unit, unit)], units[3, block_of(unit + j * 256, 256)])
+            head = lax.div(j, VAL // 256)
+            inner = block_of(lax.rem(j, VAL // 256) * 256, 256)
+            raw = columns[r % 2, block_of(head * rows, rows), inner].astype(f32)
+            grouped = columns[r % 2, block_of((heads + head) * rows, rows), inner].astype(f32)
+            sigmoid = 1.0 / (1.0 + jnp.exp(-raw))
+            tile = block_of(j * 256, 256)
+            units[0, rows_of(r), tile] = (grad * grouped * (sigmoid * (1.0 + raw * (1.0 - sigmoid)))).astype(bf16)
+            units[1, rows_of(r), tile] = grad.astype(bf16)
+
+    chunks = 4 * rows // CHUNK
+    per_piece = rows // CHUNK
+
+    def chunk_place(c):
+        piece = lax.div(c, per_piece)
+        low = lax.rem(lax.rem(piece, 2) + lax.rem(tensor, 2), 2)
+        high = lax.rem(lax.div(piece, 2) + lax.div(tensor, 2), 2)
+        return (2 * high + low) * per_piece + lax.rem(c, per_piece)
+
+    def chunk_copies(c, slot):
+        place = block_of(chunk_place(c) * CHUNK, CHUNK)
+        seat = block_of(c * CHUNK, CHUNK)
+        keys = heads * KEY
+        pieces = [
+            (field_ref.at[place, pl.ds(0, keys)], columns.at[slot, pl.ds(0, CHUNK)]),
+            (field_ref.at[place, pl.ds(keys, keys)], columns.at[slot, pl.ds(CHUNK, CHUNK)]),
+        ]
+        for h in range(heads):
+            pieces.append((field_ref.at[place, pl.ds(2 * keys + h * VAL, VAL)], columns.at[slot, pl.ds((2 + h) * CHUNK, CHUNK)]))
+            pieces.append((gate_ref.at[place, pl.ds(h * VAL, VAL)], columns.at[slot, pl.ds((4 + h) * CHUNK, CHUNK)]))
+            pieces.append((grouped_ref.at[place, pl.ds(h * VAL, VAL)], columns.at[slot, pl.ds((6 + h) * CHUNK, CHUNK)]))
+        pieces += [
+            (past_ref.at[c], past_in.at[slot]),
+            (scale_ref.at[place], scale_in.at[slot]),
+            (angle_ref.at[seat], angle_in.at[slot]),
+            (info_ref.at[seat], info_in.at[slot]),
+        ]
+        return [pltpu.make_async_copy(src, dst, chunk_sem.at[slot, i]) for i, (src, dst) in enumerate(pieces)]
+
+    def retention_steps(between):
+        @pl.loop(0, chunks)
+        def _(step):
+            c = chunks - 1 - step
+            slot = lax.rem(step, 2)
+            wait(chunk_copies(c, slot))
+
+            @pl.when(step + 1 < chunks)
+            def _():
+                start(chunk_copies(c - 1, 1 - slot))
+
+            place = block_of(chunk_place(c) * CHUNK, CHUNK)
+            angles = angle_in[slot]
+            cosine = angles[:, : KEY // 2]
+            sine = angles[:, KEY // 2 :]
+            info = info_in[slot]
+            same = info[:, 0:1] == row_ref[c]
+
+            for head in range(heads):
+                at = pl.ds(head * KEY, KEY)
+                query = turn(columns[slot, pl.ds(0, CHUNK), at].astype(f32), cosine, sine).astype(bf16)
+                key = turn(columns[slot, pl.ds(CHUNK, CHUNK), at].astype(f32), cosine, sine)
+                key = (key * key_scale).astype(bf16)
+                value = columns[slot, pl.ds((2 + head) * CHUNK, CHUNK)]
+                gate = columns[slot, pl.ds((4 + head) * CHUNK, CHUNK)].astype(f32)
+                grouped = columns[slot, pl.ds((6 + head) * CHUNK, CHUNK)].astype(f32)
+                into = info[:, 1 + 2 * head : 2 + 2 * head]
+                onto = info[:, 2 + 2 * head : 3 + 2 * head]
+                scale = scale_in[slot, :, head : head + 1]
+                past = past_in[slot, head]
+                out_grad_in = units[1, place, pl.ds(head * VAL, VAL)].astype(f32)
+                c_in = out_grad_in * (gate / (1.0 + jnp.exp(-gate)))
+                mean_c = jnp.mean(c_in, axis=-1, keepdims=True)
+                mean_cx = jnp.mean(c_in * grouped, axis=-1, keepdims=True)
+                out_grad = (scale * (c_in - mean_c - grouped * mean_cx)).astype(bf16)
+                state = state_ref[head]
+                state_low = state.astype(bf16)
+                masked = jnp.where(same, decay_ref[head], 0.0)
+                weights = (masked * dot_nt(query, key)).astype(bf16)
+                score_grad = (masked * dot_nt(out_grad, value)).astype(bf16)
+                value_grad = dot_tn(weights, out_grad) + onto * dot_nn(key, state_low)
+                query_grad = dot_nn(score_grad, key) + into * dot_nt(out_grad, past)
+                key_grad = dot_tn(score_grad, query) + onto * dot_nt(value, state_low)
+                moved = (query.astype(f32) * into).astype(bf16)
+                state_ref[head] = into[CHUNK - 1 :, :] * state + dot_tn(moved, out_grad)
+                big[place, pl.ds(head * KEY, KEY)] = turn_back(query_grad, cosine, sine).astype(bf16)
+                big[place, pl.ds((heads + head) * KEY, KEY)] = (turn_back(key_grad, cosine, sine) * key_scale).astype(bf16)
+                big[place, pl.ds(2 * heads * KEY + head * VAL, VAL)] = value_grad.astype(bf16)
+
+            between(step)
+
+
+    def block_copy(ref, i, slot):
+        return pltpu.make_async_copy(ref.at[block_of(i * 64, 64)], blocks.at[slot], block_sem.at[slot])
+
+    def stream(ref, use):
+        @pl.loop(0, rows // 64)
+        def _(i):
+            slot = lax.rem(i, 4)
+            block_copy(ref, i, slot).wait()
+            use(block_of(i * 64, 64), blocks[slot])
+
+            @pl.when(i + 4 < rows // 64)
+            def _():
+                block_copy(ref, i + 4, slot).start()
+
+
+    own_load = pltpu.make_async_copy(low_ref, big.at[rows_of(0)], mixed_sem.at[0])
+    own_load.start()
+    for r in range(2):
+        for k in range(4):
+            given_copy(r, k).start()
+    start(out_load)
+    start(gate_copies(0))
+    start(gate_copies(1))
+    start(feed_load)
+
+    barrier = pltpu.get_barrier_semaphore()
+
+    def partner(k):
+        other = lax.rem(here + k, peers)
+        return other, (lax.div(other, 4), lax.rem(other, 4))
+
+    @pl.loop(1, peers)
+    def _(k):
+        pl.semaphore_signal(barrier, inc=1, device_id=partner(k)[1], device_id_type=MESH)
+
+    pl.semaphore_wait(barrier, peers - 1)
+
+    own_load.wait()
+    start(over)
+    for k in range(4):
+        given_copy(0, k).wait()
+        send_to_twin(0, k)
+        if k > 0:
+            settle(0, k - 1)
+            push(0, k - 1)
+    settle(0, 3)
+    for k in range(4):
+        given_copy(1, k).wait()
+        send_to_twin(1, k)
+        if k > 0:
+            settle(1, k - 1)
+    settle(1, 3)
+    wait(out_load)
+    gate_back(0)
+    start(gate_copies(2))
+    pass_on(0, 0)
+    push(1, 0)
+    pass_on(0, 1)
+    push(1, 1)
+    pass_on(0, 2)
+    for copy in over:
+        copy.wait_recv()
+    start(onward)
+    gate_back(1)
+    start(gate_copies(3))
+    finish(0)
+    push(1, 2)
+    gate_back(2)
+    pass_on(1, 0)
+    pass_on(1, 1)
+    wait(feed_load)
+    start(gated_load)
+    for copy in onward:
+        copy.wait_recv()
+    send_halves(0)
+    gate_back(3)
+    prefetch(2)
+    start(w_gate_load)
+    pass_on(1, 2)
+    state_ref[...] = jnp.zeros_like(state_ref)
+
+    def produce(r, k, pushed=True):
+        multiply(r, k)
+        if k > 0:
+            settle(r, k - 1)
+            if pushed:
+                push(r, k - 1)
+
+    produce(2, 0)
+    produce(2, 1)
+    finish(1)
+    produce(2, 2)
+    produce(2, 3)
+    settle(2, 3)
+    start(chunk_copies(chunks - 1, 0))
+    wait(gated_load)
+    produce(3, 0)
+    produce(3, 1, False)
+    take_halves(0)
+    pass_on(2, 0)
+    push(3, 0)
+    produce(3, 2, False)
+    produce(3, 3, False)
+    settle(3, 3)
+    start(w_value_load)
+    for copy in over + onward:
+        copy.wait_send()
+
+    def between(step):
+        @pl.when(step == 1)
+        def _():
+            pass_on(2, 1)
+            push(3, 1)
+
+        @pl.when(step == 2)
+        def _():
+            pass_on(2, 2)
+
+        @pl.when(step == 5)
+        def _():
+            finish(2)
+            push(3, 2)
+
+    retention_steps(between)
+    start(w_key_load)
+    prefetch(4)
+    pass_on(3, 0)
+    for copy in halves:
+        copy.wait_send()
+    wait(w_gate_load)
+    wait(w_value_load)
+    wait(w_key_load)
+    project(3)
+    send_halves(1)
+    for i in range(4):
+        block_copy(plus_ref, i, i).start()
+    produce(4, 0)
+    produce(4, 1)
+    pass_on(3, 1)
+    for copy in fulls:
+        copy.wait_recv()
+
+    def add_result(place, value):
+        full_in[0, place] = (value.astype(f32) + full_in[0, place].astype(f32) + full_in[1, place].astype(f32)).astype(bf16)
+
+    stream(plus_ref, add_result)
+    result_copy = pltpu.make_async_copy(full_in.at[0], result_ref, mixed_sem.at[1])
+    result_copy.start()
+    for copy in fulls:
+        copy.wait_send()
+    pass_on(3, 2)
+    project(1)
+    result_copy.wait()
+    for i, side in enumerate(sides):
+        pl.semaphore_signal(full_free.at[i], inc=1, device_id=side, device_id_type=MESH)
+    project(2)
+    take_halves(1)
+    finish(3)
+    produce(4, 2)
+    produce(4, 3, False)
+    push(4, 2)
+    settle(4, 3)
+    prefetch(5)
+    pass_on(4, 0)
+    produce(5, 0)
+    produce(5, 1)
+    pass_on(4, 1)
+    produce(5, 2)
+    pass_on(4, 2)
+    produce(5, 3, False)
+    settle(5, 3)
+    for copy in halves:
+        copy.wait_send()
+    project(0)
+    finish(4)
+    push(5, 2)
+    pass_on(5, 0)
+    pass_on(5, 1)
+    for copy in fulls:
+        copy.wait_recv()
+        copy.wait_send()
+    last_loads = [
+        pltpu.make_async_copy(token_ref, terms.at[0], mixed_sem.at[2]),
+        pltpu.make_async_copy(low_ref, terms.at[1], mixed_sem.at[0]),
+    ]
+    start(last_loads)
+    total[...] = jnp.zeros_like(total)
+    wait(last_loads)
+
+    @pl.loop(0, rows // 64)
+    def _(i):
+        place = block_of(i * 64, 64)
+        normed_grad = terms[2, place].astype(f32) + full_in[0, place].astype(f32) + full_in[1, place].astype(f32)
+        plain, scale = normalize(terms[0, place].astype(f32))
+        grad = terms[1, place].astype(f32) + normalize_back(normed_grad, plain, scale, gain_ref[...])
+        full_in[0, place] = grad.astype(bf16)
+        total[0:1, :] += jnp.sum(normed_grad * plain, axis=0, keepdims=True)
+        total[1:2, :] += jnp.sum(normed_grad, axis=0, keepdims=True)
+
+    grad_copy = pltpu.make_async_copy(full_in.at[0], grad_ref, mixed_sem.at[3])
+    grad_copy.start()
+
+    total[2:4, :] = late_ref[...]
+    for k in range(peers // 2):
+        given[k] = total[:, k * 128 : (k + 1) * 128]
+
+    def sum_copy(k):
+        other, device = partner(k)
+        return remote(given.at[lax.div(other, 2)], landed.at[k], sum_send.at[k], sum_recv.at[k], device)
+
+    @pl.loop(1, peers)
+    def _(k):
+        sum_copy(k).start()
+
+    pass_on(5, 2)
+    sums_ref[...] = given[lax.div(here, 2)]
+
+    @pl.loop(1, peers)
+    def _(k):
+        sum_copy(k).wait()
+        sums_ref[...] += landed[k]
+
+    finish(5)
+
+    for r in (4, 5):
+        for k in range(4):
+            to_twin(r, k).wait_send()
+            if k < 3:
+                along(r, k, 0, end).wait_send()
+    wait(outputs(4) + outputs(5))
+    grad_copy.wait()
+
+
+def closing_exchange(heads, operands, small):
+    token_rows, width = operands[-1].shape
+    rows = 4 * token_rows
+    depth = width // 8
+    keys, values = heads * KEY, heads * VAL
+    unit = operands[1].shape[1]
+    anywhere = pl.BlockSpec(memory_space=pl.ANY)
+    in_vmem = pl.BlockSpec(memory_space=pltpu.VMEM)
+    sem = pltpu.SemaphoreType.DMA
+    regular = pltpu.SemaphoreType.REGULAR
+    vmem = pltpu.VMEM
+    return pl.pallas_call(
+        functools.partial(closing_kernel, heads),
+        out_shape=[
+            jax.ShapeDtypeStruct((token_rows, width), bf16),
+            jax.ShapeDtypeStruct((token_rows, width), bf16),
+            jax.ShapeDtypeStruct((depth, keys), bf16),
+            jax.ShapeDtypeStruct((depth, keys), bf16),
+            jax.ShapeDtypeStruct((depth, values), bf16),
+            jax.ShapeDtypeStruct((depth, values), bf16),
+            jax.ShapeDtypeStruct((depth, unit), bf16),
+            jax.ShapeDtypeStruct((depth, unit), bf16),
+            jax.ShapeDtypeStruct((depth, unit), bf16),
+            jax.ShapeDtypeStruct((8, 128), f32),
+        ],
+        in_specs=[anywhere] * len(operands) + [in_vmem] * len(small),
+        out_specs=[anywhere] * 9 + [in_vmem],
+        scratch_shapes=[
+            vmem((rows, width), bf16),
+            vmem((4, rows, unit), bf16),
+            vmem((2, rows, 2 * depth), bf16),
+            vmem((3, token_rows, width), bf16),
+            vmem((2, token_rows // 2, width), bf16),
+            vmem((2, token_rows, width), bf16),
+            vmem((2, 4, 2 * depth, unit), bf16),
+            vmem((2, depth, unit), bf16),
+            vmem((5, depth, unit), bf16),
+            vmem((heads, KEY, VAL), f32),
+            vmem((2, heads, KEY, VAL), bf16),
+            vmem((2, CHUNK, 128), f32),
+            vmem((2, CHUNK, KEY), f32),
+            vmem((2, CHUNK, 128), f32),
+            vmem((4, 64, width), bf16),
+            vmem((16, 8, 128), f32),
+            vmem((32, 8, 128), f32),
+            vmem((8, width), f32),
+            sem((10,)), sem((8,)), sem((2, 12)), sem((4,)), sem((2, 2)), sem((4,)),
+            sem((2,)), sem((2,)), sem((2,)), sem((2,)),
+            sem((2,)), sem((2,)), sem((2,)), sem((2,)),
+            sem((2, 4)), sem((2,)), sem((2, 3)), sem((5,)), sem((32,)), sem((32,)),
+            regular((2,)), regular((3,)), regular((2,)), regular((2,)),
+        ],
+        compiler_params=pltpu.CompilerParams(
+            collective_id=3, has_side_effects=True, vmem_limit_bytes=63_400_000
+        ),
+        name="closing_exchange",
+    )(*operands, *small)
+
+
 def body(tokens, cotangent, segment, first_gain, first_bias, query_weight, key_weight, value_weight, gate_weight, out_weight, second_gain, second_bias, up_weight, down_weight):
     devices = lax.axis_size("tensor")
     rows = tokens.shape[0]
@@ -591,7 +1267,6 @@
     w_up = lax.all_gather(after(up_weight, w_down), "dp", axis=0, tiled=True)
 
     token_rows = tokens.astype(f32)
-    unit1, scale1 = normalize(token_rows)
     tables = retention_tables(segment, heads, here * heads)
     field = dot_nn(normed1_all, w_qkv).astype(bf16)
     gate = dot_nn(normed1_all, w_gate).astype(bf16)
@@ -622,54 +1297,74 @@
     gain2_grad = jnp.sum(normed2_grad * unit2, axis=0)
     bias2_grad = jnp.sum(normed2_grad, axis=0)
     mixed_low = mixed_grad.astype(bf16)
-    mixed_pieces = gather_pieces(mixed_low, devices)
-
     hidden_all = jnp.concatenate(after(hidden, *terms), axis=0)
-    down_weight_grad = dot_tn(hidden_all, cot_all).astype(bf16)
-    down_sum = lax.psum_scatter(down_weight_grad, "dp", scatter_dimension=1, tiled=True).astype(f32)
-    normed2_all = jnp.concatenate(after(normed2_pieces, mixed_low), axis=0)
-    up_weight_grad = dot_tn(normed2_all, jnp.concatenate(up_grad, axis=0)).astype(bf16)
-    up_sum = lax.psum_scatter(up_weight_grad, "dp", scatter_dimension=0, tiled=True).astype(f32)
-    ffn_terms = per_piece(dot_nn(after(hidden_all, mixed_low), w_down).astype(bf16))
-
-    gated_grad, gate_grad = [], []
-    for piece, unit, raw in zip(mixed_pieces, per_piece(grouped), per_piece(gate)):
-        grad = dot_nt(after(piece, *ffn_terms), w_out)
-        raw = raw.astype(f32)
+    normed2_all = jnp.concatenate(after(normed2_pieces, *terms), axis=0)
+    up_grad_all = jnp.concatenate(after(up_grad, *terms), axis=0)
+    feed_terms = dot_nn(hidden_all, w_down).astype(bf16)
+    own_term = feed_terms[:rows].astype(f32)
+    up_weight_grad = dot_tn(normed2_all, up_grad_all).astype(bf16)
+    down_weight_grad = dot_tn(cot_all, hidden_all).astype(bf16)
+    angles, info, keys, decay = tables
+
+    if devices == 4 and lax.axis_size("dp") == 8:
+        result, input_grad, query_sum, key_sum, value_sum, gate_sum, out_sum, up_sum, down_sum, sums = closing_exchange(
+            heads,
+            (
+                normed1_all, up_weight_grad, down_weight_grad, feed_terms, w_out, w_qkv, w_gate,
+                gate, grouped, gated, group_scale, field, past, angles, info,
+                mixed_low, (mixed + own_term).astype(bf16), tokens,
+            ),
+            (keys, decay, first_gain.reshape(1, -1), jnp.stack([gain2_grad, bias2_grad])),
+        )
+        part = first_gain.shape[0] // 32
+        sums = lax.dynamic_slice_in_dim(sums, (here % 2) * part, part, 1)
+        norm_sums = [sums[0], sums[1], sums[2], sums[3]]
+        query_sum, key_sum, value_sum, gate_sum, up_sum = (
+            v.astype(f32) for v in (query_sum, key_sum, value_sum, gate_sum, up_sum)
+        )
+        out_sum, down_sum = out_sum.astype(f32).T, down_sum.astype(f32).T
+    else:
+        def summed(gradient, dimension):
+            return lax.psum_scatter(
+                gradient.astype(bf16), "dp", scatter_dimension=dimension, tiled=True
+            ).astype(f32)
+
+        up_sum = summed(up_weight_grad, 0)
+        down_sum = summed(down_weight_grad, 0).T
+        mixed_all = jnp.concatenate(gather_pieces(mixed_low, devices), axis=0)
+        ffn, _, _ = scatter_sum([term.astype(f32) for term in per_piece(feed_terms)])
+        result = (mixed + ffn).astype(bf16)
+        gated_grad = dot_nt(mixed_all, w_out)
+        raw = gate.astype(f32)
         sigmoid = 1.0 / (1.0 + jnp.exp(-raw))
-        both = after((
-            grad.astype(bf16),
-            (grad * unit.astype(f32) * (sigmoid * (1.0 + raw * (1.0 - sigmoid)))).astype(bf16),
-        ))
-        gated_grad.append(both[0])
-        gate_grad.append(both[1])
-    gate_weight_grad = dot_tn(normed1_all, jnp.concatenate(gate_grad, axis=0)).astype(bf16)
-    gate_sum = lax.psum_scatter(gate_weight_grad, "dp", scatter_dimension=0, tiled=True).astype(f32)
-    ffn, ffn_begun, ffn_done = scatter_sum([term.astype(f32) for term in after(ffn_terms, mixed_pieces[3])])
-    result = (mixed + ffn).astype(bf16)
-    out_weight_grad = dot_tn(gated, jnp.concatenate(after(mixed_pieces, gate_weight_grad), axis=0)).astype(bf16)
-    out_sum = lax.psum_scatter(out_weight_grad, "dp", scatter_dimension=1, tiled=True).astype(f32)
-    back = retention_call(
-        True, which, rows, heads, field, gate, tables,
-        (jnp.concatenate(after(gated_grad, out_weight_grad, *ffn_begun), axis=0), grouped, group_scale, past),
-    )
-    terms = [dot_nt(first, w_qkv) + dot_nt(second, w_gate) for first, second in zip(per_piece(back), gate_grad)]
-    normed1_grad, begun, _ = scatter_sum(terms)
-    qkv_weight_grad = dot_tn(normed1_all, after(back, terms[-1], *ffn_done, up_sum, down_sum)).astype(bf16)
-    qkv_sum = lax.psum_scatter(qkv_weight_grad, "dp", scatter_dimension=0, tiled=True)
-    input_grad = mixed_grad + normalize_back(normed1_grad, unit1, scale1, first_gain)
-    gain1_grad = jnp.sum(normed1_grad * unit1, axis=0)
-    bias1_grad = jnp.sum(normed1_grad, axis=0)
-    norm_sums = spread_sum([gain1_grad, bias1_grad, gain2_grad, bias2_grad])
-    keys_end = heads * KEY
+        gate_grad = (gated_grad * grouped.astype(f32) * (sigmoid * (1.0 + raw * (1.0 - sigmoid)))).astype(bf16)
+        back = retention_call(
+            True, which, rows, heads, field, gate, tables, (gated_grad.astype(bf16), grouped, group_scale, past)
+        )
+        gate_sum = summed(dot_tn(normed1_all, gate_grad), 0)
+        out_sum = summed(dot_tn(gated, mixed_all), 1)
+        qkv_sum = summed(dot_tn(normed1_all, back), 0)
+        keys_end = heads * KEY
+        query_sum = qkv_sum[:, :keys_end]
+        key_sum = qkv_sum[:, keys_end : 2 * keys_end]
+        value_sum = qkv_sum[:, 2 * keys_end :]
+        terms = [
+            dot_nt(first, w_qkv) + dot_nt(second, w_gate) for first, second in zip(per_piece(back), per_piece(gate_grad))
+        ]
+        normed1_grad, _, _ = scatter_sum(terms)
+        unit1, scale1 = normalize(token_rows)
+        input_grad = (mixed_grad + normalize_back(normed1_grad, unit1, scale1, first_gain)).astype(bf16)
+        gain1_grad = jnp.sum(normed1_grad * unit1, axis=0)
+        bias1_grad = jnp.sum(normed1_grad, axis=0)
+        norm_sums = spread_sum([gain1_grad, bias1_grad, gain2_grad, bias2_grad])
     return (
         result,
-        input_grad.astype(bf16),
+        input_grad,
         norm_sums[0],
         norm_sums[1],
-        qkv_sum[:, :keys_end].astype(f32),
-        qkv_sum[:, keys_end : 2 * keys_end].astype(f32),
-        qkv_sum[:, 2 * keys_end :].astype(f32),
+        query_sum,
+        key_sum,
+        value_sum,
         gate_sum,
         out_sum,
         norm_sums[2],

time: 792 us -> 762 us (0.962)
  Pallas kernels: 161 us -> 377 us
  matrix products: 266 us -> 136 us
  waiting for transfers between devices: 216 us -> 139 us
  other arithmetic: 64.8 us -> 35.8 us
    pallas_call x1, Pallas kernels: 9.82 us -> 247 us  [closing_exchange(): pl.pallas_call(functools.partial(closing_kernel, heads), out_shape=[jax.S...]
    dot_general x17 -> x5, matrix products: 110 us -> 22.8 us  [dot_nt(): lax.dot_general(left, right, (((1,), (1,)), ((), ())), preferred_element_...]
    ppermute x28 -> x16, waiting for transfers between devices: 212 us -> 133 us  [tensor_permute(): return lax.ppermute(values, 'tensor', pairs)]
    dot_general x5 -> x2, matrix products: 74.1 us -> 26.2 us  [dot_tn(): lax.dot_general(left, right, (((0,), (0,)), ((), ())), preferred_element_...]
    pallas_call x2 -> x1, Pallas kernels: 37.9 us -> 16.5 us  [retention_call(): pl.pallas_call(functools.partial(retention_backward if backward else rete...]
    convert_element_type x9 -> x6, other arithmetic: 27.3 us -> 12.7 us  [the longest x5 9.06 us: body(): v.astype(f32)]
    ppermute x28 -> x16, starting transfers between devices: 24.9 us -> 18.3 us  [tensor_permute(): return lax.ppermute(values, 'tensor', pairs)]
    unnamed x155 -> x86, local copies, waits for them, and re-layouts: 12.9 us -> 18.3 us
  transfers between devices with their start and end apart: 36 -> 19, of which waited for: 18 -> 11; matrix products, arithmetic and copies ran while one was open for 42% -> 19% of each run, Pallas kernels for 6% -> 2%
where the time goes in v4:
time: 762 us; the launch traced here: 754 us
  Pallas kernels  377 us (49%)
  waiting for transfers between devices  139 us (18%)
  matrix products  136 us (18%)
  other arithmetic  35.8 us (5%)
  local copies, waits for them, and re-layouts  31.4 us (4%)
  starting transfers between devices  18.6 us (2%)
  between operations  15.4 us (2%)
    pallas_call x1, Pallas kernels, closing_exchange(): pl.pallas_call(functools.partial(closing_kernel, heads), out_shape=[jax.S...  247 us
    ppermute x16, waiting for transfers between devices, tensor_permute(): return lax.ppermute(values, 'tensor', pairs)  133 us
    pallas_call x1, Pallas kernels, opening_exchange(): pl.pallas_call(opening_kernel, out_shape=[jax.ShapeDtypeStruct((dp * dept...  114 us
    dot_general x11, matrix products, dot_nn(): lax.dot_general(left, right, (((1,), (0,)), ((), ())), preferred_element_...  87.4 us
    dot_general x2, matrix products, dot_tn(): lax.dot_general(left, right, (((0,), (0,)), ((), ())), preferred_element_...  26.2 us
    dot_general x5, matrix products, dot_nt(): lax.dot_general(left, right, (((1,), (1,)), ((), ())), preferred_element_...  22.8 us
    unnamed x86, local copies, waits for them, and re-layouts  18.3 us
    ppermute x16, starting transfers between devices, tensor_permute(): return lax.ppermute(values, 'tensor', pairs)  18.3 us
  transfers between devices with their start and end apart: 19, of which 11 were waited for; matrix products, arithmetic and copies ran while one was open for 19% of the time, Pallas kernels for 2%

profile of v4, /device:TPU:0, one launch (start us, length us, event | category | flops | bytes accessed | tf_op | source)
XLA Modules:
  0.0 753.9 jit_solution(8370419377134760603)
XLA Ops:
  7.2 113.5 %opening_exchange.1 = (bf16[2048,2048]{1,0:T(8,128)(2,1)}, bf16[2048,1024]{1,0:T(8,128)(2,1)}, bf16[2048,2048]{1,0:T(8,128)(2,1)}, bf16[2,256,2048]{2,1,0:T(8,128)(2,1)}) custom-call(bf16[256,512]{1,0:T(8,128)(2,1)} %query_ref.1, bf16[256,512]{1,0:T(8,128)(2,1)} %key_ref.1, bf16[256,1024]{1,0:T(8,128)(2,1)} %value_ref.1, bf16[256,1024]{1,0:T(8,128)(2,1)} %gate_ref.1, ...), custom_call_target="tpu_custom_call" | custom-call | tf_op jit(solution)/shard_map/opening_exchange/pallas_call | solution.py:526
  121.9 1.5 collective-permute-start
  123.4 1.9 collective-permute-start.1
  125.3 3.1 slice_bitcast_fusion
  131.3 14.0 %convolution_convert_fusion.3.gate_ref = bf16[2048,1024]{1,0:T(8,128)(2,1)} fusion(bf16[2048,2048]{1,0:T(8,128)(2,1)} %get-tuple-element.68.normed1_ref, bf16[2048,1024]{1,0:T(8,128)(2,1)} %get-tuple-element.70.w_gate_ref), kind=kOutput, calls=%fused_computation.28 | convolution fusion | flops 8592031744 | bytes 16777216 | tf_op jit(solution)/shard_map/dot_general | solution.py:24
  145.2 23.6 %convolution_convert_fusion.1.field_ref = bf16[2048,2048]{1,0:T(8,128)(2,1)} fusion(bf16[2048,2048]{1,0:T(8,128)(2,1)} %get-tuple-element.68.normed1_ref, bf16[2048,2048]{1,0:T(8,128)(2,1)} %get-tuple-element.69.w_qkv_ref), kind=kOutput, calls=%fused_computation.9 | convolution fusion | flops 17184063488 | bytes 25165824 | tf_op jit(solution)/shard_map/dot_general | solution.py:24
  169.0 6.3 all-gather.4.cloned.1.call-done.w_out_ref
  178.2 1.6 collective-permute-start.3
  179.8 4.3 multiply_cosine_fusion
  184.3 16.5 %retention_forward.1 = (bf16[2048,1024]{1,0:T(8,128)(2,1)}, bf16[2048,1024]{1,0:T(8,128)(2,1)}, f32[2048,128]{1,0:T(8,128)S(1)}, bf16[8,2,256,512]{3,2,1,0:T(8,128)(2,1)}) custom-call(s32[1]{0:T(128)} %bitcast.2.which, bf16[2048,2048]{1,0:T(8,128)(2,1)} %convolution_convert_fusion.1.field_ref, bf16[2048,1024]{1,0:T(8,128)(2,1)} %convolution_convert_fusion.3.gate_ref, ...), custom_call_target="tpu_custom_call" | custom-call | flops 3758096384 | bytes 25165824 | tf_op jit(solution)/shard_map/retention_forward/pallas_call | solution.py:323
  200.9 2.9 collective-permute-done.3
  203.8 4.0 convolution_convert_fusion.5
  208.1 1.6 collective-permute-start.6
  209.7 1.5 collective-permute-start.4
  211.2 2.4 fusion.56
  213.5 2.4 fusion.59
  216.2 16.5 %collective-permute-done.6 = bf16[256,2048]{1,0:T(8,128)(2,1)S(1)} collective-permute-done((bf16[256,2048]{1,0:T(8,128)(2,1)S(1)}, bf16[256,2048]{1,0:T(8,128)(2,1)S(1)}, u32[]{:S(2)}, u32[]{:S(2)}) %collective-permute-start.6) | collective-permute-done | bytes 1048608 | tf_op jit(solution)/shard_map/ppermute | solution.py:37
  233.1 1.6 pad_maximum_fusion.2
  234.6 1.5 collective-permute-start.7
  236.4 1.6 pad_maximum_fusion.1
  238.0 1.5 collective-permute-start.5
  239.5 41.6 %collective-permute-done.7 = bf16[512,2048]{1,0:T(8,128)(2,1)} collective-permute-done((bf16[512,2048]{1,0:T(8,128)(2,1)}, bf16[512,2048]{1,0:T(8,128)(2,1)}, u32[]{:S(2)}, u32[]{:S(2)}) %collective-permute-start.7) | collective-permute-done | bytes 2097184 | tf_op jit(solution)/shard_map/ppermute | solution.py:37
  281.1 3.1 collective-permute-done.5
  284.2 7.3 fusion.74
  292.3 2.1 add_convert_fusion.2
  294.9 1.5 collective-permute-start.8
  296.6 1.4 constant_dynamic-update-slice_fusion.4
  298.0 1.3 constant_dynamic-update-slice_fusion.3
  299.3 1.3 constant_dynamic-update-slice_fusion.2
  300.6 1.4 constant_dynamic-update-slice_fusion.1
  302.2 37.4 %collective-permute-done.9 = bf16[512,2048]{1,0:T(8,128)(2,1)} collective-permute-done((bf16[512,2048]{1,0:T(8,128)(2,1)}, bf16[512,2048]{1,0:T(8,128)(2,1)}, u32[]{:S(2)}, u32[]{:S(2)}) %collective-permute-start.9) | collective-permute-done | bytes 2097184 | tf_op jit(solution)/shard_map/ppermute | solution.py:37
  339.6 2.3 slice.175
  341.9 1.3 slice.176
  343.2 10.7 %convolution_convert_fusion.2 = bf16[2048,1024]{1,0:T(8,128)(2,1)} fusion(bf16[2048,2048]{1,0:T(8,128)(2,1)S(1)} %constant_dynamic-update-slice_fusion, bf16[1024,2048]{1,0:T(8,128)(2,1)S(1)} %copy-done.24), kind=kOutput, calls=%fused_computation.27 | convolution fusion | flops 8592031744 | bytes 16777216 | tf_op jit(solution)/shard_map/dot_general | solution.py:28
  353.9 5.3 fusion.77
  359.3 4.1 fusion.75
  363.4 8.4 %fusion.43 = (bf16[512,1024]{1,0:T(8,128)(2,1)S(1)}, bf16[512,1024]{1,0:T(8,128)(2,1)S(1)}, bf16[512,1024]{1,0:T(8,128)(2,1)S(1)}, bf16[512,1024]{1,0:T(8,128)(2...) fusion(bf16[2048,1024]{1,0:T(8,128)(2,1)S(1)} %copy-done.30, f32[512,1024]{1,0:T(8,128)S(1)} %fusion.77, ...), kind=kOutput, calls=%fused_computation.63 | convolution fusion | flops 2182086656 | bytes 19922944 | tf_op jit(solution)/shard_map/dot_general | solution.py:24
  371.9 1.5 collective-permute-start.10
  374.0 2.4 fusion.78
  376.4 2.4 fusion.79
  379.1 2.4 fusion.76
  381.5 12.0 %collective-permute-done.10 = bf16[256,2048]{1,0:T(8,128)(2,1)S(1)} collective-permute-done((bf16[256,2048]{1,0:T(8,128)(2,1)S(1)}, bf16[256,2048]{1,0:T(8,128)(2,1)S(1)}, u32[]{:S(2)}, u32[]{:S(2)}) %collective-permute-start.10) | collective-permute-done | bytes 1048608 | tf_op jit(solution)/shard_map/ppermute | solution.py:37
  393.6 1.1 collective-permute-done.11
  394.8 3.7 fusion.51
  398.5 5.0 fusion.80
  409.6 12.5 %convolution_convert_fusion.4.down_ref = bf16[2048,1024]{1,0:T(8,128)(2,1)} fusion(bf16[2048,2048]{1,0:T(8,128)(2,1)S(1)} %bitcast.76, bf16[2048,1024]{1,0:T(8,128)(2,1)} %constant_dynamic-update-slice_fusion.9), kind=kOutput, calls=%fused_computation.29 | convolution fusion | flops 8592031744 | bytes 16777216 | tf_op jit(solution)/shard_map/dot_general | solution.py:32
  422.1 3.1 collective-permute-done.14
  425.5 1.6 pad_maximum_fusion.4
  427.9 1.5 pad_maximum_fusion.3
  429.4 1.2 collective-permute-start.13
  430.6 13.7 %fusion.15.up_ref = bf16[2048,1024]{1,0:T(8,128)(2,1)} fusion(bf16[512,1024]{1,0:T(8,128)(2,1)} %copy-done.31, bf16[512,1024]{1,0:T(8,128)(2,1)S(1)} %copy-done.27, bf16[512,1024]{1,0:T(8,128)(2,1)} %copy-done.28, bf16[512,1024]{1,0:T(8,128)(2,1)} %copy-done.29, bf16[512,2048]{1,0:T(8,128)(2,1)} %copy-done.19, ...), kind=kOutput, calls=%fused_computation.26 | convolution fusion | flops 8642363392 | bytes 16777216 | tf_op jit(solution)/shard_map/dot_general | solution.py:32
  444.3 12.2 %convolution_convert_fusion.feed_ref = bf16[2048,2048]{1,0:T(8,128)(2,1)S(1)} fusion(bf16[2048,1024]{1,0:T(8,128)(2,1)} %constant_dynamic-update-slice_fusion.9, bf16[1024,2048]{1,0:T(8,128)(2,1)} %all-gather.6.cloned.1.call-done), kind=kOutput, calls=%fused_computation.8 | convolution fusion | flops 8594128896 | bytes 16777216 | tf_op jit(solution)/shard_map/dot_general | solution.py:24
  456.6 14.0 %collective-permute-done.15 = bf16[512,2048]{1,0:T(8,128)(2,1)} collective-permute-done((bf16[512,2048]{1,0:T(8,128)(2,1)}, bf16[512,2048]{1,0:T(8,128)(2,1)}, u32[]{:S(2)}, u32[]{:S(2)}) %collective-permute-start.15) | collective-permute-done | bytes 2097184 | tf_op jit(solution)/shard_map/ppermute | solution.py:37
  471.4 4.3 multiply_reduce_fusion
  476.3 3.7 add_convert_fusion
  480.0 247.3 %closing_exchange.1 = (bf16[512,2048]{1,0:T(8,128)(2,1)}, bf16[512,2048]{1,0:T(8,128)(2,1)}, bf16[256,512]{1,0:T(8,128)(2,1)}, bf16[256,512]{1,0:T(8,128)(2,1)},...) custom-call(bf16[2048,2048]{1,0:T(8,128)(2,1)} %get-tuple-element.68, ...), custom_call_target="tpu_custom_call" | custom-call | tf_op jit(solution)/shard_map/closing_exchange/pallas_call | solution.py:1204
  728.7 1.9 convert_element_type.204
  730.5 1.8 convert_element_type.205
  732.3 2.2 convert_element_type.206
  734.5 2.1 convert_element_type.207
  736.8 1.3 copy.44
  739.3 1.3 copy.45
  740.6 3.2 copy.60
  743.7 3.2 copy.61
  (149 shorter events, 21.7 us)
Async XLA Ops:
  7.2 113.6 %copy-start.7 = (bf16[512,2048]{1,0:T(8,128)(2,1)S(1)}, bf16[512,2048]{1,0:T(8,128)(2,1)}, u32[]{:S(2)}) copy-start(bf16[512,2048]{1,0:T(8,128)(2,1)} %cot_ref.1) | copy-start | bytes 6291460
  7.2 168.1 %all-gather.4.cloned.1.call-start = ((), (), s32[]{:S(2)}) async-start(), calls=%async_computation | async-start | bytes 4718592 | tf_op jit(solution)/shard_map/all_gather | solution.py:1265
  120.8 7.9 %copy-start.20 = (s32[2048]{0:T(1024)S(1)}, s32[2048]{0:T(1024)}, u32[]{:S(2)}) copy-start(s32[2048]{0:T(1024)} %param.16) | copy-start | bytes 24580
  121.9 56.3 %collective-permute-start = (bf16[256,2048]{1,0:T(8,128)(2,1)}, bf16[256,2048]{1,0:T(8,128)(2,1)}, u32[]{:S(2)}, u32[]{:S(2)}) collective-permute-start(bf16[256,2048]{1,0:T(8,128)(2,1)} %slice.126), channel_id=1, source_target_pairs={{0,1},{1,0},{2,3},{3,2},{4,5},{5,4},{6,7},{7,6},{8,9},{9,8},{10,11... | collective-permute-start | bytes 3145736 | tf_op jit(solution)/shard_map/ppermute | solution.py:37
  123.4 60.9 %collective-permute-start.1 = (bf16[256,2048]{1,0:T(8,128)(2,1)}, bf16[256,2048]{1,0:T(8,128)(2,1)}, u32[]{:S(2)}, u32[]{:S(2)}) collective-permute-start(bf16[256,2048]{1,0:T(8,128)(2,1)} %slice.126), channel_id=1, source_target_pairs={{0,2},{1,3},{2,0},{3,1},{4,6},{5,7},{6,4},{7,5},{8,10},{9,11},{10,... | collective-permute-start | bytes 3145736 | tf_op jit(solution)/shard_map/ppermute | solution.py:37
  128.4 72.5 %collective-permute-start.2 = (bf16[256,2048]{1,0:T(8,128)(2,1)}, bf16[256,2048]{1,0:T(8,128)(2,1)}, u32[]{:S(2)}, u32[]{:S(2)}) collective-permute-start(bf16[256,2048]{1,0:T(8,128)(2,1)} %get-tuple-element.82), channel_id=1, source_target_pairs={{0,1},{1,0},{2,3},{3,2},{4,5},{5,4},{6,7},{7,6},{8,9},{9,8},{10,11... | collective-permute-start | bytes 3145736 | tf_op jit(solution)/shard_map/ppermute | solution.py:37
  128.6 110.9 %all-gather.6.cloned.1.call-start = ((), (), s32[]{:S(2)}) async-start(), calls=%async_computation.1 | async-start | bytes 4718592 | tf_op jit(solution)/shard_map/all_gather | solution.py:1266
  129.9 1.4 copy-start.23
  175.3 178.7 %all-gather.8.cloned.1.call-start = ((), (), s32[]{:S(2)}) async-start(), calls=%async_computation.2 | async-start | bytes 4718592 | tf_op jit(solution)/shard_map/all_gather | solution.py:1267
  176.3 8.0 %copy-start.4 = (f32[2048]{0:T(1024)}, f32[2048]{0:T(1024)S(1)}, u32[]{:S(2)}) copy-start(f32[2048]{0:T(1024)S(1)} %get-tuple-element.202) | copy-start | bytes 24580
  177.3 23.5 %copy-start.1 = (f32[2048,128]{1,0:T(8,128)}, f32[2048,128]{1,0:T(8,128)S(1)}, u32[]{:S(2)}) copy-start(f32[2048,128]{1,0:T(8,128)S(1)} %pad.4.info_ref) | copy-start | bytes 3145732
  178.2 22.7 %copy-start.2 = (f32[2,256,256]{2,1,0:T(8,128)}, f32[2,256,256]{2,1,0:T(8,128)S(1)}, u32[]{:S(2)}) copy-start(f32[2,256,256]{2,1,0:T(8,128)S(1)} %exponential_select_fusion.decay_ref) | copy-start | bytes 1572868
  178.2 25.6 %collective-permute-start.3 = (bf16[256,2048]{1,0:T(8,128)(2,1)}, bf16[256,2048]{1,0:T(8,128)(2,1)S(1)}, u32[]{:S(2)}, u32[]{:S(2)}) collective-permute-start(bf16[256,2048]{1,0:T(8,128)(2,1)} %collective-permute-done), channel_id=1, source_target_pairs={{0,2},{1,3},{2,0},{3,1},{4,6},{5,7},{6,4},{7,5},{8,10},{9,11},{10,... | collective-permute-start | bytes 3145736 | tf_op jit(solution)/shard_map/ppermute | solution.py:37
  184.3 16.6 %copy-start = (f32[2048,256]{1,0:T(8,128)}, f32[2048,256]{1,0:T(8,128)S(1)}, u32[]{:S(2)}) copy-start(f32[2048,256]{1,0:T(8,128)S(1)} %pad_maximum_fusion.angle_ref) | copy-start | bytes 6291460
  184.3 19.5 %copy-start.9 = (bf16[1024,2048]{1,0:T(8,128)(2,1)S(1)}, bf16[1024,2048]{1,0:T(8,128)(2,1)}, u32[]{:S(2)}) copy-start(bf16[1024,2048]{1,0:T(8,128)(2,1)} %all-gather.4.cloned.1.call-done.w_out_ref) | copy-start | bytes 12582916
  200.9 6.9 copy-start.3
  203.8 4.0 copy-start.12
  207.8 3.3 copy-start.10
  208.1 24.7 %collective-permute-start.6 = (bf16[256,2048]{1,0:T(8,128)(2,1)S(1)}, bf16[256,2048]{1,0:T(8,128)(2,1)S(1)}, u32[]{:S(2)}, u32[]{:S(2)}) collective-permute-start(bf16[256,2048]{1,0:T(8,128)(2,1)S(1)} %get-tuple-element.197), channel_id=1, source_target_pairs={{0,1},{1,0},{2,3},{3,2},{4,5},{5,4},{6,7},{7,6},{8,9},{9,8},{10,11... | collective-permute-start | bytes 3145736 | tf_op jit(solution)/shard_map/ppermute | solution.py:37
  209.7 26.5 %collective-permute-start.4 = (bf16[256,2048]{1,0:T(8,128)(2,1)S(1)}, bf16[256,2048]{1,0:T(8,128)(2,1)S(1)}, u32[]{:S(2)}, u32[]{:S(2)}) collective-permute-start(bf16[256,2048]{1,0:T(8,128)(2,1)S(1)} %get-tuple-element.196), channel_id=1, source_target_pairs={{0,2},{1,3},{2,0},{3,1},{4,6},{5,7},{6,4},{7,5},{8,10},{9,11},{10,... | collective-permute-start | bytes 3145736 | tf_op jit(solution)/shard_map/ppermute | solution.py:37
  234.6 46.5 %collective-permute-start.7 = (bf16[512,2048]{1,0:T(8,128)(2,1)}, bf16[512,2048]{1,0:T(8,128)(2,1)}, u32[]{:S(2)}, u32[]{:S(2)}) collective-permute-start(bf16[512,2048]{1,0:T(8,128)(2,1)} %pad_maximum_fusion.2), channel_id=1, source_target_pairs={{0,2},{1,3},{2,0},{3,1},{4,6},{5,7},{6,4},{7,5},{8,10},{9,11},{10,... | collective-permute-start | bytes 6291464 | tf_op jit(solution)/shard_map/ppermute | solution.py:37
  238.0 46.2 %collective-permute-start.5 = (bf16[512,2048]{1,0:T(8,128)(2,1)}, bf16[512,2048]{1,0:T(8,128)(2,1)}, u32[]{:S(2)}, u32[]{:S(2)}) collective-permute-start(bf16[512,2048]{1,0:T(8,128)(2,1)} %pad_maximum_fusion.1), channel_id=1, source_target_pairs={{0,1},{1,0},{2,3},{3,2},{4,5},{5,4},{6,7},{7,6},{8,9},{9,8},{10,11... | collective-permute-start | bytes 6291464 | tf_op jit(solution)/shard_map/ppermute | solution.py:37
  291.5 2.9 copy-start.5
  291.5 0.7 copy-start.21
  291.5 0.8 copy-start.22
  292.3 4.2 copy-start.11
  294.3 45.3 %collective-permute-start.9 = (bf16[512,2048]{1,0:T(8,128)(2,1)}, bf16[512,2048]{1,0:T(8,128)(2,1)}, u32[]{:S(2)}, u32[]{:S(2)}) collective-permute-start(bf16[512,2048]{1,0:T(8,128)(2,1)} %add_convert_fusion.2), channel_id=1, source_target_pairs={{0,2},{1,3},{2,0},{3,1},{4,6},{5,7},{6,4},{7,5},{8,10},{9,11},{10,... | collective-permute-start | bytes 6291464 | tf_op jit(solution)/shard_map/ppermute | solution.py:37
  294.9 47.0 %collective-permute-start.8 = (bf16[512,2048]{1,0:T(8,128)(2,1)}, bf16[512,2048]{1,0:T(8,128)(2,1)}, u32[]{:S(2)}, u32[]{:S(2)}) collective-permute-start(bf16[512,2048]{1,0:T(8,128)(2,1)} %add_convert_fusion.2), channel_id=1, source_target_pairs={{0,1},{1,0},{2,3},{3,2},{4,5},{5,4},{6,7},{7,6},{8,9},{9,8},{10,11... | collective-permute-start | bytes 6291464 | tf_op jit(solution)/shard_map/ppermute | solution.py:37
  296.6 5.5 copy-start.13
  300.6 42.6 %copy-start.24 = (bf16[1024,2048]{1,0:T(8,128)(2,1)S(1)}, bf16[1024,2048]{1,0:T(8,128)(2,1)}, u32[]{:S(2)}) copy-start(bf16[1024,2048]{1,0:T(8,128)(2,1)} %all-gather.6.cloned.1.call-done) | copy-start | bytes 12582916
  302.2 41.0 %copy-start.18 = (bf16[2048,2048]{1,0:T(8,128)(2,1)}, bf16[2048,2048]{1,0:T(8,128)(2,1)S(1)}, u32[]{:S(2)}) copy-start(bf16[2048,2048]{1,0:T(8,128)(2,1)S(1)} %constant_dynamic-update-slice_fusion) | copy-start | bytes 25165828
  353.9 5.3 copy-start.25
  359.3 4.1 copy-start.30
  363.4 8.5 %copy-start.14 = (bf16[256,2048]{1,0:T(8,128)(2,1)S(1)}, bf16[256,2048]{1,0:T(8,128)(2,1)}, u32[]{:S(2)}) copy-start(bf16[256,2048]{1,0:T(8,128)(2,1)} %slice.175) | copy-start | bytes 3145732
  371.8 4.5 copy-start.26
  371.8 4.5 copy-start.28
  371.8 7.2 copy-start.29
  371.9 21.6 %collective-permute-start.10 = (bf16[256,2048]{1,0:T(8,128)(2,1)S(1)}, bf16[256,2048]{1,0:T(8,128)(2,1)S(1)}, u32[]{:S(2)}, u32[]{:S(2)}) collective-permute-start(bf16[256,2048]{1,0:T(8,128)(2,1)S(1)} %copy-done.14), channel_id=1, source_target_pairs={{0,1},{1,0},{2,3},{3,2},{4,5},{5,4},{6,7},{7,6},{8,9},{9,8},{10,11... | collective-permute-start | bytes 3145736 | tf_op jit(solution)/shard_map/ppermute | solution.py:37
  373.4 21.3 %collective-permute-start.11 = (bf16[256,2048]{1,0:T(8,128)(2,1)S(1)}, bf16[256,2048]{1,0:T(8,128)(2,1)S(1)}, u32[]{:S(2)}, u32[]{:S(2)}) collective-permute-start(bf16[256,2048]{1,0:T(8,128)(2,1)S(1)} %slice.176), channel_id=1, source_target_pairs={{0,2},{1,3},{2,0},{3,1},{4,6},{5,7},{6,4},{7,5},{8,10},{9,11},{10,... | collective-permute-start | bytes 3145736 | tf_op jit(solution)/shard_map/ppermute | solution.py:37
  394.8 3.7 copy-start.19
  398.5 5.0 copy-start.31
  398.5 11.1 %slice-start = ((s8[8388608]{0:T(1024)(128)(4,1)}), s8[4194304]{0:T(1024)(128)(4,1)S(1)}, s32[]{:S(2)}) async-start(s8[8388608]{0:T(1024)(128)(4,1)} %bitcast.75), calls=%async_computation.3 | async-start | bytes 8388608
  398.5 11.1 %slice-start.1 = ((s8[8388608]{0:T(1024)(128)(4,1)}), s8[4194304]{0:T(1024)(128)(4,1)S(1)}, s32[]{:S(2)}) async-start(s8[8388608]{0:T(1024)(128)(4,1)} %bitcast.75), calls=%async_computation.4 | async-start | bytes 8388608
  404.8 20.4 %collective-permute-start.14 = (bf16[256,2048]{1,0:T(8,128)(2,1)S(1)}, bf16[256,2048]{1,0:T(8,128)(2,1)S(1)}, u32[]{:S(2)}, u32[]{:S(2)}) collective-permute-start(bf16[256,2048]{1,0:T(8,128)(2,1)S(1)} %get-tuple-element.192), channel_id=1, source_target_pairs={{0,1},{1,0},{2,3},{3,2},{4,5},{5,4},{6,7},{7,6},{8,9},{9,8},{10,11... | collective-permute-start | bytes 3145736 | tf_op jit(solution)/shard_map/ppermute | solution.py:37
  405.4 22.2 %collective-permute-start.12 = (bf16[256,2048]{1,0:T(8,128)(2,1)S(1)}, bf16[256,2048]{1,0:T(8,128)(2,1)S(1)}, u32[]{:S(2)}, u32[]{:S(2)}) collective-permute-start(bf16[256,2048]{1,0:T(8,128)(2,1)S(1)} %get-tuple-element.191), channel_id=1, source_target_pairs={{0,2},{1,3},{2,0},{3,1},{4,6},{5,7},{6,4},{7,5},{8,10},{9,11},{10,... | collective-permute-start | bytes 3145736 | tf_op jit(solution)/shard_map/ppermute | solution.py:37
  427.0 3.6 copy-start.27
  427.0 43.6 %collective-permute-start.15 = (bf16[512,2048]{1,0:T(8,128)(2,1)}, bf16[512,2048]{1,0:T(8,128)(2,1)}, u32[]{:S(2)}, u32[]{:S(2)}) collective-permute-start(bf16[512,2048]{1,0:T(8,128)(2,1)} %pad_maximum_fusion.4), channel_id=1, source_target_pairs={{0,2},{1,3},{2,0},{3,1},{4,6},{5,7},{6,4},{7,5},{8,10},{9,11},{10,... | collective-permute-start | bytes 6291464 | tf_op jit(solution)/shard_map/ppermute | solution.py:37
  429.4 41.9 %collective-permute-start.13 = (bf16[512,2048]{1,0:T(8,128)(2,1)}, bf16[512,2048]{1,0:T(8,128)(2,1)}, u32[]{:S(2)}, u32[]{:S(2)}) collective-permute-start(bf16[512,2048]{1,0:T(8,128)(2,1)} %pad_maximum_fusion.3), channel_id=1, source_target_pairs={{0,1},{1,0},{2,3},{3,2},{4,5},{5,4},{6,7},{7,6},{8,9},{9,8},{10,11... | collective-permute-start | bytes 6291464 | tf_op jit(solution)/shard_map/ppermute | solution.py:37
  444.3 27.0 %copy-start.6 = (f32[512,2048]{1,0:T(8,128)S(1)}, f32[512,2048]{1,0:T(8,128)}, u32[]{:S(2)}) copy-start(f32[512,2048]{1,0:T(8,128)} %copy-done.5) | copy-start | bytes 12582916
  456.6 19.7 %copy-start.8 = (bf16[2048,2048]{1,0:T(8,128)(2,1)}, bf16[2048,2048]{1,0:T(8,128)(2,1)S(1)}, u32[]{:S(2)}) copy-start(bf16[2048,2048]{1,0:T(8,128)(2,1)S(1)} %convolution_convert_fusion.feed_ref) | copy-start | bytes 25165828
  727.3 9.3 %copy-start.17 = (bf16[256,1024]{1,0:T(8,128)(2,1)S(1)}, bf16[256,1024]{1,0:T(8,128)(2,1)}, u32[]{:S(2)}) copy-start(bf16[256,1024]{1,0:T(8,128)(2,1)} %get-tuple-element.120) | copy-start | bytes 1572868
  728.7 9.4 %copy-start.16 = (bf16[256,1024]{1,0:T(8,128)(2,1)S(1)}, bf16[256,1024]{1,0:T(8,128)(2,1)}, u32[]{:S(2)}) copy-start(bf16[256,1024]{1,0:T(8,128)(2,1)} %get-tuple-element.121) | copy-start | bytes 1572868
  732.3 6.8 copy-start.15
Sparse Core Ops, SparseCore 0:
  128.7 46.4 all-gather.3
  176.8 46.0 all-gather.5
  239.6 43.5 all-gather.7

commit v5 on v4

--- a/solution.py
+++ b/solution.py
@@ -577,6 +577,394 @@
     normed1_all = jnp.concatenate(gather_pieces((unit * gain + bias).astype(bf16), devices), axis=0)
     cots = gather_pieces(cotangent, devices)
     return w_qkv, w_gate, normed1_all, cots, (cots[0],)
+
+
+def middle_kernel(
+    gated_ref, w_out_ref, up_ref, down_ref, cot_ref, token_ref, gain_ref, bias_ref,
+    low_ref, plus_ref, feed_ref, up_grad_out, down_grad_out, late_ref,
+    big, units, columns, staged, terms, half_in, full_in, mixed, plus, total,
+    load_sem, column_sem, staged_sem, feed_sem, out_sem, up_send, up_recv, below_send, below_recv, core_send, core_recv,
+    row_send, row_recv, half_send, half_recv, full_send, full_recv, half_free, full_free, big_free,
+):
+    dp = lax.axis_index("dp")
+    tensor = lax.axis_index("tensor")
+    z = lax.div(dp, 2)
+    layers = 4
+    rows = token_ref.shape[0]
+    half = rows // 2
+    width = token_ref.shape[1]
+    unit = units.shape[2]
+    depth = up_ref.shape[0]
+    above = (dp + 2, tensor)
+    below = (dp - 2, tensor)
+    twin = (dp + 1 - 2 * lax.rem(dp, 2), tensor)
+    over_x = (dp, tensor + 1 - 2 * lax.rem(tensor, 2))
+    over_y = (dp, lax.rem(tensor + 2, 4))
+    sides = (over_x, over_y)
+
+    def block_of(start, count):
+        return pl.ds(pl.multiple_of(start, count), count)
+
+    def start(copies):
+        for copy in copies:
+            copy.start()
+
+    def wait(copies):
+        for copy in copies:
+            copy.wait()
+
+    def remote(src, dst, send, recv, device):
+        return pltpu.make_async_remote_copy(
+            src_ref=src, dst_ref=dst, send_sem=send, recv_sem=recv, device_id=device, device_id_type=MESH
+        )
+
+    mine = block_of(dp * depth, depth)
+    shard_loads = [
+        pltpu.make_async_copy(down_ref, units.at[3, mine], load_sem.at[0]),
+        pltpu.make_async_copy(up_ref, units.at[2, mine], load_sem.at[1]),
+    ]
+    first_loads = [
+        pltpu.make_async_copy(gated_ref, units.at[0], load_sem.at[2]),
+        pltpu.make_async_copy(w_out_ref.at[:, pl.ds(0, unit)], units.at[1, pl.ds(0, unit)], load_sem.at[3]),
+        pltpu.make_async_copy(w_out_ref.at[:, pl.ds(unit, unit)], units.at[1, pl.ds(unit, unit)], load_sem.at[4]),
+    ]
+    token_load = pltpu.make_async_copy(token_ref, plus, load_sem.at[5])
+    cot_load = pltpu.make_async_copy(cot_ref, big, load_sem.at[6])
+    start(shard_loads)
+    start(first_loads)
+    token_load.start()
+    cot_load.start()
+
+    barrier = pltpu.get_barrier_semaphore()
+
+    def greet(device):
+        pl.semaphore_signal(barrier, inc=1, device_id=device, device_id_type=MESH)
+
+    for device in (twin, over_x, over_y):
+        greet(device)
+    pl.when(z < layers - 1)(lambda: greet(above))
+    pl.when(z > 0)(lambda: greet(below))
+    pl.semaphore_wait(barrier, 3 + (z < layers - 1).astype(jnp.int32) + (z > 0).astype(jnp.int32))
+
+
+    def shard_copy(a, shard, send_sem, recv_sem, index, device):
+        place = block_of(shard * depth, depth)
+        ref = units.at[3 - a, place]
+        return remote(ref, ref, send_sem.at[a, index], recv_sem.at[a, index], device)
+
+    def rise(a, j):
+        return shard_copy(a, dp - 2 * j, up_send, up_recv, j, above)
+
+    def sink(a, j):
+        return shard_copy(a, dp + 2 * j, below_send, below_recv, j, below)
+
+    def to_twin(a, j):
+        return shard_copy(a, dp + 2 * j, core_send, core_recv, j + 3, twin)
+
+    def from_twin(a, j):
+        return shard_copy(a, twin[0] + 2 * j, core_send, core_recv, j + 3, twin)
+
+    def first_step(a):
+        shard_loads[a].wait()
+        pl.when(z < layers - 1)(lambda: rise(a, 0).start())
+        pl.when(z > 0)(lambda: sink(a, 0).start())
+        to_twin(a, 0).start()
+
+    def step(a, j):
+        @pl.when(z - j >= 0)
+        def _():
+            shard_copy(a, dp - 2 * j, up_send, up_recv, j - 1, twin).wait_recv()
+            if j < 3:
+                pl.when(z < layers - 1)(lambda: rise(a, j).start())
+            to_twin(a, -j).start()
+
+        @pl.when(z + j < layers)
+        def _():
+            shard_copy(a, dp + 2 * j, below_send, below_recv, j - 1, twin).wait_recv()
+            if j < 3:
+                pl.when(z > 0)(lambda: sink(a, j).start())
+            to_twin(a, j).start()
+
+    def gathered(a):
+        for j in range(-3, 4):
+            @pl.when((z + j >= 0) & (z + j < layers))
+            def _():
+                from_twin(a, j).wait_recv()
+
+
+    def rows_of(r, first=0, count=rows):
+        return pl.ds(r * rows + first, count)
+
+    halves = [
+        remote(terms.at[2, pl.ds(0, half)], half_in.at[0], half_send.at[0], half_recv.at[0], over_x),
+        remote(terms.at[2, pl.ds(half, half)], half_in.at[1], half_send.at[1], half_recv.at[1], over_y),
+    ]
+    fulls = [
+        remote(terms.at[0], full_in.at[0], full_send.at[0], full_recv.at[0], over_x),
+        remote(terms.at[1], full_in.at[1], full_send.at[1], full_recv.at[1], over_y),
+    ]
+    lower, upper = (0, half), (half, half)
+
+    def row_copy(index, source, first, target, device):
+        return remote(
+            big.at[rows_of(source, *first)], big.at[rows_of(target, *first)],
+            row_send.at[index], row_recv.at[index], device,
+        )
+
+    early = [row_copy(0, 0, lower, 1, over_x), row_copy(1, 0, upper, 2, over_y)]
+    across = [row_copy(2, 2, upper, 3, over_x), row_copy(3, 1, lower, 3, over_y)]
+    late = [row_copy(4, 0, upper, 1, over_x), row_copy(5, 0, lower, 2, over_y)]
+
+    def send_halves(stage):
+        for i, copy in enumerate(halves):
+            if stage == 1:
+                pl.semaphore_wait(half_free.at[i], 1)
+            copy.start()
+
+    def take_halves(stage):
+        for copy in halves:
+            copy.wait_recv()
+        for term, first, slot in ((1, 0, 0), (0, half, 1)):
+            @pl.loop(0, half // 64)
+            def _(i):
+                place = block_of(first + i * 64, 64)
+                grown = terms[term, place].astype(f32) + half_in[slot, block_of(i * 64, 64)].astype(f32)
+                terms[term, place] = grown.astype(bf16)
+
+        for i, copy in enumerate(fulls):
+            if stage == 0:
+                pl.semaphore_signal(half_free.at[i], inc=1, device_id=sides[i], device_id_type=MESH)
+            else:
+                pl.semaphore_wait(full_free.at[i], 1)
+            copy.start()
+
+    def slot_of(r):
+        return (3, 0, 1, 2)[r]
+
+    def branch_term(r):
+        @pl.loop(0, width // 256)
+        def _(j):
+            top = lax.div(j, unit // 256) * unit
+            inner = block_of(lax.rem(j, unit // 256) * 256, 256)
+            term = dot_nn(units[0, rows_of(r)], units[1, pl.ds(pl.multiple_of(top, unit), unit), inner])
+            terms[slot_of(r), :, block_of(j * 256, 256)] = term.astype(bf16)
+
+    def feed_grads():
+        @pl.loop(0, unit // 256)
+        def _(j):
+            tile = block_of(j * 256, 256)
+            for r in range(4):
+                units[4, rows_of(r), tile] = dot_nn(big[rows_of(r)], units[3, :, tile]).astype(bf16)
+
+    def feed(r):
+        @pl.loop(0, unit // 256)
+        def _(j):
+            tile = block_of(j * 256, 256)
+            value, slope = gelu_both(dot_nn(big[rows_of(r)], units[2, :, tile]))
+            units[0, rows_of(r), tile] = value.astype(bf16)
+            units[1, rows_of(r), tile] = (units[4, rows_of(r), tile].astype(f32) * slope).astype(bf16)
+
+    def back_term(r):
+        @pl.loop(0, width // 256)
+        def _(j):
+            tile = block_of(j * 256, 256)
+            terms[slot_of(r), :, tile] = dot_nt(units[1, rows_of(r)], units[2, tile]).astype(bf16)
+
+
+    first_step(0)
+    wait(first_loads)
+    branch_term(3)
+    send_halves(0)
+    step(0, 1)
+    branch_term(1)
+    branch_term(2)
+    step(0, 2)
+    first_step(1)
+    take_halves(0)
+    branch_term(0)
+    step(0, 3)
+    cot_load.wait()
+    gathered(0)
+    feed_grads()
+    for side in sides:
+        pl.semaphore_signal(big_free, inc=1, device_id=side, device_id_type=MESH)
+    step(1, 1)
+    step(1, 2)
+    step(1, 3)
+    gathered(1)
+    token_load.wait()
+    for copy in fulls:
+        copy.wait_recv()
+
+    @pl.loop(0, rows // 64)
+    def _(i):
+        place = block_of(i * 64, 64)
+        value = plus[place].astype(f32) + terms[3, place].astype(f32)
+        value = value + full_in[0, place].astype(f32) + full_in[1, place].astype(f32)
+        mixed[place] = value
+        plain, _ = normalize(value)
+        big[place] = (plain * gain_ref[...] + bias_ref[...]).astype(bf16)
+
+    for i, side in enumerate(sides):
+        pl.semaphore_signal(full_free.at[i], inc=1, device_id=side, device_id_type=MESH)
+    pl.semaphore_wait(big_free, 2)
+    start(early)
+    feed(0)
+    for copy in halves + fulls:
+        copy.wait_send()
+    back_term(0)
+    for copy in early:
+        copy.wait_recv()
+    start(across)
+    start(late)
+
+    def cot_columns(t):
+        return pltpu.make_async_copy(cot_ref.at[:, pl.ds(t * 512, 512)], columns.at[t % 2], column_sem.at[t])
+
+    cot_columns(0).start()
+    cot_columns(1).start()
+    for copy in across:
+        copy.wait_recv()
+    feed(3)
+    back_term(3)
+    send_halves(1)
+    for copy in late:
+        copy.wait_recv()
+    feed(1)
+    feed(2)
+    back_term(1)
+    back_term(2)
+    take_halves(1)
+
+    def staged_out(out, t, slot):
+        return pltpu.make_async_copy(staged.at[slot], out.at[pl.ds(t * 512, 512)], staged_sem.at[slot])
+
+    def weight_grad(out, t, left_of, right):
+        for j in range(unit // 256):
+            tile = pl.ds(j * 256, 256)
+            product = None
+            for place in (pl.ds(0, 2 * rows), pl.ds(2 * rows, 2 * rows)):
+                more = dot_tn(left_of(place), units[right, place, tile])
+                product = more if product is None else product + more
+            staged[t % 2, :, tile] = product.astype(bf16)
+        staged_out(out, t, t % 2).start()
+
+    for t in range(4):
+        cot_columns(t).wait()
+        if t >= 2:
+            staged_out(down_grad_out, t - 2, t % 2).wait()
+        weight_grad(down_grad_out, t, lambda place: columns[t % 2, place], 0)
+        if t < 2:
+            cot_columns(t + 2).start()
+    for t in range(4):
+        if t < 2:
+            staged_out(down_grad_out, t + 2, t % 2).wait()
+        else:
+            staged_out(up_grad_out, t - 2, t % 2).wait()
+        weight_grad(up_grad_out, t, lambda place: big[place, pl.ds(t * 512, 512)], 1)
+
+    def feed_out(t):
+        return pltpu.make_async_copy(columns.at[t % 2], feed_ref.at[:, pl.ds(t * 512, 512)], feed_sem.at[t % 2])
+
+    for t in range(4):
+        if t >= 2:
+            feed_out(t - 2).wait()
+
+        @pl.loop(0, 4)
+        def _(r):
+            place = block_of(r * rows, rows)
+            columns[t % 2, place] = dot_nt(units[0, place], units[3, pl.ds(t * 512, 512)]).astype(bf16)
+
+        feed_out(t).start()
+
+        @pl.loop(0, rows // 64)
+        def _(i):
+            place = block_of(i * 64, 64)
+            tile = pl.ds(t * 512, 512)
+            plus[place, tile] = (mixed[place, tile] + columns[t % 2, place].astype(f32)).astype(bf16)
+
+    plus_out = pltpu.make_async_copy(plus, plus_ref, out_sem.at[0])
+    plus_out.start()
+    for copy in halves:
+        copy.wait_send()
+    cot_own = pltpu.make_async_copy(cot_ref.at[pl.ds(0, rows)], terms.at[2], load_sem.at[7])
+    cot_own.start()
+    total[...] = jnp.zeros_like(total)
+    cot_own.wait()
+    for copy in fulls:
+        copy.wait_recv()
+
+    @pl.loop(0, rows // 64)
+    def _(i):
+        place = block_of(i * 64, 64)
+        grad = terms[3, place].astype(f32) + full_in[0, place].astype(f32) + full_in[1, place].astype(f32)
+        plain, scale = normalize(mixed[place])
+        back = terms[2, place].astype(f32) + normalize_back(grad, plain, scale, gain_ref[...])
+        full_in[0, place] = back.astype(bf16)
+        total[0:1, :] += jnp.sum(grad * plain, axis=0, keepdims=True)
+        total[1:2, :] += jnp.sum(grad, axis=0, keepdims=True)
+
+    low_out = pltpu.make_async_copy(full_in.at[0], low_ref, out_sem.at[1])
+    low_out.start()
+    late_ref[...] = total[...]
+
+    for t in (2, 3):
+        staged_out(up_grad_out, t, t % 2).wait()
+        feed_out(t).wait()
+    for copy in fulls + early + across + late:
+        copy.wait_send()
+    for a in range(2):
+        for j in range(3):
+            pl.when((z < layers - 1) & (z - j >= 0))(lambda: rise(a, j).wait_send())
+            pl.when((z > 0) & (z + j < layers))(lambda: sink(a, j).wait_send())
+        for j in range(-3, 4):
+            pl.when((z + j >= 0) & (z + j < layers))(lambda: to_twin(a, j).wait_send())
+    plus_out.wait()
+    low_out.wait()
+
+
+def middle_exchange(gated, w_out, up_shard, down_shard, cot_all, tokens, gain, bias):
+    token_rows, width = tokens.shape
+    rows = 4 * token_rows
+    unit = gated.shape[1]
+    anywhere = pl.BlockSpec(memory_space=pl.ANY)
+    in_vmem = pl.BlockSpec(memory_space=pltpu.VMEM)
+    sem = pltpu.SemaphoreType.DMA
+    regular = pltpu.SemaphoreType.REGULAR
+    vmem = pltpu.VMEM
+    return pl.pallas_call(
+        middle_kernel,
+        out_shape=[
+            jax.ShapeDtypeStruct((token_rows, width), bf16),
+            jax.ShapeDtypeStruct((token_rows, width), bf16),
+            jax.ShapeDtypeStruct((rows, width), bf16),
+            jax.ShapeDtypeStruct((width, unit), bf16),
+            jax.ShapeDtypeStruct((width, unit), bf16),
+            jax.ShapeDtypeStruct((2, width), f32),
+        ],
+        in_specs=[anywhere] * 6 + [in_vmem] * 2,
+        out_specs=[anywhere] * 5 + [in_vmem],
+        scratch_shapes=[
+            vmem((rows, width), bf16),
+            vmem((5, rows, unit), bf16),
+            vmem((2, rows, 512), bf16),
+            vmem((2, 512, unit), bf16),
+            vmem((4, token_rows, width), bf16),
+            vmem((2, token_rows // 2, width), bf16),
+            vmem((2, token_rows, width), bf16),
+            vmem((token_rows, width), f32),
+            vmem((token_rows, width), bf16),
+            vmem((2, width), f32),
+            sem((8,)), sem((4,)), sem((2,)), sem((2,)), sem((2,)),
+            sem((2, 3)), sem((2, 3)), sem((2, 3)), sem((2, 3)), sem((2, 7)), sem((2, 7)),
+            sem((6,)), sem((6,)), sem((2,)), sem((2,)), sem((2,)), sem((2,)),
+            regular((2,)), regular((2,)), regular,
+        ],
+        compiler_params=pltpu.CompilerParams(
+            collective_id=4, has_side_effects=True, vmem_limit_bytes=63_400_000
+        ),
+        name="middle_exchange",
+    )(gated, w_out, up_shard, down_shard, cot_all, tokens, gain.reshape(1, width), bias.reshape(1, width))
 
 
 def closing_kernel(
@@ -1263,58 +1651,29 @@
         query_weight, key_weight, value_weight, gate_weight, tokens, first_gain, first_bias, cotangent, devices
     )
     w_out = lax.all_gather(after(out_weight, w_gate), "dp", axis=1, tiled=True)
-    w_down = lax.all_gather(after(down_weight, w_out), "dp", axis=1, tiled=True)
-    w_up = lax.all_gather(after(up_weight, w_down), "dp", axis=0, tiled=True)
-
     token_rows = tokens.astype(f32)
+    down_shard = down_weight.T
     tables = retention_tables(segment, heads, here * heads)
     field = dot_nn(normed1_all, w_qkv).astype(bf16)
     gate = dot_nn(normed1_all, w_gate).astype(bf16)
     gated, grouped, group_scale, past = retention_call(
         False, which, rows, heads, field, after(gate, *cot_begun), tables, ()
     )
-    branch, begun, _ = scatter_sum([dot_nn(piece, w_out) for piece in per_piece(after(gated, *cots))])
-
-    mixed = token_rows + branch
-    unit2, scale2 = normalize(mixed)
-    normed2 = (unit2 * second_gain + second_bias).astype(bf16)
-    cot_all = jnp.concatenate(after(cots, *begun), axis=0)
-    hidden_grads = per_piece(dot_nt(cot_all, after(w_down, normed2)).astype(bf16))
-
-    def feed(piece, hidden_grad):
-        value, slope = gelu_both(dot_nn(piece, w_up))
-        return after((value.astype(bf16), (hidden_grad.astype(f32) * slope).astype(bf16)))
-
-    fed_own = feed(normed2, hidden_grads[0])
-    normed2_pieces = gather_pieces(normed2, devices, fed_own)
-    fed = [fed_own] + [feed(piece, grad) for piece, grad in zip(normed2_pieces[1:-1], hidden_grads[1:-1])]
-    fed.append(feed(after(normed2_pieces[-1], *fed), hidden_grads[-1]))
-    hidden = [f[0] for f in fed]
-    up_grad = [f[1] for f in fed]
-    terms = [dot_nt(piece, w_up) for piece in up_grad]
-    normed2_grad, _, _ = scatter_sum(terms)
-    mixed_grad = cotangent.astype(f32) + normalize_back(normed2_grad, unit2, scale2, second_gain)
-    gain2_grad = jnp.sum(normed2_grad * unit2, axis=0)
-    bias2_grad = jnp.sum(normed2_grad, axis=0)
-    mixed_low = mixed_grad.astype(bf16)
-    hidden_all = jnp.concatenate(after(hidden, *terms), axis=0)
-    normed2_all = jnp.concatenate(after(normed2_pieces, *terms), axis=0)
-    up_grad_all = jnp.concatenate(after(up_grad, *terms), axis=0)
-    feed_terms = dot_nn(hidden_all, w_down).astype(bf16)
-    own_term = feed_terms[:rows].astype(f32)
-    up_weight_grad = dot_tn(normed2_all, up_grad_all).astype(bf16)
-    down_weight_grad = dot_tn(cot_all, hidden_all).astype(bf16)
+    cot_all = jnp.concatenate(cots, axis=0)
     angles, info, keys, decay = tables
 
     if devices == 4 and lax.axis_size("dp") == 8:
+        mixed_low, plus, feed_terms, up_weight_grad, down_weight_grad, late = middle_exchange(
+            gated, w_out, up_weight, down_shard, cot_all, tokens, second_gain, second_bias
+        )
         result, input_grad, query_sum, key_sum, value_sum, gate_sum, out_sum, up_sum, down_sum, sums = closing_exchange(
             heads,
             (
                 normed1_all, up_weight_grad, down_weight_grad, feed_terms, w_out, w_qkv, w_gate,
                 gate, grouped, gated, group_scale, field, past, angles, info,
-                mixed_low, (mixed + own_term).astype(bf16), tokens,
+                mixed_low, plus, tokens,
             ),
-            (keys, decay, first_gain.reshape(1, -1), jnp.stack([gain2_grad, bias2_grad])),
+            (keys, decay, first_gain.reshape(1, -1), late),
         )
         part = first_gain.shape[0] // 32
         sums = lax.dynamic_slice_in_dim(sums, (here % 2) * part, part, 1)
@@ -1324,6 +1683,39 @@
         )
         out_sum, down_sum = out_sum.astype(f32).T, down_sum.astype(f32).T
     else:
+        w_down = lax.all_gather(after(down_weight, w_out), "dp", axis=1, tiled=True)
+        w_up = lax.all_gather(after(up_weight, w_down), "dp", axis=0, tiled=True)
+        branch, begun, _ = scatter_sum([dot_nn(piece, w_out) for piece in per_piece(after(gated, *cots))])
+
+        mixed = token_rows + branch
+        unit2, scale2 = normalize(mixed)
+        normed2 = (unit2 * second_gain + second_bias).astype(bf16)
+        hidden_grads = per_piece(dot_nt(cot_all, after(w_down, normed2)).astype(bf16))
+
+        def feed(piece, hidden_grad):
+            value, slope = gelu_both(dot_nn(piece, w_up))
+            return after((value.astype(bf16), (hidden_grad.astype(f32) * slope).astype(bf16)))
+
+        fed_own = feed(normed2, hidden_grads[0])
+        normed2_pieces = gather_pieces(normed2, devices, fed_own)
+        fed = [fed_own] + [feed(piece, grad) for piece, grad in zip(normed2_pieces[1:-1], hidden_grads[1:-1])]
+        fed.append(feed(after(normed2_pieces[-1], *fed), hidden_grads[-1]))
+        hidden = [f[0] for f in fed]
+        up_grad = [f[1] for f in fed]
+        terms = [dot_nt(piece, w_up) for piece in up_grad]
+        normed2_grad, _, _ = scatter_sum(terms)
+        mixed_grad = cotangent.astype(f32) + normalize_back(normed2_grad, unit2, scale2, second_gain)
+        gain2_grad = jnp.sum(normed2_grad * unit2, axis=0)
+        bias2_grad = jnp.sum(normed2_grad, axis=0)
+        mixed_low = mixed_grad.astype(bf16)
+        hidden_all = jnp.concatenate(after(hidden, *terms), axis=0)
+        normed2_all = jnp.concatenate(after(normed2_pieces, *terms), axis=0)
+        up_grad_all = jnp.concatenate(after(up_grad, *terms), axis=0)
+        feed_terms = dot_nn(hidden_all, w_down).astype(bf16)
+        own_term = feed_terms[:rows].astype(f32)
+        up_weight_grad = dot_tn(normed2_all, up_grad_all).astype(bf16)
+        down_weight_grad = dot_tn(cot_all, hidden_all).astype(bf16)
+
         def summed(gradient, dimension):
             return lax.psum_scatter(
                 gradient.astype(bf16), "dp", scatter_dimension=dimension, tiled=True

time: 762 us -> 726 us (0.953)
  Pallas kernels: 377 us -> 610 us
  waiting for transfers between devices: 139 us -> 0.03 us
  matrix products: 136 us -> 39 us
  other arithmetic: 35.8 us -> 17 us
  starting transfers between devices: 18.6 us -> 4.35 us
    pallas_call x0 -> x1, Pallas kernels: none -> 229 us  [middle_exchange(): pl.pallas_call(middle_kernel, out_shape=[jax.ShapeDtypeStruct((token_rows...]
    ppermute x16 -> x4, waiting for transfers between devices: 133 us -> 0.01 us  [tensor_permute(): return lax.ppermute(values, 'tensor', pairs)]
    dot_general x7 -> x0, matrix products: 49 us -> none  [the longest x2 26.2 us: dot_tn(): lax.dot_general(left, right, (((0,), (0,)), ((), ())), preferred_element_...]
    dot_general x11 -> x2, matrix products: 87.4 us -> 39 us  [dot_nn(): lax.dot_general(left, right, (((1,), (0,)), ((), ())), preferred_element_...]
    ppermute x16 -> x4, starting transfers between devices: 18.3 us -> 4.31 us  [tensor_permute(): return lax.ppermute(values, 'tensor', pairs)]
    unnamed x86 -> x37, local copies, waits for them, and re-layouts: 18.3 us -> 24 us
  transfers between devices with their start and end apart: 19 -> 5, of which waited for: 11 -> 0; matrix products, arithmetic and copies ran while one was open for 19% -> 9% of each run, Pallas kernels for 2% -> 2%
where the time goes in v5:
time: 726 us; the launch traced here: 718 us
  Pallas kernels  610 us (84%)
  matrix products  39 us (5%)
  local copies, waits for them, and re-layouts  32.7 us (5%)
  other arithmetic  17 us (2%)
  between operations  14.8 us (2%)
    pallas_call x1, Pallas kernels, closing_exchange(): pl.pallas_call(functools.partial(closing_kernel, heads), out_shape=[jax.S...  253 us
    pallas_call x1, Pallas kernels, middle_exchange(): pl.pallas_call(middle_kernel, out_shape=[jax.ShapeDtypeStruct((token_rows...  229 us
    pallas_call x1, Pallas kernels, opening_exchange(): pl.pallas_call(opening_kernel, out_shape=[jax.ShapeDtypeStruct((dp * dept...  113 us
    dot_general x2, matrix products, dot_nn(): lax.dot_general(left, right, (((1,), (0,)), ((), ())), preferred_element_...  39 us
    unnamed x37, local copies, waits for them, and re-layouts  24 us
    pallas_call x1, Pallas kernels, retention_call(): pl.pallas_call(functools.partial(retention_backward if backward else rete...  15.4 us
  transfers between devices with their start and end apart: 5, of which 0 were waited for; matrix products, arithmetic and copies ran while one was open for 9% of the time, Pallas kernels for 2%

profile of v5, /device:TPU:0, one launch (start us, length us, event | category | flops | bytes accessed | tf_op | source)
XLA Modules:
  0.0 718.1 jit_solution(13202223236523440125)
XLA Ops:
  7.2 0.0 copy-start.5
  7.2 0.0 all-gather.2.cloned.1.call-start
  7.2 113.4 %opening_exchange.1 = (bf16[2048,2048]{1,0:T(8,128)(2,1)}, bf16[2048,1024]{1,0:T(8,128)(2,1)}, bf16[2048,2048]{1,0:T(8,128)(2,1)}, bf16[2,256,2048]{2,1,0:T(8,128)(2,1)}) custom-call(bf16[256,512]{1,0:T(8,128)(2,1)} %query_ref.1, bf16[256,512]{1,0:T(8,128)(2,1)} %key_ref.1, bf16[256,1024]{1,0:T(8,128)(2,1)} %value_ref.1, bf16[256,1024]{1,0:T(8,128)(2,1)} %gate_ref.1, ...), custom_call_target="tpu_custom_call" | custom-call | tf_op jit(solution)/shard_map/opening_exchange/pallas_call | solution.py:526
  120.7 2.3 slice.53
  123.0 1.6 collective-permute-start.1
  124.6 1.8 collective-permute-start
  126.4 0.0 all-gather.2.cloned.1.call-update
  126.4 2.3 slice_bitcast_fusion
  128.7 0.2 collective-permute-start.2
  129.0 0.1 slice_compare_fusion
  129.0 0.2 slice_reduce_fusion.1
  129.2 0.2 slice_reduce_fusion.2
  129.4 0.1 convert_compare_fusion
  129.5 1.5 constant_dynamic-update-slice_fusion.5
  131.0 0.1 pad_add_fusion
  131.1 0.1 broadcast_bitcast_fusion.1
  131.2 0.1 broadcast_bitcast_fusion
  131.2 0.1 add_select_fusion.1
  131.3 0.3 reduce-window.9
  131.6 0.1 slice.69
  131.7 0.1 slice_reduce_fusion
  131.8 0.1 fusion.1
  131.9 14.2 %convolution_convert_fusion.1.gate_ref = bf16[2048,1024]{1,0:T(8,128)(2,1)} fusion(bf16[2048,2048]{1,0:T(8,128)(2,1)} %get-tuple-element.40.normed1_ref, bf16[2048,1024]{1,0:T(8,128)(2,1)} %get-tuple-element.42.w_gate_ref), kind=kOutput, calls=%fused_computation.1 | convolution fusion | flops 8592031744 | bytes 16777216 | tf_op jit(solution)/shard_map/dot_general | solution.py:24
  146.1 0.9 exponential_select_fusion.decay_ref
  147.0 0.6 fusion.8
  147.6 3.7 multiply_cosine_fusion
  151.3 0.1 pad_maximum_fusion.angle_ref
  151.5 0.0 copy-start
  151.5 0.0 copy-start.9
  151.5 24.8 %convolution_convert_fusion.field_ref = bf16[2048,2048]{1,0:T(8,128)(2,1)} fusion(bf16[2048,2048]{1,0:T(8,128)(2,1)} %get-tuple-element.40.normed1_ref, bf16[2048,2048]{1,0:T(8,128)(2,1)} %get-tuple-element.41.w_qkv_ref), kind=kOutput, calls=%fused_computation | convolution fusion | flops 17184063488 | bytes 25165824 | tf_op jit(solution)/shard_map/dot_general | solution.py:24
  176.3 0.7 exponential_select_fusion.1
  177.0 1.0 bitcast_dynamic-update-slice_fusion
  178.0 0.7 exponential_select_fusion.3
  178.7 1.0 copy.47
  179.7 0.1 stack.23
  179.8 0.4 copy.46
  180.2 0.1 pad.4.info_ref
  180.2 0.0 copy-start.1
  180.3 0.0 collective-permute-done
  180.3 0.7 collective-permute-start.3
  181.0 2.4 constant_dynamic-update-slice_fusion.4
  183.4 2.3 constant_dynamic-update-slice_fusion.3
  185.7 2.3 constant_dynamic-update-slice_fusion.2
  188.0 2.3 constant_dynamic-update-slice_fusion.1
  190.3 1.0 copy-done.2
  191.3 15.4 %retention_forward.1 = (bf16[2048,1024]{1,0:T(8,128)(2,1)}, bf16[2048,1024]{1,0:T(8,128)(2,1)}, f32[2048,128]{1,0:T(8,128)S(1)}, bf16[8,2,256,512]{3,2,1,0:T(8,128)(2,1)}) custom-call(s32[1]{0:T(128)} %bitcast.2.which, bf16[2048,2048]{1,0:T(8,128)(2,1)} %convolution_convert_fusion.field_ref, bf16[2048,1024]{1,0:T(8,128)(2,1)} %convolution_convert_fusion.1.gate_ref, ...), custom_call_target="tpu_custom_call" | custom-call | flops 3758096384 | bytes 25165824 | tf_op jit(solution)/shard_map/retention_forward/pallas_call | solution.py:323
  206.8 0.0 copy-start.3
  206.8 1.0 copy-done.3
  207.7 1.1 constant_dynamic-update-slice_fusion.cot_ref
  208.9 228.9 %middle_exchange.1 = (bf16[512,2048]{1,0:T(8,128)(2,1)}, bf16[512,2048]{1,0:T(8,128)(2,1)}, bf16[2048,2048]{1,0:T(8,128)(2,1)}, bf16[2048,1024]{1,0:T(8,128)(2,1...) custom-call(bf16[2048,1024]{1,0:T(8,128)(2,1)} %get-tuple-element.46.gated_ref, ...), custom_call_target="tpu_custom_call" | custom-call | tf_op jit(solution)/shard_map/middle_exchange/pallas_call | solution.py:935
  437.7 252.5 %closing_exchange.1 = (bf16[512,2048]{1,0:T(8,128)(2,1)}, bf16[512,2048]{1,0:T(8,128)(2,1)}, bf16[256,512]{1,0:T(8,128)(2,1)}, bf16[256,512]{1,0:T(8,128)(2,1)},...) custom-call(bf16[2048,2048]{1,0:T(8,128)(2,1)} %get-tuple-element.40, ...), custom_call_target="tpu_custom_call" | custom-call | tf_op jit(solution)/shard_map/closing_exchange/pallas_call | solution.py:1592
  690.3 0.8 constant_dynamic-slice_fusion
  691.2 0.5 slice_bitcast_fusion.1
  691.7 1.8 convert_element_type.72
  693.5 1.8 convert_element_type.73
  695.3 2.1 convert_element_type.74
  697.4 2.1 convert_element_type.75
  699.5 1.1 convert_bitcast_fusion.1
  700.7 1.3 copy.48
  702.0 1.1 convert_element_type.76
  703.1 0.1 convert_bitcast_fusion
  703.2 1.3 copy.49
  704.5 3.2 copy.60
  707.7 3.2 copy.61
  (27 shorter events, 0.2 us)
Async XLA Ops:
  7.2 122.3 %copy-start.5 = (bf16[512,2048]{1,0:T(8,128)(2,1)S(1)}, bf16[512,2048]{1,0:T(8,128)(2,1)}, u32[]{:S(2)}) copy-start(bf16[512,2048]{1,0:T(8,128)(2,1)} %cot_ref.1) | copy-start | bytes 6291460
  7.2 121.8 %copy-start.10 = (s32[2048]{0:T(1024)S(1)}, s32[2048]{0:T(1024)}, u32[]{:S(2)}) copy-start(s32[2048]{0:T(1024)} %param.16) | copy-start | bytes 24580
  7.2 201.7 %all-gather.2.cloned.1.call-start = ((), (), s32[]{:S(2)}) async-start(), calls=%async_computation | async-start | bytes 4718592 | tf_op jit(solution)/shard_map/all_gather | solution.py:1653
  123.0 62.7 %collective-permute-start.1 = (bf16[256,2048]{1,0:T(8,128)(2,1)}, bf16[256,2048]{1,0:T(8,128)(2,1)}, u32[]{:S(2)}, u32[]{:S(2)}) collective-permute-start(bf16[256,2048]{1,0:T(8,128)(2,1)} %slice.53), channel_id=1, source_target_pairs={{0,2},{1,3},{2,0},{3,1},{4,6},{5,7},{6,4},{7,5},{8,10},{9,11},{10,... | collective-permute-start | bytes 3145736 | tf_op jit(solution)/shard_map/ppermute | solution.py:37
  124.6 55.7 %collective-permute-start = (bf16[256,2048]{1,0:T(8,128)(2,1)}, bf16[256,2048]{1,0:T(8,128)(2,1)}, u32[]{:S(2)}, u32[]{:S(2)}) collective-permute-start(bf16[256,2048]{1,0:T(8,128)(2,1)} %slice.53), channel_id=1, source_target_pairs={{0,1},{1,0},{2,3},{3,2},{4,5},{5,4},{6,7},{7,6},{8,9},{9,8},{10,11... | collective-permute-start | bytes 3145736 | tf_op jit(solution)/shard_map/ppermute | solution.py:37
  128.7 59.2 %collective-permute-start.2 = (bf16[256,2048]{1,0:T(8,128)(2,1)}, bf16[256,2048]{1,0:T(8,128)(2,1)}, u32[]{:S(2)}, u32[]{:S(2)}) collective-permute-start(bf16[256,2048]{1,0:T(8,128)(2,1)} %slice_bitcast_fusion), channel_id=1, source_target_pairs={{0,1},{1,0},{2,3},{3,2},{4,5},{5,4},{6,7},{7,6},{8,9},{9,8},{10,11... | collective-permute-start | bytes 3145736 | tf_op jit(solution)/shard_map/ppermute | solution.py:37
  151.5 38.8 %copy-start = (f32[2048,256]{1,0:T(8,128)}, f32[2048,256]{1,0:T(8,128)S(1)}, u32[]{:S(2)}) copy-start(f32[2048,256]{1,0:T(8,128)S(1)} %pad_maximum_fusion.angle_ref) | copy-start | bytes 6291460
  151.5 25.5 %copy-start.6 = (bf16[2,256,2048]{2,1,0:T(8,128)(2,1)S(1)}, bf16[2,256,2048]{2,1,0:T(8,128)(2,1)}, u32[]{:S(2)}) copy-start(bf16[2,256,2048]{2,1,0:T(8,128)(2,1)} %get-tuple-element.43) | copy-start | bytes 6291460
  151.5 27.2 %copy-start.9 = (bf16[1024,256]{1,0:T(8,128)(2,1)S(1)}, bf16[1024,256]{1,0:T(8,128)(2,1)}, u32[]{:S(2)}) copy-start(bf16[1024,256]{1,0:T(8,128)(2,1)} %param.27) | copy-start | bytes 1572868
  178.0 28.7 %copy-start.4 = (f32[2048]{0:T(1024)}, f32[2048]{0:T(1024)S(1)}, u32[]{:S(2)}) copy-start(f32[2048]{0:T(1024)S(1)} %get-tuple-element.125) | copy-start | bytes 24580
  180.2 26.5 %copy-start.1 = (f32[2048,128]{1,0:T(8,128)}, f32[2048,128]{1,0:T(8,128)S(1)}, u32[]{:S(2)}) copy-start(f32[2048,128]{1,0:T(8,128)S(1)} %pad.4.info_ref) | copy-start | bytes 3145732
  180.3 27.5 %collective-permute-start.3 = (bf16[256,2048]{1,0:T(8,128)(2,1)}, bf16[256,2048]{1,0:T(8,128)(2,1)S(1)}, u32[]{:S(2)}, u32[]{:S(2)}) collective-permute-start(bf16[256,2048]{1,0:T(8,128)(2,1)} %collective-permute-done), channel_id=1, source_target_pairs={{0,2},{1,3},{2,0},{3,1},{4,6},{5,7},{6,4},{7,5},{8,10},{9,11},{10,... | collective-permute-start | bytes 3145736 | tf_op jit(solution)/shard_map/ppermute | solution.py:37
  190.3 1.0 copy-start.2
  206.8 1.0 copy-start.3
  690.3 11.7 %copy-start.8 = (bf16[256,1024]{1,0:T(8,128)(2,1)S(1)}, bf16[256,1024]{1,0:T(8,128)(2,1)}, u32[]{:S(2)}) copy-start(bf16[256,1024]{1,0:T(8,128)(2,1)} %get-tuple-element.65) | copy-start | bytes 1572868
  690.3 12.8 %copy-start.7 = (bf16[256,1024]{1,0:T(8,128)(2,1)S(1)}, bf16[256,1024]{1,0:T(8,128)(2,1)}, u32[]{:S(2)}) copy-start(bf16[256,1024]{1,0:T(8,128)(2,1)} %get-tuple-element.66) | copy-start | bytes 1572868
Sparse Core Ops, SparseCore 0:
  126.6 45.5 all-gather.1

commit v6 on v5

--- a/solution.py
+++ b/solution.py
@@ -346,16 +346,19 @@
 
 
 def opening_kernel(
-    query_ref, key_ref, value_ref, gate_ref, token_ref, gain_ref, bias_ref, cot_ref,
-    w_qkv_ref, w_gate_ref, normed_ref, cot_all_ref,
-    w_qkv, w_gate, normed, token_own, cot_own, cot_got,
-    local_sem, out_sem, up_send, up_recv, down_send, down_recv, core_send, core_recv, row_send, row_recv,
+    heads, query_ref, key_ref, value_ref, gate_ref, out_ref, token_ref, cot_ref, segment_ref, row_ref, rate_ref, gain_ref, bias_ref,
+    w_qkv_ref, w_gate_ref, w_out_ref, normed_ref, cot_all_ref, field_ref, gate_raw_ref, gated_ref, grouped_ref, scale_ref, past_ref,
+    angle_ref, info_ref, decay_ref,
+    w_qkv, w_gate, w_out, normed, product, blocks, angles, info, decay, state, field_out, gate_out, gated_out, grouped_out,
+    scale_out, past_out,
+    local_sem, block_sem, out_sem, stage_sem, table_sem, up_send, up_recv, down_send, down_recv, core_send, core_recv,
+    row_send, row_recv,
 ):
     dp = lax.axis_index("dp")
     tensor = lax.axis_index("tensor")
     z = lax.div(dp, 2)
-    layers = lax.div(lax.axis_size("dp"), 2)
-    shard_rows = query_ref.shape[0]
+    layers = 4
+    depth = query_ref.shape[0]
     rows = token_ref.shape[0]
     half = rows // 2
     above = (dp + 2, tensor)
@@ -363,21 +366,46 @@
     twin = (dp + 1 - 2 * lax.rem(dp, 2), tensor)
     over_x = (dp, tensor + 1 - 2 * lax.rem(tensor, 2))
     over_y = (dp, lax.rem(tensor + 2, 4))
-
-    keys = query_ref.shape[1]
-    values = value_ref.shape[1]
-    mine = pl.ds(pl.multiple_of(dp * shard_rows, shard_rows), shard_rows)
-    places = [
-        (query_ref, w_qkv.at[mine, pl.ds(0, keys)]),
-        (key_ref, w_qkv.at[mine, pl.ds(keys, keys)]),
-        (value_ref, w_qkv.at[mine, pl.ds(2 * keys, values)]),
-        (gate_ref, w_gate.at[mine]),
-        (token_ref, token_own),
-        (cot_ref.at[pl.ds(0, half)], cot_own),
+    keys = heads * KEY
+    values = heads * VAL
+
+    def block_of(start, count):
+        return pl.ds(pl.multiple_of(start, count), count)
+
+    def start(copies):
+        for copy in copies:
+            copy.start()
+
+    def wait(copies):
+        for copy in copies:
+            copy.wait()
+
+    def remote(src, dst, send, recv, device):
+        return pltpu.make_async_remote_copy(
+            src_ref=src, dst_ref=dst, send_sem=send, recv_sem=recv, device_id=device, device_id_type=MESH
+        )
+
+    mine = block_of(dp * depth, depth)
+    local = [
+        pltpu.make_async_copy(src, dst, local_sem.at[i])
+        for i, (src, dst) in enumerate((
+            (query_ref, w_qkv.at[mine, pl.ds(0, keys)]),
+            (key_ref, w_qkv.at[mine, pl.ds(keys, keys)]),
+            (value_ref, w_qkv.at[mine, pl.ds(2 * keys, values)]),
+            (gate_ref, w_gate.at[mine]),
+            (out_ref, w_out.at[mine]),
+            (segment_ref, info),
+        ))
     ]
-    local = [pltpu.make_async_copy(a, b, local_sem.at[i]) for i, (a, b) in enumerate(places)]
-    for copy in local:
-        copy.start()
+    start(local)
+
+    def token_block(i, slot):
+        return pltpu.make_async_copy(token_ref.at[block_of(i * 64, 64)], blocks.at[slot], block_sem.at[slot])
+
+    for i in range(4):
+        token_block(i, i).start()
+    own_cot = pltpu.make_async_copy(cot_ref, cot_all_ref.at[pl.ds(0, rows)], local_sem.at[6])
+    own_cot.start()
 
     barrier = pltpu.get_barrier_semaphore()
 
@@ -389,194 +417,366 @@
     pl.when(z < layers - 1)(lambda: greet(above))
     pl.when(z > 0)(lambda: greet(below))
     pl.semaphore_wait(barrier, 3 + (z < layers - 1).astype(jnp.int32) + (z > 0).astype(jnp.int32))
-    for copy in local[:4]:
-        copy.wait()
-
-    def weight_copies(shard, send_sem, recv_sem, step, device):
-        place = pl.ds(pl.multiple_of(shard * shard_rows, shard_rows), shard_rows)
+    wait(local[:5])
+
+
+    groups = ((w_qkv, w_gate), (w_out,))
+
+    def shard_copies(g, shard, send_sem, recv_sem, index, device):
+        place = block_of(shard * depth, depth)
         return [
-            pltpu.make_async_remote_copy(
-                src_ref=ref.at[place], dst_ref=ref.at[place],
-                send_sem=send_sem.at[step, i], recv_sem=recv_sem.at[step, i],
-                device_id=device, device_id_type=MESH,
-            )
-            for i, ref in enumerate((w_qkv, w_gate))
+            remote(ref.at[place], ref.at[place], send_sem.at[index, i + 2 * g], recv_sem.at[index, i + 2 * g], device)
+            for i, ref in enumerate(groups[g])
         ]
 
-    def shard_out(shard, slot):
-        place = pl.ds(pl.multiple_of(shard * shard_rows, shard_rows), shard_rows)
-        return [
-            pltpu.make_async_copy(w_qkv.at[place], w_qkv_ref.at[place], out_sem.at[slot, 0]),
-            pltpu.make_async_copy(w_gate.at[place], w_gate_ref.at[place], out_sem.at[slot, 1]),
-        ]
-
-    def start(copies):
+    def rise(g, j):
+        return shard_copies(g, dp - 2 * j, up_send, up_recv, j, above)
+
+    def sink(g, j):
+        return shard_copies(g, dp + 2 * j, down_send, down_recv, j, below)
+
+    def to_twin(g, j):
+        return shard_copies(g, dp + 2 * j, core_send, core_recv, j + 3, twin)
+
+    def from_twin(g, j):
+        return shard_copies(g, twin[0] + 2 * j, core_send, core_recv, j + 3, twin)
+
+    def wait_recv(copies):
         for copy in copies:
-            copy.start()
+            copy.wait_recv()
 
     def wait_send(copies):
         for copy in copies:
             copy.wait_send()
 
-    def wait_recv(copies):
-        for copy in copies:
-            copy.wait_recv()
-
-    def up(j):
-        return weight_copies(dp - 2 * j, up_send, up_recv, j, above)
-
-    def down(j):
-        return weight_copies(dp + 2 * j, down_send, down_recv, j, below)
-
-    def to_twin(j):
-        return weight_copies(dp + 2 * j, core_send, core_recv, j + 3, twin)
-
-    def from_twin(j):
-        return weight_copies(twin[0] + 2 * j, core_send, core_recv, j + 3, twin)
-
-    def step(j):
+    def first_step(g):
+        pl.when(z < layers - 1)(lambda: start(rise(g, 0)))
+        pl.when(z > 0)(lambda: start(sink(g, 0)))
+        start(to_twin(g, 0))
+
+    def step(g, j):
         @pl.when(z - j >= 0)
         def _():
-            wait_recv(weight_copies(dp - 2 * j, up_send, up_recv, j - 1, twin))
+            wait_recv(shard_copies(g, dp - 2 * j, up_send, up_recv, j - 1, twin))
             if j < 3:
-                pl.when(z < layers - 1)(lambda: start(up(j)))
-            start(to_twin(-j))
-            start(shard_out(dp - 2 * j, 3 - j))
+                pl.when(z < layers - 1)(lambda: start(rise(g, j)))
+            start(to_twin(g, -j))
 
         @pl.when(z + j < layers)
         def _():
-            wait_recv(weight_copies(dp + 2 * j, down_send, down_recv, j - 1, twin))
+            wait_recv(shard_copies(g, dp + 2 * j, down_send, down_recv, j - 1, twin))
             if j < 3:
-                pl.when(z > 0)(lambda: start(down(j)))
-            start(to_twin(j))
-            start(shard_out(dp + 2 * j, 3 + j))
-
-    pl.when(z < layers - 1)(lambda: start(up(0)))
-    pl.when(z > 0)(lambda: start(down(0)))
-    start(to_twin(0))
-    start(shard_out(dp, 3))
-
-    local[4].wait()
+                pl.when(z > 0)(lambda: start(sink(g, j)))
+            start(to_twin(g, j))
+
+    def twin_step(g, j):
+        for signed in sorted({-j, j}):
+            @pl.when((z + signed >= 0) & (z + signed < layers))
+            def _():
+                wait_recv(from_twin(g, signed))
+
+    first_step(0)
 
     @pl.loop(0, rows // 64)
     def _(i):
-        block = pl.ds(pl.multiple_of(i * 64, 64), 64)
-        unit, _ = normalize(token_own[block, :].astype(f32))
-        normed[block, :] = (unit * gain_ref[...] + bias_ref[...]).astype(bf16)
+        slot = lax.rem(i, 4)
+        token_block(i, slot).wait()
+        plain, _ = normalize(blocks[slot].astype(f32))
+        normed[block_of(i * 64, 64), :] = (plain * gain_ref[...] + bias_ref[...]).astype(bf16)
+
+        @pl.when(i + 4 < rows // 64)
+        def _():
+            token_block(i + 4, slot).start()
+
+    def rows_of(r, first=0, count=rows):
+        return pl.ds(r * rows + first, count)
 
     def row_copy(index, src, dst, device):
-        return pltpu.make_async_remote_copy(
-            src_ref=src, dst_ref=dst, send_sem=row_send.at[index], recv_sem=row_recv.at[index],
-            device_id=device, device_id_type=MESH,
-        )
-
-    local[5].wait()
+        return remote(src, dst, row_send.at[index], row_recv.at[index], device)
+
     over = [
-        row_copy(0, normed.at[pl.ds(0, rows)], normed.at[pl.ds(rows, rows)], over_x),
-        row_copy(1, normed.at[pl.ds(0, rows)], normed.at[pl.ds(2 * rows, rows)], over_y),
+        row_copy(0, normed.at[rows_of(0)], normed.at[rows_of(1)], over_x),
+        row_copy(1, normed.at[rows_of(0)], normed.at[rows_of(2)], over_y),
+    ]
+    onward = [
+        row_copy(2, normed.at[rows_of(2, 0, half)], normed.at[rows_of(3, 0, half)], over_x),
+        row_copy(3, normed.at[rows_of(1, half, half)], normed.at[rows_of(3, half, half)], over_y),
+    ]
+    cot_over = [
+        row_copy(4, cot_ref, cot_all_ref.at[rows_of(1)], over_x),
+        row_copy(5, cot_ref, cot_all_ref.at[rows_of(2)], over_y),
+    ]
+    cot_onward = [
+        row_copy(6, cot_all_ref.at[rows_of(2, 0, half)], cot_all_ref.at[rows_of(3, 0, half)], over_x),
+        row_copy(7, cot_all_ref.at[rows_of(1, half, half)], cot_all_ref.at[rows_of(3, half, half)], over_y),
     ]
     start(over)
-    step(1)
+
+    local[5].wait()
+    half_key = KEY // 2
+    lanes = lax.broadcasted_iota(jnp.int32, (CHUNK, half_key), 1).astype(f32)
+    frequency = jnp.exp(lanes * (-9.210340371976184 / half_key))
+    chunks = 4 * rows // CHUNK
+
+    @pl.loop(0, chunks)
+    def _(c):
+        seat = block_of(c * CHUNK, CHUNK)
+        own = info[seat, 0:1]
+        ranked = jnp.where(own < 0, 3.0, own)
+        before = jnp.zeros((CHUNK, 1), f32)
+        for other in range(chunks):
+            seen = row_ref[other]
+            seen = jnp.where(seen < 0, 3.0, seen)
+            before = before + jnp.sum((seen < ranked).astype(f32), axis=1, keepdims=True)
+        index = lax.broadcasted_iota(jnp.int32, (CHUNK, 1), 0) + c * CHUNK
+        turned = (index.astype(f32) - before) * frequency
+        angles[seat, 0:half_key] = jnp.cos(turned)
+        angles[seat, half_key:KEY] = jnp.sin(turned)
+
+    distance = lax.broadcasted_iota(jnp.int32, (CHUNK, CHUNK), 0) - lax.broadcasted_iota(jnp.int32, (CHUNK, CHUNK), 1)
+    span = jnp.maximum(distance, 0).astype(f32)
+    for head in range(heads):
+        decay[head] = jnp.where(distance >= 0, jnp.exp(rate_ref[head : head + 1, 0:1] * span), 0.0)
+    table_outs = [
+        pltpu.make_async_copy(angles, angle_ref, table_sem.at[0]),
+        pltpu.make_async_copy(decay, decay_ref, table_sem.at[1]),
+    ]
+    start(table_outs)
+
+
+    at_end = (z == 0) | (z == 3)
+
+    def seen_from_end(index):
+        return jnp.where(z >= 2, 3 - index, index)
+
+    order = [z, jnp.where(at_end, seen_from_end(1), seen_from_end(0)), seen_from_end(2), seen_from_end(3)]
+
+    def project(r, s):
+        deep = block_of(order[s] * 2 * depth, 2 * depth)
+
+        @pl.loop(0, (2 * keys + values) // 512)
+        def _(j):
+            tile = block_of(j * 512, 512)
+            more = dot_nn(normed[rows_of(r), deep], w_qkv[deep, tile])
+            product[rows_of(r), tile] = more if s == 0 else product[rows_of(r), tile] + more
+
+        @pl.loop(0, values // 512)
+        def _(j):
+            tile = block_of(j * 512, 512)
+            more = dot_nn(normed[rows_of(r), deep], w_gate[deep, tile])
+            place = block_of(2 * keys + values + j * 512, 512)
+            product[rows_of(r), place] = more if s == 0 else product[rows_of(r), place] + more
+
+
+    per_piece = rows // CHUNK
+
+    def chunk_place(c):
+        piece = lax.div(c, per_piece)
+        low = lax.rem(lax.rem(piece, 2) + lax.rem(tensor, 2), 2)
+        high = lax.rem(lax.div(piece, 2) + lax.div(tensor, 2), 2)
+        return (2 * high + low) * per_piece + lax.rem(c, per_piece)
+
+    def chunk_outs(c):
+        place = block_of(chunk_place(c) * CHUNK, CHUNK)
+        pairs = (
+            (field_out, field_ref.at[place]),
+            (gate_out, gate_raw_ref.at[place]),
+            (gated_out, gated_ref.at[place]),
+            (grouped_out, grouped_ref.at[place]),
+            (scale_out, scale_ref.at[place]),
+            (past_out, past_ref.at[c]),
+        )
+        return [pltpu.make_async_copy(src, dst, stage_sem.at[i]) for i, (src, dst) in enumerate(pairs)]
+
+    def retention(between):
+        state[...] = jnp.zeros_like(state)
+
+        @pl.loop(0, chunks)
+        def _(c):
+            place = block_of(chunk_place(c) * CHUNK, CHUNK)
+            seat = block_of(c * CHUNK, CHUNK)
+            cosine = angles[seat, 0:half_key]
+            sine = angles[seat, half_key:KEY]
+            own = info[seat, 0:1]
+            same = own == row_ref[c]
+            entering = (own == row_ref[jnp.maximum(c - 1, 0)][:, CHUNK - 1 :]) & (c > 0)
+            leaving = own == row_ref[c][:, CHUNK - 1 :]
+            offset = lax.broadcasted_iota(jnp.int32, (CHUNK, 1), 0).astype(f32)
+            lane = lax.broadcasted_iota(jnp.int32, (CHUNK, 128), 1)
+            facts = jnp.where(lane == 0, own, 0.0)
+            scales = jnp.zeros((CHUNK, 128), f32)
+
+            @pl.when(c > 0)
+            def _():
+                wait(chunk_outs(c - 1))
+
+            for head in range(heads):
+                rate = rate_ref[head : head + 1, 0:1]
+                into = jnp.where(entering, jnp.exp(rate * (offset + 1.0)), 0.0)
+                onto = jnp.where(leaving, jnp.exp(rate * (CHUNK - 1.0 - offset)), 0.0)
+                facts = jnp.where(lane == 1 + 2 * head, into, facts)
+                facts = jnp.where(lane == 2 + 2 * head, onto, facts)
+                query_raw = product[place, pl.ds(head * KEY, KEY)]
+                key_raw = product[place, pl.ds(keys + head * KEY, KEY)]
+                value = product[place, pl.ds(2 * keys + head * VAL, VAL)].astype(bf16)
+                gate = product[place, pl.ds(2 * keys + values + head * VAL, VAL)]
+                query_raw = query_raw.astype(bf16)
+                key_raw = key_raw.astype(bf16)
+                gate_low = gate.astype(bf16)
+                field_out[:, pl.ds(head * KEY, KEY)] = query_raw
+                field_out[:, pl.ds(keys + head * KEY, KEY)] = key_raw
+                field_out[:, pl.ds(2 * keys + head * VAL, VAL)] = value
+                gate_out[:, pl.ds(head * VAL, VAL)] = gate_low
+                query = turn(query_raw.astype(f32), cosine, sine).astype(bf16)
+                key = (turn(key_raw.astype(f32), cosine, sine) * key_scale).astype(bf16)
+                memory = state[head]
+                memory_low = memory.astype(bf16)
+                past_out[head] = memory_low
+                scores = dot_nt(query, key)
+                weights = (jnp.where(same, decay[head], 0.0) * scores).astype(bf16)
+                retained = dot_nn(weights, value) + into * dot_nn(query, memory_low)
+                moved = (key.astype(f32) * onto).astype(bf16)
+                state[head] = into[CHUNK - 1 :, :] * memory + dot_tn(moved, value)
+                centred = retained - jnp.mean(retained, axis=-1, keepdims=True)
+                scale = lax.rsqrt(jnp.mean(centred * centred, axis=-1, keepdims=True) + group_floor)
+                grouped = centred * scale
+                columns = pl.ds(head * VAL, VAL)
+                gated_out[:, columns] = (gate / (1.0 + jnp.exp(-gate)) * grouped).astype(bf16)
+                grouped_out[:, columns] = grouped.astype(bf16)
+                scales = jnp.where(lane == head, scale, scales)
+            info[seat, :] = facts
+            scale_out[...] = scales
+            start(chunk_outs(c))
+            between(c)
+
+        wait(chunk_outs(chunks - 1))
+
+
+    twin_step(0, 0)
+    project(0, 0)
+    step(0, 1)
+    twin_step(0, 1)
+    project(0, 1)
     wait_recv(over)
-    onward = [
-        row_copy(2, normed.at[pl.ds(2 * rows, half)], normed.at[pl.ds(3 * rows, half)], over_x),
-        row_copy(3, normed.at[pl.ds(rows + half, half)], normed.at[pl.ds(3 * rows + half, half)], over_y),
+    start(onward)
+    start(cot_over)
+    for r in (1, 2):
+        for s in (0, 1):
+            project(r, s)
+    step(0, 2)
+    first_step(1)
+    twin_step(0, 2)
+    for r in (0, 1, 2):
+        project(r, 2)
+    wait_recv(onward)
+    normed_out = pltpu.make_async_copy(normed, normed_ref, local_sem.at[7])
+    normed_out.start()
+    for s in (0, 1, 2):
+        project(3, s)
+    step(0, 3)
+    twin_step(0, 3)
+    for r in range(4):
+        project(r, 3)
+    step(1, 1)
+    w_outs = [
+        pltpu.make_async_copy(w_qkv, w_qkv_ref, out_sem.at[0]),
+        pltpu.make_async_copy(w_gate, w_gate_ref, out_sem.at[1]),
     ]
-    start(onward)
-    cots = [
-        row_copy(4, cot_own, cot_got.at[0], over_x),
-        row_copy(5, cot_own, cot_got.at[1], over_y),
-    ]
-    start(cots)
-    step(2)
-    wait_recv(onward)
-    normed_out = pltpu.make_async_copy(normed, normed_ref, local_sem.at[6])
-    normed_out.start()
-    wait_recv(cots)
-    cot_out = pltpu.make_async_copy(cot_got, cot_all_ref, local_sem.at[7])
-    cot_out.start()
-    step(3)
-
-    for j in range(-3, 4):
-        @pl.when((z + j >= 0) & (z + j < layers))
+    start(w_outs)
+
+    def between(c):
+        @pl.when(c == 3)
         def _():
-            wait_recv(from_twin(j))
-            start(shard_out(twin[0] + 2 * j, 10 + j))
-    wait_send(over + onward + cots)
-    for j in range(3):
-        pl.when((z < layers - 1) & (z - j >= 0))(lambda: wait_send(up(j)))
-        pl.when((z > 0) & (z + j < layers))(lambda: wait_send(down(j)))
-    normed_out.wait()
-    cot_out.wait()
-    for j in range(-3, 4):
-        @pl.when((z + j >= 0) & (z + j < layers))
+            wait_recv(cot_over)
+            start(cot_onward)
+
+        @pl.when(c == 4)
         def _():
-            wait_send(to_twin(j))
-            for copy in shard_out(dp + 2 * j, 3 + j) + shard_out(twin[0] + 2 * j, 10 + j):
-                copy.wait()
-
-
-def opening_exchange(query_weight, key_weight, value_weight, gate_weight, tokens, gain, bias, cotangent):
+            step(1, 2)
+
+    retention(between)
+    info_out = pltpu.make_async_copy(info, info_ref, table_sem.at[2])
+    info_out.start()
+    step(1, 3)
+    for j in range(4):
+        twin_step(1, j)
+    w_out_out = pltpu.make_async_copy(w_out, w_out_ref, out_sem.at[2])
+    w_out_out.start()
+    wait_recv(cot_onward)
+
+    wait_send(over + onward + cot_over + cot_onward)
+    for g in range(2):
+        for j in range(3):
+            pl.when((z < layers - 1) & (z - j >= 0))(lambda: wait_send(rise(g, j)))
+            pl.when((z > 0) & (z + j < layers))(lambda: wait_send(sink(g, j)))
+        for j in range(-3, 4):
+            pl.when((z + j >= 0) & (z + j < layers))(lambda: wait_send(to_twin(g, j)))
+    wait(table_outs + w_outs + [normed_out, own_cot, info_out, w_out_out])
+
+
+def opening_exchange(heads, shards, tokens, cotangent, segment, gain, bias):
     dp = lax.axis_size("dp")
-    depth, keys = query_weight.shape
-    values = value_weight.shape[1]
-    rows, width = tokens.shape
+    depth, keys = shards[0].shape
+    values = shards[2].shape[1]
+    unit = shards[4].shape[1]
+    token_rows, width = tokens.shape
+    rows = 4 * token_rows
+    chunks = rows // CHUNK
     anywhere = pl.BlockSpec(memory_space=pl.ANY)
     in_vmem = pl.BlockSpec(memory_space=pltpu.VMEM)
-    return pl.pallas_call(
-        opening_kernel,
+    sem = pltpu.SemaphoreType.DMA
+    vmem = pltpu.VMEM
+    here = lax.axis_index("tensor") * heads
+    head_ids = (here + jnp.arange(8, dtype=jnp.int32)).astype(f32)
+    rates = jnp.broadcast_to(jnp.log1p(-jnp.exp2(-5.0 - head_ids))[:, None], (8, 128))
+    wide_segment = jnp.broadcast_to(segment.astype(f32)[:, None], (rows, 128))
+    row_segment = jnp.where(segment >= 0, segment, -7).astype(f32).reshape(chunks, 1, CHUNK)
+    results = pl.pallas_call(
+        functools.partial(opening_kernel, heads),
         out_shape=[
             jax.ShapeDtypeStruct((dp * depth, 2 * keys + values), bf16),
             jax.ShapeDtypeStruct((dp * depth, values), bf16),
-            jax.ShapeDtypeStruct((4 * rows, width), bf16),
-            jax.ShapeDtypeStruct((2, rows // 2, width), bf16),
+            jax.ShapeDtypeStruct((dp * depth, unit), bf16),
+            jax.ShapeDtypeStruct((rows, width), bf16),
+            jax.ShapeDtypeStruct((rows, width), bf16),
+            jax.ShapeDtypeStruct((rows, 2 * keys + values), bf16),
+            jax.ShapeDtypeStruct((rows, values), bf16),
+            jax.ShapeDtypeStruct((rows, values), bf16),
+            jax.ShapeDtypeStruct((rows, values), bf16),
+            jax.ShapeDtypeStruct((rows, 128), f32),
+            jax.ShapeDtypeStruct((chunks, heads, KEY, VAL), bf16),
+            jax.ShapeDtypeStruct((rows, KEY), f32),
+            jax.ShapeDtypeStruct((rows, 128), f32),
+            jax.ShapeDtypeStruct((heads, CHUNK, CHUNK), f32),
         ],
-        in_specs=[anywhere] * 5 + [in_vmem] * 2 + [anywhere],
-        out_specs=[anywhere] * 4,
+        in_specs=[anywhere] * 8 + [in_vmem] * 4,
+        out_specs=[anywhere] * 14,
         scratch_shapes=[
-            pltpu.VMEM((dp * depth, 2 * keys + values), bf16),
-            pltpu.VMEM((dp * depth, values), bf16),
-            pltpu.VMEM((4 * rows, width), bf16),
-            pltpu.VMEM((rows, width), bf16),
-            pltpu.VMEM((rows // 2, width), bf16),
-            pltpu.VMEM((2, rows // 2, width), bf16),
-            pltpu.SemaphoreType.DMA((8,)),
-            pltpu.SemaphoreType.DMA((14, 2)),
-            pltpu.SemaphoreType.DMA((3, 2)),
-            pltpu.SemaphoreType.DMA((3, 2)),
-            pltpu.SemaphoreType.DMA((3, 2)),
-            pltpu.SemaphoreType.DMA((3, 2)),
-            pltpu.SemaphoreType.DMA((7, 2)),
-            pltpu.SemaphoreType.DMA((7, 2)),
-            pltpu.SemaphoreType.DMA((6,)),
-            pltpu.SemaphoreType.DMA((6,)),
+            vmem((dp * depth, 2 * keys + values), bf16),
+            vmem((dp * depth, values), bf16),
+            vmem((dp * depth, unit), bf16),
+            vmem((rows, width), bf16),
+            vmem((rows, 2 * keys + 2 * values), f32),
+            vmem((4, 64, width), bf16),
+            vmem((rows, KEY), f32),
+            vmem((rows, 128), f32),
+            vmem((heads, CHUNK, CHUNK), f32),
+            vmem((heads, KEY, VAL), f32),
+            vmem((CHUNK, 2 * keys + values), bf16),
+            vmem((CHUNK, values), bf16),
+            vmem((CHUNK, values), bf16),
+            vmem((CHUNK, values), bf16),
+            vmem((CHUNK, 128), f32),
+            vmem((heads, KEY, VAL), bf16),
+            sem((8,)), sem((4,)), sem((3,)), sem((6,)), sem((3,)),
+            sem((3, 3)), sem((3, 3)), sem((3, 3)), sem((3, 3)), sem((7, 3)), sem((7, 3)), sem((8,)), sem((8,)),
         ],
         compiler_params=pltpu.CompilerParams(
-            collective_id=2, has_side_effects=True, vmem_limit_bytes=60 * 1024 * 1024
+            collective_id=2, has_side_effects=True, vmem_limit_bytes=63_400_000
         ),
         name="opening_exchange",
-    )(query_weight, key_weight, value_weight, gate_weight, tokens, gain.reshape(1, width), bias.reshape(1, width), cotangent)
-
-
-def opening(query_weight, key_weight, value_weight, gate_weight, tokens, gain, bias, cotangent, devices):
-    if devices == 4 and lax.axis_size("dp") == 8:
-        w_qkv, w_gate, normed1_all, cot_half = opening_exchange(
-            query_weight, key_weight, value_weight, gate_weight, tokens, gain, bias, cotangent
-        )
-        half = tokens.shape[0] // 2
-        rest = after(cotangent, cot_half)[half:]
-        rest_x = tensor_permute(rest, 1)
-        rest_y = tensor_permute(rest, 2)
-        lower = tensor_permute(cot_half[1], 1)
-        upper = tensor_permute(rest_x, 2)
-        cots = [cotangent, cot_half[0], rest_x, cot_half[1], rest_y, lower, upper]
-        return w_qkv, w_gate, normed1_all, cots, (rest_x, rest_y)
-    w_qkv = lax.all_gather(jnp.concatenate([query_weight, key_weight, value_weight], axis=1), "dp", axis=0, tiled=True)
-    w_gate = lax.all_gather(gate_weight, "dp", axis=0, tiled=True)
-    unit, _ = normalize(tokens.astype(f32))
-    normed1_all = jnp.concatenate(gather_pieces((unit * gain + bias).astype(bf16), devices), axis=0)
-    cots = gather_pieces(cotangent, devices)
-    return w_qkv, w_gate, normed1_all, cots, (cots[0],)
+    )(*shards, tokens, cotangent, wide_segment, row_segment, rates, gain.reshape(1, width), bias.reshape(1, width))
+    return results, row_segment
 
 
 def middle_kernel(
@@ -625,8 +825,7 @@
     ]
     first_loads = [
         pltpu.make_async_copy(gated_ref, units.at[0], load_sem.at[2]),
-        pltpu.make_async_copy(w_out_ref.at[:, pl.ds(0, unit)], units.at[1, pl.ds(0, unit)], load_sem.at[3]),
-        pltpu.make_async_copy(w_out_ref.at[:, pl.ds(unit, unit)], units.at[1, pl.ds(unit, unit)], load_sem.at[4]),
+        pltpu.make_async_copy(w_out_ref, units.at[1], load_sem.at[3]),
     ]
     token_load = pltpu.make_async_copy(token_ref, plus, load_sem.at[5])
     cot_load = pltpu.make_async_copy(cot_ref, big, load_sem.at[6])
@@ -744,10 +943,8 @@
     def branch_term(r):
         @pl.loop(0, width // 256)
         def _(j):
-            top = lax.div(j, unit // 256) * unit
-            inner = block_of(lax.rem(j, unit // 256) * 256, 256)
-            term = dot_nn(units[0, rows_of(r)], units[1, pl.ds(pl.multiple_of(top, unit), unit), inner])
-            terms[slot_of(r), :, block_of(j * 256, 256)] = term.astype(bf16)
+            tile = block_of(j * 256, 256)
+            terms[slot_of(r), :, tile] = dot_nt(units[0, rows_of(r)], units[1, tile]).astype(bf16)
 
     def feed_grads():
         @pl.loop(0, unit // 256)
@@ -1020,12 +1217,6 @@
     def whole(index, ref, sem):
         return [pltpu.make_async_copy(ref, units.at[index], unit_sem.at[sem])]
 
-    def folded(index, ref, sem):
-        return [
-            pltpu.make_async_copy(ref.at[:, pl.ds(0, unit)], units.at[index, pl.ds(0, unit)], unit_sem.at[sem]),
-            pltpu.make_async_copy(ref.at[:, pl.ds(unit, unit)], units.at[index, pl.ds(unit, unit)], unit_sem.at[sem + 1]),
-        ]
-
     def part(index, ref, start, sem):
         return [pltpu.make_async_copy(ref.at[:, pl.ds(start, unit)], units.at[index], unit_sem.at[sem])]
 
@@ -1037,7 +1228,7 @@
         for copy in copies:
             copy.wait()
 
-    out_load = folded(3, w_out_ref, 4)
+    out_load = whole(3, w_out_ref, 4)
     feed_load = [
         pltpu.make_async_copy(feed_ref.at[pl.ds((i + 1) * rows, rows)], terms.at[i], unit_sem.at[i]) for i in range(3)
     ]
@@ -1253,8 +1444,7 @@
 
         @pl.loop(0, unit // 256)
         def _(j):
-            grad = dot_nt(big[rows_of(r), pl.ds(0, unit)], units[3, block_of(j * 256, 256)])
-            grad = grad + dot_nt(big[rows_of(r), pl.ds(unit, unit)], units[3, block_of(unit + j * 256, 256)])
+            grad = dot_nn(big[rows_of(r)], units[3, :, block_of(j * 256, 256)])
             head = lax.div(j, VAL // 256)
             inner = block_of(lax.rem(j, VAL // 256) * 256, 256)
             raw = columns[r % 2, block_of(head * rows, rows), inner].astype(f32)
@@ -1647,24 +1837,12 @@
     def per_piece(values):
         return [values[i * rows : (i + 1) * rows] for i in range(devices)]
 
-    w_qkv, w_gate, normed1_all, cots, cot_begun = opening(
-        query_weight, key_weight, value_weight, gate_weight, tokens, first_gain, first_bias, cotangent, devices
-    )
-    w_out = lax.all_gather(after(out_weight, w_gate), "dp", axis=1, tiled=True)
-    token_rows = tokens.astype(f32)
-    down_shard = down_weight.T
-    tables = retention_tables(segment, heads, here * heads)
-    field = dot_nn(normed1_all, w_qkv).astype(bf16)
-    gate = dot_nn(normed1_all, w_gate).astype(bf16)
-    gated, grouped, group_scale, past = retention_call(
-        False, which, rows, heads, field, after(gate, *cot_begun), tables, ()
-    )
-    cot_all = jnp.concatenate(cots, axis=0)
-    angles, info, keys, decay = tables
-
     if devices == 4 and lax.axis_size("dp") == 8:
+        shards = (query_weight, key_weight, value_weight, gate_weight, out_weight.T)
+        opened, keys = opening_exchange(heads, shards, tokens, cotangent, segment, first_gain, first_bias)
+        w_qkv, w_gate, w_out, normed1_all, cot_all, field, gate, gated, grouped, group_scale, past, angles, info, decay = opened
         mixed_low, plus, feed_terms, up_weight_grad, down_weight_grad, late = middle_exchange(
-            gated, w_out, up_weight, down_shard, cot_all, tokens, second_gain, second_bias
+            gated, w_out, up_weight, down_weight.T, cot_all, tokens, second_gain, second_bias
         )
         result, input_grad, query_sum, key_sum, value_sum, gate_sum, out_sum, up_sum, down_sum, sums = closing_exchange(
             heads,
@@ -1683,9 +1861,24 @@
         )
         out_sum, down_sum = out_sum.astype(f32).T, down_sum.astype(f32).T
     else:
+        w_qkv = lax.all_gather(
+            jnp.concatenate([query_weight, key_weight, value_weight], axis=1), "dp", axis=0, tiled=True
+        )
+        w_gate = lax.all_gather(gate_weight, "dp", axis=0, tiled=True)
+        w_out = lax.all_gather(out_weight, "dp", axis=1, tiled=True)
+        token_rows = tokens.astype(f32)
+        unit1, scale1 = normalize(token_rows)
+        normed1_all = jnp.concatenate(
+            gather_pieces((unit1 * first_gain + first_bias).astype(bf16), devices), axis=0
+        )
+        cot_all = jnp.concatenate(gather_pieces(cotangent, devices), axis=0)
+        tables = retention_tables(segment, heads, here * heads)
+        field = dot_nn(normed1_all, w_qkv).astype(bf16)
+        gate = dot_nn(normed1_all, w_gate).astype(bf16)
+        gated, grouped, group_scale, past = retention_call(False, which, rows, heads, field, gate, tables, ())
         w_down = lax.all_gather(after(down_weight, w_out), "dp", axis=1, tiled=True)
         w_up = lax.all_gather(after(up_weight, w_down), "dp", axis=0, tiled=True)
-        branch, begun, _ = scatter_sum([dot_nn(piece, w_out) for piece in per_piece(after(gated, *cots))])
+        branch, begun, _ = scatter_sum([dot_nn(piece, w_out) for piece in per_piece(gated)])
 
         mixed = token_rows + branch
         unit2, scale2 = normalize(mixed)
@@ -1744,7 +1937,6 @@
             dot_nt(first, w_qkv) + dot_nt(second, w_gate) for first, second in zip(per_piece(back), per_piece(gate_grad))
         ]
         normed1_grad, _, _ = scatter_sum(terms)
-        unit1, scale1 = normalize(token_rows)
         input_grad = (mixed_grad + normalize_back(normed1_grad, unit1, scale1, first_gain)).astype(bf16)
         gain1_grad = jnp.sum(normed1_grad * unit1, axis=0)
         bias1_grad = jnp.sum(normed1_grad, axis=0)

time: 726 us -> 677 us (0.933)
  matrix products: 39 us -> 0 us
  Pallas kernels: 610 us -> 641 us
  local copies, waits for them, and re-layouts: 32.7 us -> 14.6 us
  between operations: 14.8 us -> 1.17 us
    dot_general x2 -> x0, matrix products: 39 us -> none  [dot_nn(): lax.dot_general(left, right, (((1,), (0,)), ((), ())), preferred_element_...]
    pallas_call x2 -> x1, Pallas kernels: 129 us -> 162 us  [opening_exchange(): pl.pallas_call(functools.partial(opening_kernel, heads), out_shape=[jax.S...]
    unnamed x37 -> x14, local copies, waits for them, and re-layouts: 24 us -> 11.2 us
  transfers between devices with their start and end apart: 5 -> 0, of which waited for: 0 -> 0; matrix products, arithmetic and copies ran while one was open for 9% -> 0% of each run, Pallas kernels for 2% -> 0%
where the time goes in v6:
time: 677 us; the launch traced here: 667 us
  Pallas kernels  641 us (95%)
  local copies, waits for them, and re-layouts  14.6 us (2%)
  other arithmetic  10.6 us (2%)
    pallas_call x1, Pallas kernels, closing_exchange(): pl.pallas_call(functools.partial(closing_kernel, heads), out_shape=[jax.S...  248 us
    pallas_call x1, Pallas kernels, middle_exchange(): pl.pallas_call(middle_kernel, out_shape=[jax.ShapeDtypeStruct((token_rows...  231 us
    pallas_call x1, Pallas kernels, opening_exchange(): pl.pallas_call(functools.partial(opening_kernel, heads), out_shape=[jax.S...  162 us

profile of v6, /device:TPU:0, one launch (start us, length us, event | category | flops | bytes accessed | tf_op | source)
XLA Modules:
  0.0 667.2 jit_solution(15196234652422802599)
XLA Ops:
  0.7 0.7 broadcast_in_dim.18.rate_ref
  1.3 1.4 fusion
  2.7 2.0 copy.27
  4.8 2.0 copy.28
  6.8 1.3 broadcast_in_dim.7.segment_ref
  8.1 161.7 %opening_exchange.1 = (bf16[2048,2048]{1,0:T(8,128)(2,1)}, bf16[2048,1024]{1,0:T(8,128)(2,1)}, bf16[2048,1024]{1,0:T(8,128)(2,1)}, bf16[2048,2048]{1,0:T(8,128)(...) custom-call(bf16[256,512]{1,0:T(8,128)(2,1)} %query_ref.1, ...), custom_call_target="tpu_custom_call" | custom-call | tf_op jit(solution)/shard_map/opening_exchange/pallas_call | solution.py:734
  169.8 231.2 %middle_exchange.1 = (bf16[512,2048]{1,0:T(8,128)(2,1)}, bf16[512,2048]{1,0:T(8,128)(2,1)}, bf16[2048,2048]{1,0:T(8,128)(2,1)}, bf16[2048,1024]{1,0:T(8,128)(2,1...) custom-call(bf16[2048,1024]{1,0:T(8,128)(2,1)} %get-tuple-element.44.gated_ref, ...), custom_call_target="tpu_custom_call" | custom-call | tf_op jit(solution)/shard_map/middle_exchange/pallas_call | solution.py:1132
  401.0 248.0 %closing_exchange.1 = (bf16[512,2048]{1,0:T(8,128)(2,1)}, bf16[512,2048]{1,0:T(8,128)(2,1)}, bf16[256,512]{1,0:T(8,128)(2,1)}, bf16[256,512]{1,0:T(8,128)(2,1)},...) custom-call(bf16[2048,2048]{1,0:T(8,128)(2,1)} %get-tuple-element.43, ...), custom_call_target="tpu_custom_call" | custom-call | tf_op jit(solution)/shard_map/closing_exchange/pallas_call | solution.py:1782
  649.1 0.0 copy-start.1
  649.1 0.0 copy-start.2
  649.1 0.0 copy-start.3
  649.1 0.9 constant_dynamic-slice_fusion
  650.0 0.5 slice_bitcast_fusion
  650.5 1.8 convert_element_type.33
  652.3 1.8 convert_element_type.34
  654.1 2.1 convert_element_type.35
  656.2 2.1 convert_element_type.36
  658.4 0.0 copy-done.1
  658.4 1.1 convert_element_type.37
  659.4 0.0 copy-done.2
  659.4 0.0 copy-done.3
  659.4 0.2 convert_bitcast_fusion
  659.7 1.3 copy.30
  661.0 0.0 copy-start
  661.0 1.3 copy.29
  662.3 3.2 copy.33
  665.5 0.0 copy-done
  665.5 1.3 copy.34
  (1 shorter events, 0.0 us)
Async XLA Ops:
  649.1 9.3 %copy-start.1 = (bf16[256,1024]{1,0:T(8,128)(2,1)S(1)}, bf16[256,1024]{1,0:T(8,128)(2,1)}, u32[]{:S(2)}) copy-start(bf16[256,1024]{1,0:T(8,128)(2,1)} %get-tuple-element.71) | copy-start | bytes 1572868
  649.1 10.4 %copy-start.2 = (bf16[256,1024]{1,0:T(8,128)(2,1)S(1)}, bf16[256,1024]{1,0:T(8,128)(2,1)}, u32[]{:S(2)}) copy-start(bf16[256,1024]{1,0:T(8,128)(2,1)} %get-tuple-element.70) | copy-start | bytes 1572868
  649.1 10.4 %copy-start.3 = (bf16[256,1024]{1,0:T(8,128)(2,1)S(1)}, bf16[256,1024]{1,0:T(8,128)(2,1)}, u32[]{:S(2)}) copy-start(bf16[256,1024]{1,0:T(8,128)(2,1)} %get-tuple-element.72) | copy-start | bytes 1572868
  661.0 4.5 copy-start

commit v7 on v6

--- a/solution.py
+++ b/solution.py
@@ -346,10 +346,10 @@
 
 
 def opening_kernel(
-    heads, query_ref, key_ref, value_ref, gate_ref, out_ref, token_ref, cot_ref, segment_ref, row_ref, rate_ref, gain_ref, bias_ref,
+    heads, query_ref, key_ref, value_ref, gate_ref, out_ref, down_ref, token_ref, cot_ref, segment_ref, row_ref, rate_ref, gain_ref, bias_ref,
     w_qkv_ref, w_gate_ref, w_out_ref, normed_ref, cot_all_ref, field_ref, gate_raw_ref, gated_ref, grouped_ref, scale_ref, past_ref,
-    angle_ref, info_ref, decay_ref,
-    w_qkv, w_gate, w_out, normed, product, blocks, angles, info, decay, state, field_out, gate_out, gated_out, grouped_out,
+    angle_ref, info_ref, decay_ref, down_turned_ref,
+    w_qkv, w_gate, w_out, tall, down_turned, normed, product, blocks, angles, info, decay, state, field_out, gate_out, gated_out, grouped_out,
     scale_out, past_out,
     local_sem, block_sem, out_sem, stage_sem, table_sem, up_send, up_recv, down_send, down_recv, core_send, core_recv,
     row_send, row_recv,
@@ -393,7 +393,7 @@
             (key_ref, w_qkv.at[mine, pl.ds(keys, keys)]),
             (value_ref, w_qkv.at[mine, pl.ds(2 * keys, values)]),
             (gate_ref, w_gate.at[mine]),
-            (out_ref, w_out.at[mine]),
+            (out_ref, tall),
             (segment_ref, info),
         ))
     ]
@@ -417,7 +417,7 @@
     pl.when(z < layers - 1)(lambda: greet(above))
     pl.when(z > 0)(lambda: greet(below))
     pl.semaphore_wait(barrier, 3 + (z < layers - 1).astype(jnp.int32) + (z > 0).astype(jnp.int32))
-    wait(local[:5])
+    wait(local[:4])
 
 
     groups = ((w_qkv, w_gate), (w_out,))
@@ -475,7 +475,24 @@
             def _():
                 wait_recv(from_twin(g, signed))
 
+    def rows_of(r, first=0, count=rows):
+        return pl.ds(r * rows + first, count)
+
+    def row_copy(index, src, dst, device):
+        return remote(src, dst, row_send.at[index], row_recv.at[index], device)
+
+    piece = 64
+    cot_early = [
+        row_copy(8, cot_ref.at[pl.ds(0, piece)], cot_all_ref.at[rows_of(1, 0, piece)], over_x),
+        row_copy(9, cot_ref.at[pl.ds(0, piece)], cot_all_ref.at[rows_of(2, 0, piece)], over_y),
+    ]
+    cot_over = [
+        row_copy(4, cot_ref.at[pl.ds(piece, rows - piece)], cot_all_ref.at[rows_of(1, piece, rows - piece)], over_x),
+        row_copy(5, cot_ref.at[pl.ds(piece, rows - piece)], cot_all_ref.at[rows_of(2, piece, rows - piece)], over_y),
+    ]
+
     first_step(0)
+    start(cot_early)
 
     @pl.loop(0, rows // 64)
     def _(i):
@@ -487,12 +504,6 @@
         @pl.when(i + 4 < rows // 64)
         def _():
             token_block(i + 4, slot).start()
-
-    def rows_of(r, first=0, count=rows):
-        return pl.ds(r * rows + first, count)
-
-    def row_copy(index, src, dst, device):
-        return remote(src, dst, row_send.at[index], row_recv.at[index], device)
 
     over = [
         row_copy(0, normed.at[rows_of(0)], normed.at[rows_of(1)], over_x),
@@ -502,15 +513,16 @@
         row_copy(2, normed.at[rows_of(2, 0, half)], normed.at[rows_of(3, 0, half)], over_x),
         row_copy(3, normed.at[rows_of(1, half, half)], normed.at[rows_of(3, half, half)], over_y),
     ]
-    cot_over = [
-        row_copy(4, cot_ref, cot_all_ref.at[rows_of(1)], over_x),
-        row_copy(5, cot_ref, cot_all_ref.at[rows_of(2)], over_y),
-    ]
     cot_onward = [
         row_copy(6, cot_all_ref.at[rows_of(2, 0, half)], cot_all_ref.at[rows_of(3, 0, half)], over_x),
         row_copy(7, cot_all_ref.at[rows_of(1, half, half)], cot_all_ref.at[rows_of(3, half, half)], over_y),
     ]
     start(over)
+
+    local[4].wait()
+    w_out[mine, :] = tall[...].T
+    down_load = pltpu.make_async_copy(down_ref, tall, local_sem.at[4])
+    down_load.start()
 
     local[5].wait()
     half_key = KEY // 2
@@ -537,7 +549,10 @@
     span = jnp.maximum(distance, 0).astype(f32)
     for head in range(heads):
         decay[head] = jnp.where(distance >= 0, jnp.exp(rate_ref[head : head + 1, 0:1] * span), 0.0)
+    down_load.wait()
+    down_turned[...] = tall[...].T
     table_outs = [
+        pltpu.make_async_copy(down_turned, down_turned_ref, table_sem.at[3]),
         pltpu.make_async_copy(angles, angle_ref, table_sem.at[0]),
         pltpu.make_async_copy(decay, decay_ref, table_sem.at[1]),
     ]
@@ -685,9 +700,9 @@
     start(w_outs)
 
     def between(c):
-        @pl.when(c == 3)
+        @pl.when(c == 2)
         def _():
-            wait_recv(cot_over)
+            wait_recv(cot_early + cot_over)
             start(cot_onward)
 
         @pl.when(c == 4)
@@ -704,7 +719,7 @@
     w_out_out.start()
     wait_recv(cot_onward)
 
-    wait_send(over + onward + cot_over + cot_onward)
+    wait_send(over + onward + cot_early + cot_over + cot_onward)
     for g in range(2):
         for j in range(3):
             pl.when((z < layers - 1) & (z - j >= 0))(lambda: wait_send(rise(g, j)))
@@ -718,7 +733,7 @@
     dp = lax.axis_size("dp")
     depth, keys = shards[0].shape
     values = shards[2].shape[1]
-    unit = shards[4].shape[1]
+    unit = shards[4].shape[0]
     token_rows, width = tokens.shape
     rows = 4 * token_rows
     chunks = rows // CHUNK
@@ -748,13 +763,16 @@
             jax.ShapeDtypeStruct((rows, KEY), f32),
             jax.ShapeDtypeStruct((rows, 128), f32),
             jax.ShapeDtypeStruct((heads, CHUNK, CHUNK), f32),
+            jax.ShapeDtypeStruct((depth, unit), bf16),
         ],
-        in_specs=[anywhere] * 8 + [in_vmem] * 4,
-        out_specs=[anywhere] * 14,
+        in_specs=[anywhere] * 9 + [in_vmem] * 4,
+        out_specs=[anywhere] * 15,
         scratch_shapes=[
             vmem((dp * depth, 2 * keys + values), bf16),
             vmem((dp * depth, values), bf16),
             vmem((dp * depth, unit), bf16),
+            vmem((unit, depth), bf16),
+            vmem((depth, unit), bf16),
             vmem((rows, width), bf16),
             vmem((rows, 2 * keys + 2 * values), f32),
             vmem((4, 64, width), bf16),
@@ -768,8 +786,8 @@
             vmem((CHUNK, values), bf16),
             vmem((CHUNK, 128), f32),
             vmem((heads, KEY, VAL), bf16),
-            sem((8,)), sem((4,)), sem((3,)), sem((6,)), sem((3,)),
-            sem((3, 3)), sem((3, 3)), sem((3, 3)), sem((3, 3)), sem((7, 3)), sem((7, 3)), sem((8,)), sem((8,)),
+            sem((8,)), sem((4,)), sem((3,)), sem((6,)), sem((4,)),
+            sem((3, 3)), sem((3, 3)), sem((3, 3)), sem((3, 3)), sem((7, 3)), sem((7, 3)), sem((10,)), sem((10,)),
         ],
         compiler_params=pltpu.CompilerParams(
             collective_id=2, has_side_effects=True, vmem_limit_bytes=63_400_000
@@ -946,12 +964,11 @@
             tile = block_of(j * 256, 256)
             terms[slot_of(r), :, tile] = dot_nt(units[0, rows_of(r)], units[1, tile]).astype(bf16)
 
-    def feed_grads():
+    def feed_grads(r):
         @pl.loop(0, unit // 256)
         def _(j):
             tile = block_of(j * 256, 256)
-            for r in range(4):
-                units[4, rows_of(r), tile] = dot_nn(big[rows_of(r)], units[3, :, tile]).astype(bf16)
+            units[4, rows_of(r), tile] = dot_nn(big[rows_of(r)], units[3, :, tile]).astype(bf16)
 
     def feed(r):
         @pl.loop(0, unit // 256)
@@ -982,19 +999,22 @@
     step(0, 3)
     cot_load.wait()
     gathered(0)
-    feed_grads()
+    step(1, 1)
+    feed_grads(0)
+    feed_grads(1)
+    step(1, 2)
+    feed_grads(2)
+    feed_grads(3)
     for side in sides:
         pl.semaphore_signal(big_free, inc=1, device_id=side, device_id_type=MESH)
-    step(1, 1)
-    step(1, 2)
     step(1, 3)
     gathered(1)
     token_load.wait()
+    pl.semaphore_wait(big_free, 2)
     for copy in fulls:
         copy.wait_recv()
 
-    @pl.loop(0, rows // 64)
-    def _(i):
+    def second_norm(i):
         place = block_of(i * 64, 64)
         value = plus[place].astype(f32) + terms[3, place].astype(f32)
         value = value + full_in[0, place].astype(f32) + full_in[1, place].astype(f32)
@@ -1002,10 +1022,12 @@
         plain, _ = normalize(value)
         big[place] = (plain * gain_ref[...] + bias_ref[...]).astype(bf16)
 
+    pl.loop(0, half // 64)(second_norm)
+    early[0].start()
+    pl.loop(half // 64, rows // 64)(second_norm)
+    early[1].start()
     for i, side in enumerate(sides):
         pl.semaphore_signal(full_free.at[i], inc=1, device_id=side, device_id_type=MESH)
-    pl.semaphore_wait(big_free, 2)
-    start(early)
     feed(0)
     for copy in halves + fulls:
         copy.wait_send()
@@ -1168,11 +1190,11 @@
     heads,
     normed1_ref, up_ref, down_ref, feed_ref, w_out_ref, w_qkv_ref, w_gate_ref,
     gate_ref, grouped_ref, gated_ref, scale_ref, field_ref, past_ref, angle_ref, info_ref,
-    low_ref, plus_ref, token_ref, row_ref, decay_ref, gain_ref, late_ref,
+    low_ref, token_ref, row_ref, decay_ref, gain_ref, late_ref,
     result_ref, grad_ref, query_out, key_out, value_out, gate_out, out_out, up_out, down_out, sums_ref,
     big, units, columns, terms, half_in, full_in, products, twin_in, line_in,
-    state_ref, past_in, scale_in, angle_in, info_in, blocks, given, landed, total,
-    unit_sem, column_sem, chunk_sem, block_sem, out_sem, mixed_sem, over_send, over_recv, onward_send, onward_recv,
+    state_ref, past_in, scale_in, angle_in, info_in, given, landed, total,
+    unit_sem, column_sem, chunk_sem, out_sem, mixed_sem, over_send, over_recv, onward_send, onward_recv,
     half_send, half_recv, full_send, full_recv, twin_send, twin_recv, line_send, line_recv, sum_send, sum_recv,
     twin_free, line_free, half_free, full_free,
 ):
@@ -1279,15 +1301,15 @@
         if sources[r] is not None:
             column_copy(r, k).wait()
 
-        @pl.loop(0, unit // 256)
+        @pl.loop(0, unit // 512)
         def _(j):
-            tile = block_of(j * 256, 256)
+            tile = block_of(j * 512, 512)
             product = None
             for place in (pl.ds(0, 2 * rows), pl.ds(2 * rows, 2 * rows)):
                 if r < 4:
                     right = units[(None, None, 0, 2)[r], place, tile]
                 else:
-                    right = big[place, block_of((r - 4) * unit + j * 256, 256)]
+                    right = big[place, block_of((r - 4) * unit + j * 512, 512)]
                 if sources[r] is None:
                     left = big[place, block_of(targets[k] * 2 * depth, 2 * depth)]
                 else:
@@ -1419,9 +1441,9 @@
     def project(r):
         slot = (2, 0, 1, 2)[r]
 
-        @pl.loop(0, width // 256)
+        @pl.loop(0, width // 512)
         def _(j):
-            tile = block_of(j * 256, 256)
+            tile = block_of(j * 512, 512)
             term = dot_nt(big[rows_of(r), pl.ds(0, unit)], units[1, tile])
             term = term + dot_nt(big[rows_of(r), pl.ds(unit, unit)], units[2, tile])
             term = term + dot_nt(units[0, rows_of(r)], units[3, tile])
@@ -1533,21 +1555,6 @@
                 big[place, pl.ds(2 * heads * KEY + head * VAL, VAL)] = value_grad.astype(bf16)
 
             between(step)
-
-
-    def block_copy(ref, i, slot):
-        return pltpu.make_async_copy(ref.at[block_of(i * 64, 64)], blocks.at[slot], block_sem.at[slot])
-
-    def stream(ref, use):
-        @pl.loop(0, rows // 64)
-        def _(i):
-            slot = lax.rem(i, 4)
-            block_copy(ref, i, slot).wait()
-            use(block_of(i * 64, 64), blocks[slot])
-
-            @pl.when(i + 4 < rows // 64)
-            def _():
-                block_copy(ref, i + 4, slot).start()
 
 
     own_load = pltpu.make_async_copy(low_ref, big.at[rows_of(0)], mixed_sem.at[0])
@@ -1630,10 +1637,10 @@
     produce(2, 3)
     settle(2, 3)
     start(chunk_copies(chunks - 1, 0))
+    take_halves(0)
     wait(gated_load)
     produce(3, 0)
     produce(3, 1, False)
-    take_halves(0)
     pass_on(2, 0)
     push(3, 0)
     produce(3, 2, False)
@@ -1669,27 +1676,20 @@
     wait(w_key_load)
     project(3)
     send_halves(1)
-    for i in range(4):
-        block_copy(plus_ref, i, i).start()
+    for copy in fulls:
+        copy.wait_recv()
+    result_copy = pltpu.make_async_copy(full_in, result_ref, mixed_sem.at[1])
+    result_copy.start()
     produce(4, 0)
     produce(4, 1)
     pass_on(3, 1)
-    for copy in fulls:
-        copy.wait_recv()
-
-    def add_result(place, value):
-        full_in[0, place] = (value.astype(f32) + full_in[0, place].astype(f32) + full_in[1, place].astype(f32)).astype(bf16)
-
-    stream(plus_ref, add_result)
-    result_copy = pltpu.make_async_copy(full_in.at[0], result_ref, mixed_sem.at[1])
-    result_copy.start()
-    for copy in fulls:
-        copy.wait_send()
-    pass_on(3, 2)
-    project(1)
     result_copy.wait()
     for i, side in enumerate(sides):
         pl.semaphore_signal(full_free.at[i], inc=1, device_id=side, device_id_type=MESH)
+    for copy in fulls:
+        copy.wait_send()
+    project(1)
+    pass_on(3, 2)
     project(2)
     take_halves(1)
     finish(3)
@@ -1706,13 +1706,14 @@
     pass_on(4, 2)
     produce(5, 3, False)
     settle(5, 3)
+    finish(4)
+    push(5, 2)
+    pass_on(5, 0)
     for copy in halves:
         copy.wait_send()
     project(0)
-    finish(4)
-    push(5, 2)
-    pass_on(5, 0)
     pass_on(5, 1)
+    pass_on(5, 2)
     for copy in fulls:
         copy.wait_recv()
         copy.wait_send()
@@ -1749,7 +1750,6 @@
     def _(k):
         sum_copy(k).start()
 
-    pass_on(5, 2)
     sums_ref[...] = given[lax.div(here, 2)]
 
     @pl.loop(1, peers)
@@ -1766,6 +1766,44 @@
                 along(r, k, 0, end).wait_send()
     wait(outputs(4) + outputs(5))
     grad_copy.wait()
+
+
+def cast_kernel(plus_ref, parts_ref, *refs):
+    count = len(refs) // 2
+    total = plus_ref[...].astype(f32) + parts_ref[0].astype(f32) + parts_ref[1].astype(f32)
+    refs[count][...] = total.astype(bf16)
+    for i, (source, target) in enumerate(zip(refs[:count], refs[count + 1 :])):
+        value = source[...].astype(target.dtype)
+        target[...] = value.T if i >= count - 2 else value
+
+
+def cast_all(plus, parts, arrays):
+    steps = 2
+
+    def slab(rows, width):
+        return pl.BlockSpec((rows // steps, width), lambda j: (j, 0))
+
+    rows, width = plus.shape
+    in_specs = [slab(rows, width), pl.BlockSpec((2, rows // steps, width), lambda j: (0, j, 0))]
+    out_specs, shapes = [slab(rows, width)], [jax.ShapeDtypeStruct(plus.shape, bf16)]
+    for i, v in enumerate(arrays):
+        rows, width = v.shape
+        in_specs.append(slab(rows, width))
+        if i >= len(arrays) - 2:
+            out_specs.append(pl.BlockSpec((width, rows // steps), lambda j: (0, j)))
+            shapes.append(jax.ShapeDtypeStruct((width, rows), f32))
+        else:
+            out_specs.append(slab(rows, width))
+            shapes.append(jax.ShapeDtypeStruct((rows, width), bf16 if i == 0 else f32))
+    return pl.pallas_call(
+        cast_kernel,
+        grid=(steps,),
+        in_specs=in_specs,
+        out_specs=out_specs,
+        out_shape=shapes,
+        compiler_params=pltpu.CompilerParams(vmem_limit_bytes=60 * 1024 * 1024),
+        name="last_casts",
+    )(plus, parts, *arrays)
 
 
 def closing_exchange(heads, operands, small):
@@ -1782,7 +1820,7 @@
     return pl.pallas_call(
         functools.partial(closing_kernel, heads),
         out_shape=[
-            jax.ShapeDtypeStruct((token_rows, width), bf16),
+            jax.ShapeDtypeStruct((2, token_rows, width), bf16),
             jax.ShapeDtypeStruct((token_rows, width), bf16),
             jax.ShapeDtypeStruct((depth, keys), bf16),
             jax.ShapeDtypeStruct((depth, keys), bf16),
@@ -1810,11 +1848,10 @@
             vmem((2, CHUNK, 128), f32),
             vmem((2, CHUNK, KEY), f32),
             vmem((2, CHUNK, 128), f32),
-            vmem((4, 64, width), bf16),
             vmem((16, 8, 128), f32),
             vmem((32, 8, 128), f32),
             vmem((8, width), f32),
-            sem((10,)), sem((8,)), sem((2, 12)), sem((4,)), sem((2, 2)), sem((4,)),
+            sem((10,)), sem((8,)), sem((2, 12)), sem((2, 2)), sem((4,)),
             sem((2,)), sem((2,)), sem((2,)), sem((2,)),
             sem((2,)), sem((2,)), sem((2,)), sem((2,)),
             sem((2, 4)), sem((2,)), sem((2, 3)), sem((5,)), sem((32,)), sem((32,)),
@@ -1838,28 +1875,28 @@
         return [values[i * rows : (i + 1) * rows] for i in range(devices)]
 
     if devices == 4 and lax.axis_size("dp") == 8:
-        shards = (query_weight, key_weight, value_weight, gate_weight, out_weight.T)
+        shards = (query_weight, key_weight, value_weight, gate_weight, out_weight, down_weight)
         opened, keys = opening_exchange(heads, shards, tokens, cotangent, segment, first_gain, first_bias)
-        w_qkv, w_gate, w_out, normed1_all, cot_all, field, gate, gated, grouped, group_scale, past, angles, info, decay = opened
+        w_qkv, w_gate, w_out, normed1_all, cot_all, field, gate, gated, grouped, group_scale, past = opened[:11]
+        angles, info, decay, down_shard = opened[11:]
         mixed_low, plus, feed_terms, up_weight_grad, down_weight_grad, late = middle_exchange(
-            gated, w_out, up_weight, down_weight.T, cot_all, tokens, second_gain, second_bias
+            gated, w_out, up_weight, down_shard, cot_all, tokens, second_gain, second_bias
         )
-        result, input_grad, query_sum, key_sum, value_sum, gate_sum, out_sum, up_sum, down_sum, sums = closing_exchange(
+        parts, input_grad, query_sum, key_sum, value_sum, gate_sum, out_sum, up_sum, down_sum, sums = closing_exchange(
             heads,
             (
                 normed1_all, up_weight_grad, down_weight_grad, feed_terms, w_out, w_qkv, w_gate,
                 gate, grouped, gated, group_scale, field, past, angles, info,
-                mixed_low, plus, tokens,
+                mixed_low, tokens,
             ),
             (keys, decay, first_gain.reshape(1, -1), late),
         )
         part = first_gain.shape[0] // 32
         sums = lax.dynamic_slice_in_dim(sums, (here % 2) * part, part, 1)
         norm_sums = [sums[0], sums[1], sums[2], sums[3]]
-        query_sum, key_sum, value_sum, gate_sum, up_sum = (
-            v.astype(f32) for v in (query_sum, key_sum, value_sum, gate_sum, up_sum)
+        result, input_grad, query_sum, key_sum, value_sum, gate_sum, up_sum, out_sum, down_sum = cast_all(
+            plus, parts, (input_grad, query_sum, key_sum, value_sum, gate_sum, up_sum, out_sum, down_sum)
         )
-        out_sum, down_sum = out_sum.astype(f32).T, down_sum.astype(f32).T
     else:
         w_qkv = lax.all_gather(
             jnp.concatenate([query_weight, key_weight, value_weight], axis=1), "dp", axis=0, tiled=True

time: 677 us -> 652 us (0.963)
  local copies, waits for them, and re-layouts: 14.6 us -> 2.58 us
  other arithmetic: 10.6 us -> 1.39 us
    unnamed x14 -> x2, local copies, waits for them, and re-layouts: 11.2 us -> 0.01 us
    convert_element_type x5 -> x0, other arithmetic: 8.94 us -> none  [body(): v.astype(f32)]
    pallas_call x0 -> x1, Pallas kernels: none -> 8.18 us  [cast_all(): pl.pallas_call(cast_kernel, grid=(steps,), in_specs=in_specs, out_specs=o...]
    pallas_call x1, Pallas kernels: 248 us -> 240 us  [closing_exchange(): pl.pallas_call(functools.partial(closing_kernel, heads), out_shape=[jax.S...]
where the time goes in v7:
time: 652 us; the launch traced here: 643 us
  Pallas kernels  638 us (98%)
    pallas_call x1, Pallas kernels, closing_exchange(): pl.pallas_call(functools.partial(closing_kernel, heads), out_shape=[jax.S...  240 us
    pallas_call x1, Pallas kernels, middle_exchange(): pl.pallas_call(middle_kernel, out_shape=[jax.ShapeDtypeStruct((token_rows...  231 us
    pallas_call x1, Pallas kernels, opening_exchange(): pl.pallas_call(functools.partial(opening_kernel, heads), out_shape=[jax.S...  159 us

profile of v7, /device:TPU:0, one launch (start us, length us, event | category | flops | bytes accessed | tf_op | source)
XLA Modules:
  0.0 643.2 jit_solution(11219228781331879608)
XLA Ops:
  0.6 1.4 fusion
  2.0 1.3 broadcast_in_dim.7.segment_ref
  3.3 0.7 broadcast_in_dim.18.rate_ref
  4.0 158.8 %opening_exchange.1 = (bf16[2048,2048]{1,0:T(8,128)(2,1)}, bf16[2048,1024]{1,0:T(8,128)(2,1)}, bf16[2048,1024]{1,0:T(8,128)(2,1)}, bf16[2048,2048]{1,0:T(8,128)(...) custom-call(bf16[256,512]{1,0:T(8,128)(2,1)} %query_ref.1, ...), custom_call_target="tpu_custom_call" | custom-call | tf_op jit(solution)/shard_map/opening_exchange/pallas_call | solution.py:749
  162.8 230.9 %middle_exchange.1 = (bf16[512,2048]{1,0:T(8,128)(2,1)}, bf16[512,2048]{1,0:T(8,128)(2,1)}, bf16[2048,2048]{1,0:T(8,128)(2,1)}, bf16[2048,1024]{1,0:T(8,128)(2,1...) custom-call(bf16[2048,1024]{1,0:T(8,128)(2,1)} %get-tuple-element.53.gated_ref, ...), custom_call_target="tpu_custom_call" | custom-call | tf_op jit(solution)/shard_map/middle_exchange/pallas_call | solution.py:1154
  393.7 240.2 %closing_exchange.1 = (bf16[2,512,2048]{2,1,0:T(8,128)(2,1)}, bf16[512,2048]{1,0:T(8,128)(2,1)}, bf16[256,512]{1,0:T(8,128)(2,1)}, bf16[256,512]{1,0:T(8,128)(2,...) custom-call(bf16[2048,2048]{1,0:T(8,128)(2,1)} %get-tuple-element.58, ...), custom_call_target="tpu_custom_call" | custom-call | tf_op jit(solution)/shard_map/closing_exchange/pallas_call | solution.py:1820
  633.9 0.0 copy-start
  634.0 8.2 %last_casts.1 = (bf16[512,2048]{1,0:T(8,128)(2,1)}, bf16[512,2048]{1,0:T(8,128)(2,1)}, f32[256,512]{1,0:T(8,128)}, f32[256,512]{1,0:T(8,128)}, f32[256,1024]{1,0...) custom-call(bf16[512,2048]{1,0:T(8,128)(2,1)} %get-tuple-element.57.plus_ref, ...), custom_call_target="tpu_custom_call" | custom-call | tf_op jit(solution)/shard_map/last_casts/pallas_call | solution.py:1798
  642.1 0.0 copy-done
  642.2 0.1 constant_dynamic-slice_fusion
  642.2 0.5 slice_bitcast_fusion
  (1 shorter events, 0.0 us)
Async XLA Ops:
  633.9 8.2 %copy-start = (f32[8,128]{1,0:T(8,128)S(1)}, f32[8,128]{1,0:T(8,128)}, u32[]{:S(2)}) copy-start(f32[8,128]{1,0:T(8,128)} %get-tuple-element.85) | copy-start | bytes 12292

commit v8 on v7

--- a/solution.py
+++ b/solution.py
@@ -916,10 +916,16 @@
         remote(terms.at[2, pl.ds(0, half)], half_in.at[0], half_send.at[0], half_recv.at[0], over_x),
         remote(terms.at[2, pl.ds(half, half)], half_in.at[1], half_send.at[1], half_recv.at[1], over_y),
     ]
-    fulls = [
-        remote(terms.at[0], full_in.at[0], full_send.at[0], full_recv.at[0], over_x),
-        remote(terms.at[1], full_in.at[1], full_send.at[1], full_recv.at[1], over_y),
-    ]
+
+    def part_copy(index, term, first, device):
+        place = pl.ds(first, half)
+        return remote(
+            terms.at[term, place], full_in.at[term, place], full_send.at[index], full_recv.at[index], device
+        )
+
+    plain_parts = [part_copy(0, 0, 0, over_x), part_copy(1, 1, half, over_y)]
+    grown_parts = [part_copy(2, 0, half, over_x), part_copy(3, 1, 0, over_y)]
+    fulls = plain_parts + grown_parts
     lower, upper = (0, half), (half, half)
 
     def row_copy(index, source, first, target, device):
@@ -948,12 +954,15 @@
                 grown = terms[term, place].astype(f32) + half_in[slot, block_of(i * 64, 64)].astype(f32)
                 terms[term, place] = grown.astype(bf16)
 
-        for i, copy in enumerate(fulls):
+        for i, copy in enumerate(grown_parts):
             if stage == 0:
                 pl.semaphore_signal(half_free.at[i], inc=1, device_id=sides[i], device_id_type=MESH)
-            else:
-                pl.semaphore_wait(full_free.at[i], 1)
             copy.start()
+
+    def send_plain(stage, i):
+        if stage == 1:
+            pl.semaphore_wait(full_free.at[i], 1)
+        plain_parts[i].start()
 
     def slot_of(r):
         return (3, 0, 1, 2)[r]
@@ -991,7 +1000,9 @@
     send_halves(0)
     step(0, 1)
     branch_term(1)
+    send_plain(0, 0)
     branch_term(2)
+    send_plain(0, 1)
     step(0, 2)
     first_step(1)
     take_halves(0)
@@ -1050,9 +1061,11 @@
     for copy in late:
         copy.wait_recv()
     feed(1)
+    back_term(1)
+    send_plain(1, 0)
     feed(2)
-    back_term(1)
     back_term(2)
+    send_plain(1, 1)
     take_halves(1)
 
     def staged_out(out, t, slot):
@@ -1176,7 +1189,7 @@
             vmem((2, width), f32),
             sem((8,)), sem((4,)), sem((2,)), sem((2,)), sem((2,)),
             sem((2, 3)), sem((2, 3)), sem((2, 3)), sem((2, 3)), sem((2, 7)), sem((2, 7)),
-            sem((6,)), sem((6,)), sem((2,)), sem((2,)), sem((2,)), sem((2,)),
+            sem((6,)), sem((6,)), sem((2,)), sem((2,)), sem((4,)), sem((4,)),
             regular((2,)), regular((2,)), regular,
         ],
         compiler_params=pltpu.CompilerParams(
@@ -1259,6 +1272,14 @@
     w_value_load = part(2, w_qkv_ref, unit, 8)
     w_key_load = part(1, w_qkv_ref, 0, 9)
 
+    def wait_recv(copies):
+        for copy in copies:
+            copy.wait_recv()
+
+    def wait_send(copies):
+        for copy in copies:
+            copy.wait_send()
+
 
     sources = [up_ref, down_ref, normed1_ref, None, normed1_ref, normed1_ref]
 
@@ -1320,6 +1341,8 @@
 
         if sources[r] is not None and k + 2 < 4:
             column_copy(r, k + 2).start()
+        elif r == 4:
+            column_copy(5, k - 2).start()
         send_to_twin(r, k)
 
     def add_to_mine(r, k, others):
@@ -1409,10 +1432,16 @@
         remote(terms.at[2, pl.ds(0, half)], half_in.at[0], half_send.at[0], half_recv.at[0], over_x),
         remote(terms.at[2, pl.ds(half, half)], half_in.at[1], half_send.at[1], half_recv.at[1], over_y),
     ]
-    fulls = [
-        remote(terms.at[0], full_in.at[0], full_send.at[0], full_recv.at[0], over_x),
-        remote(terms.at[1], full_in.at[1], full_send.at[1], full_recv.at[1], over_y),
-    ]
+
+    def part_copy(index, term, first, device):
+        place = pl.ds(first, half)
+        return remote(
+            terms.at[term, place], full_in.at[term, place], full_send.at[index], full_recv.at[index], device
+        )
+
+    plain_parts = [part_copy(0, 0, 0, over_x), part_copy(1, 1, half, over_y)]
+    grown_parts = [part_copy(2, 0, half, over_x), part_copy(3, 1, 0, over_y)]
+    fulls = plain_parts + grown_parts
     sides = (over_x, over_y)
 
     def send_halves(stage):
@@ -1431,12 +1460,15 @@
                 grown = terms[term, place].astype(f32) + half_in[slot, block_of(i * 64, 64)].astype(f32)
                 terms[term, place] = grown.astype(bf16)
 
-        for i, copy in enumerate(fulls):
+        for i, copy in enumerate(grown_parts):
             if stage == 0:
                 pl.semaphore_signal(half_free.at[i], inc=1, device_id=sides[i], device_id_type=MESH)
-            else:
-                pl.semaphore_wait(full_free.at[i], 1)
             copy.start()
+
+    def send_plain(stage, i):
+        if stage == 1:
+            pl.semaphore_wait(full_free.at[i], 1)
+        plain_parts[i].start()
 
     def project(r):
         slot = (2, 0, 1, 2)[r]
@@ -1459,22 +1491,26 @@
             )
             for i, ref in enumerate((gate_ref, grouped_ref))
             for h in range(heads)
-        ]
+        ] + [pltpu.make_async_copy(scale_ref.at[rows_of(r)], scale_in.at[r % 2], chunk_sem.at[r % 2, 2 * heads])]
 
     def gate_back(r):
         wait(gate_copies(r))
-
-        @pl.loop(0, unit // 256)
-        def _(j):
-            grad = dot_nn(big[rows_of(r)], units[3, :, block_of(j * 256, 256)])
-            head = lax.div(j, VAL // 256)
-            inner = block_of(lax.rem(j, VAL // 256) * 256, 256)
-            raw = columns[r % 2, block_of(head * rows, rows), inner].astype(f32)
-            grouped = columns[r % 2, block_of((heads + head) * rows, rows), inner].astype(f32)
-            sigmoid = 1.0 / (1.0 + jnp.exp(-raw))
-            tile = block_of(j * 256, 256)
-            units[0, rows_of(r), tile] = (grad * grouped * (sigmoid * (1.0 + raw * (1.0 - sigmoid)))).astype(bf16)
-            units[1, rows_of(r), tile] = grad.astype(bf16)
+        for head in range(heads):
+            tile = pl.ds(head * VAL, VAL)
+
+            @pl.loop(0, rows // CHUNK)
+            def _(i):
+                place = block_of(r * rows + i * CHUNK, CHUNK)
+                grad = dot_nn(big[place], units[3, :, tile])
+                raw = columns[r % 2, block_of(head * rows + i * CHUNK, CHUNK)].astype(f32)
+                grouped = columns[r % 2, block_of((heads + head) * rows + i * CHUNK, CHUNK)].astype(f32)
+                sigmoid = 1.0 / (1.0 + jnp.exp(-raw))
+                units[0, place, tile] = (grad * grouped * (sigmoid * (1.0 + raw * (1.0 - sigmoid)))).astype(bf16)
+                c = grad * (raw * sigmoid)
+                mean_c = jnp.mean(c, axis=-1, keepdims=True)
+                mean_cx = jnp.mean(c * grouped, axis=-1, keepdims=True)
+                scale = scale_in[r % 2, block_of(i * CHUNK, CHUNK), head : head + 1]
+                units[1, place, tile] = (scale * (c - mean_c - grouped * mean_cx)).astype(bf16)
 
     chunks = 4 * rows // CHUNK
     per_piece = rows // CHUNK
@@ -1495,11 +1531,8 @@
         ]
         for h in range(heads):
             pieces.append((field_ref.at[place, pl.ds(2 * keys + h * VAL, VAL)], columns.at[slot, pl.ds((2 + h) * CHUNK, CHUNK)]))
-            pieces.append((gate_ref.at[place, pl.ds(h * VAL, VAL)], columns.at[slot, pl.ds((4 + h) * CHUNK, CHUNK)]))
-            pieces.append((grouped_ref.at[place, pl.ds(h * VAL, VAL)], columns.at[slot, pl.ds((6 + h) * CHUNK, CHUNK)]))
         pieces += [
             (past_ref.at[c], past_in.at[slot]),
-            (scale_ref.at[place], scale_in.at[slot]),
             (angle_ref.at[seat], angle_in.at[slot]),
             (info_ref.at[seat], info_in.at[slot]),
         ]
@@ -1529,17 +1562,10 @@
                 key = turn(columns[slot, pl.ds(CHUNK, CHUNK), at].astype(f32), cosine, sine)
                 key = (key * key_scale).astype(bf16)
                 value = columns[slot, pl.ds((2 + head) * CHUNK, CHUNK)]
-                gate = columns[slot, pl.ds((4 + head) * CHUNK, CHUNK)].astype(f32)
-                grouped = columns[slot, pl.ds((6 + head) * CHUNK, CHUNK)].astype(f32)
                 into = info[:, 1 + 2 * head : 2 + 2 * head]
                 onto = info[:, 2 + 2 * head : 3 + 2 * head]
-                scale = scale_in[slot, :, head : head + 1]
                 past = past_in[slot, head]
-                out_grad_in = units[1, place, pl.ds(head * VAL, VAL)].astype(f32)
-                c_in = out_grad_in * (gate / (1.0 + jnp.exp(-gate)))
-                mean_c = jnp.mean(c_in, axis=-1, keepdims=True)
-                mean_cx = jnp.mean(c_in * grouped, axis=-1, keepdims=True)
-                out_grad = (scale * (c_in - mean_c - grouped * mean_cx)).astype(bf16)
+                out_grad = units[1, place, pl.ds(head * VAL, VAL)]
                 state = state_ref[head]
                 state_low = state.astype(bf16)
                 masked = jnp.where(same, decay_ref[head], 0.0)
@@ -1563,6 +1589,7 @@
         for k in range(4):
             given_copy(r, k).start()
     start(out_load)
+    start(gated_load)
     start(gate_copies(0))
     start(gate_copies(1))
     start(feed_load)
@@ -1587,131 +1614,135 @@
         if k > 0:
             settle(0, k - 1)
             push(0, k - 1)
-    settle(0, 3)
     for k in range(4):
         given_copy(1, k).wait()
         send_to_twin(1, k)
-        if k > 0:
-            settle(1, k - 1)
-    settle(1, 3)
+        settle(*((1, k - 1) if k > 0 else (0, 3)))
     wait(out_load)
+    pass_on(0, 0)
+    pass_on(0, 1)
+    push(1, 0)
     gate_back(0)
     start(gate_copies(2))
-    pass_on(0, 0)
-    push(1, 0)
-    pass_on(0, 1)
     push(1, 1)
-    pass_on(0, 2)
-    for copy in over:
-        copy.wait_recv()
+    wait_recv(over)
     start(onward)
     gate_back(1)
     start(gate_copies(3))
+    settle(1, 3)
+    gate_back(2)
+    pass_on(0, 2)
+    pass_on(1, 0)
     finish(0)
+    pass_on(1, 1)
     push(1, 2)
-    gate_back(2)
-    pass_on(1, 0)
-    pass_on(1, 1)
+    wait_recv(onward)
     wait(feed_load)
-    start(gated_load)
-    for copy in onward:
-        copy.wait_recv()
     send_halves(0)
+    send_plain(0, 0)
+    send_plain(0, 1)
     gate_back(3)
     prefetch(2)
     start(w_gate_load)
+    multiply(2, 0)
     pass_on(1, 2)
+    settle(2, 0)
+    push(2, 0)
+    multiply(2, 1)
+    multiply(2, 2)
+    settle(2, 1)
+    multiply(2, 3)
+    start(chunk_copies(chunks - 1, 0))
+    settle(2, 2)
+    finish(1)
+    push(2, 1)
+    wait(gated_load)
+    multiply(3, 0)
+    pass_on(2, 0)
+    settle(2, 3)
+    multiply(3, 1)
+    settle(3, 0)
+    multiply(3, 2)
+    push(2, 2)
+    settle(3, 1)
+    multiply(3, 3)
+    start(w_value_load)
+    wait_send(over + onward)
     state_ref[...] = jnp.zeros_like(state_ref)
 
-    def produce(r, k, pushed=True):
-        multiply(r, k)
-        if k > 0:
-            settle(r, k - 1)
-            if pushed:
-                push(r, k - 1)
-
-    produce(2, 0)
-    produce(2, 1)
-    finish(1)
-    produce(2, 2)
-    produce(2, 3)
-    settle(2, 3)
-    start(chunk_copies(chunks - 1, 0))
-    take_halves(0)
-    wait(gated_load)
-    produce(3, 0)
-    produce(3, 1, False)
-    pass_on(2, 0)
-    push(3, 0)
-    produce(3, 2, False)
-    produce(3, 3, False)
-    settle(3, 3)
-    start(w_value_load)
-    for copy in over + onward:
-        copy.wait_send()
-
     def between(step):
+        @pl.when(step == 0)
+        def _():
+            push(3, 0)
+
         @pl.when(step == 1)
         def _():
             pass_on(2, 1)
-            push(3, 1)
-
-        @pl.when(step == 2)
+
+        @pl.when(step == 4)
         def _():
-            pass_on(2, 2)
+            take_halves(0)
 
         @pl.when(step == 5)
         def _():
-            finish(2)
-            push(3, 2)
+            settle(3, 2)
+            pass_on(2, 2)
+            push(3, 1)
 
     retention_steps(between)
     start(w_key_load)
     prefetch(4)
+    wait_send(halves)
+    wait(w_gate_load + w_value_load + w_key_load)
+    project(3)
     pass_on(3, 0)
-    for copy in halves:
-        copy.wait_send()
-    wait(w_gate_load)
-    wait(w_value_load)
-    wait(w_key_load)
-    project(3)
+    settle(3, 3)
     send_halves(1)
-    for copy in fulls:
-        copy.wait_recv()
+    push(3, 2)
+    finish(2)
+    multiply(4, 0)
+    settle(4, 0)
+    multiply(4, 1)
+    pass_on(3, 1)
+    push(4, 0)
+    wait_recv(fulls)
     result_copy = pltpu.make_async_copy(full_in, result_ref, mixed_sem.at[1])
     result_copy.start()
-    produce(4, 0)
-    produce(4, 1)
-    pass_on(3, 1)
     result_copy.wait()
     for i, side in enumerate(sides):
         pl.semaphore_signal(full_free.at[i], inc=1, device_id=side, device_id_type=MESH)
-    for copy in fulls:
-        copy.wait_send()
+    wait_send(fulls)
     project(1)
+    send_plain(1, 0)
     pass_on(3, 2)
+    settle(4, 1)
+    multiply(4, 2)
+    push(4, 1)
     project(2)
+    send_plain(1, 1)
+    settle(4, 2)
+    push(4, 2)
+    multiply(4, 3)
+    pass_on(4, 0)
+    finish(3)
+    multiply(5, 0)
+    settle(4, 3)
+    multiply(5, 1)
+    settle(5, 0)
+    pass_on(4, 1)
+    settle(5, 1)
+    push(5, 0)
+    pass_on(4, 2)
+    multiply(5, 2)
     take_halves(1)
-    finish(3)
-    produce(4, 2)
-    produce(4, 3, False)
-    push(4, 2)
-    settle(4, 3)
-    prefetch(5)
-    pass_on(4, 0)
-    produce(5, 0)
-    produce(5, 1)
-    pass_on(4, 1)
-    produce(5, 2)
-    pass_on(4, 2)
-    produce(5, 3, False)
-    settle(5, 3)
+    multiply(5, 3)
+    pass_on(5, 0)
+    push(5, 1)
     finish(4)
+    wait_send(halves)
+    project(0)
+    settle(5, 2)
     push(5, 2)
-    pass_on(5, 0)
-    for copy in halves:
-        copy.wait_send()
-    project(0)
     pass_on(5, 1)
     pass_on(5, 2)
     for copy in fulls:
@@ -1757,6 +1788,7 @@
         sum_copy(k).wait()
         sums_ref[...] += landed[k]
 
+    settle(5, 3)
     finish(5)
 
     for r in (4, 5):
@@ -1845,7 +1877,7 @@
             vmem((5, depth, unit), bf16),
             vmem((heads, KEY, VAL), f32),
             vmem((2, heads, KEY, VAL), bf16),
-            vmem((2, CHUNK, 128), f32),
+            vmem((2, token_rows, 128), f32),
             vmem((2, CHUNK, KEY), f32),
             vmem((2, CHUNK, 128), f32),
             vmem((16, 8, 128), f32),
@@ -1853,7 +1885,7 @@
             vmem((8, width), f32),
             sem((10,)), sem((8,)), sem((2, 12)), sem((2, 2)), sem((4,)),
             sem((2,)), sem((2,)), sem((2,)), sem((2,)),
-            sem((2,)), sem((2,)), sem((2,)), sem((2,)),
+            sem((2,)), sem((2,)), sem((4,)), sem((4,)),
             sem((2, 4)), sem((2,)), sem((2, 3)), sem((5,)), sem((32,)), sem((32,)),
             regular((2,)), regular((3,)), regular((2,)), regular((2,)),
         ],

time: 652 us -> 641 us (0.983)
  Pallas kernels: 638 us -> 627 us
where the time goes in v8:
time: 641 us; the launch traced here: 632 us
  Pallas kernels  627 us (98%)
    pallas_call x1, Pallas kernels, closing_exchange(): pl.pallas_call(functools.partial(closing_kernel, heads), out_shape=[jax.S...  234 us
    pallas_call x1, Pallas kernels, middle_exchange(): pl.pallas_call(middle_kernel, out_shape=[jax.ShapeDtypeStruct((token_rows...  226 us
    pallas_call x1, Pallas kernels, opening_exchange(): pl.pallas_call(functools.partial(opening_kernel, heads), out_shape=[jax.S...  159 us

profile of v8, /device:TPU:0, one launch (start us, length us, event | category | flops | bytes accessed | tf_op | source)
XLA Modules:
  0.0 632.2 jit_solution(9812803625681977236)
XLA Ops:
  0.6 1.4 fusion
  2.0 1.3 broadcast_in_dim.7.segment_ref
  3.3 0.7 broadcast_in_dim.18.rate_ref
  4.0 158.8 %opening_exchange.1 = (bf16[2048,2048]{1,0:T(8,128)(2,1)}, bf16[2048,1024]{1,0:T(8,128)(2,1)}, bf16[2048,1024]{1,0:T(8,128)(2,1)}, bf16[2048,2048]{1,0:T(8,128)(...) custom-call(bf16[256,512]{1,0:T(8,128)(2,1)} %query_ref.1, ...), custom_call_target="tpu_custom_call" | custom-call | tf_op jit(solution)/shard_map/opening_exchange/pallas_call | solution.py:749
  162.8 226.3 %middle_exchange.1 = (bf16[512,2048]{1,0:T(8,128)(2,1)}, bf16[512,2048]{1,0:T(8,128)(2,1)}, bf16[2048,2048]{1,0:T(8,128)(2,1)}, bf16[2048,1024]{1,0:T(8,128)(2,1...) custom-call(bf16[2048,1024]{1,0:T(8,128)(2,1)} %get-tuple-element.53.gated_ref, ...), custom_call_target="tpu_custom_call" | custom-call | tf_op jit(solution)/shard_map/middle_exchange/pallas_call | solution.py:1167
  389.1 233.8 %closing_exchange.1 = (bf16[2,512,2048]{2,1,0:T(8,128)(2,1)}, bf16[512,2048]{1,0:T(8,128)(2,1)}, bf16[256,512]{1,0:T(8,128)(2,1)}, bf16[256,512]{1,0:T(8,128)(2,...) custom-call(bf16[2048,2048]{1,0:T(8,128)(2,1)} %get-tuple-element.58, ...), custom_call_target="tpu_custom_call" | custom-call | tf_op jit(solution)/shard_map/closing_exchange/pallas_call | solution.py:1852
  622.9 0.0 copy-start
  622.9 8.2 %last_casts.1 = (bf16[512,2048]{1,0:T(8,128)(2,1)}, bf16[512,2048]{1,0:T(8,128)(2,1)}, f32[256,512]{1,0:T(8,128)}, f32[256,512]{1,0:T(8,128)}, f32[256,1024]{1,0...) custom-call(bf16[512,2048]{1,0:T(8,128)(2,1)} %get-tuple-element.57.plus_ref, ...), custom_call_target="tpu_custom_call" | custom-call | tf_op jit(solution)/shard_map/last_casts/pallas_call | solution.py:1830
  631.1 0.0 copy-done
  631.1 0.1 constant_dynamic-slice_fusion
  631.2 0.5 slice_bitcast_fusion
  (1 shorter events, 0.0 us)
Async XLA Ops:
  622.9 8.2 %copy-start = (f32[8,128]{1,0:T(8,128)S(1)}, f32[8,128]{1,0:T(8,128)}, u32[]{:S(2)}) copy-start(f32[8,128]{1,0:T(8,128)} %get-tuple-element.85) | copy-start | bytes 12292

commit v9 on v8

--- a/solution.py
+++ b/solution.py
@@ -346,12 +346,12 @@
 
 
 def opening_kernel(
-    heads, query_ref, key_ref, value_ref, gate_ref, out_ref, down_ref, token_ref, cot_ref, segment_ref, row_ref, rate_ref, gain_ref, bias_ref,
+    heads, query_ref, key_ref, value_ref, gate_ref, out_ref, down_ref, token_ref, cot_ref, row_ref, rate_ref, gain_ref, bias_ref,
     w_qkv_ref, w_gate_ref, w_out_ref, normed_ref, cot_all_ref, field_ref, gate_raw_ref, gated_ref, grouped_ref, scale_ref, past_ref,
     angle_ref, info_ref, decay_ref, down_turned_ref,
-    w_qkv, w_gate, w_out, tall, down_turned, normed, product, blocks, angles, info, decay, state, field_out, gate_out, gated_out, grouped_out,
+    w_qkv, w_gate, w_out, tall, normed, product, angles, info, decay, state, field_out, gate_out, gated_out, grouped_out,
     scale_out, past_out,
-    local_sem, block_sem, out_sem, stage_sem, table_sem, up_send, up_recv, down_send, down_recv, core_send, core_recv,
+    local_sem, token_sem, out_sem, stage_sem, table_sem, up_send, up_recv, down_send, down_recv, core_send, core_recv,
     row_send, row_recv,
 ):
     dp = lax.axis_index("dp")
@@ -359,7 +359,7 @@
     z = lax.div(dp, 2)
     layers = 4
     depth = query_ref.shape[0]
-    rows = token_ref.shape[0]
+    rows, width = token_ref.shape
     half = rows // 2
     above = (dp + 2, tensor)
     below = (dp - 2, tensor)
@@ -394,16 +394,17 @@
             (value_ref, w_qkv.at[mine, pl.ds(2 * keys, values)]),
             (gate_ref, w_gate.at[mine]),
             (out_ref, tall),
-            (segment_ref, info),
         ))
     ]
     start(local)
 
-    def token_block(i, slot):
-        return pltpu.make_async_copy(token_ref.at[block_of(i * 64, 64)], blocks.at[slot], block_sem.at[slot])
-
-    for i in range(4):
-        token_block(i, i).start()
+    half_width = width // 2
+    token_loads = [
+        pltpu.make_async_copy(token_ref.at[pl.ds(0, half)], field_out, token_sem.at[0]),
+        pltpu.make_async_copy(token_ref.at[pl.ds(half, half), pl.ds(0, half_width)], gated_out, token_sem.at[1]),
+        pltpu.make_async_copy(token_ref.at[pl.ds(half, half), pl.ds(half_width, half_width)], grouped_out, token_sem.at[2]),
+    ]
+    start(token_loads)
     own_cot = pltpu.make_async_copy(cot_ref, cot_all_ref.at[pl.ds(0, rows)], local_sem.at[6])
     own_cot.start()
 
@@ -468,6 +469,9 @@
             if j < 3:
                 pl.when(z > 0)(lambda: start(sink(g, j)))
             start(to_twin(g, j))
+
+    def when_end(wanted, work):
+        pl.when(((z == 0) | (z == 3)) == wanted)(work)
 
     def twin_step(g, j):
         for signed in sorted({-j, j}):
@@ -494,16 +498,20 @@
     first_step(0)
     start(cot_early)
 
-    @pl.loop(0, rows // 64)
+    wait(token_loads)
+
+    @pl.loop(0, half // 64)
     def _(i):
-        slot = lax.rem(i, 4)
-        token_block(i, slot).wait()
-        plain, _ = normalize(blocks[slot].astype(f32))
-        normed[block_of(i * 64, 64), :] = (plain * gain_ref[...] + bias_ref[...]).astype(bf16)
-
-        @pl.when(i + 4 < rows // 64)
-        def _():
-            token_block(i + 4, slot).start()
+        place = block_of(i * 64, 64)
+        plain, _ = normalize(field_out[place].astype(f32))
+        normed[place] = (plain * gain_ref[...] + bias_ref[...]).astype(bf16)
+
+    @pl.loop(0, half // 64)
+    def _(i):
+        place = block_of(i * 64, 64)
+        both = jnp.concatenate([gated_out[place], grouped_out[place]], axis=1)
+        plain, _ = normalize(both.astype(f32))
+        normed[block_of(half + i * 64, 64)] = (plain * gain_ref[...] + bias_ref[...]).astype(bf16)
 
     over = [
         row_copy(0, normed.at[rows_of(0)], normed.at[rows_of(1)], over_x),
@@ -524,7 +532,6 @@
     down_load = pltpu.make_async_copy(down_ref, tall, local_sem.at[4])
     down_load.start()
 
-    local[5].wait()
     half_key = KEY // 2
     lanes = lax.broadcasted_iota(jnp.int32, (CHUNK, half_key), 1).astype(f32)
     frequency = jnp.exp(lanes * (-9.210340371976184 / half_key))
@@ -533,7 +540,9 @@
     @pl.loop(0, chunks)
     def _(c):
         seat = block_of(c * CHUNK, CHUNK)
-        own = info[seat, 0:1]
+        diagonal = lax.broadcasted_iota(jnp.int32, (CHUNK, CHUNK), 0) == lax.broadcasted_iota(jnp.int32, (CHUNK, CHUNK), 1)
+        own = jnp.sum(jnp.where(diagonal, jnp.maximum(row_ref[c], -1.0), 0.0), axis=1, keepdims=True)
+        info[seat, :] = jnp.broadcast_to(own, (CHUNK, 128))
         ranked = jnp.where(own < 0, 3.0, own)
         before = jnp.zeros((CHUNK, 1), f32)
         for other in range(chunks):
@@ -550,9 +559,9 @@
     for head in range(heads):
         decay[head] = jnp.where(distance >= 0, jnp.exp(rate_ref[head : head + 1, 0:1] * span), 0.0)
     down_load.wait()
-    down_turned[...] = tall[...].T
+    gate_out[...] = tall[...].T
     table_outs = [
-        pltpu.make_async_copy(down_turned, down_turned_ref, table_sem.at[3]),
+        pltpu.make_async_copy(gate_out, down_turned_ref, table_sem.at[3]),
         pltpu.make_async_copy(angles, angle_ref, table_sem.at[0]),
         pltpu.make_async_copy(decay, decay_ref, table_sem.at[1]),
     ]
@@ -621,10 +630,6 @@
             facts = jnp.where(lane == 0, own, 0.0)
             scales = jnp.zeros((CHUNK, 128), f32)
 
-            @pl.when(c > 0)
-            def _():
-                wait(chunk_outs(c - 1))
-
             for head in range(heads):
                 rate = rate_ref[head : head + 1, 0:1]
                 into = jnp.where(entering, jnp.exp(rate * (offset + 1.0)), 0.0)
@@ -637,16 +642,10 @@
                 gate = product[place, pl.ds(2 * keys + values + head * VAL, VAL)]
                 query_raw = query_raw.astype(bf16)
                 key_raw = key_raw.astype(bf16)
-                gate_low = gate.astype(bf16)
-                field_out[:, pl.ds(head * KEY, KEY)] = query_raw
-                field_out[:, pl.ds(keys + head * KEY, KEY)] = key_raw
-                field_out[:, pl.ds(2 * keys + head * VAL, VAL)] = value
-                gate_out[:, pl.ds(head * VAL, VAL)] = gate_low
                 query = turn(query_raw.astype(f32), cosine, sine).astype(bf16)
                 key = (turn(key_raw.astype(f32), cosine, sine) * key_scale).astype(bf16)
                 memory = state[head]
                 memory_low = memory.astype(bf16)
-                past_out[head] = memory_low
                 scores = dot_nt(query, key)
                 weights = (jnp.where(same, decay[head], 0.0) * scores).astype(bf16)
                 retained = dot_nn(weights, value) + into * dot_nn(query, memory_low)
@@ -656,6 +655,16 @@
                 scale = lax.rsqrt(jnp.mean(centred * centred, axis=-1, keepdims=True) + group_floor)
                 grouped = centred * scale
                 columns = pl.ds(head * VAL, VAL)
+                if head == 0:
+                    @pl.when(c > 0)
+                    def _():
+                        wait(chunk_outs(c - 1))
+
+                field_out[:, pl.ds(head * KEY, KEY)] = query_raw
+                field_out[:, pl.ds(keys + head * KEY, KEY)] = key_raw
+                field_out[:, pl.ds(2 * keys + head * VAL, VAL)] = value
+                gate_out[:, columns] = gate.astype(bf16)
+                past_out[head] = memory_low
                 gated_out[:, columns] = (gate / (1.0 + jnp.exp(-gate)) * grouped).astype(bf16)
                 grouped_out[:, columns] = grouped.astype(bf16)
                 scales = jnp.where(lane == head, scale, scales)
@@ -688,27 +697,32 @@
     normed_out.start()
     for s in (0, 1, 2):
         project(3, s)
+    when_end(False, lambda: step(1, 1))
     step(0, 3)
     twin_step(0, 3)
-    for r in range(4):
-        project(r, 3)
-    step(1, 1)
     w_outs = [
         pltpu.make_async_copy(w_qkv, w_qkv_ref, out_sem.at[0]),
         pltpu.make_async_copy(w_gate, w_gate_ref, out_sem.at[1]),
     ]
     start(w_outs)
+    project(0, 3)
+    project(1, 3)
+    when_end(False, lambda: step(1, 2))
+    wait_recv(cot_early + cot_over)
+    start(cot_onward)
+    project(2, 3)
+    project(3, 3)
 
     def between(c):
-        @pl.when(c == 2)
+        @pl.when((c == 1) & at_end)
         def _():
-            wait_recv(cot_early + cot_over)
-            start(cot_onward)
-
-        @pl.when(c == 4)
+            step(1, 1)
+
+        @pl.when((c == 4) & at_end)
         def _():
             step(1, 2)
 
+    wait(table_outs)
     retention(between)
     info_out = pltpu.make_async_copy(info, info_ref, table_sem.at[2])
     info_out.start()
@@ -726,7 +740,7 @@
             pl.when((z > 0) & (z + j < layers))(lambda: wait_send(sink(g, j)))
         for j in range(-3, 4):
             pl.when((z + j >= 0) & (z + j < layers))(lambda: wait_send(to_twin(g, j)))
-    wait(table_outs + w_outs + [normed_out, own_cot, info_out, w_out_out])
+    wait(w_outs + [normed_out, own_cot, info_out, w_out_out])
 
 
 def opening_exchange(heads, shards, tokens, cotangent, segment, gain, bias):
@@ -744,7 +758,6 @@
     here = lax.axis_index("tensor") * heads
     head_ids = (here + jnp.arange(8, dtype=jnp.int32)).astype(f32)
     rates = jnp.broadcast_to(jnp.log1p(-jnp.exp2(-5.0 - head_ids))[:, None], (8, 128))
-    wide_segment = jnp.broadcast_to(segment.astype(f32)[:, None], (rows, 128))
     row_segment = jnp.where(segment >= 0, segment, -7).astype(f32).reshape(chunks, 1, CHUNK)
     results = pl.pallas_call(
         functools.partial(opening_kernel, heads),
@@ -765,17 +778,15 @@
             jax.ShapeDtypeStruct((heads, CHUNK, CHUNK), f32),
             jax.ShapeDtypeStruct((depth, unit), bf16),
         ],
-        in_specs=[anywhere] * 9 + [in_vmem] * 4,
+        in_specs=[anywhere] * 8 + [in_vmem] * 4,
         out_specs=[anywhere] * 15,
         scratch_shapes=[
             vmem((dp * depth, 2 * keys + values), bf16),
             vmem((dp * depth, values), bf16),
             vmem((dp * depth, unit), bf16),
             vmem((unit, depth), bf16),
-            vmem((depth, unit), bf16),
             vmem((rows, width), bf16),
             vmem((rows, 2 * keys + 2 * values), f32),
-            vmem((4, 64, width), bf16),
             vmem((rows, KEY), f32),
             vmem((rows, 128), f32),
             vmem((heads, CHUNK, CHUNK), f32),
@@ -786,14 +797,14 @@
             vmem((CHUNK, values), bf16),
             vmem((CHUNK, 128), f32),
             vmem((heads, KEY, VAL), bf16),
-            sem((8,)), sem((4,)), sem((3,)), sem((6,)), sem((4,)),
+            sem((8,)), sem((3,)), sem((3,)), sem((6,)), sem((4,)),
             sem((3, 3)), sem((3, 3)), sem((3, 3)), sem((3, 3)), sem((7, 3)), sem((7, 3)), sem((10,)), sem((10,)),
         ],
         compiler_params=pltpu.CompilerParams(
             collective_id=2, has_side_effects=True, vmem_limit_bytes=63_400_000
         ),
         name="opening_exchange",
-    )(*shards, tokens, cotangent, wide_segment, row_segment, rates, gain.reshape(1, width), bias.reshape(1, width))
+    )(*shards, tokens, cotangent, row_segment, rates, gain.reshape(1, width), bias.reshape(1, width))
     return results, row_segment
 
 
@@ -1810,7 +1821,7 @@
 
 
 def cast_all(plus, parts, arrays):
-    steps = 2
+    steps = 4
 
     def slab(rows, width):
         return pl.BlockSpec((rows // steps, width), lambda j: (j, 0))
@@ -1820,11 +1831,12 @@
     out_specs, shapes = [slab(rows, width)], [jax.ShapeDtypeStruct(plus.shape, bf16)]
     for i, v in enumerate(arrays):
         rows, width = v.shape
-        in_specs.append(slab(rows, width))
         if i >= len(arrays) - 2:
-            out_specs.append(pl.BlockSpec((width, rows // steps), lambda j: (0, j)))
+            in_specs.append(pl.BlockSpec((rows, width // steps), lambda j: (0, j)))
+            out_specs.append(pl.BlockSpec((width // steps, rows), lambda j: (j, 0)))
             shapes.append(jax.ShapeDtypeStruct((width, rows), f32))
         else:
+            in_specs.append(slab(rows, width))
             out_specs.append(slab(rows, width))
             shapes.append(jax.ShapeDtypeStruct((rows, width), bf16 if i == 0 else f32))
     return pl.pallas_call(

time: 641 us -> 632 us (0.986)
  Pallas kernels: 627 us -> 620 us
where the time goes in v9:
time: 632 us; the launch traced here: 624 us
  Pallas kernels  620 us (98%)
    pallas_call x1, Pallas kernels, closing_exchange(): pl.pallas_call(functools.partial(closing_kernel, heads), out_shape=[jax.S...  234 us
    pallas_call x1, Pallas kernels, middle_exchange(): pl.pallas_call(middle_kernel, out_shape=[jax.ShapeDtypeStruct((token_rows...  225 us
    pallas_call x1, Pallas kernels, opening_exchange(): pl.pallas_call(functools.partial(opening_kernel, heads), out_shape=[jax.S...  153 us

profile of v9, /device:TPU:0, one launch (start us, length us, event | category | flops | bytes accessed | tf_op | source)
XLA Modules:
  0.0 623.6 jit_solution(747547271604229999)
XLA Ops:
  0.6 1.3 fusion
  2.0 0.7 broadcast_in_dim.11.rate_ref
  2.6 152.9 %opening_exchange.1 = (bf16[2048,2048]{1,0:T(8,128)(2,1)}, bf16[2048,1024]{1,0:T(8,128)(2,1)}, bf16[2048,1024]{1,0:T(8,128)(2,1)}, bf16[2048,2048]{1,0:T(8,128)(...) custom-call(bf16[256,512]{1,0:T(8,128)(2,1)} %query_ref.1, ...), custom_call_target="tpu_custom_call" | custom-call | tf_op jit(solution)/shard_map/opening_exchange/pallas_call | solution.py:762
  155.6 224.5 %middle_exchange.1 = (bf16[512,2048]{1,0:T(8,128)(2,1)}, bf16[512,2048]{1,0:T(8,128)(2,1)}, bf16[2048,2048]{1,0:T(8,128)(2,1)}, bf16[2048,1024]{1,0:T(8,128)(2,1...) custom-call(bf16[2048,1024]{1,0:T(8,128)(2,1)} %get-tuple-element.53.gated_ref, ...), custom_call_target="tpu_custom_call" | custom-call | tf_op jit(solution)/shard_map/middle_exchange/pallas_call | solution.py:1178
  380.1 234.5 %closing_exchange.1 = (bf16[2,512,2048]{2,1,0:T(8,128)(2,1)}, bf16[512,2048]{1,0:T(8,128)(2,1)}, bf16[256,512]{1,0:T(8,128)(2,1)}, bf16[256,512]{1,0:T(8,128)(2,...) custom-call(bf16[2048,2048]{1,0:T(8,128)(2,1)} %get-tuple-element.58, ...), custom_call_target="tpu_custom_call" | custom-call | tf_op jit(solution)/shard_map/closing_exchange/pallas_call | solution.py:1864
  614.6 0.0 copy-start
  614.6 7.9 %last_casts.1 = (bf16[512,2048]{1,0:T(8,128)(2,1)}, bf16[512,2048]{1,0:T(8,128)(2,1)}, f32[256,512]{1,0:T(8,128)}, f32[256,512]{1,0:T(8,128)}, f32[256,1024]{1,0...) custom-call(bf16[512,2048]{1,0:T(8,128)(2,1)} %get-tuple-element.57.plus_ref, ...), custom_call_target="tpu_custom_call" | custom-call | tf_op jit(solution)/shard_map/last_casts/pallas_call | solution.py:1842
  622.5 0.0 copy-done
  622.6 0.1 constant_dynamic-slice_fusion
  622.6 0.5 slice_bitcast_fusion
  (1 shorter events, 0.0 us)
Async XLA Ops:
  614.6 8.0 %copy-start = (f32[8,128]{1,0:T(8,128)S(1)}, f32[8,128]{1,0:T(8,128)}, u32[]{:S(2)}) copy-start(f32[8,128]{1,0:T(8,128)} %get-tuple-element.85) | copy-start | bytes 12292

commit v10 on v9

--- a/solution.py
+++ b/solution.py
@@ -928,14 +928,20 @@
         remote(terms.at[2, pl.ds(half, half)], half_in.at[1], half_send.at[1], half_recv.at[1], over_y),
     ]
 
-    def part_copy(index, term, first, device):
-        place = pl.ds(first, half)
+    def part_copy(index, term, first, device, count=half):
+        place = pl.ds(first, count)
         return remote(
             terms.at[term, place], full_in.at[term, place], full_send.at[index], full_recv.at[index], device
         )
 
     plain_parts = [part_copy(0, 0, 0, over_x), part_copy(1, 1, half, over_y)]
-    grown_parts = [part_copy(2, 0, half, over_x), part_copy(3, 1, 0, over_y)]
+    quarter = half // 2
+    grown_parts = [
+        part_copy(2, 0, half, over_x, quarter),
+        part_copy(3, 1, 0, over_y, quarter),
+        part_copy(4, 0, half + quarter, over_x, quarter),
+        part_copy(5, 1, quarter, over_y, quarter),
+    ]
     fulls = plain_parts + grown_parts
     lower, upper = (0, half), (half, half)
 
@@ -966,7 +972,7 @@
                 terms[term, place] = grown.astype(bf16)
 
         for i, copy in enumerate(grown_parts):
-            if stage == 0:
+            if stage == 0 and i < 2:
                 pl.semaphore_signal(half_free.at[i], inc=1, device_id=sides[i], device_id_type=MESH)
             copy.start()
 
@@ -1033,8 +1039,6 @@
     gathered(1)
     token_load.wait()
     pl.semaphore_wait(big_free, 2)
-    for copy in fulls:
-        copy.wait_recv()
 
     def second_norm(i):
         place = block_of(i * 64, 64)
@@ -1044,9 +1048,15 @@
         plain, _ = normalize(value)
         big[place] = (plain * gain_ref[...] + bias_ref[...]).astype(bf16)
 
-    pl.loop(0, half // 64)(second_norm)
+    for copy in plain_parts + grown_parts[:2]:
+        copy.wait_recv()
+    pl.loop(0, quarter // 64)(second_norm)
+    pl.loop(half // 64, (half + quarter) // 64)(second_norm)
+    for copy in grown_parts[2:]:
+        copy.wait_recv()
+    pl.loop(quarter // 64, half // 64)(second_norm)
     early[0].start()
-    pl.loop(half // 64, rows // 64)(second_norm)
+    pl.loop((half + quarter) // 64, rows // 64)(second_norm)
     early[1].start()
     for i, side in enumerate(sides):
         pl.semaphore_signal(full_free.at[i], inc=1, device_id=side, device_id_type=MESH)
@@ -1134,11 +1144,8 @@
     cot_own.start()
     total[...] = jnp.zeros_like(total)
     cot_own.wait()
-    for copy in fulls:
-        copy.wait_recv()
-
-    @pl.loop(0, rows // 64)
-    def _(i):
+
+    def second_norm_back(i):
         place = block_of(i * 64, 64)
         grad = terms[3, place].astype(f32) + full_in[0, place].astype(f32) + full_in[1, place].astype(f32)
         plain, scale = normalize(mixed[place])
@@ -1147,6 +1154,14 @@
         total[0:1, :] += jnp.sum(grad * plain, axis=0, keepdims=True)
         total[1:2, :] += jnp.sum(grad, axis=0, keepdims=True)
 
+    for copy in plain_parts + grown_parts[:2]:
+        copy.wait_recv()
+    pl.loop(0, quarter // 64)(second_norm_back)
+    pl.loop(half // 64, (half + quarter) // 64)(second_norm_back)
+    for copy in grown_parts[2:]:
+        copy.wait_recv()
+    pl.loop(quarter // 64, half // 64)(second_norm_back)
+    pl.loop((half + quarter) // 64, rows // 64)(second_norm_back)
     low_out = pltpu.make_async_copy(full_in.at[0], low_ref, out_sem.at[1])
     low_out.start()
     late_ref[...] = total[...]
@@ -1200,7 +1215,7 @@
             vmem((2, width), f32),
             sem((8,)), sem((4,)), sem((2,)), sem((2,)), sem((2,)),
             sem((2, 3)), sem((2, 3)), sem((2, 3)), sem((2, 3)), sem((2, 7)), sem((2, 7)),
-            sem((6,)), sem((6,)), sem((2,)), sem((2,)), sem((4,)), sem((4,)),
+            sem((6,)), sem((6,)), sem((2,)), sem((2,)), sem((6,)), sem((6,)),
             regular((2,)), regular((2,)), regular,
         ],
         compiler_params=pltpu.CompilerParams(
@@ -1292,7 +1307,7 @@
             copy.wait_send()
 
 
-    sources = [up_ref, down_ref, normed1_ref, None, normed1_ref, normed1_ref]
+    sources = [up_ref, down_ref, None, normed1_ref, normed1_ref, normed1_ref]
 
     def given_copy(r, k):
         place = block_of(targets[k] * 2 * depth, 2 * depth)
@@ -1339,7 +1354,7 @@
             product = None
             for place in (pl.ds(0, 2 * rows), pl.ds(2 * rows, 2 * rows)):
                 if r < 4:
-                    right = units[(None, None, 0, 2)[r], place, tile]
+                    right = units[(None, None, 2, 0)[r], place, tile]
                 else:
                     right = big[place, block_of((r - 4) * unit + j * 512, 512)]
                 if sources[r] is None:
@@ -1405,7 +1420,7 @@
                 pltpu.make_async_copy(slot.at[mine, pl.ds(0, keys)], query_out, out_sem.at[0, 0]),
                 pltpu.make_async_copy(slot.at[mine, pl.ds(keys, keys)], key_out, out_sem.at[0, 1]),
             ]
-        out = (up_out, down_out, gate_out, out_out, None, value_out)[r]
+        out = (up_out, down_out, out_out, gate_out, None, value_out)[r]
         return [pltpu.make_async_copy(slot.at[mine], out, out_sem.at[r % 2, 0])]
 
     def finish(r):
@@ -1444,14 +1459,20 @@
         remote(terms.at[2, pl.ds(half, half)], half_in.at[1], half_send.at[1], half_recv.at[1], over_y),
     ]
 
-    def part_copy(index, term, first, device):
-        place = pl.ds(first, half)
+    def part_copy(index, term, first, device, count=half):
+        place = pl.ds(first, count)
         return remote(
             terms.at[term, place], full_in.at[term, place], full_send.at[index], full_recv.at[index], device
         )
 
     plain_parts = [part_copy(0, 0, 0, over_x), part_copy(1, 1, half, over_y)]
-    grown_parts = [part_copy(2, 0, half, over_x), part_copy(3, 1, 0, over_y)]
+    quarter = half // 2
+    grown_parts = [
+        part_copy(2, 0, half, over_x, quarter),
+        part_copy(3, 1, 0, over_y, quarter),
+        part_copy(4, 0, half + quarter, over_x, quarter),
+        part_copy(5, 1, quarter, over_y, quarter),
+    ]
     fulls = plain_parts + grown_parts
     sides = (over_x, over_y)
 
@@ -1472,7 +1493,7 @@
                 terms[term, place] = grown.astype(bf16)
 
         for i, copy in enumerate(grown_parts):
-            if stage == 0:
+            if stage == 0 and i < 2:
                 pl.semaphore_signal(half_free.at[i], inc=1, device_id=sides[i], device_id_type=MESH)
             copy.start()
 
@@ -1593,6 +1614,18 @@
 
             between(step)
 
+    blocks = width // columns.shape[2]
+    last_loads = [
+        pltpu.make_async_copy(
+            ref.at[:, pl.ds(q * columns.shape[2], columns.shape[2])], columns.at[i, rows_of(q)], chunk_sem.at[i, q]
+        )
+        for i, ref in enumerate((token_ref, low_ref))
+        for q in range(blocks)
+    ]
+
+    def laid_out(slot, i):
+        return jnp.concatenate([columns[slot, block_of(q * rows + i * 64, 64)] for q in range(blocks)], axis=1)
+
 
     own_load = pltpu.make_async_copy(low_ref, big.at[rows_of(0)], mixed_sem.at[0])
     own_load.start()
@@ -1630,92 +1663,83 @@
         send_to_twin(1, k)
         settle(*((1, k - 1) if k > 0 else (0, 3)))
     wait(out_load)
+    settle(1, 3)
     pass_on(0, 0)
-    pass_on(0, 1)
     push(1, 0)
     gate_back(0)
     start(gate_copies(2))
-    push(1, 1)
     wait_recv(over)
     start(onward)
+    pass_on(0, 1)
     gate_back(1)
     start(gate_copies(3))
-    settle(1, 3)
+    push(1, 1)
     gate_back(2)
     pass_on(0, 2)
     pass_on(1, 0)
+    push(1, 2)
     finish(0)
-    pass_on(1, 1)
-    push(1, 2)
     wait_recv(onward)
     wait(feed_load)
     send_halves(0)
     send_plain(0, 0)
     send_plain(0, 1)
-    gate_back(3)
-    prefetch(2)
-    start(w_gate_load)
+    wait(gated_load)
     multiply(2, 0)
+    multiply(2, 1)
     pass_on(1, 2)
     settle(2, 0)
     push(2, 0)
-    multiply(2, 1)
+    pass_on(1, 1)
+    gate_back(3)
+    prefetch(3)
+    start(w_gate_load)
+    settle(2, 1)
     multiply(2, 2)
-    settle(2, 1)
     multiply(2, 3)
-    start(chunk_copies(chunks - 1, 0))
+    start(w_value_load)
     settle(2, 2)
+    push(2, 1)
+    multiply(3, 0)
     finish(1)
-    push(2, 1)
-    wait(gated_load)
-    multiply(3, 0)
-    pass_on(2, 0)
+    push(2, 2)
     settle(2, 3)
     multiply(3, 1)
+    take_halves(0)
     settle(3, 0)
+    pass_on(2, 0)
     multiply(3, 2)
-    push(2, 2)
     settle(3, 1)
     multiply(3, 3)
-    start(w_value_load)
+    start(chunk_copies(chunks - 1, 0))
+    push(3, 0)
     wait_send(over + onward)
     state_ref[...] = jnp.zeros_like(state_ref)
 
     def between(step):
-        @pl.when(step == 0)
-        def _():
-            push(3, 0)
-
         @pl.when(step == 1)
         def _():
+            pass_on(2, 2)
             pass_on(2, 1)
-
-        @pl.when(step == 4)
+            settle(3, 2)
+
+        @pl.when(step == 2)
         def _():
-            take_halves(0)
-
-        @pl.when(step == 5)
-        def _():
-            settle(3, 2)
-            pass_on(2, 2)
             push(3, 1)
 
     retention_steps(between)
     start(w_key_load)
     prefetch(4)
+    settle(3, 3)
+    multiply(4, 0)
+    push(3, 2)
+    pass_on(3, 0)
+    finish(2)
+    multiply(4, 1)
     wait_send(halves)
     wait(w_gate_load + w_value_load + w_key_load)
     project(3)
-    pass_on(3, 0)
-    settle(3, 3)
     send_halves(1)
-    push(3, 2)
-    finish(2)
-    multiply(4, 0)
-    settle(4, 0)
-    multiply(4, 1)
-    pass_on(3, 1)
-    push(4, 0)
     wait_recv(fulls)
     result_copy = pltpu.make_async_copy(full_in, result_ref, mixed_sem.at[1])
     result_copy.start()
@@ -1723,60 +1747,62 @@
     for i, side in enumerate(sides):
         pl.semaphore_signal(full_free.at[i], inc=1, device_id=side, device_id_type=MESH)
     wait_send(fulls)
+    pass_on(3, 1)
+    settle(4, 0)
+    push(4, 0)
+    pass_on(3, 2)
+    multiply(4, 2)
+    settle(4, 1)
+    project(2)
+    push(4, 1)
+    settle(4, 2)
     project(1)
+    pass_on(4, 0)
     send_plain(1, 0)
-    pass_on(3, 2)
-    settle(4, 1)
-    multiply(4, 2)
-    push(4, 1)
-    project(2)
     send_plain(1, 1)
-    settle(4, 2)
+    multiply(4, 3)
+    finish(3)
     push(4, 2)
-    multiply(4, 3)
-    pass_on(4, 0)
-    finish(3)
+    pass_on(4, 2)
+    pass_on(4, 1)
+    take_halves(1)
+    settle(4, 3)
     multiply(5, 0)
-    settle(4, 3)
     multiply(5, 1)
     settle(5, 0)
-    pass_on(4, 1)
+    push(5, 0)
+    multiply(5, 2)
     settle(5, 1)
-    push(5, 0)
-    pass_on(4, 2)
-    multiply(5, 2)
-    take_halves(1)
-    multiply(5, 3)
+    settle(5, 2)
+    finish(4)
     pass_on(5, 0)
     push(5, 1)
-    finish(4)
+    multiply(5, 3)
+    start(last_loads)
     wait_send(halves)
     project(0)
-    settle(5, 2)
-    push(5, 2)
     pass_on(5, 1)
     pass_on(5, 2)
-    for copy in fulls:
-        copy.wait_recv()
-        copy.wait_send()
-    last_loads = [
-        pltpu.make_async_copy(token_ref, terms.at[0], mixed_sem.at[2]),
-        pltpu.make_async_copy(low_ref, terms.at[1], mixed_sem.at[0]),
-    ]
-    start(last_loads)
+    push(5, 2)
+    settle(5, 3)
     total[...] = jnp.zeros_like(total)
     wait(last_loads)
 
-    @pl.loop(0, rows // 64)
-    def _(i):
+    def first_norm_back(i):
         place = block_of(i * 64, 64)
         normed_grad = terms[2, place].astype(f32) + full_in[0, place].astype(f32) + full_in[1, place].astype(f32)
-        plain, scale = normalize(terms[0, place].astype(f32))
-        grad = terms[1, place].astype(f32) + normalize_back(normed_grad, plain, scale, gain_ref[...])
+        plain, scale = normalize(laid_out(0, i).astype(f32))
+        grad = laid_out(1, i).astype(f32) + normalize_back(normed_grad, plain, scale, gain_ref[...])
         full_in[0, place] = grad.astype(bf16)
         total[0:1, :] += jnp.sum(normed_grad * plain, axis=0, keepdims=True)
         total[1:2, :] += jnp.sum(normed_grad, axis=0, keepdims=True)
 
+    wait_recv(plain_parts + grown_parts[:2])
+    pl.loop(0, quarter // 64)(first_norm_back)
+    pl.loop(half // 64, (half + quarter) // 64)(first_norm_back)
+    wait_recv(grown_parts[2:])
+    pl.loop(quarter // 64, half // 64)(first_norm_back)
+    pl.loop((half + quarter) // 64, rows // 64)(first_norm_back)
     grad_copy = pltpu.make_async_copy(full_in.at[0], grad_ref, mixed_sem.at[3])
     grad_copy.start()
 
@@ -1799,9 +1825,9 @@
         sum_copy(k).wait()
         sums_ref[...] += landed[k]
 
-    settle(5, 3)
     finish(5)
 
+    wait_send(fulls)
     for r in (4, 5):
         for k in range(4):
             to_twin(r, k).wait_send()
@@ -1897,7 +1923,7 @@
             vmem((8, width), f32),
             sem((10,)), sem((8,)), sem((2, 12)), sem((2, 2)), sem((4,)),
             sem((2,)), sem((2,)), sem((2,)), sem((2,)),
-            sem((2,)), sem((2,)), sem((4,)), sem((4,)),
+            sem((2,)), sem((2,)), sem((6,)), sem((6,)),
             sem((2, 4)), sem((2,)), sem((2, 3)), sem((5,)), sem((32,)), sem((32,)),
             regular((2,)), regular((3,)), regular((2,)), regular((2,)),
         ],

time: 632 us -> 625 us (0.989)
  Pallas kernels: 620 us -> 612 us
where the time goes in v10:
time: 625 us; the launch traced here: 616 us
  Pallas kernels  612 us (98%)
    pallas_call x1, Pallas kernels, closing_exchange(): pl.pallas_call(functools.partial(closing_kernel, heads), out_shape=[jax.S...  229 us
    pallas_call x1, Pallas kernels, middle_exchange(): pl.pallas_call(middle_kernel, out_shape=[jax.ShapeDtypeStruct((token_rows...  223 us
    pallas_call x1, Pallas kernels, opening_exchange(): pl.pallas_call(functools.partial(opening_kernel, heads), out_shape=[jax.S...  153 us

profile of v10, /device:TPU:0, one launch (start us, length us, event | category | flops | bytes accessed | tf_op | source)
XLA Modules:
  0.0 616.1 jit_solution(8177116202518562528)
XLA Ops:
  0.6 1.3 fusion
  2.0 0.7 broadcast_in_dim.11.rate_ref
  2.6 152.9 %opening_exchange.1 = (bf16[2048,2048]{1,0:T(8,128)(2,1)}, bf16[2048,1024]{1,0:T(8,128)(2,1)}, bf16[2048,1024]{1,0:T(8,128)(2,1)}, bf16[2048,2048]{1,0:T(8,128)(...) custom-call(bf16[256,512]{1,0:T(8,128)(2,1)} %query_ref.1, ...), custom_call_target="tpu_custom_call" | custom-call | tf_op jit(solution)/shard_map/opening_exchange/pallas_call | solution.py:762
  155.6 222.7 %middle_exchange.1 = (bf16[512,2048]{1,0:T(8,128)(2,1)}, bf16[512,2048]{1,0:T(8,128)(2,1)}, bf16[2048,2048]{1,0:T(8,128)(2,1)}, bf16[2048,1024]{1,0:T(8,128)(2,1...) custom-call(bf16[2048,1024]{1,0:T(8,128)(2,1)} %get-tuple-element.53.gated_ref, ...), custom_call_target="tpu_custom_call" | custom-call | tf_op jit(solution)/shard_map/middle_exchange/pallas_call | solution.py:1193
  378.3 228.8 %closing_exchange.1 = (bf16[2,512,2048]{2,1,0:T(8,128)(2,1)}, bf16[512,2048]{1,0:T(8,128)(2,1)}, bf16[256,512]{1,0:T(8,128)(2,1)}, bf16[256,512]{1,0:T(8,128)(2,...) custom-call(bf16[2048,2048]{1,0:T(8,128)(2,1)} %get-tuple-element.58, ...), custom_call_target="tpu_custom_call" | custom-call | tf_op jit(solution)/shard_map/closing_exchange/pallas_call | solution.py:1890
  607.1 0.0 copy-start
  607.1 7.9 %last_casts.1 = (bf16[512,2048]{1,0:T(8,128)(2,1)}, bf16[512,2048]{1,0:T(8,128)(2,1)}, f32[256,512]{1,0:T(8,128)}, f32[256,512]{1,0:T(8,128)}, f32[256,1024]{1,0...) custom-call(bf16[512,2048]{1,0:T(8,128)(2,1)} %get-tuple-element.57.plus_ref, ...), custom_call_target="tpu_custom_call" | custom-call | tf_op jit(solution)/shard_map/last_casts/pallas_call | solution.py:1868
  615.0 0.0 copy-done
  615.0 0.1 constant_dynamic-slice_fusion
  615.1 0.5 slice_bitcast_fusion
  (1 shorter events, 0.0 us)
Async XLA Ops:
  607.1 8.0 %copy-start = (f32[8,128]{1,0:T(8,128)S(1)}, f32[8,128]{1,0:T(8,128)}, u32[]{:S(2)}) copy-start(f32[8,128]{1,0:T(8,128)} %get-tuple-element.85) | copy-start | bytes 12292

commit v11 on v10

--- a/solution.py
+++ b/solution.py
@@ -852,9 +852,9 @@
         pltpu.make_async_copy(down_ref, units.at[3, mine], load_sem.at[0]),
         pltpu.make_async_copy(up_ref, units.at[2, mine], load_sem.at[1]),
     ]
-    first_loads = [
-        pltpu.make_async_copy(gated_ref, units.at[0], load_sem.at[2]),
-        pltpu.make_async_copy(w_out_ref, units.at[1], load_sem.at[3]),
+    first_loads = [pltpu.make_async_copy(w_out_ref, units.at[1], load_sem.at[3])] + [
+        pltpu.make_async_copy(gated_ref.at[pl.ds(r * rows, rows)], units.at[0, pl.ds(r * rows, rows)], load_sem.at[8 + r])
+        for r in (3, 1, 2, 0)
     ]
     token_load = pltpu.make_async_copy(token_ref, plus, load_sem.at[5])
     cot_load = pltpu.make_async_copy(cot_ref, big, load_sem.at[6])
@@ -1012,9 +1012,10 @@
 
 
     first_step(0)
-    wait(first_loads)
+    wait(first_loads[:2])
     branch_term(3)
     send_halves(0)
+    wait(first_loads[2:])
     step(0, 1)
     branch_term(1)
     send_plain(0, 0)
@@ -1213,7 +1214,7 @@
             vmem((token_rows, width), f32),
             vmem((token_rows, width), bf16),
             vmem((2, width), f32),
-            sem((8,)), sem((4,)), sem((2,)), sem((2,)), sem((2,)),
+            sem((12,)), sem((4,)), sem((2,)), sem((2,)), sem((2,)),
             sem((2, 3)), sem((2, 3)), sem((2, 3)), sem((2, 3)), sem((2, 7)), sem((2, 7)),
             sem((6,)), sem((6,)), sem((2,)), sem((2,)), sem((6,)), sem((6,)),
             regular((2,)), regular((2,)), regular,
@@ -1447,8 +1448,8 @@
         return pl.ds(r * rows + first, count)
 
     over = [
-        remote(big.at[rows_of(0)], big.at[rows_of(1)], over_send.at[0], over_recv.at[0], over_x),
-        remote(big.at[rows_of(0)], big.at[rows_of(2)], over_send.at[1], over_recv.at[1], over_y),
+        remote(low_ref, big.at[rows_of(1)], over_send.at[0], over_recv.at[0], over_x),
+        remote(low_ref, big.at[rows_of(2)], over_send.at[1], over_recv.at[1], over_y),
     ]
     onward = [
         remote(big.at[rows_of(2, 0, half)], big.at[rows_of(3, 0, half)], onward_send.at[0], onward_recv.at[0], over_x),
@@ -1650,7 +1651,6 @@
 
     pl.semaphore_wait(barrier, peers - 1)
 
-    own_load.wait()
     start(over)
     for k in range(4):
         given_copy(0, k).wait()
@@ -1663,6 +1663,7 @@
         send_to_twin(1, k)
         settle(*((1, k - 1) if k > 0 else (0, 3)))
     wait(out_load)
+    own_load.wait()
     settle(1, 3)
     pass_on(0, 0)
     push(1, 0)

time: 625 us -> 620 us (level)
  no operation moved by 1% of the time
where the time goes in v11:
time: 620 us; the launch traced here: 611 us
  Pallas kernels  607 us (98%)
    pallas_call x1, Pallas kernels, closing_exchange(): pl.pallas_call(functools.partial(closing_kernel, heads), out_shape=[jax.S...  224 us
    pallas_call x1, Pallas kernels, middle_exchange(): pl.pallas_call(middle_kernel, out_shape=[jax.ShapeDtypeStruct((token_rows...  222 us
    pallas_call x1, Pallas kernels, opening_exchange(): pl.pallas_call(functools.partial(opening_kernel, heads), out_shape=[jax.S...  153 us

profile of v11, /device:TPU:0, one launch (start us, length us, event | category | flops | bytes accessed | tf_op | source)
XLA Modules:
  0.0 611.1 jit_solution(5240548408687922172)
XLA Ops:
  0.6 1.3 fusion
  2.0 0.7 broadcast_in_dim.11.rate_ref
  2.6 152.9 %opening_exchange.1 = (bf16[2048,2048]{1,0:T(8,128)(2,1)}, bf16[2048,1024]{1,0:T(8,128)(2,1)}, bf16[2048,1024]{1,0:T(8,128)(2,1)}, bf16[2048,2048]{1,0:T(8,128)(...) custom-call(bf16[256,512]{1,0:T(8,128)(2,1)} %query_ref.1, ...), custom_call_target="tpu_custom_call" | custom-call | tf_op jit(solution)/shard_map/opening_exchange/pallas_call | solution.py:762
  155.6 222.1 %middle_exchange.1 = (bf16[512,2048]{1,0:T(8,128)(2,1)}, bf16[512,2048]{1,0:T(8,128)(2,1)}, bf16[2048,2048]{1,0:T(8,128)(2,1)}, bf16[2048,1024]{1,0:T(8,128)(2,1...) custom-call(bf16[2048,1024]{1,0:T(8,128)(2,1)} %get-tuple-element.53.gated_ref, ...), custom_call_target="tpu_custom_call" | custom-call | tf_op jit(solution)/shard_map/middle_exchange/pallas_call | solution.py:1194
  377.6 224.4 %closing_exchange.1 = (bf16[2,512,2048]{2,1,0:T(8,128)(2,1)}, bf16[512,2048]{1,0:T(8,128)(2,1)}, bf16[256,512]{1,0:T(8,128)(2,1)}, bf16[256,512]{1,0:T(8,128)(2,...) custom-call(bf16[2048,2048]{1,0:T(8,128)(2,1)} %get-tuple-element.58, ...), custom_call_target="tpu_custom_call" | custom-call | tf_op jit(solution)/shard_map/closing_exchange/pallas_call | solution.py:1891
  602.0 0.0 copy-start
  602.0 7.9 %last_casts.1 = (bf16[512,2048]{1,0:T(8,128)(2,1)}, bf16[512,2048]{1,0:T(8,128)(2,1)}, f32[256,512]{1,0:T(8,128)}, f32[256,512]{1,0:T(8,128)}, f32[256,1024]{1,0...) custom-call(bf16[512,2048]{1,0:T(8,128)(2,1)} %get-tuple-element.57.plus_ref, ...), custom_call_target="tpu_custom_call" | custom-call | tf_op jit(solution)/shard_map/last_casts/pallas_call | solution.py:1869
  610.0 0.0 copy-done
  610.0 0.1 constant_dynamic-slice_fusion
  610.1 0.5 slice_bitcast_fusion
  (1 shorter events, 0.0 us)
Async XLA Ops:
  602.0 8.0 %copy-start = (f32[8,128]{1,0:T(8,128)S(1)}, f32[8,128]{1,0:T(8,128)}, u32[]{:S(2)}) copy-start(f32[8,128]{1,0:T(8,128)} %get-tuple-element.85) | copy-start | bytes 12292

commit v12 on v11

--- a/solution.py
+++ b/solution.py
@@ -707,11 +707,15 @@
     start(w_outs)
     project(0, 3)
     project(1, 3)
+    def hand_on():
+        wait_recv(cot_early + cot_over)
+        start(cot_onward)
+
     when_end(False, lambda: step(1, 2))
-    wait_recv(cot_early + cot_over)
-    start(cot_onward)
+    when_end(False, hand_on)
     project(2, 3)
     project(3, 3)
+    when_end(True, hand_on)
 
     def between(c):
         @pl.when((c == 1) & at_end)
@@ -726,11 +730,18 @@
     retention(between)
     info_out = pltpu.make_async_copy(info, info_ref, table_sem.at[2])
     info_out.start()
+
+    def layer_out(s):
+        place = block_of(order[s] * 2 * depth, 2 * depth)
+        return pltpu.make_async_copy(w_out.at[place], w_out_ref.at[place], out_sem.at[2 + s])
+
+    for j in range(3):
+        twin_step(1, j)
+    for s in range(3):
+        layer_out(s).start()
     step(1, 3)
-    for j in range(4):
-        twin_step(1, j)
-    w_out_out = pltpu.make_async_copy(w_out, w_out_ref, out_sem.at[2])
-    w_out_out.start()
+    twin_step(1, 3)
+    layer_out(3).start()
     wait_recv(cot_onward)
 
     wait_send(over + onward + cot_early + cot_over + cot_onward)
@@ -740,7 +751,7 @@
             pl.when((z > 0) & (z + j < layers))(lambda: wait_send(sink(g, j)))
         for j in range(-3, 4):
             pl.when((z + j >= 0) & (z + j < layers))(lambda: wait_send(to_twin(g, j)))
-    wait(w_outs + [normed_out, own_cot, info_out, w_out_out])
+    wait(w_outs + [normed_out, own_cot, info_out] + [layer_out(s) for s in range(4)])
 
 
 def opening_exchange(heads, shards, tokens, cotangent, segment, gain, bias):
@@ -797,7 +808,7 @@
             vmem((CHUNK, values), bf16),
             vmem((CHUNK, 128), f32),
             vmem((heads, KEY, VAL), bf16),
-            sem((8,)), sem((3,)), sem((3,)), sem((6,)), sem((4,)),
+            sem((8,)), sem((3,)), sem((6,)), sem((6,)), sem((4,)),
             sem((3, 3)), sem((3, 3)), sem((3, 3)), sem((3, 3)), sem((7, 3)), sem((7, 3)), sem((10,)), sem((10,)),
         ],
         compiler_params=pltpu.CompilerParams(

time: 620 us -> 616 us (level)
  no operation moved by 1% of the time
where the time goes in v12:
time: 616 us; the launch traced here: 608 us
  Pallas kernels  605 us (98%)
    pallas_call x1, Pallas kernels, closing_exchange(): pl.pallas_call(functools.partial(closing_kernel, heads), out_shape=[jax.S...  224 us
    pallas_call x1, Pallas kernels, middle_exchange(): pl.pallas_call(middle_kernel, out_shape=[jax.ShapeDtypeStruct((token_rows...  220 us
    pallas_call x1, Pallas kernels, opening_exchange(): pl.pallas_call(functools.partial(opening_kernel, heads), out_shape=[jax.S...  152 us

profile of v12, /device:TPU:0, one launch (start us, length us, event | category | flops | bytes accessed | tf_op | source)
XLA Modules:
  0.0 608.2 jit_solution(17242275970676436928)
XLA Ops:
  0.6 1.3 fusion
  2.0 0.7 broadcast_in_dim.11.rate_ref
  2.6 152.1 %opening_exchange.1 = (bf16[2048,2048]{1,0:T(8,128)(2,1)}, bf16[2048,1024]{1,0:T(8,128)(2,1)}, bf16[2048,1024]{1,0:T(8,128)(2,1)}, bf16[2048,2048]{1,0:T(8,128)(...) custom-call(bf16[256,512]{1,0:T(8,128)(2,1)} %query_ref.1, ...), custom_call_target="tpu_custom_call" | custom-call | tf_op jit(solution)/shard_map/opening_exchange/pallas_call | solution.py:773
  154.8 220.3 %middle_exchange.1 = (bf16[512,2048]{1,0:T(8,128)(2,1)}, bf16[512,2048]{1,0:T(8,128)(2,1)}, bf16[2048,2048]{1,0:T(8,128)(2,1)}, bf16[2048,1024]{1,0:T(8,128)(2,1...) custom-call(bf16[2048,1024]{1,0:T(8,128)(2,1)} %get-tuple-element.53.gated_ref, ...), custom_call_target="tpu_custom_call" | custom-call | tf_op jit(solution)/shard_map/middle_exchange/pallas_call | solution.py:1205
  375.1 224.4 %closing_exchange.1 = (bf16[2,512,2048]{2,1,0:T(8,128)(2,1)}, bf16[512,2048]{1,0:T(8,128)(2,1)}, bf16[256,512]{1,0:T(8,128)(2,1)}, bf16[256,512]{1,0:T(8,128)(2,...) custom-call(bf16[2048,2048]{1,0:T(8,128)(2,1)} %get-tuple-element.58, ...), custom_call_target="tpu_custom_call" | custom-call | tf_op jit(solution)/shard_map/closing_exchange/pallas_call | solution.py:1902
  599.4 0.0 copy-start
  599.5 7.9 %last_casts.1 = (bf16[512,2048]{1,0:T(8,128)(2,1)}, bf16[512,2048]{1,0:T(8,128)(2,1)}, f32[256,512]{1,0:T(8,128)}, f32[256,512]{1,0:T(8,128)}, f32[256,1024]{1,0...) custom-call(bf16[512,2048]{1,0:T(8,128)(2,1)} %get-tuple-element.57.plus_ref, ...), custom_call_target="tpu_custom_call" | custom-call | tf_op jit(solution)/shard_map/last_casts/pallas_call | solution.py:1880
  607.4 0.0 copy-done
  607.4 0.1 constant_dynamic-slice_fusion
  607.5 0.5 slice_bitcast_fusion
  (1 shorter events, 0.0 us)
Async XLA Ops:
  599.4 8.0 %copy-start = (f32[8,128]{1,0:T(8,128)S(1)}, f32[8,128]{1,0:T(8,128)}, u32[]{:S(2)}) copy-start(f32[8,128]{1,0:T(8,128)} %get-tuple-element.85) | copy-start | bytes 12292
